TPU v7x, 32 devices: a whole 2x2x4 slice. The times are simulated.
32 devices in a mesh: parts: 2 (over y), ctx: 4 (over z), mp: 4 (over x, core).
Axes of the slice: x: 2, y: 2, z: 4, core: 2. Of those that a mesh axis runs over, the one named last changes fastest.
Arguments:
- inputs: bfloat16 [1024, 3, 4096], P(('parts', 'ctx'), None, 'mp'), parts along dimension 0, may hold values from -6 to 6
- short_filter: bfloat16 [3, 3, 4096], P(None, None, 'mp'), may hold values from -3.5 to 3.5
- long_filter: bfloat16 [256, 128], P('mp'), may hold values from -0.5 to 0.5
- skip_gain: float32 [4096], P('mp'), may hold values from -1 to 1
- queries: bfloat16 [1024, 4096], P(('parts', 'ctx'), 'mp'), parts along dimension 0, may hold values from -6 to 6
- key_rows: bfloat16 [1024, 4096], P(('parts', 'ctx'), 'mp'), parts along dimension 0, may hold values from -6 to 6
- out_weight: bfloat16 [4096, 4096], P('mp'), may hold values from -0.25 to 0.25
Outputs:
- block_output: bfloat16 [1024, 4096], P(('parts', 'ctx'), 'mp'), parts along dimension 0
There are 2 independent parts, one for each index of `parts`. A program takes and returns all parts, laid end to end along the dimension named above; an argument that names none is the same for every part. Nothing has to cross between parts.
All inputs are finite; a program needn't handle non-finite values.
Results may differ from a plain program's by a relative error of at most 0.014.
Values may be sent and summed in bfloat16 or wider, within the bound.
No kernel may reach another device: no remote copies, remote signals or barrier semaphores. Data moves between devices by JAX's collectives and lax.ppermute only.
A program may use at most 64 MiB of HBM per device.

v0:
```python
import jax
import jax.numpy as jnp
from jax import lax
from jax.sharding import PartitionSpec as P

HEAD_DIM = 128


masked_score = -1e30


def passed_along(value, axis, steps):
    count = lax.axis_size(axis)
    initial, last = (max(0, -steps), min(count, count - steps))
    return lax.ppermute(value, axis, [(source, source + steps) for source in range(initial, last)])


def toeplitz_taps(filters, row_count):
    group_count = filters.shape[0]
    tap_count = filters.shape[1]
    span = row_count + tap_count - 1
    flipped = filters[:, ::-1]
    padded_taps = jnp.concatenate(
        [flipped, jnp.zeros((group_count, row_count), filters.dtype)], axis=1
    )
    repeated = jnp.tile(padded_taps, (1, row_count))
    return repeated[:, : row_count * span].reshape(group_count, row_count, span)


def short_features(extended, short_filter, row_count):
    tap_count = short_filter.shape[0]
    features = jnp.zeros((row_count,) + extended.shape[1:], jnp.float32)
    for lag_index in range(tap_count):
        delayed = extended[
            tap_count - 1 - lag_index : tap_count - 1 - lag_index + row_count
        ].astype(jnp.float32)
        features = features + short_filter[lag_index].astype(jnp.float32)[None] * delayed
    return features


def attend(running, head_queries, query_pos, key_piece, value_piece):
    running_max, weight_sum, accumulated = running
    key_count = key_piece.shape[0]
    head_count = head_queries.shape[1]
    key_heads = key_piece.reshape(key_count, head_count, -1)
    value_heads = value_piece.reshape(key_count, head_count, -1)
    scores = jnp.einsum(
        "qhd,khd->hqk", head_queries, key_heads, preferred_element_type=jnp.float32
    ) * head_queries.shape[2] ** (-0.5)
    key_pos = lax.iota(jnp.int32, key_count)
    allowed = (key_pos[None, :] <= query_pos[:, None])[None]
    new_max = jnp.maximum(running_max, jnp.max(jnp.where(allowed, scores, masked_score), axis=2))
    probabilities = jnp.where(allowed, jnp.exp(scores - new_max[..., None]), 0.0)
    weight_sum = jnp.sum(probabilities, axis=2)
    mixed = jnp.einsum(
        "hqk,khd->hqd",
        probabilities.astype(jnp.bfloat16),
        value_heads,
        preferred_element_type=jnp.float32,
    )
    accumulated = mixed
    return (new_max, weight_sum, accumulated)


def start_state(head_count, row_count, width):
    return (
        jnp.full((head_count, row_count), masked_score, jnp.float32),
        jnp.zeros((head_count, row_count), jnp.float32),
        jnp.zeros((head_count, row_count, width), jnp.float32),
    )


def finish(running):
    running_max, weight_sum, accumulated = running
    result = accumulated / weight_sum[..., None]
    return jnp.transpose(result, (1, 0, 2)).reshape(result.shape[1], -1).astype(jnp.bfloat16)


def per_device(inputs, short_filter, long_filter, skip_gain, queries, key_rows, out_weight):
    row_count = inputs.shape[0]
    channels = inputs.shape[2]
    groups = long_filter.shape[0]
    tap_count = long_filter.shape[1]
    short_reach = short_filter.shape[0] - 1
    position = lax.axis_index("ctx")
    rim = passed_along(inputs[row_count - short_reach :], "ctx", 1)
    extended = jnp.concatenate([rim, inputs], axis=0)
    features = short_features(extended, short_filter, row_count)
    gate_product = (features[:, 1] * features[:, 2]).astype(jnp.bfloat16)
    gate_prev = passed_along(gate_product[row_count - (tap_count - 1) :], "ctx", 1)
    gate_ext = jnp.concatenate([gate_prev, gate_product], axis=0)
    toeplitz = toeplitz_taps(long_filter, row_count)
    filtered = jnp.einsum(
        "gtr,rgc->tgc",
        toeplitz,
        gate_ext.reshape(row_count + tap_count - 1, groups, channels // groups),
        preferred_element_type=jnp.float32,
    ).reshape(row_count, channels)
    values = (
        features[:, 0] * (filtered + skip_gain[None] * gate_product.astype(jnp.float32))
    ).astype(jnp.bfloat16)
    head_count = channels // HEAD_DIM
    head_queries = queries.reshape(row_count, head_count, HEAD_DIM)
    query_pos = position * row_count + lax.iota(jnp.int32, row_count)
    initial = start_state(head_count, row_count, HEAD_DIM)
    folded = attend(
        initial,
        head_queries,
        query_pos,
        lax.all_gather(key_rows, "ctx", axis=0, tiled=True),
        lax.all_gather(values, "ctx", axis=0, tiled=True),
    )
    attended = finish(folded)
    partial_out = jnp.dot(attended, out_weight, preferred_element_type=jnp.float32)
    return lax.psum_scatter(partial_out.astype(jnp.bfloat16), "mp", scatter_dimension=1, tiled=True)


def solution(mesh):
    placed = (
        P(("parts", "ctx"), None, "mp"),
        P(None, None, "mp"),
        P("mp", None),
        P("mp"),
        P(("parts", "ctx"), "mp"),
        P(("parts", "ctx"), "mp"),
        P("mp", None),
    )
    return jax.shard_map(
        per_device, mesh=mesh, in_specs=placed, out_specs=P(("parts", "ctx"), "mp"), check_vma=False
    )
```

profile of v0, /device:TPU:0, one launch (start us, length us, event | category | flops | bytes accessed | tf_op | source)
XLA Modules:
  0.0 113.8 jit_solution(9529709808530906281)
XLA Ops:
  6.5 0.9 slice.38
  7.4 4.9 %collective-permute-start = (bf16[2,3,1024]{2,0,1:T(2,128)(2,1)S(1)}, bf16[2,3,1024]{2,0,1:T(2,128)(2,1)S(1)}, u32[]{:S(2)}, u32[]{:S(2)}) collective-permute-start(bf16[2,3,1024]{2,0,1:T(2,128)(2,1)S(1)} %slice.38), channel_id=1, source_target_pairs={{0,4},{4,8},{8,12},{1,5},{5,9},{9,13},{2,6},{6,10},{10,14},{3,7},{... | collective-permute-start | bytes 36872 | tf_op jit(solution)/shard_map/ppermute | solution.py:15
  12.3 1.8 %copy.12 = bf16[128,1024]{0,1:T(8,128)(2,1)} copy(bf16[128,1024]{1,0:T(8,128)(2,1)} %param.12) | data formatting | bytes 524288 | tf_op args[5]
  14.2 0.7 bitcast_convert_fusion.2
  14.9 2.4 %multiply_add_fusion = f32[128,3,1024]{2,0,1:T(8,128)S(1)} fusion(bf16[128,3,1024]{2,0,1:T(8,128)(2,1)} %param.7, bf16[2,3,1024]{2,0,1:T(2,128)(2,1)S(1)} %collective-permute-done, f32[3,1024]{1,0:T(4,128)S(1)} %get-tuple-element.6, f32[3,1024]{1,0:T(4,128)S(1)} %get-tuple-element.7, f32[3,1024]{1,0:T(4,128)S(1)} %get-tuple-element.5), kind=kLoop, calls=%fused_computation.5 | loop fusion | flops 5505024 | bytes 2408448 | tf_op jit(solution)/shard_map/add | solution.py:37
  17.5 3.5 %collective-permute-start.1 = (bf16[127,1024]{1,0:T(8,128)(2,1)S(1)}, bf16[127,1024]{1,0:T(8,128)(2,1)S(1)}, u32[]{:S(2)}, u32[]{:S(2)}) collective-permute-start(bf16[127,1024]{1,0:T(8,128)(2,1)S(1)} %slice_bitcast_fusion.1), channel_id=1, source_target_pairs={{0,4},{4,8},{8,12},{1,5},{5,9},{9,13},{2,6},{6,10},{10,14},{3,7},{... | collective-permute-start | bytes 780296 | tf_op jit(solution)/shard_map/ppermute | solution.py:15
  21.0 0.1 rev.3
  21.1 0.3 tile.4
  21.4 2.6 %copy.20 = bf16[8,8,128,256]{3,1,2,0:T(8,128)(2,1)S(1)} copy(bf16[8,8,128,256]{3,2,1,0:T(8,128)(2,1)S(1)} %bitcast.51) | data formatting | bytes 8388608
  24.0 2.2 %slice.54 = bf16[64,32640]{1,0:T(8,128)(2,1)} slice(bf16[64,32768]{1,0:T(8,128)(2,1)S(1)} %bitcast.52), slice={[0:64], [0:32640]} | slice | bytes 8355840 | tf_op jit(solution)/shard_map/slice | solution.py:27
  26.2 15.8 %reshape.58 = bf16[64,128,255]{2,1,0:T(8,128)(2,1)} reshape(bf16[64,32640]{1,0:T(8,128)(2,1)} %slice.54) | data formatting | bytes 8355840 | tf_op jit(solution)/shard_map/reshape | solution.py:27
  42.1 0.1 pad_maximum_fusion.1
  42.2 0.2 copy.15
  42.4 3.4 %fusion.18 = f32[64,16,128]{2,1,0:T(8,128)S(1)} fusion(bf16[255,64,16]{0,2,1:T(8,128)(2,1)S(1)} %bitcast.53, bf16[64,128,255]{2,1,0:T(8,128)(2,1)} %reshape.58), kind=kOutput, calls=%fused_computation.35 | convolution fusion | flops 66846720 | bytes 5224448 | tf_op jit(solution)/shard_map/gtr,rgc->tgc/dot_general | solution.py:93
  45.8 0.2 copy.16
  46.0 0.9 fusion.12
  47.0 0.1 iota_compare_fusion
  47.1 1.8 %select_reduce_fusion = (f32[8,128]{1,0:T(8,128)S(1)}, f32[8,128,512]{2,1,0:T(8,128)S(1)}) fusion(pred[128,512]{1,0:T(8,128)(4,1)S(1)} %iota_compare_fusion, bf16[512,8,128]{0,2,1:T(8,128)(2,1)} %bitcast.56, bf16[128,1024]{1,0:T(8,128)(2,1)S(1)} %copy-done), kind=kOutput, calls=%fused_computation.2 | convolution fusion | flops 135789568 | bytes 3477504 | tf_op jit(solution)/shard_map/qhd,khd->hqk/dot_general | solution.py:47
  48.9 0.7 fusion
  49.6 25.3 %all-gather.5.cloned.1.call-done = bf16[512,1024]{1,0:T(8,128)(2,1)} async-done(((bf16[128,1024]{1,0:T(8,128)(2,1)}), bf16[512,1024]{1,0:T(8,128)(2,1)}) %all-gather.5.cloned.1.call-update) | async-done | bytes 1048592 | tf_op jit(solution)/shard_map/all_gather | solution.py:111
  74.9 1.5 %copy.17 = bf16[512,1024]{0,1:T(8,128)(2,1)S(1)} copy(bf16[512,1024]{1,0:T(8,128)(2,1)} %all-gather.5.cloned.1.call-done) | data formatting | bytes 2097152 | tf_op jit(solution)/shard_map/all_gather | solution.py:111
  76.4 0.7 fusion.3
  77.1 5.6 %convolution_convert_fusion = bf16[128,4096]{1,0:T(8,128)(2,1)} fusion(bf16[128,1024]{0,1:T(8,128)(2,1)S(1)} %bitcast.57, bf16[1024,4096]{1,0:T(8,128)(2,1)} %param.13), kind=kOutput, calls=%fused_computation | convolution fusion | flops 1074266112 | bytes 9699328 | tf_op jit(solution)/shard_map/dot_general | solution.py:114
  82.8 24.5 %reduce-scatter.2.cloned.1.call-done = bf16[128,1024]{1,0:T(8,128)(2,1)} async-done(((bf16[128,4096]{1,0:T(8,128)(2,1)}), bf16[128,1024]{1,0:T(8,128)(2,1)}) %reduce-scatter.2.cloned.1.call-update) | async-done | bytes 262160 | tf_op jit(solution)/shard_map/reduce_scatter | solution.py:115
  (21 shorter events, 0.4 us)
Async XLA Ops:
  6.5 40.6 %copy-start = (bf16[128,1024]{1,0:T(8,128)(2,1)S(1)}, bf16[128,1024]{1,0:T(8,128)(2,1)}, u32[]{:S(2)}) copy-start(bf16[128,1024]{1,0:T(8,128)(2,1)} %param.11) | copy-start | bytes 786436
  6.5 40.6 %all-gather.3.cloned.1.call-start = ((), (), s32[]{:S(2)}) async-start(), calls=%async_computation.1 | async-start | bytes 1310720 | tf_op jit(solution)/shard_map/all_gather | solution.py:110
  7.4 7.5 %collective-permute-start = (bf16[2,3,1024]{2,0,1:T(2,128)(2,1)S(1)}, bf16[2,3,1024]{2,0,1:T(2,128)(2,1)S(1)}, u32[]{:S(2)}, u32[]{:S(2)}) collective-permute-start(bf16[2,3,1024]{2,0,1:T(2,128)(2,1)S(1)} %slice.38), channel_id=1, source_target_pairs={{0,4},{4,8},{8,12},{1,5},{5,9},{9,13},{2,6},{6,10},{10,14},{3,7},{... | collective-permute-start | bytes 36872 | tf_op jit(solution)/shard_map/ppermute | solution.py:15
  14.1 60.8 %all-gather.5.cloned.1.call-start = ((), (), s32[]{:S(2)}) async-start(), calls=%async_computation.2 | async-start | bytes 1310720 | tf_op jit(solution)/shard_map/all_gather | solution.py:111
  14.9 6.0 %copy-start.1 = (bf16[64,128]{1,0:T(8,128)(2,1)S(1)}, bf16[64,128]{1,0:T(8,128)(2,1)}, u32[]{:S(2)}) copy-start(bf16[64,128]{1,0:T(8,128)(2,1)} %param.9) | copy-start | bytes 49156
  17.5 24.7 %collective-permute-start.1 = (bf16[127,1024]{1,0:T(8,128)(2,1)S(1)}, bf16[127,1024]{1,0:T(8,128)(2,1)S(1)}, u32[]{:S(2)}, u32[]{:S(2)}) collective-permute-start(bf16[127,1024]{1,0:T(8,128)(2,1)S(1)} %slice_bitcast_fusion.1), channel_id=1, source_target_pairs={{0,4},{4,8},{8,12},{1,5},{5,9},{9,13},{2,6},{6,10},{10,14},{3,7},{... | collective-permute-start | bytes 780296 | tf_op jit(solution)/shard_map/ppermute | solution.py:15
  42.4 3.6 %copy-start.2 = (f32[1024]{0:T(1024)S(1)}, f32[1024]{0:T(1024)}, u32[]{:S(2)}) copy-start(f32[1024]{0:T(1024)} %param.10) | copy-start | bytes 12292
  46.9 60.3 %reduce-scatter.2.cloned.1.call-start = ((), (), s32[]{:S(2)}) async-start(), calls=%async_computation.3 | async-start | bytes 1310720 | tf_op jit(solution)/shard_map/reduce_scatter | solution.py:115
Sparse Core Ops, SparseCore 0:
  14.3 31.3 all-gather.2
  47.2 27.7 all-gather.4
  82.9 24.3 reduce-scatter.1
where the time goes:
time: 114 us
  waiting for transfers between devices  49.9 us (44%)
  local copies, waits for them, and re-layouts  25.7 us (23%)
  between operations  13.3 us (12%)
  matrix products  11.4 us (10%)
  starting transfers between devices  8.51 us (7%)
  other arithmetic  4.94 us (4%)
    all_gather x1, waiting for transfers between devices, per_device(): lax.all_gather(values, 'ctx', axis=0, tiled=True)  25.3 us
    reduce_scatter x1, waiting for transfers between devices, per_device(): lax.psum_scatter(partial_out.astype(jnp.bfloat16), 'mp', scatter_dimensio...  24.5 us
    reshape x1, local copies, waits for them, and re-layouts, toeplitz_taps(): return repeated[:, :row_count * span].reshape(group_count, row_count, span)  15.8 us
    ppermute x2, starting transfers between devices, passed_along(): lax.ppermute(value, axis, [(source, source + steps) for source in range(i...  8.43 us
    dot_general x1, matrix products, per_device(): jnp.dot(attended, out_weight, preferred_element_type=jnp.float32)  5.65 us
    unnamed x8, local copies, waits for them, and re-layouts  4.4 us
    dot_general x1, matrix products, per_device(): jnp.einsum('gtr,rgc->tgc', toeplitz, gate_ext.reshape(row_count + tap_cou...  3.36 us
    add x1, other arithmetic, short_features(): features + short_filter[lag_index].astype(jnp.float32)[None] * delayed  2.38 us
  transfers between devices with their start and end apart: 5, of which 2 were waited for; matrix products, arithmetic and copies ran while one was open for 29% of the time, Pallas kernels for 0%

commit v1 on v0

--- a/solution.py
+++ b/solution.py
@@ -38,8 +38,7 @@
     return features
 
 
-def attend(running, head_queries, query_pos, key_piece, value_piece):
-    running_max, weight_sum, accumulated = running
+def attend(head_queries, query_pos, key_piece, value_piece):
     key_count = key_piece.shape[0]
     head_count = head_queries.shape[1]
     key_heads = key_piece.reshape(key_count, head_count, -1)
@@ -49,8 +48,8 @@
     ) * head_queries.shape[2] ** (-0.5)
     key_pos = lax.iota(jnp.int32, key_count)
     allowed = (key_pos[None, :] <= query_pos[:, None])[None]
-    new_max = jnp.maximum(running_max, jnp.max(jnp.where(allowed, scores, masked_score), axis=2))
-    probabilities = jnp.where(allowed, jnp.exp(scores - new_max[..., None]), 0.0)
+    peak = jnp.max(jnp.where(allowed, scores, masked_score), axis=2)
+    probabilities = jnp.where(allowed, jnp.exp(scores - peak[..., None]), 0.0)
     weight_sum = jnp.sum(probabilities, axis=2)
     mixed = jnp.einsum(
         "hqk,khd->hqd",
@@ -58,25 +57,11 @@
         value_heads,
         preferred_element_type=jnp.float32,
     )
-    accumulated = mixed
-    return (new_max, weight_sum, accumulated)
-
-
-def start_state(head_count, row_count, width):
-    return (
-        jnp.full((head_count, row_count), masked_score, jnp.float32),
-        jnp.zeros((head_count, row_count), jnp.float32),
-        jnp.zeros((head_count, row_count, width), jnp.float32),
-    )
-
-
-def finish(running):
-    running_max, weight_sum, accumulated = running
-    result = accumulated / weight_sum[..., None]
+    result = mixed / weight_sum[..., None]
     return jnp.transpose(result, (1, 0, 2)).reshape(result.shape[1], -1).astype(jnp.bfloat16)
 
 
-def per_device(inputs, short_filter, long_filter, skip_gain, queries, key_rows, out_weight):
+def by_rows(inputs, short_filter, long_filter, skip_gain, queries, key_rows):
     row_count = inputs.shape[0]
     channels = inputs.shape[2]
     groups = long_filter.shape[0]
@@ -102,15 +87,66 @@
     head_count = channels // HEAD_DIM
     head_queries = queries.reshape(row_count, head_count, HEAD_DIM)
     query_pos = position * row_count + lax.iota(jnp.int32, row_count)
-    initial = start_state(head_count, row_count, HEAD_DIM)
-    folded = attend(
-        initial,
+    return attend(
         head_queries,
         query_pos,
         lax.all_gather(key_rows, "ctx", axis=0, tiled=True),
         lax.all_gather(values, "ctx", axis=0, tiled=True),
     )
-    attended = finish(folded)
+
+
+def by_heads(inputs, short_filter, long_filter, skip_gain, queries, key_rows):
+    count = lax.axis_size("ctx")
+    position = lax.axis_index("ctx")
+    row_count, streams, channels = inputs.shape
+    own = channels // count
+    groups, tap_count = long_filter.shape
+    own_groups = groups // count
+    window = row_count * count
+    arrays = [inputs[:, 1], inputs[:, 2], inputs[:, 0], queries, key_rows]
+    sent = jnp.stack(
+        [jnp.transpose(a.reshape(row_count, count, own), (1, 0, 2)) for a in arrays], axis=1
+    )
+    got = lax.all_to_all(sent, "ctx", 0, 0)
+    got = jnp.transpose(got, (1, 0, 2, 3)).reshape(len(arrays), window, own)
+    own_short = lax.dynamic_slice_in_dim(short_filter, position * own, own, 2).astype(jnp.float32)
+    own_long = lax.dynamic_slice_in_dim(long_filter, position * own_groups, own_groups, 0)
+    own_gain = lax.dynamic_slice_in_dim(skip_gain, position * own, own, 0)
+
+    def feature(stream, which):
+        signal = got[which].astype(jnp.float32)
+        total = own_short[0, stream][None] * signal
+        for lag in range(1, short_filter.shape[0]):
+            total = total + own_short[lag, stream][None] * jnp.pad(signal, ((lag, 0), (0, 0)))[:window]
+        return total
+
+    gate = (feature(1, 0) * feature(2, 1)).astype(jnp.bfloat16)
+    blocks = gate.reshape(count, row_count, own_groups, own // own_groups)
+    earlier = jnp.concatenate([jnp.zeros_like(blocks[:1]), blocks[:-1]], axis=0)[:, row_count - tap_count + 1 :]
+    extended = jnp.concatenate([earlier, blocks], axis=1)
+    filtered = jnp.einsum(
+        "gtr,brgc->btgc",
+        toeplitz_taps(own_long, row_count),
+        extended,
+        preferred_element_type=jnp.float32,
+    ).reshape(window, own)
+    values = (feature(0, 2) * (filtered + own_gain[None] * gate.astype(jnp.float32))).astype(jnp.bfloat16)
+    attended = attend(
+        got[3].reshape(window, own // HEAD_DIM, HEAD_DIM),
+        lax.iota(jnp.int32, window),
+        got[4],
+        values,
+    )
+    back = lax.all_to_all(attended.reshape(count, row_count, own), "ctx", 0, 0)
+    return jnp.transpose(back, (1, 0, 2)).reshape(row_count, channels)
+
+
+def per_device(inputs, short_filter, long_filter, skip_gain, queries, key_rows, out_weight):
+    row_count, _, channels = inputs.shape
+    count = lax.axis_size("ctx")
+    splits = channels % (count * HEAD_DIM) == 0 and row_count + 1 >= long_filter.shape[1]
+    mix = by_heads if splits else by_rows
+    attended = mix(inputs, short_filter, long_filter, skip_gain, queries, key_rows)
     partial_out = jnp.dot(attended, out_weight, preferred_element_type=jnp.float32)
     return lax.psum_scatter(partial_out.astype(jnp.bfloat16), "mp", scatter_dimension=1, tiled=True)
 

time: 114 us -> 103 us (0.904)
  local copies, waits for them, and re-layouts: 25.7 us -> 12.9 us
  blocking collectives: 0 us -> 10.8 us
  matrix products: 11.4 us -> 7.87 us
  starting transfers between devices: 8.51 us -> 6.32 us
  waiting for transfers between devices: 49.9 us -> 48 us
  other arithmetic: 4.94 us -> 3.24 us
    all_gather x2 -> x0, waiting for transfers between devices: 25.4 us -> none  [the longest x1 25.3 us: per_device(): lax.all_gather(values, 'ctx', axis=0, tiled=True)]
    all_to_all x0 -> x1, waiting for transfers between devices: none -> 23.9 us  [by_heads(): got = lax.all_to_all(sent, 'ctx', 0, 0)]
    reshape x1, local copies, waits for them, and re-layouts: 15.8 us -> 4.37 us  [toeplitz_taps(): return repeated[:, :row_count * span].reshape(group_count, row_count, span)]
    all_to_all x0 -> x1, blocking collectives: none -> 10.8 us  [by_heads(): back = lax.all_to_all(attended.reshape(count, row_count, own), 'ctx', 0, 0)]
    ppermute x2 -> x0, starting transfers between devices: 8.43 us -> none  [passed_along(): lax.ppermute(value, axis, [(source, source + steps) for source in range(i...]
    all_to_all x0 -> x1, starting transfers between devices: none -> 6.32 us  [by_heads(): got = lax.all_to_all(sent, 'ctx', 0, 0)]
    dot_general x1, matrix products: 3.36 us -> 0.51 us  [by_heads(): jnp.einsum('gtr,brgc->btgc', toeplitz_taps(own_long, row_count), extended...]
    add x2 -> x0, other arithmetic: 2.39 us -> none  [the longest x1 2.38 us: short_features(): features + short_filter[lag_index].astype(jnp.float32)[None] * delayed]
  transfers between devices with their start and end apart: 5 -> 2, of which waited for: 2 -> 2; matrix products, arithmetic and copies ran while one was open for 29% -> 7% of each run, Pallas kernels for 0% -> 0%
where the time goes in v1:
time: 103 us
  waiting for transfers between devices  48 us (47%)
  between operations  13.7 us (13%)
  local copies, waits for them, and re-layouts  12.9 us (13%)
  blocking collectives  10.8 us (10%)
  matrix products  7.87 us (8%)
  starting transfers between devices  6.32 us (6%)
  other arithmetic  3.24 us (3%)
    reduce_scatter x1, waiting for transfers between devices, per_device(): lax.psum_scatter(partial_out.astype(jnp.bfloat16), 'mp', scatter_dimensio...  24.2 us
    all_to_all x1, waiting for transfers between devices, by_heads(): got = lax.all_to_all(sent, 'ctx', 0, 0)  23.9 us
    all_to_all x1, blocking collectives, by_heads(): back = lax.all_to_all(attended.reshape(count, row_count, own), 'ctx', 0, 0)  10.8 us
    all_to_all x1, starting transfers between devices, by_heads(): got = lax.all_to_all(sent, 'ctx', 0, 0)  6.32 us
    dot_general x1, matrix products, per_device(): jnp.dot(attended, out_weight, preferred_element_type=jnp.float32)  5.65 us
    reshape x1, local copies, waits for them, and re-layouts, toeplitz_taps(): return repeated[:, :row_count * span].reshape(group_count, row_count, span)  4.37 us
    unnamed x21, local copies, waits for them, and re-layouts  2.43 us
  transfers between devices with their start and end apart: 2, of which 2 were waited for; matrix products, arithmetic and copies ran while one was open for 7% of the time, Pallas kernels for 0%

profile of v1, /device:TPU:0, one launch (start us, length us, event | category | flops | bytes accessed | tf_op | source)
XLA Modules:
  0.0 102.8 jit_solution(11347167961309809606)
XLA Ops:
  6.5 1.2 %fusion.48 = (bf16[128,1,1024]{2,0,1:T(8,128)(2,1)S(1)}, bf16[128,1,1024]{2,0,1:T(8,128)(2,1)S(1)}, bf16[128,1,1024]{2,0,1:T(8,128)(2,1)S(1)}) fusion(bf16[128,3,1024]{2,0,1:T(8,128)(2,1)} %param.7), kind=kLoop, calls=%fused_computation.64 | loop fusion | bytes 1572864 | tf_op jit(solution)/shard_map/slice | solution.py:106
  8.9 1.2 %copy.50 = bf16[4,5,128,256]{2,3,1,0:T(8,128)(2,1)} copy(bf16[4,5,128,256]{2,3,0,1:T(8,128)(2,1)S(1)} %constant_dynamic-update-slice_fusion) | data formatting | bytes 2621440 | tf_op jit(solution)/shard_map/stack | solution.py:107
  10.0 6.3 %all-to-all-start = ((bf16[4,5,128,256]{2,3,1,0:T(8,128)(2,1)}), bf16[4,5,128,256]{2,3,1,0:T(8,128)(2,1)S(1)}, u32[]{:S(2)}, u32[]{:S(2)}) async-start(bf16[4,5,128,256]{2,3,1,0:T(8,128)(2,1)} %copy.50), calls=%async_computation | async-start | bytes 2621440 | tf_op jit(solution)/shard_map/all_to_all | solution.py:110
  16.5 0.6 copy.71
  17.2 4.4 %reshape.81 = bf16[16,128,255,1]{2,1,0,3:T(8,128)(2,1)} reshape(bf16[16,32640]{1,0:T(8,128)(2,1)S(1)} %slice.128) | data formatting | bytes 2088960 | tf_op jit(solution)/shard_map/reshape | solution.py:27
  21.6 0.8 dynamic_slice.11
  22.3 0.7 dynamic-slice_convert_fusion
  23.0 0.8 iota_compare_fusion
  23.8 23.9 %all-to-all-done = bf16[4,5,128,256]{2,3,1,0:T(8,128)(2,1)S(1)} async-done(((bf16[4,5,128,256]{2,3,1,0:T(8,128)(2,1)}), bf16[4,5,128,256]{2,3,1,0:T(8,128)(2,1)S(1)}, u32[]{:S(2)}, u32[]{:S(2)}) %all-to-all-start) | async-done | bytes 1310752 | tf_op jit(solution)/shard_map/all_to_all | solution.py:110
  47.7 0.6 copy.51
  48.5 0.3 fusion.22
  49.7 0.6 copy-done.1
  50.3 0.5 convolution_bitcast_fusion.1
  50.8 0.2 copy.58
  51.0 0.2 copy.59
  51.2 0.2 fusion.16
  51.8 0.4 fusion.31
  52.2 0.2 copy-done.4
  52.4 1.0 fusion.50
  53.5 1.3 %fusion.6 = bf16[512,2,128]{2,0,1:T(8,128)(2,1)S(1)} fusion(bf16[512,2,128]{0,2,1:T(8,128)(2,1)S(1)} %bitcast.91, f32[512,2]{0,1:T(2,128)S(1)} %bitcast.101, f32[2,512,512]{1,2,0:T(8,128)S(1)} %fusion.31, pred[512,512]{0,1:T(8,128)(4,1)S(1)} %copy-done.4), kind=kOutput, calls=%fused_computation.9 | convolution fusion | flops 137627136 | bytes 2887680 | tf_op jit(solution)/shard_map/hqk,khd->hqd/dot_general | solution.py:54
  54.7 0.3 copy.63
  55.2 10.8 %all_to_all.10 = bf16[4,128,256]{2,1,0:T(8,128)(2,1)S(1)} all-to-all(bf16[4,128,256]{2,1,0:T(8,128)(2,1)S(1)} %convert_element_type.63), channel_id=1, replica_groups=mesh['parts'=2,'ctx'=4,'mp'=4] {'ctx'}, dimensions={0} | all-to-all | bytes 524288 | tf_op jit(solution)/shard_map/all_to_all | solution.py:140
  66.1 5.6 %convolution_convert_fusion = bf16[128,4096]{1,0:T(8,128)(2,1)} fusion(bf16[128,1024]{0,1:T(8,128)(2,1)S(1)} %bitcast.84, bf16[1024,4096]{1,0:T(8,128)(2,1)} %param.13), kind=kOutput, calls=%fused_computation.1 | convolution fusion | flops 1074266112 | bytes 9699328 | tf_op jit(solution)/shard_map/dot_general | solution.py:150
  71.8 24.2 %reduce-scatter.2.cloned.1.call-done = bf16[128,1024]{1,0:T(8,128)(2,1)} async-done(((bf16[128,4096]{1,0:T(8,128)(2,1)}), bf16[128,1024]{1,0:T(8,128)(2,1)}) %reduce-scatter.2.cloned.1.call-update) | async-done | bytes 262160 | tf_op jit(solution)/shard_map/reduce_scatter | solution.py:151
  (43 shorter events, 2.9 us)
Async XLA Ops:
  6.5 9.8 %copy-start = (bf16[64,128]{1,0:T(8,128)(2,1)S(1)}, bf16[64,128]{1,0:T(8,128)(2,1)}, u32[]{:S(2)}) copy-start(bf16[64,128]{1,0:T(8,128)(2,1)} %param.9) | copy-start | bytes 49156
  6.5 1.8 %copy-start.2 = (bf16[128,1024]{1,0:T(8,128)(2,1)S(1)}, bf16[128,1024]{1,0:T(8,128)(2,1)}, u32[]{:S(2)}) copy-start(bf16[128,1024]{1,0:T(8,128)(2,1)} %param.11) | copy-start | bytes 786436
  6.5 2.0 %copy-start.3 = (bf16[128,1024]{1,0:T(8,128)(2,1)S(1)}, bf16[128,1024]{1,0:T(8,128)(2,1)}, u32[]{:S(2)}) copy-start(bf16[128,1024]{1,0:T(8,128)(2,1)} %param.12) | copy-start | bytes 786436
  10.0 37.7 %all-to-all-start = ((bf16[4,5,128,256]{2,3,1,0:T(8,128)(2,1)}), bf16[4,5,128,256]{2,3,1,0:T(8,128)(2,1)S(1)}, u32[]{:S(2)}, u32[]{:S(2)}) async-start(bf16[4,5,128,256]{2,3,1,0:T(8,128)(2,1)} %copy.50), calls=%async_computation | async-start | bytes 2621440 | tf_op jit(solution)/shard_map/all_to_all | solution.py:110
  16.3 79.6 %reduce-scatter.2.cloned.1.call-start = ((), (), s32[]{:S(2)}) async-start(), calls=%async_computation.3 | async-start | bytes 1310720 | tf_op jit(solution)/shard_map/reduce_scatter | solution.py:151
  49.0 1.2 %copy-start.1 = (bf16[16,128,255,1]{2,1,0,3:T(8,128)(2,1)S(1)}, bf16[16,128,255,1]{2,1,0,3:T(8,128)(2,1)}, u32[]{:S(2)}) copy-start(bf16[16,128,255,1]{2,1,0,3:T(8,128)(2,1)} %reshape.81) | copy-start | bytes 3133444
  51.5 1.0 copy-start.4
Sparse Core Ops, SparseCore 0:
  71.9 23.9 reduce-scatter.1

commit v2 on v0

--- a/solution.py
+++ b/solution.py
@@ -1,6 +1,8 @@
 import jax
 import jax.numpy as jnp
 from jax import lax
+from jax.experimental import pallas as pl
+from jax.experimental.pallas import tpu as pltpu
 from jax.sharding import PartitionSpec as P
 
 HEAD_DIM = 128
@@ -38,8 +40,7 @@
     return features
 
 
-def attend(running, head_queries, query_pos, key_piece, value_piece):
-    running_max, weight_sum, accumulated = running
+def attend(head_queries, query_pos, key_piece, value_piece):
     key_count = key_piece.shape[0]
     head_count = head_queries.shape[1]
     key_heads = key_piece.reshape(key_count, head_count, -1)
@@ -49,8 +50,8 @@
     ) * head_queries.shape[2] ** (-0.5)
     key_pos = lax.iota(jnp.int32, key_count)
     allowed = (key_pos[None, :] <= query_pos[:, None])[None]
-    new_max = jnp.maximum(running_max, jnp.max(jnp.where(allowed, scores, masked_score), axis=2))
-    probabilities = jnp.where(allowed, jnp.exp(scores - new_max[..., None]), 0.0)
+    peak = jnp.max(jnp.where(allowed, scores, masked_score), axis=2)
+    probabilities = jnp.where(allowed, jnp.exp(scores - peak[..., None]), 0.0)
     weight_sum = jnp.sum(probabilities, axis=2)
     mixed = jnp.einsum(
         "hqk,khd->hqd",
@@ -58,25 +59,11 @@
         value_heads,
         preferred_element_type=jnp.float32,
     )
-    accumulated = mixed
-    return (new_max, weight_sum, accumulated)
-
-
-def start_state(head_count, row_count, width):
-    return (
-        jnp.full((head_count, row_count), masked_score, jnp.float32),
-        jnp.zeros((head_count, row_count), jnp.float32),
-        jnp.zeros((head_count, row_count, width), jnp.float32),
-    )
-
-
-def finish(running):
-    running_max, weight_sum, accumulated = running
-    result = accumulated / weight_sum[..., None]
+    result = mixed / weight_sum[..., None]
     return jnp.transpose(result, (1, 0, 2)).reshape(result.shape[1], -1).astype(jnp.bfloat16)
 
 
-def per_device(inputs, short_filter, long_filter, skip_gain, queries, key_rows, out_weight):
+def by_rows(inputs, short_filter, long_filter, skip_gain, queries, key_rows):
     row_count = inputs.shape[0]
     channels = inputs.shape[2]
     groups = long_filter.shape[0]
@@ -102,15 +89,253 @@
     head_count = channels // HEAD_DIM
     head_queries = queries.reshape(row_count, head_count, HEAD_DIM)
     query_pos = position * row_count + lax.iota(jnp.int32, row_count)
-    initial = start_state(head_count, row_count, HEAD_DIM)
-    folded = attend(
-        initial,
+    return attend(
         head_queries,
         query_pos,
         lax.all_gather(key_rows, "ctx", axis=0, tiled=True),
         lax.all_gather(values, "ctx", axis=0, tiled=True),
     )
-    attended = finish(folded)
+
+
+def delayed(signal, lag):
+    if lag == 0:
+        return signal
+    row = lax.broadcasted_iota(jnp.int32, signal.shape, 0)
+    return jnp.where(row < lag, 0.0, pltpu.roll(signal, lag, 0))
+
+
+def featured(signal, taps):
+    total = taps[0] * signal
+    for lag in range(1, len(taps)):
+        total = total + taps[lag] * delayed(signal, lag)
+    return total
+
+
+def pack_kernel(inputs_ref, short_ref, queries_ref, keys_ref, out_ref):
+    count, _, own = out_ref.shape
+    rows = queries_ref.shape[0]
+    edge_row = lax.broadcasted_iota(jnp.int32, (8, own), 0)
+    for target in range(count):
+        columns = slice(target * own, (target + 1) * own)
+        features, edges = [], []
+        for stream in (1, 2):
+            signal = inputs_ref[stream, :, columns].astype(jnp.float32)
+            taps = [short_ref[lag, stream : stream + 1, columns].astype(jnp.float32) for lag in range(3)]
+            features.append(featured(signal, taps))
+            last = pltpu.roll(signal[rows - 8 :], 4, 0)
+            edges.append(jnp.where(edge_row < 2, signal[:8], jnp.where(edge_row < 4, last, 0.0)))
+        out_ref[target, 0:rows] = (features[0] * features[1]).astype(jnp.bfloat16)
+        out_ref[target, rows : 2 * rows] = inputs_ref[0, :, columns]
+        out_ref[target, 2 * rows : 3 * rows] = queries_ref[:, columns]
+        out_ref[target, 3 * rows : 4 * rows] = keys_ref[:, columns]
+        out_ref[target, 4 * rows :] = jnp.concatenate(edges, axis=0).astype(jnp.bfloat16)
+
+
+def band_kernel(_, filter_ref, out_ref):
+    groups, taps = filter_ref.shape
+    span = out_ref.shape[1]
+    source = lax.broadcasted_iota(jnp.int32, (taps, span), 0)
+    target = lax.broadcasted_iota(jnp.int32, (taps, span), 1)
+    flip = (source + target == taps).astype(jnp.bfloat16)
+    first = jnp.dot(filter_ref[...], flip, preferred_element_type=jnp.float32)
+    for group in range(groups):
+        repeated = jnp.broadcast_to(first[group : group + 1], (taps, span))
+        banded = pltpu.roll(repeated, 0, 1, stride=1, stride_axis=0)
+        out_ref[group * taps : (group + 1) * taps] = banded.astype(jnp.bfloat16)
+
+
+def mixer_kernel(_, got_ref, band_ref, short_ref, gain_ref, out_ref, gate_s, value_s):
+    count, rows, own = out_ref.shape
+    window = count * rows
+    groups = band_ref.shape[0] // rows
+    per_group = own // groups
+    taps = [[short_ref[lag, stream : stream + 1].astype(jnp.float32) for lag in range(3)] for stream in range(3)]
+    gate_s[0:rows] = jnp.zeros((rows, own), jnp.bfloat16)
+    edge_row = lax.broadcasted_iota(jnp.int32, (8, own), 0)
+    head_row = lax.broadcasted_iota(jnp.int32, (16, own), 0)
+    for block in range(count):
+        gate_s[(block + 1) * rows : (block + 2) * rows] = got_ref[block, 0:rows]
+        if block == 0:
+            continue
+        fixed = 1.0
+        before = got_ref[block - 1, 4 * rows :].astype(jnp.float32)
+        here = got_ref[block, 4 * rows :].astype(jnp.float32)
+        for which, stream in enumerate((1, 2)):
+            old = pltpu.roll(before[8 * which : 8 * which + 8], 6, 0)
+            new = pltpu.roll(here[8 * which : 8 * which + 8], 2, 0)
+            joined = jnp.where(edge_row < 2, old, new)
+            fixed = fixed * (
+                taps[stream][0] * pltpu.roll(joined, 6, 0)
+                + taps[stream][1] * pltpu.roll(joined, 7, 0)
+                + taps[stream][2] * joined
+            )
+        head = got_ref[block, 0:16].astype(jnp.float32)
+        head = jnp.where(head_row < 2, jnp.concatenate([fixed, fixed], axis=0), head)
+        gate_s[(block + 1) * rows : (block + 1) * rows + 16] = head.astype(jnp.bfloat16)
+    signal = jnp.concatenate([got_ref[block, rows : 2 * rows] for block in range(count)], axis=0)
+    feature = featured(signal.astype(jnp.float32), taps[0])
+    gain = gain_ref[...]
+    per_tile = HEAD_DIM // per_group
+    lane = lax.broadcasted_iota(jnp.int32, (rows, HEAD_DIM), 1) // per_group
+    for block in range(count):
+        for tile in range(own // HEAD_DIM):
+            columns = slice(tile * HEAD_DIM, (tile + 1) * HEAD_DIM)
+            mixed = jnp.dot(
+                band_ref[tile * per_tile * rows : (tile + 1) * per_tile * rows],
+                gate_s[block * rows : (block + 2) * rows, columns],
+                preferred_element_type=jnp.float32,
+            )
+            filtered = mixed[:rows]
+            for group in range(1, per_tile):
+                filtered = jnp.where(lane == group, mixed[group * rows : (group + 1) * rows], filtered)
+            here = slice(block * rows, (block + 1) * rows)
+            gate = gate_s[(block + 1) * rows : (block + 2) * rows, columns].astype(jnp.float32)
+            value_s[here, columns] = (
+                feature[here, columns] * (filtered + gain[:, columns] * gate)
+            ).astype(jnp.bfloat16)
+    causal = lax.broadcasted_iota(jnp.int32, (rows, rows), 1) <= lax.broadcasted_iota(jnp.int32, (rows, rows), 0)
+    for head in range(own // HEAD_DIM):
+        columns = slice(head * HEAD_DIM, (head + 1) * HEAD_DIM)
+        for block in range(count):
+            query = got_ref[block, 2 * rows : 3 * rows, columns]
+            keys = jnp.concatenate(
+                [got_ref[other, 3 * rows : 4 * rows, columns] for other in range(block + 1)], axis=0
+            )
+            scores = lax.dot_general(
+                query, keys, (((1,), (1,)), ((), ())), preferred_element_type=jnp.float32
+            ) * HEAD_DIM ** (-0.5)
+            own_scores = jnp.where(causal, scores[:, block * rows :], masked_score)
+            pieces = [scores[:, : block * rows], own_scores] if block else [own_scores]
+            scores = jnp.concatenate(pieces, axis=1)
+            peak = jnp.max(scores, axis=1, keepdims=True)
+            weights = jnp.exp(scores - peak)
+            total = jnp.sum(weights, axis=1, keepdims=True)
+            mixed = jnp.dot(
+                weights.astype(jnp.bfloat16),
+                value_s[0 : (block + 1) * rows, columns],
+                preferred_element_type=jnp.float32,
+            )
+            out_ref[block, :, columns] = (mixed / total).astype(jnp.bfloat16)
+
+
+def project_kernel(_, attended_ref, weight_ref, out_ref):
+    count, rows, own = attended_ref.shape
+    attended = jnp.concatenate([attended_ref[source] for source in range(count)], axis=1)
+    out_ref[0] = jnp.dot(attended, weight_ref[...], preferred_element_type=jnp.float32).astype(jnp.bfloat16)
+
+
+VMEM_LIMIT = 40 * 1024 * 1024
+
+
+def whole(array):
+    shape = array.shape
+    return pl.BlockSpec(shape, lambda *_: (0,) * len(shape))
+
+
+def by_heads(inputs, short_filter, long_filter, skip_gain, queries, key_rows):
+    count = lax.axis_size("ctx")
+    position = lax.axis_index("ctx").reshape(1)
+    rows, streams, channels = inputs.shape
+    own = channels // count
+    groups, taps = long_filter.shape
+    own_groups = groups // count
+    params = pltpu.CompilerParams(vmem_limit_bytes=VMEM_LIMIT)
+    sent = pl.pallas_call(
+        pack_kernel,
+        out_shape=jax.ShapeDtypeStruct((count, 4 * rows + 16, own), jnp.bfloat16),
+        compiler_params=params,
+        name="pack",
+    )(jnp.transpose(inputs, (1, 0, 2)), short_filter, queries, key_rows)
+    got = lax.all_to_all(sent, "ctx", 0, 0)
+    band = pl.pallas_call(
+        band_kernel,
+        out_shape=jax.ShapeDtypeStruct((own_groups * taps, 2 * taps), jnp.bfloat16),
+        grid_spec=pltpu.PrefetchScalarGridSpec(
+            num_scalar_prefetch=1,
+            grid=(1,),
+            in_specs=[pl.BlockSpec((own_groups, taps), lambda _, at: (at[0], 0))],
+            out_specs=pl.BlockSpec((own_groups * taps, 2 * taps), lambda _, at: (0, 0)),
+        ),
+        compiler_params=params,
+        name="band",
+    )(position, long_filter)
+    attended = pl.pallas_call(
+        mixer_kernel,
+        out_shape=jax.ShapeDtypeStruct((count, rows, own), jnp.bfloat16),
+        grid_spec=pltpu.PrefetchScalarGridSpec(
+            num_scalar_prefetch=1,
+            grid=(1,),
+            in_specs=[
+                whole(got),
+                whole(band),
+                pl.BlockSpec((3, streams, own), lambda _, at: (0, 0, at[0])),
+                pl.BlockSpec((1, own), lambda _, at: (0, at[0])),
+            ],
+            out_specs=pl.BlockSpec((count, rows, own), lambda _, at: (0, 0, 0)),
+            scratch_shapes=[
+                pltpu.VMEM(((count + 1) * rows, own), jnp.bfloat16),
+                pltpu.VMEM((count * rows, own), jnp.bfloat16),
+            ],
+        ),
+        compiler_params=params,
+        name="mixer",
+    )(position, got, band, short_filter, skip_gain.reshape(1, channels))
+    return lax.all_to_all(attended, "ctx", 0, 0)
+
+
+def projected(attended, out_weight, blocks, width):
+    count, rows, own = attended.shape
+    chunk = width // 2
+    number = blocks.shape[0]
+    return pl.pallas_call(
+        project_kernel,
+        out_shape=jax.ShapeDtypeStruct((number, rows, width), jnp.bfloat16),
+        grid_spec=pltpu.PrefetchScalarGridSpec(
+            num_scalar_prefetch=1,
+            grid=(number * 2,),
+            in_specs=[
+                whole(attended),
+                pl.BlockSpec((count * own, chunk), lambda step, at: (0, at[step // 2] * 2 + step % 2)),
+            ],
+            out_specs=pl.BlockSpec((1, rows, chunk), lambda step, at: (step // 2, 0, step % 2)),
+        ),
+        compiler_params=pltpu.CompilerParams(vmem_limit_bytes=VMEM_LIMIT),
+        name="project",
+    )(blocks, attended, out_weight)
+
+
+def added(*terms):
+    total = terms[0].astype(jnp.float32)
+    for term in terms[1:]:
+        total = total + term.astype(jnp.float32)
+    return total.astype(jnp.bfloat16)
+
+
+def crossed(value, step):
+    return lax.ppermute(value, "mp", [(source, source ^ step) for source in range(lax.axis_size("mp"))])
+
+
+def project_and_share(attended, out_weight):
+    width = out_weight.shape[1] // lax.axis_size("mp")
+    here = lax.axis_index("mp")
+    far = projected(attended, out_weight, jnp.stack([here ^ 3, here ^ 2]), width)
+    far_given = crossed(far[0], 1)
+    near = projected(attended, out_weight, jnp.stack([here ^ 1, here]), width)
+    far_sum = added(far[1], far_given)
+    near_given = crossed(near[0], 1)
+    far_got = crossed(far_sum, 2)
+    return added(near[1], near_given, far_got)
+
+
+def per_device(inputs, short_filter, long_filter, skip_gain, queries, key_rows, out_weight):
+    rows, _, channels = inputs.shape
+    count = lax.axis_size("ctx")
+    taps = long_filter.shape[1]
+    splits = channels % (count * HEAD_DIM) == 0 and count <= 4 and rows == taps
+    if splits and lax.axis_size("mp") == 4:
+        attended = by_heads(inputs, short_filter, long_filter, skip_gain, queries, key_rows)
+        return project_and_share(attended, out_weight)
+    attended = by_rows(inputs, short_filter, long_filter, skip_gain, queries, key_rows)
     partial_out = jnp.dot(attended, out_weight, preferred_element_type=jnp.float32)
     return lax.psum_scatter(partial_out.astype(jnp.bfloat16), "mp", scatter_dimension=1, tiled=True)
 

time: 114 us -> 72.9 us (0.64)
  local copies, waits for them, and re-layouts: 25.7 us -> 8.04 us
  between operations: 13.3 us -> 0.1 us
  matrix products: 11.4 us -> 0 us
  Pallas kernels: 0 us -> 10.2 us
  waiting for transfers between devices: 49.9 us -> 41.4 us
  other arithmetic: 4.94 us -> 1.05 us
  starting transfers between devices: 8.51 us -> 11.6 us
    all_to_all x0 -> x2, waiting for transfers between devices: none -> 34.2 us  [the longest x1 25.9 us: by_heads(): got = lax.all_to_all(sent, 'ctx', 0, 0)]
    all_gather x2 -> x0, waiting for transfers between devices: 25.4 us -> none  [the longest x1 25.3 us: per_device(): lax.all_gather(values, 'ctx', axis=0, tiled=True)]
    reduce_scatter x1 -> x0, waiting for transfers between devices: 24.5 us -> none  [per_device(): lax.psum_scatter(partial_out.astype(jnp.bfloat16), 'mp', scatter_dimensio...]
    reshape x2 -> x0, local copies, waits for them, and re-layouts: 16.1 us -> none  [the longest x1 15.8 us: toeplitz_taps(): return repeated[:, :row_count * span].reshape(group_count, row_count, span)]
    dot_general x4 -> x0, matrix products: 11.4 us -> none  [the longest x1 5.65 us: per_device(): jnp.dot(attended, out_weight, preferred_element_type=jnp.float32)]
    pallas_call x0 -> x5, Pallas kernels: none -> 10.2 us  [the longest x2 4.7 us: projected(): pl.pallas_call(project_kernel, out_shape=jax.ShapeDtypeStruct((number, ro...]
    all_to_all x0 -> x2, starting transfers between devices: none -> 9.86 us  [the longest x1 6.45 us: by_heads(): got = lax.all_to_all(sent, 'ctx', 0, 0)]
    ppermute x2 -> x3, waiting for transfers between devices: 0.01 us -> 7.2 us  [crossed(): lax.ppermute(value, 'mp', [(source, source ^ step) for source in range(la...]
  transfers between devices with their start and end apart: 5 -> 5, of which waited for: 2 -> 3; matrix products, arithmetic and copies ran while one was open for 29% -> 0% of each run, Pallas kernels for 0% -> 4%
where the time goes in v2:
time: 72.9 us; the launch traced here: 72.4 us
  waiting for transfers between devices  41.4 us (57%)
  starting transfers between devices  11.6 us (16%)
  Pallas kernels  10.2 us (14%)
  local copies, waits for them, and re-layouts  8.04 us (11%)
  other arithmetic  1.05 us (1%)
    all_to_all x1, waiting for transfers between devices, by_heads(): got = lax.all_to_all(sent, 'ctx', 0, 0)  25.9 us
    all_to_all x1, waiting for transfers between devices, by_heads(): return lax.all_to_all(attended, 'ctx', 0, 0)  8.26 us
    unnamed x18, local copies, waits for them, and re-layouts  8 us
    ppermute x3, waiting for transfers between devices, crossed(): lax.ppermute(value, 'mp', [(source, source ^ step) for source in range(la...  7.2 us
    all_to_all x1, starting transfers between devices, by_heads(): got = lax.all_to_all(sent, 'ctx', 0, 0)  6.45 us
    pallas_call x2, Pallas kernels, projected(): pl.pallas_call(project_kernel, out_shape=jax.ShapeDtypeStruct((number, ro...  4.7 us
    pallas_call x1, Pallas kernels, by_heads(): pl.pallas_call(mixer_kernel, out_shape=jax.ShapeDtypeStruct((count, rows,...  3.61 us
    all_to_all x1, starting transfers between devices, by_heads(): return lax.all_to_all(attended, 'ctx', 0, 0)  3.41 us
  transfers between devices with their start and end apart: 5, of which 3 were waited for; matrix products, arithmetic and copies ran while one was open for 0% of the time, Pallas kernels for 4%

profile of v2, /device:TPU:0, one launch (start us, length us, event | category | flops | bytes accessed | tf_op | source)
XLA Modules:
  0.0 72.4 jit_solution(15678433902406989590)
XLA Ops:
  0.0 1.1 %copy-done.2 = bf16[128,3,1024]{2,0,1:T(8,128)(2,1)S(1)} copy-done((bf16[128,3,1024]{2,0,1:T(8,128)(2,1)S(1)}, bf16[128,3,1024]{2,0,1:T(8,128)(2,1)}, u32[]{:S(2)}) %copy-start.2) | copy-done | bytes 786456
  1.1 0.9 %copy-done.3 = bf16[128,1024]{1,0:T(8,128)(2,1)S(1)} copy-done((bf16[128,1024]{1,0:T(8,128)(2,1)S(1)}, bf16[128,1024]{1,0:T(8,128)(2,1)}, u32[]{:S(2)}) %copy-start.3) | copy-done | bytes 262168
  2.1 0.9 %copy-done.4 = bf16[128,1024]{1,0:T(8,128)(2,1)S(1)} copy-done((bf16[128,1024]{1,0:T(8,128)(2,1)S(1)}, bf16[128,1024]{1,0:T(8,128)(2,1)}, u32[]{:S(2)}) %copy-start.4) | copy-done | bytes 262168
  3.0 0.7 %copy-done.5 = bf16[3,3,1024]{2,1,0:T(4,128)(2,1)S(1)} copy-done((bf16[3,3,1024]{2,1,0:T(4,128)(2,1)S(1)}, bf16[3,3,1024]{2,1,0:T(4,128)(2,1)}, u32[]{:S(2)}) %copy-start.5) | copy-done | bytes 18456
  3.8 1.4 %pack.1 = bf16[4,528,256]{2,1,0:T(8,128)(2,1)} custom-call(bf16[3,128,1024]{2,1,0:T(8,128)(2,1)S(1)} %bitcast.21, bf16[3,3,1024]{2,1,0:T(4,128)(2,1)S(1)} %copy-done.5, bf16[128,1024]{1,0:T(8,128)(2,1)S(1)} %copy-done.3, bf16[128,1024]{1,0:T(8,128)(2,1)S(1)} %copy-done.4), custom_call_target="tpu_custom_call" | custom-call | tf_op jit(solution)/shard_map/pack/pallas_call | solution.py:243
  5.2 6.4 %all-to-all-start = ((bf16[4,528,256]{2,1,0:T(8,128)(2,1)}), bf16[4,528,256]{2,1,0:T(8,128)(2,1)S(1)}, u32[]{:S(2)}, u32[]{:S(2)}) async-start(bf16[4,528,256]{2,1,0:T(8,128)(2,1)} %pack.1), calls=%async_computation | async-start | bytes 2162688 | tf_op jit(solution)/shard_map/all_to_all | solution.py:249
  11.7 0.5 band.1.band_ref
  12.2 25.9 %all-to-all-done.got_ref = bf16[4,528,256]{2,1,0:T(8,128)(2,1)S(1)} async-done(((bf16[4,528,256]{2,1,0:T(8,128)(2,1)}), bf16[4,528,256]{2,1,0:T(8,128)(2,1)S(1)}, u32[]{:S(2)}, u32[]{:S(2)}) %all-to-all-start) | async-done | bytes 1081376 | tf_op jit(solution)/shard_map/all_to_all | solution.py:249
  38.1 3.6 %mixer.1 = bf16[4,128,256]{2,1,0:T(8,128)(2,1)} custom-call(s32[1]{0:T(128)} %bitcast.2._, bf16[4,528,256]{2,1,0:T(8,128)(2,1)S(1)} %all-to-all-done.got_ref, bf16[2048,256]{1,0:T(8,128)(2,1)S(1)} %band.1.band_ref, bf16[3,3,1024]{2,1,0:T(4,128)(2,1)S(1)} %copy-done.6, f32[1,1024]{1,0:T(1,128)S(1)} %bitcast.22), custom_call_target="tpu_custom_call" | custom-call | tf_op jit(solution)/shard_map/mixer/pallas_call | solution.py:262
  41.7 3.4 %all-to-all-start.1 = ((bf16[4,128,256]{2,1,0:T(8,128)(2,1)}), bf16[4,128,256]{2,1,0:T(8,128)(2,1)S(1)}, u32[]{:S(2)}, u32[]{:S(2)}) async-start(bf16[4,128,256]{2,1,0:T(8,128)(2,1)} %mixer.1), calls=%async_computation.1 | async-start | bytes 524288 | tf_op jit(solution)/shard_map/all_to_all | solution.py:283
  45.1 0.1 pad_add_fusion.1._
  45.2 8.3 %all-to-all-done.1.attended_ref = bf16[4,128,256]{2,1,0:T(8,128)(2,1)S(1)} async-done(((bf16[4,128,256]{2,1,0:T(8,128)(2,1)}), bf16[4,128,256]{2,1,0:T(8,128)(2,1)S(1)}, u32[]{:S(2)}, u32[]{:S(2)}) %all-to-all-start.1) | async-done | bytes 262176 | tf_op jit(solution)/shard_map/all_to_all | solution.py:283
  53.5 3.4 %copy-done = bf16[1024,4096]{1,0:T(8,128)(2,1)S(1)} copy-done((bf16[1024,4096]{1,0:T(8,128)(2,1)S(1)}, bf16[1024,4096]{1,0:T(8,128)(2,1)}, u32[]{:S(2)}) %copy-start) | copy-done | bytes 8388632
  56.9 2.3 %project.3 = bf16[2,128,1024]{2,1,0:T(8,128)(2,1)S(1)} custom-call(s32[2]{0:T(128)S(1)} %pad_add_fusion.1._, bf16[4,128,256]{2,1,0:T(8,128)(2,1)S(1)} %all-to-all-done.1.attended_ref, bf16[1024,4096]{1,0:T(8,128)(2,1)S(1)} %copy-done), custom_call_target="tpu_custom_call" | custom-call | tf_op jit(solution)/shard_map/project/pallas_call | solution.py:290
  59.2 0.1 collective-permute-start.1
  59.3 0.1 pad_add_fusion._
  59.4 0.8 %copy-done.1 = bf16[1024,4096]{1,0:T(8,128)(2,1)S(1)} copy-done((bf16[1024,4096]{1,0:T(8,128)(2,1)S(1)}, bf16[1024,4096]{1,0:T(8,128)(2,1)}, u32[]{:S(2)}) %copy-start.1) | copy-done | bytes 8388632
  60.2 2.4 %project.2 = bf16[2,128,1024]{2,1,0:T(8,128)(2,1)S(1)} custom-call(s32[2]{0:T(128)S(1)} %pad_add_fusion._, bf16[4,128,256]{2,1,0:T(8,128)(2,1)S(1)} %all-to-all-done.1.attended_ref, bf16[1024,4096]{1,0:T(8,128)(2,1)S(1)} %copy-done.1), custom_call_target="tpu_custom_call" | custom-call | tf_op jit(solution)/shard_map/project/pallas_call | solution.py:290
  62.6 0.1 collective-permute-start
  62.7 0.0 collective-permute-done.1
  62.7 0.1 fusion
  62.8 1.6 %collective-permute-start.2 = (bf16[128,1024]{1,0:T(8,128)(2,1)S(1)}, bf16[128,1024]{1,0:T(8,128)(2,1)S(1)}, u32[]{:S(2)}, u32[]{:S(2)}) collective-permute-start(bf16[128,1024]{1,0:T(8,128)(2,1)S(1)} %fusion), channel_id=1, source_target_pairs={{0,2},{1,3},{2,0},{3,1},{4,6},{5,7},{6,4},{7,5},{8,10},{9,11},{10,... | collective-permute-start | bytes 786440 | tf_op jit(solution)/shard_map/ppermute | solution.py:315
  64.4 7.2 %collective-permute-done.2 = bf16[128,1024]{1,0:T(8,128)(2,1)S(1)} collective-permute-done((bf16[128,1024]{1,0:T(8,128)(2,1)S(1)}, bf16[128,1024]{1,0:T(8,128)(2,1)S(1)}, u32[]{:S(2)}, u32[]{:S(2)}) %collective-permute-start.2) | collective-permute-done | bytes 262176 | tf_op jit(solution)/shard_map/ppermute | solution.py:315
  71.6 0.8 %fusion.2 = bf16[128,1024]{1,0:T(8,128)(2,1)} fusion(bf16[128,1024]{1,0:T(8,128)(2,1)S(1)} %collective-permute-done.2, bf16[128,1024]{1,0:T(8,128)(2,1)S(1)} %collective-permute-done, bf16[2,128,1024]{2,1,0:T(8,128)(2,1)S(1)} %project.2), kind=kLoop, calls=%fused_computation.4 | loop fusion | flops 786432 | bytes 1048576 | tf_op jit(solution)/shard_map/convert_element_type | solution.py:311
  (15 shorter events, 0.1 us)
Async XLA Ops:
  0.0 1.1 %copy-start.2 = (bf16[128,3,1024]{2,0,1:T(8,128)(2,1)S(1)}, bf16[128,3,1024]{2,0,1:T(8,128)(2,1)}, u32[]{:S(2)}) copy-start(bf16[128,3,1024]{2,0,1:T(8,128)(2,1)} %param.7) | copy-start | bytes 2359300
  1.1 0.9 %copy-start.3 = (bf16[128,1024]{1,0:T(8,128)(2,1)S(1)}, bf16[128,1024]{1,0:T(8,128)(2,1)}, u32[]{:S(2)}) copy-start(bf16[128,1024]{1,0:T(8,128)(2,1)} %queries_ref.1) | copy-start | bytes 786436
  2.1 0.9 %copy-start.4 = (bf16[128,1024]{1,0:T(8,128)(2,1)S(1)}, bf16[128,1024]{1,0:T(8,128)(2,1)}, u32[]{:S(2)}) copy-start(bf16[128,1024]{1,0:T(8,128)(2,1)} %keys_ref.1) | copy-start | bytes 786436
  3.0 0.7 %copy-start.5 = (bf16[3,3,1024]{2,1,0:T(4,128)(2,1)S(1)}, bf16[3,3,1024]{2,1,0:T(4,128)(2,1)}, u32[]{:S(2)}) copy-start(bf16[3,3,1024]{2,1,0:T(4,128)(2,1)} %short_ref.3) | copy-start | bytes 55300
  5.2 6.5 %copy-start.7 = (bf16[64,128]{1,0:T(8,128)(2,1)S(1)}, bf16[64,128]{1,0:T(8,128)(2,1)}, u32[]{:S(2)}) copy-start(bf16[64,128]{1,0:T(8,128)(2,1)} %filter_ref.1) | copy-start | bytes 49156
  5.2 32.9 %copy-start.6 = (bf16[3,3,1024]{2,1,0:T(4,128)(2,1)S(1)}, bf16[3,3,1024]{2,1,0:T(4,128)(2,1)}, u32[]{:S(2)}) copy-start(bf16[3,3,1024]{2,1,0:T(4,128)(2,1)} %short_ref.3) | copy-start | bytes 55300
  5.2 32.9 %copy-start.8 = (f32[1024]{0:T(1024)S(1)}, f32[1024]{0:T(1024)}, u32[]{:S(2)}) copy-start(f32[1024]{0:T(1024)} %param.10) | copy-start | bytes 12292
  5.2 32.9 %all-to-all-start = ((bf16[4,528,256]{2,1,0:T(8,128)(2,1)}), bf16[4,528,256]{2,1,0:T(8,128)(2,1)S(1)}, u32[]{:S(2)}, u32[]{:S(2)}) async-start(bf16[4,528,256]{2,1,0:T(8,128)(2,1)} %pack.1), calls=%async_computation | async-start | bytes 2162688 | tf_op jit(solution)/shard_map/all_to_all | solution.py:249
  41.7 11.8 %all-to-all-start.1 = ((bf16[4,128,256]{2,1,0:T(8,128)(2,1)}), bf16[4,128,256]{2,1,0:T(8,128)(2,1)S(1)}, u32[]{:S(2)}, u32[]{:S(2)}) async-start(bf16[4,128,256]{2,1,0:T(8,128)(2,1)} %mixer.1), calls=%async_computation.1 | async-start | bytes 524288 | tf_op jit(solution)/shard_map/all_to_all | solution.py:283
  53.5 3.4 %copy-start = (bf16[1024,4096]{1,0:T(8,128)(2,1)S(1)}, bf16[1024,4096]{1,0:T(8,128)(2,1)}, u32[]{:S(2)}) copy-start(bf16[1024,4096]{1,0:T(8,128)(2,1)} %weight_ref.3) | copy-start | bytes 25165828
  56.9 3.4 %copy-start.1 = (bf16[1024,4096]{1,0:T(8,128)(2,1)S(1)}, bf16[1024,4096]{1,0:T(8,128)(2,1)}, u32[]{:S(2)}) copy-start(bf16[1024,4096]{1,0:T(8,128)(2,1)} %weight_ref.3) | copy-start | bytes 25165828
  59.2 3.5 %collective-permute-start.1 = (bf16[128,1024]{1,0:T(8,128)(2,1)S(1)}, bf16[128,1024]{1,0:T(8,128)(2,1)S(1)}, u32[]{:S(2)}, u32[]{:S(2)}) collective-permute-start(bf16[128,1024]{1,0:T(8,128)(2,1)S(1)} %slice_bitcast_fusion), channel_id=1, source_target_pairs={{0,1},{1,0},{2,3},{3,2},{4,5},{5,4},{6,7},{7,6},{8,9},{9,8},{10,11... | collective-permute-start | bytes 786440 | tf_op jit(solution)/shard_map/ppermute | solution.py:315
  62.6 1.7 %collective-permute-start = (bf16[128,1024]{1,0:T(8,128)(2,1)S(1)}, bf16[128,1024]{1,0:T(8,128)(2,1)S(1)}, u32[]{:S(2)}, u32[]{:S(2)}) collective-permute-start(bf16[128,1024]{1,0:T(8,128)(2,1)S(1)} %slice_bitcast_fusion.2), channel_id=1, source_target_pairs={{0,1},{1,0},{2,3},{3,2},{4,5},{5,4},{6,7},{7,6},{8,9},{9,8},{10,11... | collective-permute-start | bytes 786440 | tf_op jit(solution)/shard_map/ppermute | solution.py:315
  62.8 8.8 %collective-permute-start.2 = (bf16[128,1024]{1,0:T(8,128)(2,1)S(1)}, bf16[128,1024]{1,0:T(8,128)(2,1)S(1)}, u32[]{:S(2)}, u32[]{:S(2)}) collective-permute-start(bf16[128,1024]{1,0:T(8,128)(2,1)S(1)} %fusion), channel_id=1, source_target_pairs={{0,2},{1,3},{2,0},{3,1},{4,6},{5,7},{6,4},{7,5},{8,10},{9,11},{10,... | collective-permute-start | bytes 786440 | tf_op jit(solution)/shard_map/ppermute | solution.py:315

commit v3 on v2

v3 whole, which is shorter than its diff:
```python
import functools

import jax
import jax.numpy as jnp
from jax import lax
from jax.experimental import pallas as pl
from jax.experimental.pallas import tpu as pltpu
from jax.sharding import PartitionSpec as P

HEAD_DIM = 128


masked_score = -1e30


def passed_along(value, axis, steps):
    count = lax.axis_size(axis)
    initial, last = (max(0, -steps), min(count, count - steps))
    return lax.ppermute(value, axis, [(source, source + steps) for source in range(initial, last)])


def toeplitz_taps(filters, row_count):
    group_count = filters.shape[0]
    tap_count = filters.shape[1]
    span = row_count + tap_count - 1
    flipped = filters[:, ::-1]
    padded_taps = jnp.concatenate(
        [flipped, jnp.zeros((group_count, row_count), filters.dtype)], axis=1
    )
    repeated = jnp.tile(padded_taps, (1, row_count))
    return repeated[:, : row_count * span].reshape(group_count, row_count, span)


def short_features(extended, short_filter, row_count):
    tap_count = short_filter.shape[0]
    features = jnp.zeros((row_count,) + extended.shape[1:], jnp.float32)
    for lag_index in range(tap_count):
        delayed = extended[
            tap_count - 1 - lag_index : tap_count - 1 - lag_index + row_count
        ].astype(jnp.float32)
        features = features + short_filter[lag_index].astype(jnp.float32)[None] * delayed
    return features


def attend(head_queries, query_pos, key_piece, value_piece):
    key_count = key_piece.shape[0]
    head_count = head_queries.shape[1]
    key_heads = key_piece.reshape(key_count, head_count, -1)
    value_heads = value_piece.reshape(key_count, head_count, -1)
    scores = jnp.einsum(
        "qhd,khd->hqk", head_queries, key_heads, preferred_element_type=jnp.float32
    ) * head_queries.shape[2] ** (-0.5)
    key_pos = lax.iota(jnp.int32, key_count)
    allowed = (key_pos[None, :] <= query_pos[:, None])[None]
    peak = jnp.max(jnp.where(allowed, scores, masked_score), axis=2)
    probabilities = jnp.where(allowed, jnp.exp(scores - peak[..., None]), 0.0)
    weight_sum = jnp.sum(probabilities, axis=2)
    mixed = jnp.einsum(
        "hqk,khd->hqd",
        probabilities.astype(jnp.bfloat16),
        value_heads,
        preferred_element_type=jnp.float32,
    )
    result = mixed / weight_sum[..., None]
    return jnp.transpose(result, (1, 0, 2)).reshape(result.shape[1], -1).astype(jnp.bfloat16)


def by_rows(inputs, short_filter, long_filter, skip_gain, queries, key_rows):
    row_count = inputs.shape[0]
    channels = inputs.shape[2]
    groups = long_filter.shape[0]
    tap_count = long_filter.shape[1]
    short_reach = short_filter.shape[0] - 1
    position = lax.axis_index("ctx")
    rim = passed_along(inputs[row_count - short_reach :], "ctx", 1)
    extended = jnp.concatenate([rim, inputs], axis=0)
    features = short_features(extended, short_filter, row_count)
    gate_product = (features[:, 1] * features[:, 2]).astype(jnp.bfloat16)
    gate_prev = passed_along(gate_product[row_count - (tap_count - 1) :], "ctx", 1)
    gate_ext = jnp.concatenate([gate_prev, gate_product], axis=0)
    toeplitz = toeplitz_taps(long_filter, row_count)
    filtered = jnp.einsum(
        "gtr,rgc->tgc",
        toeplitz,
        gate_ext.reshape(row_count + tap_count - 1, groups, channels // groups),
        preferred_element_type=jnp.float32,
    ).reshape(row_count, channels)
    values = (
        features[:, 0] * (filtered + skip_gain[None] * gate_product.astype(jnp.float32))
    ).astype(jnp.bfloat16)
    head_count = channels // HEAD_DIM
    head_queries = queries.reshape(row_count, head_count, HEAD_DIM)
    query_pos = position * row_count + lax.iota(jnp.int32, row_count)
    return attend(
        head_queries,
        query_pos,
        lax.all_gather(key_rows, "ctx", axis=0, tiled=True),
        lax.all_gather(values, "ctx", axis=0, tiled=True),
    )


def delayed(signal, lag):
    if lag == 0:
        return signal
    row = lax.broadcasted_iota(jnp.int32, signal.shape, 0)
    return jnp.where(row < lag, 0.0, pltpu.roll(signal, lag, 0))


def featured(signal, taps):
    total = taps[0] * signal
    for lag in range(1, len(taps)):
        total = total + taps[lag] * delayed(signal, lag)
    return total


def pack_kernel(inputs_any, short_any, queries_any, keys_any, *refs):
    count = 4
    first_refs, second_refs = refs[:count], refs[count : 2 * count]
    signal_s, short_s, gate_s, in_sems, gate_sems, plain_sems = refs[2 * count :]
    rows, own = signal_s.shape[2:]
    edged = gate_s.shape[1]
    position = lax.axis_index("ctx")
    columns = [pl.ds(pl.multiple_of((position ^ step) * own, own), own) for step in range(count)]
    order = (3, 2, 1, 0)
    load_short = pltpu.make_async_copy(short_any, short_s, in_sems.at[count])
    load_short.start()
    loads = [
        pltpu.make_async_copy(inputs_any.at[1:3, :, columns[step]], signal_s.at[step], in_sems.at[step])
        for step in range(count)
    ]
    for step in order:
        loads[step].start()
    plain = []
    for step in order:
        for index, (source, target) in enumerate(
            (
                (inputs_any.at[0, :, columns[step]], first_refs[step].at[edged:]),
                (queries_any.at[:, columns[step]], second_refs[step].at[0:rows]),
                (keys_any.at[:, columns[step]], second_refs[step].at[rows:]),
            )
        ):
            plain.append(pltpu.make_async_copy(source, target, plain_sems.at[3 * step + index]))
    for copy in plain:
        copy.start()
    edge_row = lax.broadcasted_iota(jnp.int32, (8, own), 0)
    load_short.wait()
    stores = []
    for step in order:
        loads[step].wait()
        features, edges = [], []
        for stream in (1, 2):
            signal = signal_s[step, stream - 1].astype(jnp.float32)
            taps = [short_s[lag, stream : stream + 1, columns[step]].astype(jnp.float32) for lag in range(3)]
            features.append(featured(signal, taps))
            last = pltpu.roll(signal[rows - 8 :], 4, 0)
            edges.append(jnp.where(edge_row < 2, signal[:8], jnp.where(edge_row < 4, last, 0.0)))
        gate_s[step, 0:rows] = (features[0] * features[1]).astype(jnp.bfloat16)
        gate_s[step, rows:] = jnp.concatenate(edges, axis=0).astype(jnp.bfloat16)
        store = pltpu.make_async_copy(gate_s.at[step], first_refs[step].at[0:edged], gate_sems.at[step])
        store.start()
        stores.append(store)
    for copy in plain + stores:
        copy.wait()


def ready_kernel(filter_ref, weight_any, band_ref, weight_ref, sem):
    rows, span = band_ref.shape
    taps = filter_ref.shape[1]
    groups = rows // taps
    weights = pltpu.make_async_copy(weight_any, weight_ref, sem)
    weights.start()
    source = lax.broadcasted_iota(jnp.int32, (taps, span), 0)
    target = lax.broadcasted_iota(jnp.int32, (taps, span), 1)
    flip = (source + target == taps).astype(jnp.bfloat16)
    first_group = pl.multiple_of(lax.axis_index("ctx") * groups, groups)
    first = jnp.dot(filter_ref[pl.ds(first_group, groups)], flip, preferred_element_type=jnp.float32)
    for group in range(groups):
        repeated = jnp.broadcast_to(first[group : group + 1], (taps, span))
        banded = pltpu.roll(repeated, 0, 1, stride=1, stride_axis=0)
        band_ref[group * taps : (group + 1) * taps] = banded.astype(jnp.bfloat16)
    weights.wait()


def values_kernel(at, *refs):
    count = 4
    given = refs[:count]
    band_ref, short_ref, gain_ref, out_ref, got_s, gate_s = refs[count:]
    own = out_ref.shape[1]
    rows = out_ref.shape[0] // count
    groups = band_ref.shape[0] // rows
    per_group = own // groups
    position = at[0]
    for step in range(count):
        got_s[position ^ step] = given[step][...]
    taps = [[short_ref[lag, stream : stream + 1].astype(jnp.float32) for lag in range(3)] for stream in range(3)]
    gate_s[0:rows] = jnp.zeros((rows, own), jnp.bfloat16)
    edge_row = lax.broadcasted_iota(jnp.int32, (8, own), 0)
    head_row = lax.broadcasted_iota(jnp.int32, (16, own), 0)
    for block in range(count):
        gate_s[(block + 1) * rows : (block + 2) * rows] = got_s[block, 0:rows]
        if block == 0:
            continue
        fixed = 1.0
        before = got_s[block - 1, rows : rows + 16].astype(jnp.float32)
        here = got_s[block, rows : rows + 16].astype(jnp.float32)
        for which, stream in enumerate((1, 2)):
            old = pltpu.roll(before[8 * which : 8 * which + 8], 6, 0)
            new = pltpu.roll(here[8 * which : 8 * which + 8], 2, 0)
            joined = jnp.where(edge_row < 2, old, new)
            fixed = fixed * (
                taps[stream][0] * pltpu.roll(joined, 6, 0)
                + taps[stream][1] * pltpu.roll(joined, 7, 0)
                + taps[stream][2] * joined
            )
        head = got_s[block, 0:16].astype(jnp.float32)
        head = jnp.where(head_row < 2, jnp.concatenate([fixed, fixed], axis=0), head)
        gate_s[(block + 1) * rows : (block + 1) * rows + 16] = head.astype(jnp.bfloat16)
    signal = jnp.concatenate([got_s[block, rows + 16 :] for block in range(count)], axis=0)
    feature = featured(signal.astype(jnp.float32), taps[0])
    gain = gain_ref[...]
    per_tile = HEAD_DIM // per_group
    lane = lax.broadcasted_iota(jnp.int32, (rows, HEAD_DIM), 1) // per_group
    for block in range(count):
        for tile in range(own // HEAD_DIM):
            columns = slice(tile * HEAD_DIM, (tile + 1) * HEAD_DIM)
            mixed = jnp.dot(
                band_ref[tile * per_tile * rows : (tile + 1) * per_tile * rows],
                gate_s[block * rows : (block + 2) * rows, columns],
                preferred_element_type=jnp.float32,
            )
            filtered = mixed[:rows]
            for group in range(1, per_tile):
                filtered = jnp.where(lane == group, mixed[group * rows : (group + 1) * rows], filtered)
            here = slice(block * rows, (block + 1) * rows)
            gate = gate_s[(block + 1) * rows : (block + 2) * rows, columns].astype(jnp.float32)
            out_ref[here, columns] = (
                feature[here, columns] * (filtered + gain[:, columns] * gate)
            ).astype(jnp.bfloat16)


def attend_kernel(*refs):
    count = 4
    given, value_ref = refs[:count], refs[count]
    out_refs = refs[count + 1 : 2 * count + 1]
    query_s, key_s, out_s = refs[2 * count + 1 :]
    rows, own = query_s.shape[1:]
    position = lax.axis_index("ctx")
    for step in range(count):
        query_s[position ^ step] = given[step][0:rows]
        key_s[pl.ds(pl.multiple_of((position ^ step) * rows, rows), rows)] = given[step][rows:]
    causal = lax.broadcasted_iota(jnp.int32, (rows, rows), 1) <= lax.broadcasted_iota(jnp.int32, (rows, rows), 0)
    for head in range(own // HEAD_DIM):
        columns = slice(head * HEAD_DIM, (head + 1) * HEAD_DIM)
        for block in range(count):
            scores = lax.dot_general(
                query_s[block, :, columns],
                key_s[0 : (block + 1) * rows, columns],
                (((1,), (1,)), ((), ())),
                preferred_element_type=jnp.float32,
            ) * HEAD_DIM ** (-0.5)
            own_scores = jnp.where(causal, scores[:, block * rows :], masked_score)
            pieces = [scores[:, : block * rows], own_scores] if block else [own_scores]
            scores = jnp.concatenate(pieces, axis=1)
            peak = jnp.max(scores, axis=1, keepdims=True)
            weights = jnp.exp(scores - peak)
            total = jnp.sum(weights, axis=1, keepdims=True)
            mixed = jnp.dot(
                weights.astype(jnp.bfloat16),
                value_ref[0 : (block + 1) * rows, columns],
                preferred_element_type=jnp.float32,
            )
            out_s[block, :, columns] = (mixed / total).astype(jnp.bfloat16)
    for step in range(count):
        out_refs[step][...] = out_s[position ^ step]


def project_kernel(masks, *refs):
    count = 4
    given, weight_ref = refs[:count], refs[count]
    out_refs, attended_s = refs[count + 1 : -1], refs[-1]
    own = given[0].shape[1]
    width = out_refs[0].shape[1]
    position, here = lax.axis_index("ctx"), lax.axis_index("mp")
    for step in range(count):
        attended_s[:, pl.ds(pl.multiple_of((position ^ step) * own, own), own)] = given[step][...]
    for mask, out_ref in zip(masks, out_refs):
        columns = pl.ds(pl.multiple_of((here ^ mask) * width, width), width)
        out_ref[...] = jnp.dot(
            attended_s[...], weight_ref[:, columns], preferred_element_type=jnp.float32
        ).astype(jnp.bfloat16)


VMEM_LIMIT = 40 * 1024 * 1024
WIDE_LIMIT = 60 * 1024 * 1024
IN_HBM = pl.BlockSpec(memory_space=pl.ANY)
IN_VMEM = pl.BlockSpec(memory_space=pltpu.VMEM)


def whole(array):
    shape = array.shape
    return pl.BlockSpec(shape, lambda *_: (0,) * len(shape))


def swapped(value, axis, step):
    return lax.ppermute(value, axis, [(source, source ^ step) for source in range(lax.axis_size(axis))])


def exchanged(pieces, axis):
    sent = {step: swapped(pieces[step], axis, step) for step in (3, 2, 1)}
    return [pieces[0]] + [sent[step] for step in (1, 2, 3)]


def by_heads(inputs, short_filter, long_filter, skip_gain, queries, key_rows, out_weight):
    count = lax.axis_size("ctx")
    position = lax.axis_index("ctx").reshape(1)
    rows, streams, channels = inputs.shape
    own = channels // count
    groups, taps = long_filter.shape
    own_groups = groups // count
    params = pltpu.CompilerParams(vmem_limit_bytes=VMEM_LIMIT)
    first = jax.ShapeDtypeStruct((2 * rows + 16, own), jnp.bfloat16)
    second = jax.ShapeDtypeStruct((2 * rows, own), jnp.bfloat16)
    piece = jax.ShapeDtypeStruct((rows, own), jnp.bfloat16)
    sent = pl.pallas_call(
        pack_kernel,
        out_shape=[first] * count + [second] * count,
        in_specs=[IN_HBM] * 4,
        out_specs=[IN_HBM] * (2 * count),
        scratch_shapes=[
            pltpu.VMEM((count, 2, rows, own), jnp.bfloat16),
            pltpu.VMEM(short_filter.shape, jnp.bfloat16),
            pltpu.VMEM((count, rows + 16, own), jnp.bfloat16),
            pltpu.SemaphoreType.DMA((count + 1,)),
            pltpu.SemaphoreType.DMA((count,)),
            pltpu.SemaphoreType.DMA((3 * count,)),
        ],
        compiler_params=pltpu.CompilerParams(vmem_limit_bytes=WIDE_LIMIT),
        name="pack",
    )(jnp.transpose(inputs, (1, 0, 2)), short_filter, queries, key_rows)
    first_got = exchanged(sent[:count], "ctx")
    second_got = exchanged(sent[count:], "ctx")
    band, weight = pl.pallas_call(
        ready_kernel,
        out_shape=[
            jax.ShapeDtypeStruct((own_groups * taps, 2 * taps), jnp.bfloat16),
            jax.ShapeDtypeStruct(out_weight.shape, jnp.bfloat16),
        ],
        in_specs=[IN_VMEM, IN_HBM],
        out_specs=[IN_VMEM] * 2,
        scratch_shapes=[pltpu.SemaphoreType.DMA],
        compiler_params=params,
        name="ready",
    )(long_filter, out_weight)
    values = pl.pallas_call(
        values_kernel,
        out_shape=jax.ShapeDtypeStruct((count * rows, own), jnp.bfloat16),
        grid_spec=pltpu.PrefetchScalarGridSpec(
            num_scalar_prefetch=1,
            grid=(1,),
            in_specs=[whole(first)] * count
            + [
                whole(band),
                pl.BlockSpec((3, streams, own), lambda _, at: (0, 0, at[0])),
                pl.BlockSpec((1, own), lambda _, at: (0, at[0])),
            ],
            out_specs=pl.BlockSpec((count * rows, own), lambda _, at: (0, 0)),
            scratch_shapes=[
                pltpu.VMEM((count, 2 * rows + 16, own), jnp.bfloat16),
                pltpu.VMEM(((count + 1) * rows, own), jnp.bfloat16),
            ],
        ),
        compiler_params=params,
        cost_estimate=pl.CostEstimate(flops=2 * count * rows * own * 8 * 2 * taps, bytes_accessed=2**21, transcendentals=0),
        name="values",
    )(position, *first_got, band, short_filter, skip_gain.reshape(1, channels))
    attended = pl.pallas_call(
        attend_kernel,
        out_shape=[piece] * count,
        in_specs=[IN_VMEM] * (count + 1),
        out_specs=[IN_VMEM] * count,
        scratch_shapes=[
            pltpu.VMEM((count, rows, own), jnp.bfloat16),
            pltpu.VMEM((count * rows, own), jnp.bfloat16),
            pltpu.VMEM((count, rows, own), jnp.bfloat16),
        ],
        compiler_params=params,
        name="attend",
    )(*second_got, values)
    return project_and_share(exchanged(attended, "ctx"), weight)


def projected(attended, out_weight, masks):
    rows = attended[0].shape[0]
    width = out_weight.shape[1] // lax.axis_size("mp")
    return pl.pallas_call(
        functools.partial(project_kernel, masks),
        out_shape=[jax.ShapeDtypeStruct((rows, width), jnp.bfloat16)] * len(masks),
        in_specs=[IN_VMEM] * (len(attended) + 1),
        out_specs=[IN_VMEM] * len(masks),
        scratch_shapes=[pltpu.VMEM((rows, out_weight.shape[0]), jnp.bfloat16)],
        compiler_params=pltpu.CompilerParams(vmem_limit_bytes=VMEM_LIMIT),
        cost_estimate=pl.CostEstimate(
            flops=2 * rows * out_weight.shape[0] * width * len(masks), bytes_accessed=2**22, transcendentals=0
        ),
        name="project",
    )(*attended, out_weight)


def added(*terms):
    total = terms[0].astype(jnp.float32)
    for term in terms[1:]:
        total = total + term.astype(jnp.float32)
    return total.astype(jnp.bfloat16)


def project_and_share(attended, out_weight):
    far_given, far_kept = projected(attended, out_weight, (3, 2))
    far_got = swapped(far_given, "mp", 1)
    near_given, near_kept = projected(attended, out_weight, (1, 0))
    far_sum = added(far_kept, far_got)
    near_got = swapped(near_given, "mp", 1)
    return added(near_kept, near_got, swapped(far_sum, "mp", 2))


def per_device(inputs, short_filter, long_filter, skip_gain, queries, key_rows, out_weight):
    rows, _, channels = inputs.shape
    count = lax.axis_size("ctx")
    taps = long_filter.shape[1]
    splits = channels % (count * HEAD_DIM) == 0 and count == 4 and rows == taps
    if splits and lax.axis_size("mp") == 4:
        return by_heads(inputs, short_filter, long_filter, skip_gain, queries, key_rows, out_weight)
    attended = by_rows(inputs, short_filter, long_filter, skip_gain, queries, key_rows)
    partial_out = jnp.dot(attended, out_weight, preferred_element_type=jnp.float32)
    return lax.psum_scatter(partial_out.astype(jnp.bfloat16), "mp", scatter_dimension=1, tiled=True)


def solution(mesh):
    placed = (
        P(("parts", "ctx"), None, "mp"),
        P(None, None, "mp"),
        P("mp", None),
        P("mp"),
        P(("parts", "ctx"), "mp"),
        P(("parts", "ctx"), "mp"),
        P("mp", None),
    )
    return jax.shard_map(
        per_device, mesh=mesh, in_specs=placed, out_specs=P(("parts", "ctx"), "mp"), check_vma=False
    )
```

time: 72.9 us -> 76.5 us (1.049)
  Pallas kernels: 10.2 us -> 33.4 us
  waiting for transfers between devices: 41.4 us -> 20 us
  starting transfers between devices: 11.6 us -> 21.2 us
  local copies, waits for them, and re-layouts: 8.04 us -> 0.73 us
    all_to_all x2 -> x0, waiting for transfers between devices: 34.2 us -> none  [the longest x1 25.9 us: by_heads(): got = lax.all_to_all(sent, 'ctx', 0, 0)]
    pallas_call x5 -> x6, Pallas kernels: 10.2 us -> 33.4 us  [the longest x1 25.1 us: by_heads(): pl.pallas_call(pack_kernel, out_shape=[first] * count + [second] * count,...]
    ppermute x3 -> x12, starting transfers between devices: 1.7 us -> 21.2 us  [swapped(): lax.ppermute(value, axis, [(source, source ^ step) for source in range(la...]
    ppermute x3 -> x12, waiting for transfers between devices: 7.2 us -> 20 us  [swapped(): lax.ppermute(value, axis, [(source, source ^ step) for source in range(la...]
    all_to_all x2 -> x0, starting transfers between devices: 9.86 us -> none  [the longest x1 6.45 us: by_heads(): got = lax.all_to_all(sent, 'ctx', 0, 0)]
    unnamed x18 -> x10, local copies, waits for them, and re-layouts: 8 us -> 0.73 us
  transfers between devices with their start and end apart: 5 -> 12, of which waited for: 3 -> 6; matrix products, arithmetic and copies ran while one was open for 0% -> 0% of each run, Pallas kernels for 4% -> 7%
where the time goes in v3:
time: 76.5 us; the launch traced here: 76.3 us
  Pallas kernels  33.4 us (44%)
  starting transfers between devices  21.2 us (28%)
  waiting for transfers between devices  20 us (26%)
  other arithmetic  0.89 us (1%)
    pallas_call x1, Pallas kernels, by_heads(): pl.pallas_call(pack_kernel, out_shape=[first] * count + [second] * count,...  25.1 us
    ppermute x12, starting transfers between devices, swapped(): lax.ppermute(value, axis, [(source, source ^ step) for source in range(la...  21.2 us
    ppermute x12, waiting for transfers between devices, swapped(): lax.ppermute(value, axis, [(source, source ^ step) for source in range(la...  20 us
    pallas_call x1, Pallas kernels, by_heads(): pl.pallas_call(ready_kernel, out_shape=[jax.ShapeDtypeStruct((own_groups...  3.44 us
    pallas_call x1, Pallas kernels, by_heads(): pl.pallas_call(attend_kernel, out_shape=[piece] * count, in_specs=[IN_VME...  2 us
  transfers between devices with their start and end apart: 12, of which 6 were waited for; matrix products, arithmetic and copies ran while one was open for 0% of the time, Pallas kernels for 7%

profile of v3, /device:TPU:0, one launch (start us, length us, event | category | flops | bytes accessed | tf_op | source)
XLA Modules:
  0.0 76.3 jit_solution(10600426532355808788)
XLA Ops:
  0.0 25.1 %pack.1 = (bf16[272,256]{1,0:T(8,128)(2,1)}, bf16[272,256]{1,0:T(8,128)(2,1)}, bf16[272,256]{1,0:T(8,128)(2,1)}, bf16[272,256]{1,0:T(8,128)(2,1)}, bf16[256,256]...) custom-call(bf16[3,128,1024]{2,1,0:T(8,128)(2,1)} %bitcast.4, ...), custom_call_target="tpu_custom_call" | custom-call | tf_op jit(solution)/shard_map/pack/pallas_call | solution.py:324
  25.1 3.1 %collective-permute-start.3 = (bf16[272,256]{1,0:T(8,128)(2,1)}, bf16[272,256]{1,0:T(8,128)(2,1)S(1)}, u32[]{:S(2)}, u32[]{:S(2)}) collective-permute-start(bf16[272,256]{1,0:T(8,128)(2,1)} %get-tuple-element.28), channel_id=1, source_target_pairs={{0,4},{4,0},{8,12},{12,8},{1,5},{5,1},{9,13},{13,9},{2,6},{6,2},{1... | collective-permute-start | bytes 417800 | tf_op jit(solution)/shard_map/ppermute | solution.py:305
  28.2 2.6 %collective-permute-start.4 = (bf16[272,256]{1,0:T(8,128)(2,1)}, bf16[272,256]{1,0:T(8,128)(2,1)S(1)}, u32[]{:S(2)}, u32[]{:S(2)}) collective-permute-start(bf16[272,256]{1,0:T(8,128)(2,1)} %get-tuple-element.29), channel_id=1, source_target_pairs={{0,8},{4,12},{8,0},{12,4},{1,9},{5,13},{9,1},{13,5},{2,10},{6,14},... | collective-permute-start | bytes 417800 | tf_op jit(solution)/shard_map/ppermute | solution.py:305
  30.8 0.9 %collective-permute-start = (bf16[256,256]{1,0:T(8,128)(2,1)}, bf16[256,256]{1,0:T(8,128)(2,1)S(1)}, u32[]{:S(2)}, u32[]{:S(2)}) collective-permute-start(bf16[256,256]{1,0:T(8,128)(2,1)} %get-tuple-element.24), channel_id=1, source_target_pairs={{0,4},{4,0},{8,12},{12,8},{1,5},{5,1},{9,13},{13,9},{2,6},{6,2},{1... | collective-permute-start | bytes 393224 | tf_op jit(solution)/shard_map/ppermute | solution.py:305
  31.7 3.5 %collective-permute-start.1 = (bf16[256,256]{1,0:T(8,128)(2,1)}, bf16[256,256]{1,0:T(8,128)(2,1)S(1)}, u32[]{:S(2)}, u32[]{:S(2)}) collective-permute-start(bf16[256,256]{1,0:T(8,128)(2,1)} %get-tuple-element.25), channel_id=1, source_target_pairs={{0,8},{4,12},{8,0},{12,4},{1,9},{5,13},{9,1},{13,5},{2,10},{6,14},... | collective-permute-start | bytes 393224 | tf_op jit(solution)/shard_map/ppermute | solution.py:305
  35.2 4.3 %collective-permute-start.2 = (bf16[256,256]{1,0:T(8,128)(2,1)}, bf16[256,256]{1,0:T(8,128)(2,1)S(1)}, u32[]{:S(2)}, u32[]{:S(2)}) collective-permute-start(bf16[256,256]{1,0:T(8,128)(2,1)} %get-tuple-element.26), channel_id=1, source_target_pairs={{0,12},{4,8},{8,4},{12,0},{1,13},{5,9},{9,5},{13,1},{2,14},{6,10},... | collective-permute-start | bytes 393224 | tf_op jit(solution)/shard_map/ppermute | solution.py:305
  39.6 0.7 copy-done.2
  40.3 3.4 %ready.1 = (bf16[2048,256]{1,0:T(8,128)(2,1)S(1)}, bf16[1024,4096]{1,0:T(8,128)(2,1)S(1)}) custom-call(bf16[64,128]{1,0:T(8,128)(2,1)S(1)} %copy-done.2, bf16[1024,4096]{1,0:T(8,128)(2,1)} %weight_any.1), custom_call_target="tpu_custom_call" | custom-call | tf_op jit(solution)/shard_map/ready/pallas_call | solution.py:342
  43.8 1.3 %values.1.refs_4_ = bf16[512,256]{1,0:T(8,128)(2,1)S(1)} custom-call(s32[1]{0:T(128)} %bitcast.1.at, bf16[272,256]{1,0:T(8,128)(2,1)S(1)} %copy-done.3, bf16[272,256]{1,0:T(8,128)(2,1)S(1)} %collective-permute-done.3.refs_1_, bf16[272,256]{1,0:T(8,128)(2,1)S(1)} %collective-permute-done.4.refs_2_, bf16[272,256]{1,0:T(8,128)(2,1)S(1)} %collective-permute-done.5.refs_3_, ...), custom_call_target="tpu_custom_call" | custom-call | flops 536870912 | bytes 2097152 | tf_op jit(solution)/shard_map/values/pallas_call | solution.py:354
  45.1 8.2 %collective-permute-done.1.refs_2_ = bf16[256,256]{1,0:T(8,128)(2,1)S(1)} collective-permute-done((bf16[256,256]{1,0:T(8,128)(2,1)}, bf16[256,256]{1,0:T(8,128)(2,1)S(1)}, u32[]{:S(2)}, u32[]{:S(2)}) %collective-permute-start.1) | collective-permute-done | bytes 131104 | tf_op jit(solution)/shard_map/ppermute | solution.py:305
  53.3 2.0 %attend.1 = (bf16[128,256]{1,0:T(8,128)(2,1)S(1)}, bf16[128,256]{1,0:T(8,128)(2,1)S(1)}, bf16[128,256]{1,0:T(8,128)(2,1)S(1)}, bf16[128,256]{1,0:T(8,128)(2,1)S(1)}) custom-call(bf16[256,256]{1,0:T(8,128)(2,1)S(1)} %copy-done, bf16[256,256]{1,0:T(8,128)(2,1)S(1)} %collective-permute-done.refs_1_, bf16[256,256]{1,0:T(8,128)(2,1)S(1)} %collective-permute-done.1.refs_2_, ...), custom_call_target="tpu_custom_call" | custom-call | tf_op jit(solution)/shard_map/attend/pallas_call | solution.py:376
  55.3 2.0 %collective-permute-start.6 = (bf16[128,256]{1,0:T(8,128)(2,1)S(1)}, bf16[128,256]{1,0:T(8,128)(2,1)S(1)}, u32[]{:S(2)}, u32[]{:S(2)}) collective-permute-start(bf16[128,256]{1,0:T(8,128)(2,1)S(1)} %get-tuple-element.33), channel_id=1, source_target_pairs={{0,4},{4,0},{8,12},{12,8},{1,5},{5,1},{9,13},{13,9},{2,6},{6,2},{1... | collective-permute-start | bytes 196616 | tf_op jit(solution)/shard_map/ppermute | solution.py:305
  57.4 1.1 %collective-permute-start.7 = (bf16[128,256]{1,0:T(8,128)(2,1)S(1)}, bf16[128,256]{1,0:T(8,128)(2,1)S(1)}, u32[]{:S(2)}, u32[]{:S(2)}) collective-permute-start(bf16[128,256]{1,0:T(8,128)(2,1)S(1)} %get-tuple-element.34), channel_id=1, source_target_pairs={{0,8},{4,12},{8,0},{12,4},{1,9},{5,13},{9,1},{13,5},{2,10},{6,14},... | collective-permute-start | bytes 196616 | tf_op jit(solution)/shard_map/ppermute | solution.py:305
  58.5 1.4 %collective-permute-start.8 = (bf16[128,256]{1,0:T(8,128)(2,1)S(1)}, bf16[128,256]{1,0:T(8,128)(2,1)S(1)}, u32[]{:S(2)}, u32[]{:S(2)}) collective-permute-start(bf16[128,256]{1,0:T(8,128)(2,1)S(1)} %get-tuple-element.35), channel_id=1, source_target_pairs={{0,12},{4,8},{8,4},{12,0},{1,13},{5,9},{9,5},{13,1},{2,14},{6,10},... | collective-permute-start | bytes 196616 | tf_op jit(solution)/shard_map/ppermute | solution.py:305
  59.9 0.5 collective-permute-done.6.refs_1_
  60.4 3.4 %collective-permute-done.7.refs_2_ = bf16[128,256]{1,0:T(8,128)(2,1)S(1)} collective-permute-done((bf16[128,256]{1,0:T(8,128)(2,1)S(1)}, bf16[128,256]{1,0:T(8,128)(2,1)S(1)}, u32[]{:S(2)}, u32[]{:S(2)}) %collective-permute-start.7) | collective-permute-done | bytes 65568 | tf_op jit(solution)/shard_map/ppermute | solution.py:305
  63.8 0.9 %collective-permute-done.8.refs_3_ = bf16[128,256]{1,0:T(8,128)(2,1)S(1)} collective-permute-done((bf16[128,256]{1,0:T(8,128)(2,1)S(1)}, bf16[128,256]{1,0:T(8,128)(2,1)S(1)}, u32[]{:S(2)}, u32[]{:S(2)}) %collective-permute-start.8) | collective-permute-done | bytes 65568 | tf_op jit(solution)/shard_map/ppermute | solution.py:305
  64.6 0.7 project.3
  65.4 0.7 project.2
  66.2 0.6 collective-permute-start.9
  66.7 0.2 collective-permute-done.10
  67.0 1.6 %collective-permute-start.11 = (bf16[128,1024]{1,0:T(8,128)(2,1)S(1)}, bf16[128,1024]{1,0:T(8,128)(2,1)S(1)}, u32[]{:S(2)}, u32[]{:S(2)}) collective-permute-start(bf16[128,1024]{1,0:T(8,128)(2,1)S(1)} %add_convert_fusion.1), channel_id=1, source_target_pairs={{0,2},{1,3},{2,0},{3,1},{4,6},{5,7},{6,4},{7,5},{8,10},{9,11},{10,... | collective-permute-start | bytes 786440 | tf_op jit(solution)/shard_map/ppermute | solution.py:305
  68.6 6.9 %collective-permute-done.11 = bf16[128,1024]{1,0:T(8,128)(2,1)S(1)} collective-permute-done((bf16[128,1024]{1,0:T(8,128)(2,1)S(1)}, bf16[128,1024]{1,0:T(8,128)(2,1)S(1)}, u32[]{:S(2)}, u32[]{:S(2)}) %collective-permute-start.11) | collective-permute-done | bytes 262176 | tf_op jit(solution)/shard_map/ppermute | solution.py:305
  75.4 0.8 %add_convert_fusion = bf16[128,1024]{1,0:T(8,128)(2,1)} fusion(bf16[128,1024]{1,0:T(8,128)(2,1)S(1)} %collective-permute-done.11, bf16[128,1024]{1,0:T(8,128)(2,1)S(1)} %collective-permute-done.9, bf16[128,1024]{1,0:T(8,128)(2,1)S(1)} %get-tuple-element.37), kind=kLoop, calls=%fused_computation | loop fusion | flops 786432 | bytes 1048576 | tf_op jit(solution)/shard_map/convert_element_type | solution.py:413
  (18 shorter events, 0.2 us)
Async XLA Ops:
  0.0 43.8 %copy-start.1 = (bf16[3,3,1024]{2,1,0:T(4,128)(2,1)S(1)}, bf16[3,3,1024]{2,1,0:T(4,128)(2,1)}, u32[]{:S(2)}) copy-start(bf16[3,3,1024]{2,1,0:T(4,128)(2,1)} %refs_5_.1) | copy-start | bytes 55300
  0.0 43.8 %copy-start.4 = (f32[1024]{0:T(1024)S(1)}, f32[1024]{0:T(1024)}, u32[]{:S(2)}) copy-start(f32[1024]{0:T(1024)} %param.10) | copy-start | bytes 12292
  25.1 28.2 %copy-start = (bf16[256,256]{1,0:T(8,128)(2,1)S(1)}, bf16[256,256]{1,0:T(8,128)(2,1)}, u32[]{:S(2)}) copy-start(bf16[256,256]{1,0:T(8,128)(2,1)} %get-tuple-element.23.refs_0_) | copy-start | bytes 393220
  25.1 10.1 %collective-permute-start.3 = (bf16[272,256]{1,0:T(8,128)(2,1)}, bf16[272,256]{1,0:T(8,128)(2,1)S(1)}, u32[]{:S(2)}, u32[]{:S(2)}) collective-permute-start(bf16[272,256]{1,0:T(8,128)(2,1)} %get-tuple-element.28), channel_id=1, source_target_pairs={{0,4},{4,0},{8,12},{12,8},{1,5},{5,1},{9,13},{13,9},{2,6},{6,2},{1... | collective-permute-start | bytes 417800 | tf_op jit(solution)/shard_map/ppermute | solution.py:305
  28.2 15.5 %collective-permute-start.4 = (bf16[272,256]{1,0:T(8,128)(2,1)}, bf16[272,256]{1,0:T(8,128)(2,1)S(1)}, u32[]{:S(2)}, u32[]{:S(2)}) collective-permute-start(bf16[272,256]{1,0:T(8,128)(2,1)} %get-tuple-element.29), channel_id=1, source_target_pairs={{0,8},{4,12},{8,0},{12,4},{1,9},{5,13},{9,1},{13,5},{2,10},{6,14},... | collective-permute-start | bytes 417800 | tf_op jit(solution)/shard_map/ppermute | solution.py:305
  30.8 12.9 %collective-permute-start.5 = (bf16[272,256]{1,0:T(8,128)(2,1)}, bf16[272,256]{1,0:T(8,128)(2,1)S(1)}, u32[]{:S(2)}, u32[]{:S(2)}) collective-permute-start(bf16[272,256]{1,0:T(8,128)(2,1)} %get-tuple-element.30), channel_id=1, source_target_pairs={{0,12},{4,8},{8,4},{12,0},{1,13},{5,9},{9,5},{13,1},{2,14},{6,10},... | collective-permute-start | bytes 417800 | tf_op jit(solution)/shard_map/ppermute | solution.py:305
  30.8 14.3 %collective-permute-start = (bf16[256,256]{1,0:T(8,128)(2,1)}, bf16[256,256]{1,0:T(8,128)(2,1)S(1)}, u32[]{:S(2)}, u32[]{:S(2)}) collective-permute-start(bf16[256,256]{1,0:T(8,128)(2,1)} %get-tuple-element.24), channel_id=1, source_target_pairs={{0,4},{4,0},{8,12},{12,8},{1,5},{5,1},{9,13},{13,9},{2,6},{6,2},{1... | collective-permute-start | bytes 393224 | tf_op jit(solution)/shard_map/ppermute | solution.py:305
  31.7 21.6 %collective-permute-start.1 = (bf16[256,256]{1,0:T(8,128)(2,1)}, bf16[256,256]{1,0:T(8,128)(2,1)S(1)}, u32[]{:S(2)}, u32[]{:S(2)}) collective-permute-start(bf16[256,256]{1,0:T(8,128)(2,1)} %get-tuple-element.25), channel_id=1, source_target_pairs={{0,8},{4,12},{8,0},{12,4},{1,9},{5,13},{9,1},{13,5},{2,10},{6,14},... | collective-permute-start | bytes 393224 | tf_op jit(solution)/shard_map/ppermute | solution.py:305
  35.2 18.1 %collective-permute-start.2 = (bf16[256,256]{1,0:T(8,128)(2,1)}, bf16[256,256]{1,0:T(8,128)(2,1)S(1)}, u32[]{:S(2)}, u32[]{:S(2)}) collective-permute-start(bf16[256,256]{1,0:T(8,128)(2,1)} %get-tuple-element.26), channel_id=1, source_target_pairs={{0,12},{4,8},{8,4},{12,0},{1,13},{5,9},{9,5},{13,1},{2,14},{6,10},... | collective-permute-start | bytes 393224 | tf_op jit(solution)/shard_map/ppermute | solution.py:305
  39.6 0.7 copy-start.2
  40.3 3.5 %copy-start.3 = (bf16[272,256]{1,0:T(8,128)(2,1)S(1)}, bf16[272,256]{1,0:T(8,128)(2,1)}, u32[]{:S(2)}) copy-start(bf16[272,256]{1,0:T(8,128)(2,1)} %get-tuple-element.27.refs_0_) | copy-start | bytes 417796
  55.3 5.0 %collective-permute-start.6 = (bf16[128,256]{1,0:T(8,128)(2,1)S(1)}, bf16[128,256]{1,0:T(8,128)(2,1)S(1)}, u32[]{:S(2)}, u32[]{:S(2)}) collective-permute-start(bf16[128,256]{1,0:T(8,128)(2,1)S(1)} %get-tuple-element.33), channel_id=1, source_target_pairs={{0,4},{4,0},{8,12},{12,8},{1,5},{5,1},{9,13},{13,9},{2,6},{6,2},{1... | collective-permute-start | bytes 196616 | tf_op jit(solution)/shard_map/ppermute | solution.py:305
  57.4 6.4 %collective-permute-start.7 = (bf16[128,256]{1,0:T(8,128)(2,1)S(1)}, bf16[128,256]{1,0:T(8,128)(2,1)S(1)}, u32[]{:S(2)}, u32[]{:S(2)}) collective-permute-start(bf16[128,256]{1,0:T(8,128)(2,1)S(1)} %get-tuple-element.34), channel_id=1, source_target_pairs={{0,8},{4,12},{8,0},{12,4},{1,9},{5,13},{9,1},{13,5},{2,10},{6,14},... | collective-permute-start | bytes 196616 | tf_op jit(solution)/shard_map/ppermute | solution.py:305
  58.5 6.1 %collective-permute-start.8 = (bf16[128,256]{1,0:T(8,128)(2,1)S(1)}, bf16[128,256]{1,0:T(8,128)(2,1)S(1)}, u32[]{:S(2)}, u32[]{:S(2)}) collective-permute-start(bf16[128,256]{1,0:T(8,128)(2,1)S(1)} %get-tuple-element.35), channel_id=1, source_target_pairs={{0,12},{4,8},{8,4},{12,0},{1,13},{5,9},{9,5},{13,1},{2,14},{6,10},... | collective-permute-start | bytes 196616 | tf_op jit(solution)/shard_map/ppermute | solution.py:305
  65.4 1.6 %collective-permute-start.10 = (bf16[128,1024]{1,0:T(8,128)(2,1)S(1)}, bf16[128,1024]{1,0:T(8,128)(2,1)S(1)}, u32[]{:S(2)}, u32[]{:S(2)}) collective-permute-start(bf16[128,1024]{1,0:T(8,128)(2,1)S(1)} %get-tuple-element.40), channel_id=1, source_target_pairs={{0,1},{1,0},{2,3},{3,2},{4,5},{5,4},{6,7},{7,6},{8,9},{9,8},{10,11... | collective-permute-start | bytes 786440 | tf_op jit(solution)/shard_map/ppermute | solution.py:305
  66.2 2.4 %collective-permute-start.9 = (bf16[128,1024]{1,0:T(8,128)(2,1)S(1)}, bf16[128,1024]{1,0:T(8,128)(2,1)S(1)}, u32[]{:S(2)}, u32[]{:S(2)}) collective-permute-start(bf16[128,1024]{1,0:T(8,128)(2,1)S(1)} %get-tuple-element.38), channel_id=1, source_target_pairs={{0,1},{1,0},{2,3},{3,2},{4,5},{5,4},{6,7},{7,6},{8,9},{9,8},{10,11... | collective-permute-start | bytes 786440 | tf_op jit(solution)/shard_map/ppermute | solution.py:305
  67.0 8.4 %collective-permute-start.11 = (bf16[128,1024]{1,0:T(8,128)(2,1)S(1)}, bf16[128,1024]{1,0:T(8,128)(2,1)S(1)}, u32[]{:S(2)}, u32[]{:S(2)}) collective-permute-start(bf16[128,1024]{1,0:T(8,128)(2,1)S(1)} %add_convert_fusion.1), channel_id=1, source_target_pairs={{0,2},{1,3},{2,0},{3,1},{4,6},{5,7},{6,4},{7,5},{8,10},{9,11},{10,... | collective-permute-start | bytes 786440 | tf_op jit(solution)/shard_map/ppermute | solution.py:305

commit v4 on v3

--- a/solution.py
+++ b/solution.py
@@ -116,51 +116,46 @@
 def pack_kernel(inputs_any, short_any, queries_any, keys_any, *refs):
     count = 4
     first_refs, second_refs = refs[:count], refs[count : 2 * count]
-    signal_s, short_s, gate_s, in_sems, gate_sems, plain_sems = refs[2 * count :]
-    rows, own = signal_s.shape[2:]
-    edged = gate_s.shape[1]
+    inputs_s, short_s, queries_s, keys_s, in_sems = refs[2 * count :]
+    rows, own = second_refs[0].shape[0] // 2, second_refs[0].shape[1]
+    edged = rows + 16
     position = lax.axis_index("ctx")
     columns = [pl.ds(pl.multiple_of((position ^ step) * own, own), own) for step in range(count)]
     order = (3, 2, 1, 0)
-    load_short = pltpu.make_async_copy(short_any, short_s, in_sems.at[count])
-    load_short.start()
     loads = [
-        pltpu.make_async_copy(inputs_any.at[1:3, :, columns[step]], signal_s.at[step], in_sems.at[step])
-        for step in range(count)
+        pltpu.make_async_copy(source, held, in_sems.at[index])
+        for index, (source, held) in enumerate(
+            (
+                (short_any, short_s),
+                (inputs_any.at[1], inputs_s.at[1]),
+                (inputs_any.at[2], inputs_s.at[2]),
+                (inputs_any.at[0], inputs_s.at[0]),
+                (queries_any, queries_s),
+                (keys_any, keys_s),
+            )
+        )
     ]
+    for load in loads:
+        load.start()
+    edge_row = lax.broadcasted_iota(jnp.int32, (8, own), 0)
+    for load in loads[:4]:
+        load.wait()
     for step in order:
-        loads[step].start()
-    plain = []
-    for step in order:
-        for index, (source, target) in enumerate(
-            (
-                (inputs_any.at[0, :, columns[step]], first_refs[step].at[edged:]),
-                (queries_any.at[:, columns[step]], second_refs[step].at[0:rows]),
-                (keys_any.at[:, columns[step]], second_refs[step].at[rows:]),
-            )
-        ):
-            plain.append(pltpu.make_async_copy(source, target, plain_sems.at[3 * step + index]))
-    for copy in plain:
-        copy.start()
-    edge_row = lax.broadcasted_iota(jnp.int32, (8, own), 0)
-    load_short.wait()
-    stores = []
-    for step in order:
-        loads[step].wait()
         features, edges = [], []
         for stream in (1, 2):
-            signal = signal_s[step, stream - 1].astype(jnp.float32)
+            signal = inputs_s[stream, :, columns[step]].astype(jnp.float32)
             taps = [short_s[lag, stream : stream + 1, columns[step]].astype(jnp.float32) for lag in range(3)]
             features.append(featured(signal, taps))
             last = pltpu.roll(signal[rows - 8 :], 4, 0)
             edges.append(jnp.where(edge_row < 2, signal[:8], jnp.where(edge_row < 4, last, 0.0)))
-        gate_s[step, 0:rows] = (features[0] * features[1]).astype(jnp.bfloat16)
-        gate_s[step, rows:] = jnp.concatenate(edges, axis=0).astype(jnp.bfloat16)
-        store = pltpu.make_async_copy(gate_s.at[step], first_refs[step].at[0:edged], gate_sems.at[step])
-        store.start()
-        stores.append(store)
-    for copy in plain + stores:
-        copy.wait()
+        first_refs[step][0:rows] = (features[0] * features[1]).astype(jnp.bfloat16)
+        first_refs[step][rows:edged] = jnp.concatenate(edges, axis=0).astype(jnp.bfloat16)
+        first_refs[step][edged:] = inputs_s[0, :, columns[step]]
+    for load in loads[4:]:
+        load.wait()
+    for step in order:
+        second_refs[step][0:rows] = queries_s[:, columns[step]]
+        second_refs[step][rows:] = keys_s[:, columns[step]]
 
 
 def ready_kernel(filter_ref, weight_any, band_ref, weight_ref, sem):
@@ -325,14 +320,13 @@
         pack_kernel,
         out_shape=[first] * count + [second] * count,
         in_specs=[IN_HBM] * 4,
-        out_specs=[IN_HBM] * (2 * count),
+        out_specs=[IN_VMEM] * (2 * count),
         scratch_shapes=[
-            pltpu.VMEM((count, 2, rows, own), jnp.bfloat16),
+            pltpu.VMEM((streams, rows, channels), jnp.bfloat16),
             pltpu.VMEM(short_filter.shape, jnp.bfloat16),
-            pltpu.VMEM((count, rows + 16, own), jnp.bfloat16),
-            pltpu.SemaphoreType.DMA((count + 1,)),
-            pltpu.SemaphoreType.DMA((count,)),
-            pltpu.SemaphoreType.DMA((3 * count,)),
+            pltpu.VMEM(queries.shape, jnp.bfloat16),
+            pltpu.VMEM(key_rows.shape, jnp.bfloat16),
+            pltpu.SemaphoreType.DMA((6,)),
         ],
         compiler_params=pltpu.CompilerParams(vmem_limit_bytes=WIDE_LIMIT),
         name="pack",

time: 76.5 us -> 54 us (0.71)
  Pallas kernels: 33.4 us -> 10.9 us
    pallas_call x1, Pallas kernels: 25.1 us -> 2.63 us  [by_heads(): pl.pallas_call(pack_kernel, out_shape=[first] * count + [second] * count,...]
  transfers between devices with their start and end apart: 12 -> 12, of which waited for: 6 -> 6; matrix products, arithmetic and copies ran while one was open for 0% -> 0% of each run, Pallas kernels for 7% -> 10%
where the time goes in v4:
time: 54 us; the launch traced here: 53.8 us
  starting transfers between devices  21.1 us (39%)
  waiting for transfers between devices  20 us (37%)
  Pallas kernels  10.9 us (20%)
  other arithmetic  0.89 us (2%)
  local copies, waits for them, and re-layouts  0.73 us (1%)
    ppermute x12, starting transfers between devices, swapped(): lax.ppermute(value, axis, [(source, source ^ step) for source in range(la...  21.1 us
    ppermute x12, waiting for transfers between devices, swapped(): lax.ppermute(value, axis, [(source, source ^ step) for source in range(la...  20 us
    pallas_call x1, Pallas kernels, by_heads(): pl.pallas_call(ready_kernel, out_shape=[jax.ShapeDtypeStruct((own_groups...  3.44 us
    pallas_call x1, Pallas kernels, by_heads(): pl.pallas_call(pack_kernel, out_shape=[first] * count + [second] * count,...  2.63 us
    pallas_call x1, Pallas kernels, by_heads(): pl.pallas_call(attend_kernel, out_shape=[piece] * count, in_specs=[IN_VME...  2 us
    pallas_call x2, Pallas kernels, projected(): pl.pallas_call(functools.partial(project_kernel, masks), out_shape=[jax.S...  1.47 us
    pallas_call x1, Pallas kernels, by_heads(): pl.pallas_call(values_kernel, out_shape=jax.ShapeDtypeStruct((count * row...  1.34 us
  transfers between devices with their start and end apart: 12, of which 6 were waited for; matrix products, arithmetic and copies ran while one was open for 0% of the time, Pallas kernels for 10%

profile of v4, /device:TPU:0, one launch (start us, length us, event | category | flops | bytes accessed | tf_op | source)
XLA Modules:
  0.0 53.8 jit_solution(1230554687035693105)
XLA Ops:
  0.0 2.6 %pack.1 = (bf16[272,256]{1,0:T(8,128)(2,1)}, bf16[272,256]{1,0:T(8,128)(2,1)}, bf16[272,256]{1,0:T(8,128)(2,1)}, bf16[272,256]{1,0:T(8,128)(2,1)}, bf16[256,256]...) custom-call(bf16[3,128,1024]{2,1,0:T(8,128)(2,1)} %bitcast.4, ...), custom_call_target="tpu_custom_call" | custom-call | tf_op jit(solution)/shard_map/pack/pallas_call | solution.py:319
  2.7 3.1 %collective-permute-start.3 = (bf16[272,256]{1,0:T(8,128)(2,1)}, bf16[272,256]{1,0:T(8,128)(2,1)S(1)}, u32[]{:S(2)}, u32[]{:S(2)}) collective-permute-start(bf16[272,256]{1,0:T(8,128)(2,1)} %get-tuple-element.28), channel_id=1, source_target_pairs={{0,4},{4,0},{8,12},{12,8},{1,5},{5,1},{9,13},{13,9},{2,6},{6,2},{1... | collective-permute-start | bytes 417800 | tf_op jit(solution)/shard_map/ppermute | solution.py:300
  5.7 2.6 %collective-permute-start.4 = (bf16[272,256]{1,0:T(8,128)(2,1)}, bf16[272,256]{1,0:T(8,128)(2,1)S(1)}, u32[]{:S(2)}, u32[]{:S(2)}) collective-permute-start(bf16[272,256]{1,0:T(8,128)(2,1)} %get-tuple-element.29), channel_id=1, source_target_pairs={{0,8},{4,12},{8,0},{12,4},{1,9},{5,13},{9,1},{13,5},{2,10},{6,14},... | collective-permute-start | bytes 417800 | tf_op jit(solution)/shard_map/ppermute | solution.py:300
  8.3 0.9 %collective-permute-start = (bf16[256,256]{1,0:T(8,128)(2,1)}, bf16[256,256]{1,0:T(8,128)(2,1)S(1)}, u32[]{:S(2)}, u32[]{:S(2)}) collective-permute-start(bf16[256,256]{1,0:T(8,128)(2,1)} %get-tuple-element.24), channel_id=1, source_target_pairs={{0,4},{4,0},{8,12},{12,8},{1,5},{5,1},{9,13},{13,9},{2,6},{6,2},{1... | collective-permute-start | bytes 393224 | tf_op jit(solution)/shard_map/ppermute | solution.py:300
  9.2 3.5 %collective-permute-start.1 = (bf16[256,256]{1,0:T(8,128)(2,1)}, bf16[256,256]{1,0:T(8,128)(2,1)S(1)}, u32[]{:S(2)}, u32[]{:S(2)}) collective-permute-start(bf16[256,256]{1,0:T(8,128)(2,1)} %get-tuple-element.25), channel_id=1, source_target_pairs={{0,8},{4,12},{8,0},{12,4},{1,9},{5,13},{9,1},{13,5},{2,10},{6,14},... | collective-permute-start | bytes 393224 | tf_op jit(solution)/shard_map/ppermute | solution.py:300
  12.7 4.4 %collective-permute-start.2 = (bf16[256,256]{1,0:T(8,128)(2,1)}, bf16[256,256]{1,0:T(8,128)(2,1)S(1)}, u32[]{:S(2)}, u32[]{:S(2)}) collective-permute-start(bf16[256,256]{1,0:T(8,128)(2,1)} %get-tuple-element.26), channel_id=1, source_target_pairs={{0,12},{4,8},{8,4},{12,0},{1,13},{5,9},{9,5},{13,1},{2,14},{6,10},... | collective-permute-start | bytes 393224 | tf_op jit(solution)/shard_map/ppermute | solution.py:300
  17.1 0.7 %copy-done.2 = bf16[64,128]{1,0:T(8,128)(2,1)S(1)} copy-done((bf16[64,128]{1,0:T(8,128)(2,1)S(1)}, bf16[64,128]{1,0:T(8,128)(2,1)}, u32[]{:S(2)}) %copy-start.2) | copy-done | bytes 16408
  17.8 3.4 %ready.1 = (bf16[2048,256]{1,0:T(8,128)(2,1)S(1)}, bf16[1024,4096]{1,0:T(8,128)(2,1)S(1)}) custom-call(bf16[64,128]{1,0:T(8,128)(2,1)S(1)} %copy-done.2, bf16[1024,4096]{1,0:T(8,128)(2,1)} %weight_any.1), custom_call_target="tpu_custom_call" | custom-call | tf_op jit(solution)/shard_map/ready/pallas_call | solution.py:336
  21.3 1.3 %values.1.refs_4_ = bf16[512,256]{1,0:T(8,128)(2,1)S(1)} custom-call(s32[1]{0:T(128)} %bitcast.1.at, bf16[272,256]{1,0:T(8,128)(2,1)S(1)} %copy-done.3, bf16[272,256]{1,0:T(8,128)(2,1)S(1)} %collective-permute-done.3.refs_1_, bf16[272,256]{1,0:T(8,128)(2,1)S(1)} %collective-permute-done.4.refs_2_, bf16[272,256]{1,0:T(8,128)(2,1)S(1)} %collective-permute-done.5.refs_3_, ...), custom_call_target="tpu_custom_call" | custom-call | flops 536870912 | bytes 2097152 | tf_op jit(solution)/shard_map/values/pallas_call | solution.py:348
  22.6 8.2 %collective-permute-done.1.refs_2_ = bf16[256,256]{1,0:T(8,128)(2,1)S(1)} collective-permute-done((bf16[256,256]{1,0:T(8,128)(2,1)}, bf16[256,256]{1,0:T(8,128)(2,1)S(1)}, u32[]{:S(2)}, u32[]{:S(2)}) %collective-permute-start.1) | collective-permute-done | bytes 131104 | tf_op jit(solution)/shard_map/ppermute | solution.py:300
  30.8 2.0 %attend.1 = (bf16[128,256]{1,0:T(8,128)(2,1)S(1)}, bf16[128,256]{1,0:T(8,128)(2,1)S(1)}, bf16[128,256]{1,0:T(8,128)(2,1)S(1)}, bf16[128,256]{1,0:T(8,128)(2,1)S(1)}) custom-call(bf16[256,256]{1,0:T(8,128)(2,1)S(1)} %copy-done, bf16[256,256]{1,0:T(8,128)(2,1)S(1)} %collective-permute-done.refs_1_, bf16[256,256]{1,0:T(8,128)(2,1)S(1)} %collective-permute-done.1.refs_2_, ...), custom_call_target="tpu_custom_call" | custom-call | tf_op jit(solution)/shard_map/attend/pallas_call | solution.py:370
  32.8 2.0 %collective-permute-start.6 = (bf16[128,256]{1,0:T(8,128)(2,1)S(1)}, bf16[128,256]{1,0:T(8,128)(2,1)S(1)}, u32[]{:S(2)}, u32[]{:S(2)}) collective-permute-start(bf16[128,256]{1,0:T(8,128)(2,1)S(1)} %get-tuple-element.33), channel_id=1, source_target_pairs={{0,4},{4,0},{8,12},{12,8},{1,5},{5,1},{9,13},{13,9},{2,6},{6,2},{1... | collective-permute-start | bytes 196616 | tf_op jit(solution)/shard_map/ppermute | solution.py:300
  34.9 1.1 %collective-permute-start.7 = (bf16[128,256]{1,0:T(8,128)(2,1)S(1)}, bf16[128,256]{1,0:T(8,128)(2,1)S(1)}, u32[]{:S(2)}, u32[]{:S(2)}) collective-permute-start(bf16[128,256]{1,0:T(8,128)(2,1)S(1)} %get-tuple-element.34), channel_id=1, source_target_pairs={{0,8},{4,12},{8,0},{12,4},{1,9},{5,13},{9,1},{13,5},{2,10},{6,14},... | collective-permute-start | bytes 196616 | tf_op jit(solution)/shard_map/ppermute | solution.py:300
  36.0 1.4 %collective-permute-start.8 = (bf16[128,256]{1,0:T(8,128)(2,1)S(1)}, bf16[128,256]{1,0:T(8,128)(2,1)S(1)}, u32[]{:S(2)}, u32[]{:S(2)}) collective-permute-start(bf16[128,256]{1,0:T(8,128)(2,1)S(1)} %get-tuple-element.35), channel_id=1, source_target_pairs={{0,12},{4,8},{8,4},{12,0},{1,13},{5,9},{9,5},{13,1},{2,14},{6,10},... | collective-permute-start | bytes 196616 | tf_op jit(solution)/shard_map/ppermute | solution.py:300
  37.4 0.5 collective-permute-done.6.refs_1_
  37.9 3.4 %collective-permute-done.7.refs_2_ = bf16[128,256]{1,0:T(8,128)(2,1)S(1)} collective-permute-done((bf16[128,256]{1,0:T(8,128)(2,1)S(1)}, bf16[128,256]{1,0:T(8,128)(2,1)S(1)}, u32[]{:S(2)}, u32[]{:S(2)}) %collective-permute-start.7) | collective-permute-done | bytes 65568 | tf_op jit(solution)/shard_map/ppermute | solution.py:300
  41.3 0.9 %collective-permute-done.8.refs_3_ = bf16[128,256]{1,0:T(8,128)(2,1)S(1)} collective-permute-done((bf16[128,256]{1,0:T(8,128)(2,1)S(1)}, bf16[128,256]{1,0:T(8,128)(2,1)S(1)}, u32[]{:S(2)}, u32[]{:S(2)}) %collective-permute-start.8) | collective-permute-done | bytes 65568 | tf_op jit(solution)/shard_map/ppermute | solution.py:300
  42.1 0.7 %project.3 = (bf16[128,1024]{1,0:T(8,128)(2,1)S(1)}, bf16[128,1024]{1,0:T(8,128)(2,1)S(1)}) custom-call(bf16[128,256]{1,0:T(8,128)(2,1)S(1)} %get-tuple-element.32.refs_0_, bf16[128,256]{1,0:T(8,128)(2,1)S(1)} %collective-permute-done.6.refs_1_, bf16[128,256]{1,0:T(8,128)(2,1)S(1)} %collective-permute-done.7.refs_2_, ...), custom_call_target="tpu_custom_call" | custom-call | flops 536870912 | bytes 4194304 | tf_op jit(solution)/shard_map/project/pallas_call | solution.py:389
  42.9 0.7 %project.2 = (bf16[128,1024]{1,0:T(8,128)(2,1)S(1)}, bf16[128,1024]{1,0:T(8,128)(2,1)S(1)}) custom-call(bf16[128,256]{1,0:T(8,128)(2,1)S(1)} %get-tuple-element.32.refs_0_, bf16[128,256]{1,0:T(8,128)(2,1)S(1)} %collective-permute-done.6.refs_1_, bf16[128,256]{1,0:T(8,128)(2,1)S(1)} %collective-permute-done.7.refs_2_, ...), custom_call_target="tpu_custom_call" | custom-call | flops 536870912 | bytes 4194304 | tf_op jit(solution)/shard_map/project/pallas_call | solution.py:389
  43.7 0.6 %collective-permute-start.9 = (bf16[128,1024]{1,0:T(8,128)(2,1)S(1)}, bf16[128,1024]{1,0:T(8,128)(2,1)S(1)}, u32[]{:S(2)}, u32[]{:S(2)}) collective-permute-start(bf16[128,1024]{1,0:T(8,128)(2,1)S(1)} %get-tuple-element.38), channel_id=1, source_target_pairs={{0,1},{1,0},{2,3},{3,2},{4,5},{5,4},{6,7},{7,6},{8,9},{9,8},{10,11... | collective-permute-start | bytes 786440 | tf_op jit(solution)/shard_map/ppermute | solution.py:300
  44.2 0.2 collective-permute-done.10
  44.5 1.6 %collective-permute-start.11 = (bf16[128,1024]{1,0:T(8,128)(2,1)S(1)}, bf16[128,1024]{1,0:T(8,128)(2,1)S(1)}, u32[]{:S(2)}, u32[]{:S(2)}) collective-permute-start(bf16[128,1024]{1,0:T(8,128)(2,1)S(1)} %add_convert_fusion.1), channel_id=1, source_target_pairs={{0,2},{1,3},{2,0},{3,1},{4,6},{5,7},{6,4},{7,5},{8,10},{9,11},{10,... | collective-permute-start | bytes 786440 | tf_op jit(solution)/shard_map/ppermute | solution.py:300
  46.1 6.9 %collective-permute-done.11 = bf16[128,1024]{1,0:T(8,128)(2,1)S(1)} collective-permute-done((bf16[128,1024]{1,0:T(8,128)(2,1)S(1)}, bf16[128,1024]{1,0:T(8,128)(2,1)S(1)}, u32[]{:S(2)}, u32[]{:S(2)}) %collective-permute-start.11) | collective-permute-done | bytes 262176 | tf_op jit(solution)/shard_map/ppermute | solution.py:300
  52.9 0.8 %add_convert_fusion = bf16[128,1024]{1,0:T(8,128)(2,1)} fusion(bf16[128,1024]{1,0:T(8,128)(2,1)S(1)} %collective-permute-done.11, bf16[128,1024]{1,0:T(8,128)(2,1)S(1)} %collective-permute-done.9, bf16[128,1024]{1,0:T(8,128)(2,1)S(1)} %get-tuple-element.37), kind=kLoop, calls=%fused_computation | loop fusion | flops 786432 | bytes 1048576 | tf_op jit(solution)/shard_map/convert_element_type | solution.py:407
  (18 shorter events, 0.2 us)
Async XLA Ops:
  0.0 21.3 %copy-start.1 = (bf16[3,3,1024]{2,1,0:T(4,128)(2,1)S(1)}, bf16[3,3,1024]{2,1,0:T(4,128)(2,1)}, u32[]{:S(2)}) copy-start(bf16[3,3,1024]{2,1,0:T(4,128)(2,1)} %refs_5_.1) | copy-start | bytes 55300
  0.0 21.3 %copy-start.4 = (f32[1024]{0:T(1024)S(1)}, f32[1024]{0:T(1024)}, u32[]{:S(2)}) copy-start(f32[1024]{0:T(1024)} %param.10) | copy-start | bytes 12292
  2.6 28.2 %copy-start = (bf16[256,256]{1,0:T(8,128)(2,1)S(1)}, bf16[256,256]{1,0:T(8,128)(2,1)}, u32[]{:S(2)}) copy-start(bf16[256,256]{1,0:T(8,128)(2,1)} %get-tuple-element.23.refs_0_) | copy-start | bytes 393220
  2.7 10.1 %collective-permute-start.3 = (bf16[272,256]{1,0:T(8,128)(2,1)}, bf16[272,256]{1,0:T(8,128)(2,1)S(1)}, u32[]{:S(2)}, u32[]{:S(2)}) collective-permute-start(bf16[272,256]{1,0:T(8,128)(2,1)} %get-tuple-element.28), channel_id=1, source_target_pairs={{0,4},{4,0},{8,12},{12,8},{1,5},{5,1},{9,13},{13,9},{2,6},{6,2},{1... | collective-permute-start | bytes 417800 | tf_op jit(solution)/shard_map/ppermute | solution.py:300
  5.7 15.5 %collective-permute-start.4 = (bf16[272,256]{1,0:T(8,128)(2,1)}, bf16[272,256]{1,0:T(8,128)(2,1)S(1)}, u32[]{:S(2)}, u32[]{:S(2)}) collective-permute-start(bf16[272,256]{1,0:T(8,128)(2,1)} %get-tuple-element.29), channel_id=1, source_target_pairs={{0,8},{4,12},{8,0},{12,4},{1,9},{5,13},{9,1},{13,5},{2,10},{6,14},... | collective-permute-start | bytes 417800 | tf_op jit(solution)/shard_map/ppermute | solution.py:300
  8.3 12.9 %collective-permute-start.5 = (bf16[272,256]{1,0:T(8,128)(2,1)}, bf16[272,256]{1,0:T(8,128)(2,1)S(1)}, u32[]{:S(2)}, u32[]{:S(2)}) collective-permute-start(bf16[272,256]{1,0:T(8,128)(2,1)} %get-tuple-element.30), channel_id=1, source_target_pairs={{0,12},{4,8},{8,4},{12,0},{1,13},{5,9},{9,5},{13,1},{2,14},{6,10},... | collective-permute-start | bytes 417800 | tf_op jit(solution)/shard_map/ppermute | solution.py:300
  8.3 14.3 %collective-permute-start = (bf16[256,256]{1,0:T(8,128)(2,1)}, bf16[256,256]{1,0:T(8,128)(2,1)S(1)}, u32[]{:S(2)}, u32[]{:S(2)}) collective-permute-start(bf16[256,256]{1,0:T(8,128)(2,1)} %get-tuple-element.24), channel_id=1, source_target_pairs={{0,4},{4,0},{8,12},{12,8},{1,5},{5,1},{9,13},{13,9},{2,6},{6,2},{1... | collective-permute-start | bytes 393224 | tf_op jit(solution)/shard_map/ppermute | solution.py:300
  9.2 21.6 %collective-permute-start.1 = (bf16[256,256]{1,0:T(8,128)(2,1)}, bf16[256,256]{1,0:T(8,128)(2,1)S(1)}, u32[]{:S(2)}, u32[]{:S(2)}) collective-permute-start(bf16[256,256]{1,0:T(8,128)(2,1)} %get-tuple-element.25), channel_id=1, source_target_pairs={{0,8},{4,12},{8,0},{12,4},{1,9},{5,13},{9,1},{13,5},{2,10},{6,14},... | collective-permute-start | bytes 393224 | tf_op jit(solution)/shard_map/ppermute | solution.py:300
  12.7 18.1 %collective-permute-start.2 = (bf16[256,256]{1,0:T(8,128)(2,1)}, bf16[256,256]{1,0:T(8,128)(2,1)S(1)}, u32[]{:S(2)}, u32[]{:S(2)}) collective-permute-start(bf16[256,256]{1,0:T(8,128)(2,1)} %get-tuple-element.26), channel_id=1, source_target_pairs={{0,12},{4,8},{8,4},{12,0},{1,13},{5,9},{9,5},{13,1},{2,14},{6,10},... | collective-permute-start | bytes 393224 | tf_op jit(solution)/shard_map/ppermute | solution.py:300
  17.1 0.7 %copy-start.2 = (bf16[64,128]{1,0:T(8,128)(2,1)S(1)}, bf16[64,128]{1,0:T(8,128)(2,1)}, u32[]{:S(2)}) copy-start(bf16[64,128]{1,0:T(8,128)(2,1)} %filter_ref.1) | copy-start | bytes 49156
  17.8 3.5 %copy-start.3 = (bf16[272,256]{1,0:T(8,128)(2,1)S(1)}, bf16[272,256]{1,0:T(8,128)(2,1)}, u32[]{:S(2)}) copy-start(bf16[272,256]{1,0:T(8,128)(2,1)} %get-tuple-element.27.refs_0_) | copy-start | bytes 417796
  32.8 5.0 %collective-permute-start.6 = (bf16[128,256]{1,0:T(8,128)(2,1)S(1)}, bf16[128,256]{1,0:T(8,128)(2,1)S(1)}, u32[]{:S(2)}, u32[]{:S(2)}) collective-permute-start(bf16[128,256]{1,0:T(8,128)(2,1)S(1)} %get-tuple-element.33), channel_id=1, source_target_pairs={{0,4},{4,0},{8,12},{12,8},{1,5},{5,1},{9,13},{13,9},{2,6},{6,2},{1... | collective-permute-start | bytes 196616 | tf_op jit(solution)/shard_map/ppermute | solution.py:300
  34.9 6.4 %collective-permute-start.7 = (bf16[128,256]{1,0:T(8,128)(2,1)S(1)}, bf16[128,256]{1,0:T(8,128)(2,1)S(1)}, u32[]{:S(2)}, u32[]{:S(2)}) collective-permute-start(bf16[128,256]{1,0:T(8,128)(2,1)S(1)} %get-tuple-element.34), channel_id=1, source_target_pairs={{0,8},{4,12},{8,0},{12,4},{1,9},{5,13},{9,1},{13,5},{2,10},{6,14},... | collective-permute-start | bytes 196616 | tf_op jit(solution)/shard_map/ppermute | solution.py:300
  36.0 6.1 %collective-permute-start.8 = (bf16[128,256]{1,0:T(8,128)(2,1)S(1)}, bf16[128,256]{1,0:T(8,128)(2,1)S(1)}, u32[]{:S(2)}, u32[]{:S(2)}) collective-permute-start(bf16[128,256]{1,0:T(8,128)(2,1)S(1)} %get-tuple-element.35), channel_id=1, source_target_pairs={{0,12},{4,8},{8,4},{12,0},{1,13},{5,9},{9,5},{13,1},{2,14},{6,10},... | collective-permute-start | bytes 196616 | tf_op jit(solution)/shard_map/ppermute | solution.py:300
  42.9 1.6 %collective-permute-start.10 = (bf16[128,1024]{1,0:T(8,128)(2,1)S(1)}, bf16[128,1024]{1,0:T(8,128)(2,1)S(1)}, u32[]{:S(2)}, u32[]{:S(2)}) collective-permute-start(bf16[128,1024]{1,0:T(8,128)(2,1)S(1)} %get-tuple-element.40), channel_id=1, source_target_pairs={{0,1},{1,0},{2,3},{3,2},{4,5},{5,4},{6,7},{7,6},{8,9},{9,8},{10,11... | collective-permute-start | bytes 786440 | tf_op jit(solution)/shard_map/ppermute | solution.py:300
  43.7 2.4 %collective-permute-start.9 = (bf16[128,1024]{1,0:T(8,128)(2,1)S(1)}, bf16[128,1024]{1,0:T(8,128)(2,1)S(1)}, u32[]{:S(2)}, u32[]{:S(2)}) collective-permute-start(bf16[128,1024]{1,0:T(8,128)(2,1)S(1)} %get-tuple-element.38), channel_id=1, source_target_pairs={{0,1},{1,0},{2,3},{3,2},{4,5},{5,4},{6,7},{7,6},{8,9},{9,8},{10,11... | collective-permute-start | bytes 786440 | tf_op jit(solution)/shard_map/ppermute | solution.py:300
  44.5 8.4 %collective-permute-start.11 = (bf16[128,1024]{1,0:T(8,128)(2,1)S(1)}, bf16[128,1024]{1,0:T(8,128)(2,1)S(1)}, u32[]{:S(2)}, u32[]{:S(2)}) collective-permute-start(bf16[128,1024]{1,0:T(8,128)(2,1)S(1)} %add_convert_fusion.1), channel_id=1, source_target_pairs={{0,2},{1,3},{2,0},{3,1},{4,6},{5,7},{6,4},{7,5},{8,10},{9,11},{10,... | collective-permute-start | bytes 786440 | tf_op jit(solution)/shard_map/ppermute | solution.py:300

commit v5 on v0

--- a/solution.py
+++ b/solution.py
@@ -1,9 +1,15 @@
+import functools
+
 import jax
 import jax.numpy as jnp
 from jax import lax
+from jax.experimental import pallas as pl
+from jax.experimental.pallas import tpu as pltpu
 from jax.sharding import PartitionSpec as P
 
 HEAD_DIM = 128
+COUNT = 4
+EDGE = 16
 
 
 masked_score = -1e30
@@ -38,8 +44,7 @@
     return features
 
 
-def attend(running, head_queries, query_pos, key_piece, value_piece):
-    running_max, weight_sum, accumulated = running
+def attend(head_queries, query_pos, key_piece, value_piece):
     key_count = key_piece.shape[0]
     head_count = head_queries.shape[1]
     key_heads = key_piece.reshape(key_count, head_count, -1)
@@ -49,8 +54,8 @@
     ) * head_queries.shape[2] ** (-0.5)
     key_pos = lax.iota(jnp.int32, key_count)
     allowed = (key_pos[None, :] <= query_pos[:, None])[None]
-    new_max = jnp.maximum(running_max, jnp.max(jnp.where(allowed, scores, masked_score), axis=2))
-    probabilities = jnp.where(allowed, jnp.exp(scores - new_max[..., None]), 0.0)
+    peak = jnp.max(jnp.where(allowed, scores, masked_score), axis=2)
+    probabilities = jnp.where(allowed, jnp.exp(scores - peak[..., None]), 0.0)
     weight_sum = jnp.sum(probabilities, axis=2)
     mixed = jnp.einsum(
         "hqk,khd->hqd",
@@ -58,25 +63,11 @@
         value_heads,
         preferred_element_type=jnp.float32,
     )
-    accumulated = mixed
-    return (new_max, weight_sum, accumulated)
-
-
-def start_state(head_count, row_count, width):
-    return (
-        jnp.full((head_count, row_count), masked_score, jnp.float32),
-        jnp.zeros((head_count, row_count), jnp.float32),
-        jnp.zeros((head_count, row_count, width), jnp.float32),
-    )
-
-
-def finish(running):
-    running_max, weight_sum, accumulated = running
-    result = accumulated / weight_sum[..., None]
+    result = mixed / weight_sum[..., None]
     return jnp.transpose(result, (1, 0, 2)).reshape(result.shape[1], -1).astype(jnp.bfloat16)
 
 
-def per_device(inputs, short_filter, long_filter, skip_gain, queries, key_rows, out_weight):
+def by_rows(inputs, short_filter, long_filter, skip_gain, queries, key_rows):
     row_count = inputs.shape[0]
     channels = inputs.shape[2]
     groups = long_filter.shape[0]
@@ -102,15 +93,388 @@
     head_count = channels // HEAD_DIM
     head_queries = queries.reshape(row_count, head_count, HEAD_DIM)
     query_pos = position * row_count + lax.iota(jnp.int32, row_count)
-    initial = start_state(head_count, row_count, HEAD_DIM)
-    folded = attend(
-        initial,
+    return attend(
         head_queries,
         query_pos,
         lax.all_gather(key_rows, "ctx", axis=0, tiled=True),
         lax.all_gather(values, "ctx", axis=0, tiled=True),
     )
-    attended = finish(folded)
+
+
+def delayed(signal, lag):
+    if lag == 0:
+        return signal
+    row = lax.broadcasted_iota(jnp.int32, signal.shape, 0)
+    return jnp.where(row < lag, 0.0, pltpu.roll(signal, lag, 0))
+
+
+def featured(signal, taps):
+    total = taps[0] * signal
+    for lag in range(1, len(taps)):
+        total = total + taps[lag] * delayed(signal, lag)
+    return total
+
+
+def columns_of(block, width):
+    return pl.ds(pl.multiple_of(block * width, width), width)
+
+
+def write_gate(signals, taps, out_ref):
+    rows, own = signals[0].shape
+    edge_row = lax.broadcasted_iota(jnp.int32, (8, own), 0)
+    features = [featured(signal, tap) for signal, tap in zip(signals, taps)]
+    edges = [
+        jnp.where(edge_row < 2, signal[:8], jnp.where(edge_row < 4, pltpu.roll(signal[rows - 8 :], 4, 0), 0.0))
+        for signal in signals
+    ]
+    out_ref[0:rows] = (features[0] * features[1]).astype(jnp.bfloat16)
+    out_ref[rows : rows + EDGE] = jnp.concatenate(edges, axis=0).astype(jnp.bfloat16)
+
+
+def far_heads_kernel(queries_any, keys_any, *refs):
+    out_refs, sems = refs[:-1], refs[-1]
+    rows, own = queries_any.shape[0], out_refs[0].shape[1]
+    position = lax.axis_index("ctx")
+    copies = []
+    for step, out_ref in zip((3, 2), out_refs):
+        columns = columns_of(position ^ step, own)
+        for index, source in enumerate((queries_any, keys_any)):
+            target = out_ref.at[index * rows : (index + 1) * rows]
+            copies.append(pltpu.make_async_copy(source.at[:, columns], target, sems.at[len(copies)]))
+    for copy in copies:
+        copy.start()
+    for copy in copies:
+        copy.wait()
+
+
+def far_gate_kernel(inputs_any, short_any, _, *refs):
+    out_refs, (signal_s, short_s, sems) = refs[:2], refs[2:]
+    rows, own = inputs_any.shape[1], out_refs[0].shape[1]
+    position = lax.axis_index("ctx")
+    pair = (position ^ 2) // 2
+    copies = [
+        pltpu.make_async_copy(inputs_any.at[1:3, :, columns_of(pair, 2 * own)], signal_s, sems.at[0]),
+        pltpu.make_async_copy(short_any.at[:, :, columns_of(pair, 2 * own)], short_s, sems.at[1]),
+    ]
+    for step, out_ref in zip((3, 2), out_refs):
+        target = out_ref.at[rows + EDGE :]
+        source = inputs_any.at[0, :, columns_of(position ^ step, own)]
+        copies.append(pltpu.make_async_copy(source, target, sems.at[step]))
+    for copy in copies:
+        copy.start()
+    for copy in copies[:2]:
+        copy.wait()
+    for step, out_ref in zip((3, 2), out_refs):
+        columns = columns_of((position ^ step) % 2, own)
+        signals = [signal_s[stream, :, columns].astype(jnp.float32) for stream in range(2)]
+        taps = [
+            [short_s[lag, stream : stream + 1, columns].astype(jnp.float32) for lag in range(3)] for stream in (1, 2)
+        ]
+        write_gate(signals, taps, out_ref)
+    for copy in copies[2:]:
+        copy.wait()
+
+
+def near_kernel(inputs_any, short_any, queries_any, keys_any, _, *refs):
+    (all_ref, gate_ref, heads_ref), (signal_s, short_s, sems) = refs[:3], refs[3:]
+    rows, own = inputs_any.shape[1], all_ref.shape[1]
+    position = lax.axis_index("ctx")
+    pair = position // 2
+    edged = rows + EDGE
+    mine, other = columns_of(position, own), columns_of(position ^ 1, own)
+    moves = (
+        (inputs_any.at[1:3, :, columns_of(pair, 2 * own)], signal_s),
+        (short_any.at[:, :, columns_of(pair, 2 * own)], short_s),
+        (inputs_any.at[0, :, other], all_ref.at[edged : edged + rows]),
+        (queries_any.at[:, other], all_ref.at[edged + rows : edged + 2 * rows]),
+        (keys_any.at[:, other], all_ref.at[edged + 2 * rows :]),
+        (inputs_any.at[0, :, mine], gate_ref.at[edged:]),
+        (queries_any.at[:, mine], heads_ref.at[0:rows]),
+        (keys_any.at[:, mine], heads_ref.at[rows:]),
+    )
+    copies = [pltpu.make_async_copy(*move, sems.at[index]) for index, move in enumerate(moves)]
+    for copy in copies:
+        copy.start()
+    for copy in copies[:2]:
+        copy.wait()
+    for step, out_ref in ((1, all_ref), (0, gate_ref)):
+        columns = columns_of((position ^ step) % 2, own)
+        signals = [signal_s[stream, :, columns].astype(jnp.float32) for stream in range(2)]
+        taps = [
+            [short_s[lag, stream : stream + 1, columns].astype(jnp.float32) for lag in range(3)] for stream in (1, 2)
+        ]
+        write_gate(signals, taps, out_ref)
+    for copy in copies[2:]:
+        copy.wait()
+
+
+def ready_kernel(filter_ref, weight_any, band_ref, weight_ref, sem):
+    rows, span = band_ref.shape
+    taps = filter_ref.shape[1]
+    groups = rows // taps
+    weights = pltpu.make_async_copy(weight_any, weight_ref, sem)
+    weights.start()
+    source = lax.broadcasted_iota(jnp.int32, (taps, span), 0)
+    target = lax.broadcasted_iota(jnp.int32, (taps, span), 1)
+    flip = (source + target == taps).astype(jnp.bfloat16)
+    first_group = pl.multiple_of(lax.axis_index("ctx") * groups, groups)
+    first = jnp.dot(filter_ref[pl.ds(first_group, groups)], flip, preferred_element_type=jnp.float32)
+    for group in range(groups):
+        repeated = jnp.broadcast_to(first[group : group + 1], (taps, span))
+        banded = pltpu.roll(repeated, 0, 1, stride=1, stride_axis=0)
+        band_ref[group * taps : (group + 1) * taps] = banded.astype(jnp.bfloat16)
+    weights.wait()
+
+
+def weights_kernel(own_ref, near_ref, second_ref, third_ref, weight_ref, total_ref, query_s, key_s):
+    count = COUNT
+    rows, own = own_ref.shape[0] // 2, own_ref.shape[1]
+    position = lax.axis_index("ctx")
+    skip = near_ref.shape[0] - 2 * rows
+    for step, (given, start) in enumerate(((own_ref, 0), (near_ref, skip), (second_ref, 0), (third_ref, 0))):
+        query_s[position ^ step] = given[start : start + rows]
+        key_s[columns_of(position ^ step, rows)] = given[start + rows : start + 2 * rows]
+    causal = lax.broadcasted_iota(jnp.int32, (rows, rows), 1) <= lax.broadcasted_iota(jnp.int32, (rows, rows), 0)
+    for head in range(own // HEAD_DIM):
+        columns = slice(head * HEAD_DIM, (head + 1) * HEAD_DIM)
+        for block in range(count):
+            here, seen = slice(block * rows, (block + 1) * rows), (block + 1) * rows
+            scores = lax.dot_general(
+                query_s[block, :, columns],
+                key_s[0:seen, columns],
+                (((1,), (1,)), ((), ())),
+                preferred_element_type=jnp.float32,
+            ) * HEAD_DIM ** (-0.5)
+            own_scores = jnp.where(causal, scores[:, block * rows :], masked_score)
+            pieces = [scores[:, : block * rows], own_scores] if block else [own_scores]
+            scores = jnp.concatenate(pieces, axis=1)
+            weights = jnp.exp(scores - jnp.max(scores, axis=1, keepdims=True))
+            total_ref[here, head : head + 1] = jnp.sum(weights, axis=1, keepdims=True)
+            weight_ref[head, here, 0:seen] = weights.astype(jnp.bfloat16)
+            if seen < count * rows:
+                weight_ref[head, here, seen:] = jnp.zeros((rows, count * rows - seen), jnp.bfloat16)
+
+
+def mix_rows(block, weight_ref, total_ref, value_ref, out_ref):
+    rows = out_ref.shape[0]
+    here = columns_of(block, rows)
+    for head in range(out_ref.shape[1] // HEAD_DIM):
+        columns = slice(head * HEAD_DIM, (head + 1) * HEAD_DIM)
+        mixed = jnp.dot(weight_ref[head, here], value_ref[:, columns], preferred_element_type=jnp.float32)
+        out_ref[:, columns] = (mixed / total_ref[here, head : head + 1]).astype(jnp.bfloat16)
+
+
+def values_kernel(*refs):
+    count = COUNT
+    given = refs[:count]
+    band_ref, short_ref, gain_ref, weight_ref, total_ref = refs[count : count + 5]
+    third_ref, second_ref, value_ref = refs[count + 5 : count + 8]
+    got_s, gate_s = refs[count + 8 :]
+    rows, own = second_ref.shape
+    edged = rows + EDGE
+    per_group = own * rows // band_ref.shape[0]
+    position = lax.axis_index("ctx")
+    mine = columns_of(position, own)
+    for step in range(count):
+        got_s[position ^ step] = given[step][0 : edged + rows]
+    taps = [
+        [short_ref[lag, stream : stream + 1, mine].astype(jnp.float32) for lag in range(3)] for stream in range(3)
+    ]
+    gate_s[0:rows] = jnp.zeros((rows, own), jnp.bfloat16)
+    edge_row = lax.broadcasted_iota(jnp.int32, (8, own), 0)
+    head_row = lax.broadcasted_iota(jnp.int32, (16, own), 0)
+    for block in range(count):
+        gate_s[(block + 1) * rows : (block + 2) * rows] = got_s[block, 0:rows]
+        if block == 0:
+            continue
+        fixed = 1.0
+        before = got_s[block - 1, rows:edged].astype(jnp.float32)
+        here = got_s[block, rows:edged].astype(jnp.float32)
+        for which, stream in enumerate((1, 2)):
+            old = pltpu.roll(before[8 * which : 8 * which + 8], 6, 0)
+            new = pltpu.roll(here[8 * which : 8 * which + 8], 2, 0)
+            joined = jnp.where(edge_row < 2, old, new)
+            fixed = fixed * (
+                taps[stream][0] * pltpu.roll(joined, 6, 0)
+                + taps[stream][1] * pltpu.roll(joined, 7, 0)
+                + taps[stream][2] * joined
+            )
+        head = got_s[block, 0:16].astype(jnp.float32)
+        head = jnp.where(head_row < 2, jnp.concatenate([fixed, fixed], axis=0), head)
+        gate_s[(block + 1) * rows : (block + 1) * rows + 16] = head.astype(jnp.bfloat16)
+    signal = jnp.concatenate([got_s[block, edged:] for block in range(count)], axis=0)
+    feature = featured(signal.astype(jnp.float32), taps[0])
+    gain = gain_ref[:, mine]
+    per_tile = HEAD_DIM // per_group
+    lane = lax.broadcasted_iota(jnp.int32, (rows, 2 * HEAD_DIM), 1) % HEAD_DIM // per_group
+    for tile in range(own // HEAD_DIM):
+        columns = slice(tile * HEAD_DIM, (tile + 1) * HEAD_DIM)
+        for block in range(0, count, 2):
+            windows = [gate_s[other * rows : (other + 2) * rows, columns] for other in (block, block + 1)]
+            mixed = jnp.dot(
+                band_ref[tile * per_tile * rows : (tile + 1) * per_tile * rows],
+                jnp.concatenate(windows, axis=1),
+                preferred_element_type=jnp.float32,
+            )
+            filtered = mixed[:rows]
+            for group in range(1, per_tile):
+                filtered = jnp.where(lane == group, mixed[group * rows : (group + 1) * rows], filtered)
+            for index in range(2):
+                here = slice((block + index) * rows, (block + index + 1) * rows)
+                gate = gate_s[(block + index + 1) * rows : (block + index + 2) * rows, columns].astype(jnp.float32)
+                part = filtered[:, index * HEAD_DIM : (index + 1) * HEAD_DIM]
+                value_ref[here, columns] = (
+                    feature[here, columns] * (part + gain[:, columns] * gate)
+                ).astype(jnp.bfloat16)
+    for step, out_ref in ((3, third_ref), (2, second_ref)):
+        mix_rows(position ^ step, weight_ref, total_ref, value_ref, out_ref)
+
+
+def near_rows_kernel(weight_ref, total_ref, value_ref, near_ref, own_ref):
+    position = lax.axis_index("ctx")
+    for step, out_ref in ((1, near_ref), (0, own_ref)):
+        mix_rows(position ^ step, weight_ref, total_ref, value_ref, out_ref)
+
+
+def project_kernel(masks, *refs):
+    count = COUNT
+    given, weight_ref = refs[:count], refs[count]
+    out_refs, attended_s = refs[count + 1 : -1], refs[-1]
+    own = given[0].shape[1]
+    width = out_refs[0].shape[1]
+    position, here = lax.axis_index("ctx"), lax.axis_index("mp")
+    for step in range(count):
+        attended_s[:, pl.ds(pl.multiple_of((position ^ step) * own, own), own)] = given[step][...]
+    for mask, out_ref in zip(masks, out_refs):
+        columns = pl.ds(pl.multiple_of((here ^ mask) * width, width), width)
+        out_ref[...] = jnp.dot(
+            attended_s[...], weight_ref[:, columns], preferred_element_type=jnp.float32
+        ).astype(jnp.bfloat16)
+
+
+VMEM_LIMIT = 40 * 1024 * 1024
+WIDE_LIMIT = 60 * 1024 * 1024
+IN_HBM = pl.BlockSpec(memory_space=pltpu.HBM)
+IN_VMEM = pl.BlockSpec(memory_space=pltpu.VMEM)
+
+
+def run_kernel(kernel, operands, outputs, scratch=(), spaces=None, limit=VMEM_LIMIT, cost=10**6):
+    return pl.pallas_call(
+        kernel,
+        out_shape=[jax.ShapeDtypeStruct(shape, dtype) for shape, dtype in outputs],
+        in_specs=spaces or [IN_VMEM] * len(operands),
+        out_specs=[IN_VMEM] * len(outputs),
+        scratch_shapes=scratch,
+        compiler_params=pltpu.CompilerParams(vmem_limit_bytes=limit),
+        cost_estimate=pl.CostEstimate(flops=cost, bytes_accessed=2**20, transcendentals=0),
+        name=getattr(kernel, "func", kernel).__name__,
+    )(*operands)
+
+
+def swapped(value, axis, step):
+    return lax.ppermute(value, axis, [(source, source ^ step) for source in range(lax.axis_size(axis))])
+
+
+def by_heads(inputs, short_filter, long_filter, skip_gain, queries, key_rows, out_weight):
+    rows, streams, channels = inputs.shape
+    own = channels // COUNT
+    groups, taps = long_filter.shape
+    half = jnp.bfloat16
+    gate_shape, heads_shape = ((2 * rows + EDGE, own), half), ((2 * rows, own), half)
+    piece, window = ((rows, own), half), COUNT * rows
+    streamed = jnp.transpose(inputs, (1, 0, 2))
+    staging = [
+        pltpu.VMEM((2, rows, 2 * own), half),
+        pltpu.VMEM((3, streams, 2 * own), half),
+    ]
+    heads = run_kernel(
+        far_heads_kernel,
+        (queries, key_rows),
+        [heads_shape] * 2,
+        [pltpu.SemaphoreType.DMA((4,))],
+        [IN_HBM] * 2,
+        WIDE_LIMIT,
+    )
+    heads_third, heads_second = swapped(heads[0], "ctx", 3), swapped(heads[1], "ctx", 2)
+    gates = run_kernel(
+        far_gate_kernel,
+        (streamed, short_filter, heads[0]),
+        [gate_shape] * 2,
+        staging + [pltpu.SemaphoreType.DMA((4,))],
+        [IN_HBM] * 3,
+        WIDE_LIMIT,
+    )
+    gate_third, gate_second = swapped(gates[0], "ctx", 3), swapped(gates[1], "ctx", 2)
+    near_all, own_gate, own_heads = run_kernel(
+        near_kernel,
+        (streamed, short_filter, queries, key_rows, gates[0]),
+        [((4 * rows + EDGE, own), half), gate_shape, heads_shape],
+        staging + [pltpu.SemaphoreType.DMA((8,))],
+        [IN_HBM] * 5,
+        WIDE_LIMIT,
+    )
+    near_got = swapped(near_all, "ctx", 1)
+    band, weight = run_kernel(
+        ready_kernel,
+        (long_filter, out_weight),
+        [((groups // COUNT * taps, 2 * taps), half), (out_weight.shape, half)],
+        [pltpu.SemaphoreType.DMA],
+        [IN_VMEM, IN_HBM],
+    )
+    soft, totals = run_kernel(
+        weights_kernel,
+        (own_heads, near_got, heads_second, heads_third),
+        [((own // HEAD_DIM, window, window), half), ((window, HEAD_DIM), jnp.float32)],
+        [pltpu.VMEM((COUNT, rows, own), half), pltpu.VMEM((window, own), half)],
+    )
+    third, second, values = run_kernel(
+        values_kernel,
+        (own_gate, near_got, gate_second, gate_third, band, short_filter, skip_gain.reshape(1, channels), soft, totals),
+        [piece, piece, ((window, own), half)],
+        [pltpu.VMEM((COUNT,) + gate_shape[0], half), pltpu.VMEM((window + rows, own), half)],
+    )
+    third_got, second_got = swapped(third, "ctx", 3), swapped(second, "ctx", 2)
+    near, mine = run_kernel(near_rows_kernel, (soft, totals, values), [piece] * 2)
+    attended = [mine, swapped(near, "ctx", 1), second_got, third_got]
+    return project_and_share(attended, weight)
+
+
+def projected(attended, out_weight, masks):
+    rows = attended[0].shape[0]
+    width = out_weight.shape[1] // lax.axis_size("mp")
+    return run_kernel(
+        functools.partial(project_kernel, masks),
+        (*attended, out_weight),
+        [((rows, width), jnp.bfloat16)] * len(masks),
+        [pltpu.VMEM((rows, out_weight.shape[0]), jnp.bfloat16)],
+        cost=2 * rows * out_weight.shape[0] * width * len(masks),
+    )
+
+
+def added(*terms):
+    total = terms[0].astype(jnp.float32)
+    for term in terms[1:]:
+        total = total + term.astype(jnp.float32)
+    return total.astype(jnp.bfloat16)
+
+
+def project_and_share(attended, out_weight):
+    far_given, far_kept = projected(attended, out_weight, (3, 2))
+    far_got = swapped(far_given, "mp", 1)
+    near_given, near_kept = projected(attended, out_weight, (1, 0))
+    far_sum = added(far_kept, far_got)
+    near_got = swapped(near_given, "mp", 1)
+    return added(near_kept, near_got, swapped(far_sum, "mp", 2))
+
+
+def per_device(inputs, short_filter, long_filter, skip_gain, queries, key_rows, out_weight):
+    rows, _, channels = inputs.shape
+    count = lax.axis_size("ctx")
+    taps = long_filter.shape[1]
+    splits = channels % (count * HEAD_DIM) == 0 and count == COUNT and rows == taps
+    if splits and lax.axis_size("mp") == 4:
+        return by_heads(inputs, short_filter, long_filter, skip_gain, queries, key_rows, out_weight)
+    attended = by_rows(inputs, short_filter, long_filter, skip_gain, queries, key_rows)
     partial_out = jnp.dot(attended, out_weight, preferred_element_type=jnp.float32)
     return lax.psum_scatter(partial_out.astype(jnp.bfloat16), "mp", scatter_dimension=1, tiled=True)
 

time: 114 us -> 57.4 us (0.50)
  local copies, waits for them, and re-layouts: 25.7 us -> 0.73 us
  waiting for transfers between devices: 49.9 us -> 26.4 us
  between operations: 13.3 us -> 0.13 us
  Pallas kernels: 0 us -> 12.7 us
  matrix products: 11.4 us -> 0 us
  starting transfers between devices: 8.51 us -> 16.2 us
  other arithmetic: 4.94 us -> 0.89 us
    ppermute x2 -> x11, waiting for transfers between devices: 0.01 us -> 26.4 us  [swapped(): lax.ppermute(value, axis, [(source, source ^ step) for source in range(la...]
    all_gather x2 -> x0, waiting for transfers between devices: 25.4 us -> none  [the longest x1 25.3 us: per_device(): lax.all_gather(values, 'ctx', axis=0, tiled=True)]
    reduce_scatter x1 -> x0, waiting for transfers between devices: 24.5 us -> none  [per_device(): lax.psum_scatter(partial_out.astype(jnp.bfloat16), 'mp', scatter_dimensio...]
    reshape x2 -> x0, local copies, waits for them, and re-layouts: 16.1 us -> none  [the longest x1 15.8 us: toeplitz_taps(): return repeated[:, :row_count * span].reshape(group_count, row_count, span)]
    pallas_call x0 -> x9, Pallas kernels: none -> 12.7 us  [run_kernel(): pl.pallas_call(kernel, out_shape=[jax.ShapeDtypeStruct(shape, dtype) for...]
    dot_general x4 -> x0, matrix products: 11.4 us -> none  [the longest x1 5.65 us: per_device(): jnp.dot(attended, out_weight, preferred_element_type=jnp.float32)]
    ppermute x2 -> x11, starting transfers between devices: 8.43 us -> 16.2 us  [swapped(): lax.ppermute(value, axis, [(source, source ^ step) for source in range(la...]
    unnamed x8 -> x10, local copies, waits for them, and re-layouts: 4.4 us -> 0.73 us
  transfers between devices with their start and end apart: 5 -> 11, of which waited for: 2 -> 6; matrix products, arithmetic and copies ran while one was open for 29% -> 0% of each run, Pallas kernels for 0% -> 8%
where the time goes in v5:
time: 57.4 us; the launch traced here: 57.1 us
  waiting for transfers between devices  26.4 us (46%)
  starting transfers between devices  16.2 us (28%)
  Pallas kernels  12.7 us (22%)
  other arithmetic  0.89 us (2%)
  local copies, waits for them, and re-layouts  0.73 us (1%)
    ppermute x11, waiting for transfers between devices, swapped(): lax.ppermute(value, axis, [(source, source ^ step) for source in range(la...  26.4 us
    ppermute x11, starting transfers between devices, swapped(): lax.ppermute(value, axis, [(source, source ^ step) for source in range(la...  16.2 us
    pallas_call x9, Pallas kernels, run_kernel(): pl.pallas_call(kernel, out_shape=[jax.ShapeDtypeStruct(shape, dtype) for...  12.7 us
  transfers between devices with their start and end apart: 11, of which 6 were waited for; matrix products, arithmetic and copies ran while one was open for 0% of the time, Pallas kernels for 8%

profile of v5, /device:TPU:0, one launch (start us, length us, event | category | flops | bytes accessed | tf_op | source)
XLA Modules:
  0.0 57.1 jit_solution(13551012731263349056)
XLA Ops:
  0.0 1.7 %far_heads_kernel.1 = (bf16[256,256]{1,0:T(8,128)(2,1)}, bf16[256,256]{1,0:T(8,128)(2,1)}) custom-call(bf16[128,1024]{1,0:T(8,128)(2,1)} %queries_any.3, bf16[128,1024]{1,0:T(8,128)(2,1)} %keys_any.3), custom_call_target="tpu_custom_call" | custom-call | flops 1000000 | bytes 1048576 | tf_op jit(solution)/shard_map/far_heads_kernel/pallas_call | solution.py:362
  1.7 1.9 %far_gate_kernel.1 = (bf16[272,256]{1,0:T(8,128)(2,1)}, bf16[272,256]{1,0:T(8,128)(2,1)}) custom-call(bf16[3,128,1024]{2,1,0:T(8,128)(2,1)} %bitcast.3, bf16[3,3,1024]{2,1,0:T(4,128)(2,1)} %refs_5_.1, bf16[256,256]{1,0:T(8,128)(2,1)} %get-tuple-element.25._), custom_call_target="tpu_custom_call" | custom-call | flops 1000000 | bytes 1048576 | tf_op jit(solution)/shard_map/far_gate_kernel/pallas_call | solution.py:362
  3.6 2.1 %near_kernel.1 = (bf16[528,256]{1,0:T(8,128)(2,1)}, bf16[272,256]{1,0:T(8,128)(2,1)}, bf16[256,256]{1,0:T(8,128)(2,1)}) custom-call(bf16[3,128,1024]{2,1,0:T(8,128)(2,1)} %bitcast.4, bf16[3,3,1024]{2,1,0:T(4,128)(2,1)} %refs_5_.1, bf16[128,1024]{1,0:T(8,128)(2,1)} %queries_any.3, bf16[128,1024]{1,0:T(8,128)(2,1)} %keys_any.3, ...), custom_call_target="tpu_custom_call" | custom-call | flops 1000000 | bytes 1048576 | tf_op jit(solution)/shard_map/near_kernel/pallas_call | solution.py:362
  5.7 3.1 %collective-permute-start = (bf16[528,256]{1,0:T(8,128)(2,1)}, bf16[528,256]{1,0:T(8,128)(2,1)S(1)}, u32[]{:S(2)}, u32[]{:S(2)}) collective-permute-start(bf16[528,256]{1,0:T(8,128)(2,1)} %get-tuple-element.28), channel_id=1, source_target_pairs={{0,4},{4,0},{8,12},{12,8},{1,5},{5,1},{9,13},{13,9},{2,6},{6,2},{1... | collective-permute-start | bytes 811016 | tf_op jit(solution)/shard_map/ppermute | solution.py:375
  8.8 2.6 %collective-permute-start.3 = (bf16[272,256]{1,0:T(8,128)(2,1)}, bf16[272,256]{1,0:T(8,128)(2,1)S(1)}, u32[]{:S(2)}, u32[]{:S(2)}) collective-permute-start(bf16[272,256]{1,0:T(8,128)(2,1)} %get-tuple-element.33), channel_id=1, source_target_pairs={{0,8},{4,12},{8,0},{12,4},{1,9},{5,13},{9,1},{13,5},{2,10},{6,14},... | collective-permute-start | bytes 417800 | tf_op jit(solution)/shard_map/ppermute | solution.py:375
  11.4 1.9 %collective-permute-start.1 = (bf16[256,256]{1,0:T(8,128)(2,1)}, bf16[256,256]{1,0:T(8,128)(2,1)S(1)}, u32[]{:S(2)}, u32[]{:S(2)}) collective-permute-start(bf16[256,256]{1,0:T(8,128)(2,1)} %get-tuple-element.29), channel_id=1, source_target_pairs={{0,8},{4,12},{8,0},{12,4},{1,9},{5,13},{9,1},{13,5},{2,10},{6,14},... | collective-permute-start | bytes 393224 | tf_op jit(solution)/shard_map/ppermute | solution.py:375
  13.3 1.9 %collective-permute-start.2 = (bf16[256,256]{1,0:T(8,128)(2,1)}, bf16[256,256]{1,0:T(8,128)(2,1)S(1)}, u32[]{:S(2)}, u32[]{:S(2)}) collective-permute-start(bf16[256,256]{1,0:T(8,128)(2,1)} %get-tuple-element.25._), channel_id=1, source_target_pairs={{0,12},{4,8},{8,4},{12,0},{1,13},{5,9},{9,5},{13,1},{2,14},{6,10},... | collective-permute-start | bytes 393224 | tf_op jit(solution)/shard_map/ppermute | solution.py:375
  15.3 0.7 %copy-done.3 = bf16[64,128]{1,0:T(8,128)(2,1)S(1)} copy-done((bf16[64,128]{1,0:T(8,128)(2,1)S(1)}, bf16[64,128]{1,0:T(8,128)(2,1)}, u32[]{:S(2)}) %copy-start.3) | copy-done | bytes 16408
  16.0 3.4 %ready_kernel.1 = (bf16[2048,256]{1,0:T(8,128)(2,1)S(1)}, bf16[1024,4096]{1,0:T(8,128)(2,1)S(1)}) custom-call(bf16[64,128]{1,0:T(8,128)(2,1)S(1)} %copy-done.3, bf16[1024,4096]{1,0:T(8,128)(2,1)} %weight_any.1), custom_call_target="tpu_custom_call" | custom-call | flops 1000000 | bytes 1048576 | tf_op jit(solution)/shard_map/ready_kernel/pallas_call | solution.py:362
  19.4 14.5 %collective-permute-done.1.second_ref = bf16[256,256]{1,0:T(8,128)(2,1)S(1)} collective-permute-done((bf16[256,256]{1,0:T(8,128)(2,1)}, bf16[256,256]{1,0:T(8,128)(2,1)S(1)}, u32[]{:S(2)}, u32[]{:S(2)}) %collective-permute-start.1) | collective-permute-done | bytes 131104 | tf_op jit(solution)/shard_map/ppermute | solution.py:375
  33.9 0.7 %weights_kernel.1 = (bf16[2,512,512]{2,1,0:T(8,128)(2,1)S(1)}, f32[512,128]{1,0:T(8,128)S(1)}) custom-call(bf16[256,256]{1,0:T(8,128)(2,1)S(1)} %copy-done.2, bf16[528,256]{1,0:T(8,128)(2,1)S(1)} %collective-permute-done.near_ref.refs_1_, bf16[256,256]{1,0:T(8,128)(2,1)S(1)} %collective-permute-done.1.second_ref, ...), custom_call_target="tpu_custom_call" | custom-call | flops 1000000 | bytes 1048576 | tf_op jit(solution)/shard_map/weights_kernel/pallas_call | solution.py:362
  34.7 1.2 %values_kernel.1 = (bf16[128,256]{1,0:T(8,128)(2,1)S(1)}, bf16[128,256]{1,0:T(8,128)(2,1)S(1)}, bf16[512,256]{1,0:T(8,128)(2,1)S(1)}) custom-call(bf16[272,256]{1,0:T(8,128)(2,1)S(1)} %copy-done.1, bf16[528,256]{1,0:T(8,128)(2,1)S(1)} %collective-permute-done.near_ref.refs_1_, bf16[272,256]{1,0:T(8,128)(2,1)S(1)} %collective-permute-done.3.refs_2_, ...), custom_call_target="tpu_custom_call" | custom-call | flops 1000000 | bytes 1048576 | tf_op jit(solution)/shard_map/values_kernel/pallas_call | solution.py:362
  36.1 2.0 %collective-permute-start.5 = (bf16[128,256]{1,0:T(8,128)(2,1)S(1)}, bf16[128,256]{1,0:T(8,128)(2,1)S(1)}, u32[]{:S(2)}, u32[]{:S(2)}) collective-permute-start(bf16[128,256]{1,0:T(8,128)(2,1)S(1)} %get-tuple-element.37), channel_id=1, source_target_pairs={{0,4},{4,0},{8,12},{12,8},{1,5},{5,1},{9,13},{13,9},{2,6},{6,2},{1... | collective-permute-start | bytes 196616 | tf_op jit(solution)/shard_map/ppermute | solution.py:375
  38.2 1.1 %collective-permute-start.6 = (bf16[128,256]{1,0:T(8,128)(2,1)S(1)}, bf16[128,256]{1,0:T(8,128)(2,1)S(1)}, u32[]{:S(2)}, u32[]{:S(2)}) collective-permute-start(bf16[128,256]{1,0:T(8,128)(2,1)S(1)} %get-tuple-element.38), channel_id=1, source_target_pairs={{0,8},{4,12},{8,0},{12,4},{1,9},{5,13},{9,1},{13,5},{2,10},{6,14},... | collective-permute-start | bytes 196616 | tf_op jit(solution)/shard_map/ppermute | solution.py:375
  39.3 1.4 %collective-permute-start.7 = (bf16[128,256]{1,0:T(8,128)(2,1)S(1)}, bf16[128,256]{1,0:T(8,128)(2,1)S(1)}, u32[]{:S(2)}, u32[]{:S(2)}) collective-permute-start(bf16[128,256]{1,0:T(8,128)(2,1)S(1)} %get-tuple-element.39), channel_id=1, source_target_pairs={{0,12},{4,8},{8,4},{12,0},{1,13},{5,9},{9,5},{13,1},{2,14},{6,10},... | collective-permute-start | bytes 196616 | tf_op jit(solution)/shard_map/ppermute | solution.py:375
  40.7 0.5 collective-permute-done.5.refs_1_
  41.1 3.0 %collective-permute-done.6.refs_2_ = bf16[128,256]{1,0:T(8,128)(2,1)S(1)} collective-permute-done((bf16[128,256]{1,0:T(8,128)(2,1)S(1)}, bf16[128,256]{1,0:T(8,128)(2,1)S(1)}, u32[]{:S(2)}, u32[]{:S(2)}) %collective-permute-start.6) | collective-permute-done | bytes 65568 | tf_op jit(solution)/shard_map/ppermute | solution.py:375
  44.1 1.3 %collective-permute-done.7.refs_3_ = bf16[128,256]{1,0:T(8,128)(2,1)S(1)} collective-permute-done((bf16[128,256]{1,0:T(8,128)(2,1)S(1)}, bf16[128,256]{1,0:T(8,128)(2,1)S(1)}, u32[]{:S(2)}, u32[]{:S(2)}) %collective-permute-start.7) | collective-permute-done | bytes 65568 | tf_op jit(solution)/shard_map/ppermute | solution.py:375
  45.4 0.7 %project_kernel.3 = (bf16[128,1024]{1,0:T(8,128)(2,1)S(1)}, bf16[128,1024]{1,0:T(8,128)(2,1)S(1)}) custom-call(bf16[128,256]{1,0:T(8,128)(2,1)S(1)} %get-tuple-element.36.refs_0_, bf16[128,256]{1,0:T(8,128)(2,1)S(1)} %collective-permute-done.5.refs_1_, bf16[128,256]{1,0:T(8,128)(2,1)S(1)} %collective-permute-done.6.refs_2_, ...), custom_call_target="tpu_custom_call" | custom-call | flops 536870912 | bytes 1048576 | tf_op jit(solution)/shard_map/project_kernel/pallas_call | solution.py:362
  46.3 0.7 %project_kernel.2 = (bf16[128,1024]{1,0:T(8,128)(2,1)S(1)}, bf16[128,1024]{1,0:T(8,128)(2,1)S(1)}) custom-call(bf16[128,256]{1,0:T(8,128)(2,1)S(1)} %get-tuple-element.36.refs_0_, bf16[128,256]{1,0:T(8,128)(2,1)S(1)} %collective-permute-done.5.refs_1_, bf16[128,256]{1,0:T(8,128)(2,1)S(1)} %collective-permute-done.6.refs_2_, ...), custom_call_target="tpu_custom_call" | custom-call | flops 536870912 | bytes 1048576 | tf_op jit(solution)/shard_map/project_kernel/pallas_call | solution.py:362
  47.0 0.6 collective-permute-start.8
  47.8 1.6 %collective-permute-start.10 = (bf16[128,1024]{1,0:T(8,128)(2,1)S(1)}, bf16[128,1024]{1,0:T(8,128)(2,1)S(1)}, u32[]{:S(2)}, u32[]{:S(2)}) collective-permute-start(bf16[128,1024]{1,0:T(8,128)(2,1)S(1)} %add_convert_fusion.1), channel_id=1, source_target_pairs={{0,2},{1,3},{2,0},{3,1},{4,6},{5,7},{6,4},{7,5},{8,10},{9,11},{10,... | collective-permute-start | bytes 786440 | tf_op jit(solution)/shard_map/ppermute | solution.py:375
  49.4 6.9 %collective-permute-done.10 = bf16[128,1024]{1,0:T(8,128)(2,1)S(1)} collective-permute-done((bf16[128,1024]{1,0:T(8,128)(2,1)S(1)}, bf16[128,1024]{1,0:T(8,128)(2,1)S(1)}, u32[]{:S(2)}, u32[]{:S(2)}) %collective-permute-start.10) | collective-permute-done | bytes 262176 | tf_op jit(solution)/shard_map/ppermute | solution.py:375
  56.3 0.8 %add_convert_fusion = bf16[128,1024]{1,0:T(8,128)(2,1)} fusion(bf16[128,1024]{1,0:T(8,128)(2,1)S(1)} %collective-permute-done.10, bf16[128,1024]{1,0:T(8,128)(2,1)S(1)} %collective-permute-done.8, bf16[128,1024]{1,0:T(8,128)(2,1)S(1)} %get-tuple-element.41), kind=kLoop, calls=%fused_computation | loop fusion | flops 786432 | bytes 1048576 | tf_op jit(solution)/shard_map/convert_element_type | solution.py:458
  (19 shorter events, 0.7 us)
Async XLA Ops:
  0.0 34.6 %copy-start = (bf16[3,3,1024]{2,1,0:T(4,128)(2,1)S(1)}, bf16[3,3,1024]{2,1,0:T(4,128)(2,1)}, u32[]{:S(2)}) copy-start(bf16[3,3,1024]{2,1,0:T(4,128)(2,1)} %refs_5_.1) | copy-start | bytes 55300
  0.0 34.6 %copy-start.4 = (f32[1024]{0:T(1024)S(1)}, f32[1024]{0:T(1024)}, u32[]{:S(2)}) copy-start(f32[1024]{0:T(1024)} %param.10) | copy-start | bytes 12292
  5.7 28.2 %copy-start.2 = (bf16[256,256]{1,0:T(8,128)(2,1)S(1)}, bf16[256,256]{1,0:T(8,128)(2,1)}, u32[]{:S(2)}) copy-start(bf16[256,256]{1,0:T(8,128)(2,1)} %get-tuple-element.27.own_ref) | copy-start | bytes 393220
  5.7 28.9 %copy-start.1 = (bf16[272,256]{1,0:T(8,128)(2,1)S(1)}, bf16[272,256]{1,0:T(8,128)(2,1)}, u32[]{:S(2)}) copy-start(bf16[272,256]{1,0:T(8,128)(2,1)} %get-tuple-element.32.refs_0_) | copy-start | bytes 417796
  5.7 28.2 %collective-permute-start = (bf16[528,256]{1,0:T(8,128)(2,1)}, bf16[528,256]{1,0:T(8,128)(2,1)S(1)}, u32[]{:S(2)}, u32[]{:S(2)}) collective-permute-start(bf16[528,256]{1,0:T(8,128)(2,1)} %get-tuple-element.28), channel_id=1, source_target_pairs={{0,4},{4,0},{8,12},{12,8},{1,5},{5,1},{9,13},{13,9},{2,6},{6,2},{1... | collective-permute-start | bytes 811016 | tf_op jit(solution)/shard_map/ppermute | solution.py:375
  8.8 25.8 %collective-permute-start.3 = (bf16[272,256]{1,0:T(8,128)(2,1)}, bf16[272,256]{1,0:T(8,128)(2,1)S(1)}, u32[]{:S(2)}, u32[]{:S(2)}) collective-permute-start(bf16[272,256]{1,0:T(8,128)(2,1)} %get-tuple-element.33), channel_id=1, source_target_pairs={{0,8},{4,12},{8,0},{12,4},{1,9},{5,13},{9,1},{13,5},{2,10},{6,14},... | collective-permute-start | bytes 417800 | tf_op jit(solution)/shard_map/ppermute | solution.py:375
  11.4 23.2 %collective-permute-start.4 = (bf16[272,256]{1,0:T(8,128)(2,1)}, bf16[272,256]{1,0:T(8,128)(2,1)S(1)}, u32[]{:S(2)}, u32[]{:S(2)}) collective-permute-start(bf16[272,256]{1,0:T(8,128)(2,1)} %get-tuple-element.26._), channel_id=1, source_target_pairs={{0,12},{4,8},{8,4},{12,0},{1,13},{5,9},{9,5},{13,1},{2,14},{6,10},... | collective-permute-start | bytes 417800 | tf_op jit(solution)/shard_map/ppermute | solution.py:375
  11.4 22.5 %collective-permute-start.1 = (bf16[256,256]{1,0:T(8,128)(2,1)}, bf16[256,256]{1,0:T(8,128)(2,1)S(1)}, u32[]{:S(2)}, u32[]{:S(2)}) collective-permute-start(bf16[256,256]{1,0:T(8,128)(2,1)} %get-tuple-element.29), channel_id=1, source_target_pairs={{0,8},{4,12},{8,0},{12,4},{1,9},{5,13},{9,1},{13,5},{2,10},{6,14},... | collective-permute-start | bytes 393224 | tf_op jit(solution)/shard_map/ppermute | solution.py:375
  13.3 20.6 %collective-permute-start.2 = (bf16[256,256]{1,0:T(8,128)(2,1)}, bf16[256,256]{1,0:T(8,128)(2,1)S(1)}, u32[]{:S(2)}, u32[]{:S(2)}) collective-permute-start(bf16[256,256]{1,0:T(8,128)(2,1)} %get-tuple-element.25._), channel_id=1, source_target_pairs={{0,12},{4,8},{8,4},{12,0},{1,13},{5,9},{9,5},{13,1},{2,14},{6,10},... | collective-permute-start | bytes 393224 | tf_op jit(solution)/shard_map/ppermute | solution.py:375
  15.3 0.7 %copy-start.3 = (bf16[64,128]{1,0:T(8,128)(2,1)S(1)}, bf16[64,128]{1,0:T(8,128)(2,1)}, u32[]{:S(2)}) copy-start(bf16[64,128]{1,0:T(8,128)(2,1)} %filter_ref.1) | copy-start | bytes 49156
  36.1 5.0 %collective-permute-start.5 = (bf16[128,256]{1,0:T(8,128)(2,1)S(1)}, bf16[128,256]{1,0:T(8,128)(2,1)S(1)}, u32[]{:S(2)}, u32[]{:S(2)}) collective-permute-start(bf16[128,256]{1,0:T(8,128)(2,1)S(1)} %get-tuple-element.37), channel_id=1, source_target_pairs={{0,4},{4,0},{8,12},{12,8},{1,5},{5,1},{9,13},{13,9},{2,6},{6,2},{1... | collective-permute-start | bytes 196616 | tf_op jit(solution)/shard_map/ppermute | solution.py:375
  38.2 6.0 %collective-permute-start.6 = (bf16[128,256]{1,0:T(8,128)(2,1)S(1)}, bf16[128,256]{1,0:T(8,128)(2,1)S(1)}, u32[]{:S(2)}, u32[]{:S(2)}) collective-permute-start(bf16[128,256]{1,0:T(8,128)(2,1)S(1)} %get-tuple-element.38), channel_id=1, source_target_pairs={{0,8},{4,12},{8,0},{12,4},{1,9},{5,13},{9,1},{13,5},{2,10},{6,14},... | collective-permute-start | bytes 196616 | tf_op jit(solution)/shard_map/ppermute | solution.py:375
  39.3 6.2 %collective-permute-start.7 = (bf16[128,256]{1,0:T(8,128)(2,1)S(1)}, bf16[128,256]{1,0:T(8,128)(2,1)S(1)}, u32[]{:S(2)}, u32[]{:S(2)}) collective-permute-start(bf16[128,256]{1,0:T(8,128)(2,1)S(1)} %get-tuple-element.39), channel_id=1, source_target_pairs={{0,12},{4,8},{8,4},{12,0},{1,13},{5,9},{9,5},{13,1},{2,14},{6,10},... | collective-permute-start | bytes 196616 | tf_op jit(solution)/shard_map/ppermute | solution.py:375
  46.2 1.6 %collective-permute-start.9 = (bf16[128,1024]{1,0:T(8,128)(2,1)S(1)}, bf16[128,1024]{1,0:T(8,128)(2,1)S(1)}, u32[]{:S(2)}, u32[]{:S(2)}) collective-permute-start(bf16[128,1024]{1,0:T(8,128)(2,1)S(1)} %get-tuple-element.44), channel_id=1, source_target_pairs={{0,1},{1,0},{2,3},{3,2},{4,5},{5,4},{6,7},{7,6},{8,9},{9,8},{10,11... | collective-permute-start | bytes 786440 | tf_op jit(solution)/shard_map/ppermute | solution.py:375
  47.0 2.4 %collective-permute-start.8 = (bf16[128,1024]{1,0:T(8,128)(2,1)S(1)}, bf16[128,1024]{1,0:T(8,128)(2,1)S(1)}, u32[]{:S(2)}, u32[]{:S(2)}) collective-permute-start(bf16[128,1024]{1,0:T(8,128)(2,1)S(1)} %get-tuple-element.42), channel_id=1, source_target_pairs={{0,1},{1,0},{2,3},{3,2},{4,5},{5,4},{6,7},{7,6},{8,9},{9,8},{10,11... | collective-permute-start | bytes 786440 | tf_op jit(solution)/shard_map/ppermute | solution.py:375
  47.8 8.4 %collective-permute-start.10 = (bf16[128,1024]{1,0:T(8,128)(2,1)S(1)}, bf16[128,1024]{1,0:T(8,128)(2,1)S(1)}, u32[]{:S(2)}, u32[]{:S(2)}) collective-permute-start(bf16[128,1024]{1,0:T(8,128)(2,1)S(1)} %add_convert_fusion.1), channel_id=1, source_target_pairs={{0,2},{1,3},{2,0},{3,1},{4,6},{5,7},{6,4},{7,5},{8,10},{9,11},{10,... | collective-permute-start | bytes 786440 | tf_op jit(solution)/shard_map/ppermute | solution.py:375

commit v6 on v5

--- a/solution.py
+++ b/solution.py
@@ -9,6 +9,7 @@
 
 HEAD_DIM = 128
 COUNT = 4
+ORDER = (3, 2, 1, 0)
 EDGE = 16
 
 
@@ -131,81 +132,33 @@
     out_ref[rows : rows + EDGE] = jnp.concatenate(edges, axis=0).astype(jnp.bfloat16)
 
 
-def far_heads_kernel(queries_any, keys_any, *refs):
-    out_refs, sems = refs[:-1], refs[-1]
-    rows, own = queries_any.shape[0], out_refs[0].shape[1]
+def pack_kernel(inputs_any, short_any, queries_any, keys_any, *refs):
+    plain_refs, gate_refs = refs[:COUNT], refs[COUNT : 2 * COUNT]
+    signal_s, short_s, sems = refs[2 * COUNT :]
+    rows, own = inputs_any.shape[1], plain_refs[0].shape[1]
     position = lax.axis_index("ctx")
-    copies = []
-    for step, out_ref in zip((3, 2), out_refs):
+    loads = [
+        pltpu.make_async_copy(short_any, short_s, sems.at[0]),
+        pltpu.make_async_copy(inputs_any.at[1:3], signal_s, sems.at[1]),
+    ]
+    for step in ORDER:
         columns = columns_of(position ^ step, own)
-        for index, source in enumerate((queries_any, keys_any)):
-            target = out_ref.at[index * rows : (index + 1) * rows]
-            copies.append(pltpu.make_async_copy(source.at[:, columns], target, sems.at[len(copies)]))
-    for copy in copies:
-        copy.start()
-    for copy in copies:
-        copy.wait()
-
-
-def far_gate_kernel(inputs_any, short_any, _, *refs):
-    out_refs, (signal_s, short_s, sems) = refs[:2], refs[2:]
-    rows, own = inputs_any.shape[1], out_refs[0].shape[1]
-    position = lax.axis_index("ctx")
-    pair = (position ^ 2) // 2
-    copies = [
-        pltpu.make_async_copy(inputs_any.at[1:3, :, columns_of(pair, 2 * own)], signal_s, sems.at[0]),
-        pltpu.make_async_copy(short_any.at[:, :, columns_of(pair, 2 * own)], short_s, sems.at[1]),
-    ]
-    for step, out_ref in zip((3, 2), out_refs):
-        target = out_ref.at[rows + EDGE :]
-        source = inputs_any.at[0, :, columns_of(position ^ step, own)]
-        copies.append(pltpu.make_async_copy(source, target, sems.at[step]))
-    for copy in copies:
-        copy.start()
-    for copy in copies[:2]:
-        copy.wait()
-    for step, out_ref in zip((3, 2), out_refs):
-        columns = columns_of((position ^ step) % 2, own)
+        for index, source in enumerate((queries_any, keys_any, inputs_any.at[0])):
+            target = plain_refs[step].at[index * rows : (index + 1) * rows]
+            loads.append(pltpu.make_async_copy(source.at[:, columns], target, sems.at[len(loads)]))
+    for load in loads:
+        load.start()
+    for load in loads[:2]:
+        load.wait()
+    for step in ORDER:
+        columns = columns_of(position ^ step, own)
         signals = [signal_s[stream, :, columns].astype(jnp.float32) for stream in range(2)]
         taps = [
             [short_s[lag, stream : stream + 1, columns].astype(jnp.float32) for lag in range(3)] for stream in (1, 2)
         ]
-        write_gate(signals, taps, out_ref)
-    for copy in copies[2:]:
-        copy.wait()
-
-
-def near_kernel(inputs_any, short_any, queries_any, keys_any, _, *refs):
-    (all_ref, gate_ref, heads_ref), (signal_s, short_s, sems) = refs[:3], refs[3:]
-    rows, own = inputs_any.shape[1], all_ref.shape[1]
-    position = lax.axis_index("ctx")
-    pair = position // 2
-    edged = rows + EDGE
-    mine, other = columns_of(position, own), columns_of(position ^ 1, own)
-    moves = (
-        (inputs_any.at[1:3, :, columns_of(pair, 2 * own)], signal_s),
-        (short_any.at[:, :, columns_of(pair, 2 * own)], short_s),
-        (inputs_any.at[0, :, other], all_ref.at[edged : edged + rows]),
-        (queries_any.at[:, other], all_ref.at[edged + rows : edged + 2 * rows]),
-        (keys_any.at[:, other], all_ref.at[edged + 2 * rows :]),
-        (inputs_any.at[0, :, mine], gate_ref.at[edged:]),
-        (queries_any.at[:, mine], heads_ref.at[0:rows]),
-        (keys_any.at[:, mine], heads_ref.at[rows:]),
-    )
-    copies = [pltpu.make_async_copy(*move, sems.at[index]) for index, move in enumerate(moves)]
-    for copy in copies:
-        copy.start()
-    for copy in copies[:2]:
-        copy.wait()
-    for step, out_ref in ((1, all_ref), (0, gate_ref)):
-        columns = columns_of((position ^ step) % 2, own)
-        signals = [signal_s[stream, :, columns].astype(jnp.float32) for stream in range(2)]
-        taps = [
-            [short_s[lag, stream : stream + 1, columns].astype(jnp.float32) for lag in range(3)] for stream in (1, 2)
-        ]
-        write_gate(signals, taps, out_ref)
-    for copy in copies[2:]:
-        copy.wait()
+        write_gate(signals, taps, gate_refs[step])
+    for load in loads[2:]:
+        load.wait()
 
 
 def ready_kernel(filter_ref, weight_any, band_ref, weight_ref, sem):
@@ -226,14 +179,13 @@
     weights.wait()
 
 
-def weights_kernel(own_ref, near_ref, second_ref, third_ref, weight_ref, total_ref, query_s, key_s):
+def weights_kernel(third_ref, second_ref, near_ref, own_ref, weight_ref, total_ref, query_s, key_s):
     count = COUNT
-    rows, own = own_ref.shape[0] // 2, own_ref.shape[1]
+    rows, own = query_s.shape[1:]
     position = lax.axis_index("ctx")
-    skip = near_ref.shape[0] - 2 * rows
-    for step, (given, start) in enumerate(((own_ref, 0), (near_ref, skip), (second_ref, 0), (third_ref, 0))):
-        query_s[position ^ step] = given[start : start + rows]
-        key_s[columns_of(position ^ step, rows)] = given[start + rows : start + 2 * rows]
+    for step, given in zip(ORDER, (third_ref, second_ref, near_ref, own_ref)):
+        query_s[position ^ step] = given[0:rows]
+        key_s[columns_of(position ^ step, rows)] = given[rows : 2 * rows]
     causal = lax.broadcasted_iota(jnp.int32, (rows, rows), 1) <= lax.broadcasted_iota(jnp.int32, (rows, rows), 0)
     for head in range(own // HEAD_DIM):
         columns = slice(head * HEAD_DIM, (head + 1) * HEAD_DIM)
@@ -266,17 +218,17 @@
 
 def values_kernel(*refs):
     count = COUNT
-    given = refs[:count]
-    band_ref, short_ref, gain_ref, weight_ref, total_ref = refs[count : count + 5]
-    third_ref, second_ref, value_ref = refs[count + 5 : count + 8]
-    got_s, gate_s = refs[count + 8 :]
+    plain, gates = refs[:count], refs[count : 2 * count]
+    band_ref, short_ref, gain_ref, weight_ref, total_ref = refs[2 * count : 2 * count + 5]
+    third_ref, second_ref, value_ref = refs[2 * count + 5 : 2 * count + 8]
+    signal_s, gates_s, gate_s = refs[2 * count + 8 :]
     rows, own = second_ref.shape
-    edged = rows + EDGE
     per_group = own * rows // band_ref.shape[0]
     position = lax.axis_index("ctx")
     mine = columns_of(position, own)
-    for step in range(count):
-        got_s[position ^ step] = given[step][0 : edged + rows]
+    for step, given, gate in zip(ORDER, plain, gates):
+        signal_s[columns_of(position ^ step, rows)] = given[2 * rows :]
+        gates_s[position ^ step] = gate[...]
     taps = [
         [short_ref[lag, stream : stream + 1, mine].astype(jnp.float32) for lag in range(3)] for stream in range(3)
     ]
@@ -284,12 +236,12 @@
     edge_row = lax.broadcasted_iota(jnp.int32, (8, own), 0)
     head_row = lax.broadcasted_iota(jnp.int32, (16, own), 0)
     for block in range(count):
-        gate_s[(block + 1) * rows : (block + 2) * rows] = got_s[block, 0:rows]
+        gate_s[(block + 1) * rows : (block + 2) * rows] = gates_s[block, 0:rows]
         if block == 0:
             continue
         fixed = 1.0
-        before = got_s[block - 1, rows:edged].astype(jnp.float32)
-        here = got_s[block, rows:edged].astype(jnp.float32)
+        before = gates_s[block - 1, rows:].astype(jnp.float32)
+        here = gates_s[block, rows:].astype(jnp.float32)
         for which, stream in enumerate((1, 2)):
             old = pltpu.roll(before[8 * which : 8 * which + 8], 6, 0)
             new = pltpu.roll(here[8 * which : 8 * which + 8], 2, 0)
@@ -299,11 +251,10 @@
                 + taps[stream][1] * pltpu.roll(joined, 7, 0)
                 + taps[stream][2] * joined
             )
-        head = got_s[block, 0:16].astype(jnp.float32)
+        head = gates_s[block, 0:16].astype(jnp.float32)
         head = jnp.where(head_row < 2, jnp.concatenate([fixed, fixed], axis=0), head)
         gate_s[(block + 1) * rows : (block + 1) * rows + 16] = head.astype(jnp.bfloat16)
-    signal = jnp.concatenate([got_s[block, edged:] for block in range(count)], axis=0)
-    feature = featured(signal.astype(jnp.float32), taps[0])
+    feature = featured(signal_s[...].astype(jnp.float32), taps[0])
     gain = gain_ref[:, mine]
     per_tile = HEAD_DIM // per_group
     lane = lax.broadcasted_iota(jnp.int32, (rows, 2 * HEAD_DIM), 1) % HEAD_DIM // per_group
@@ -330,21 +281,28 @@
         mix_rows(position ^ step, weight_ref, total_ref, value_ref, out_ref)
 
 
-def near_rows_kernel(weight_ref, total_ref, value_ref, near_ref, own_ref):
+def near_rows_kernel(weight_ref, total_ref, value_ref, *refs):
+    upper_ref, lower_ref, own_ref, near_s = refs
+    half = upper_ref.shape[0]
     position = lax.axis_index("ctx")
-    for step, out_ref in ((1, near_ref), (0, own_ref)):
-        mix_rows(position ^ step, weight_ref, total_ref, value_ref, out_ref)
+    mix_rows(position ^ 1, weight_ref, total_ref, value_ref, near_s)
+    upper_ref[...] = near_s[0:half]
+    lower_ref[...] = near_s[half:]
+    mix_rows(position, weight_ref, total_ref, value_ref, own_ref)
 
 
 def project_kernel(masks, *refs):
-    count = COUNT
-    given, weight_ref = refs[:count], refs[count]
-    out_refs, attended_s = refs[count + 1 : -1], refs[-1]
+    given, weight_ref = refs[:5], refs[5]
+    out_refs, attended_s = refs[6:-1], refs[-1]
     own = given[0].shape[1]
     width = out_refs[0].shape[1]
     position, here = lax.axis_index("ctx"), lax.axis_index("mp")
-    for step in range(count):
-        attended_s[:, pl.ds(pl.multiple_of((position ^ step) * own, own), own)] = given[step][...]
+    third, second, upper, lower, mine = given
+    half = upper.shape[0]
+    attended_s[0:half, columns_of(position ^ 1, own)] = upper[...]
+    attended_s[half:, columns_of(position ^ 1, own)] = lower[...]
+    for step, piece in ((0, mine), (2, second), (3, third)):
+        attended_s[:, columns_of(position ^ step, own)] = piece[...]
     for mask, out_ref in zip(masks, out_refs):
         columns = pl.ds(pl.multiple_of((here ^ mask) * width, width), width)
         out_ref[...] = jnp.dot(
@@ -380,40 +338,22 @@
     own = channels // COUNT
     groups, taps = long_filter.shape
     half = jnp.bfloat16
-    gate_shape, heads_shape = ((2 * rows + EDGE, own), half), ((2 * rows, own), half)
     piece, window = ((rows, own), half), COUNT * rows
-    streamed = jnp.transpose(inputs, (1, 0, 2))
-    staging = [
-        pltpu.VMEM((2, rows, 2 * own), half),
-        pltpu.VMEM((3, streams, 2 * own), half),
-    ]
-    heads = run_kernel(
-        far_heads_kernel,
-        (queries, key_rows),
-        [heads_shape] * 2,
-        [pltpu.SemaphoreType.DMA((4,))],
-        [IN_HBM] * 2,
+    packed = run_kernel(
+        pack_kernel,
+        (jnp.transpose(inputs, (1, 0, 2)), short_filter, queries, key_rows),
+        [((3 * rows, own), half)] * COUNT + [((rows + EDGE, own), half)] * COUNT,
+        [
+            pltpu.VMEM((2, rows, channels), half),
+            pltpu.VMEM(short_filter.shape, half),
+            pltpu.SemaphoreType.DMA((3 * COUNT + 2,)),
+        ],
+        [IN_HBM] * 4,
         WIDE_LIMIT,
     )
-    heads_third, heads_second = swapped(heads[0], "ctx", 3), swapped(heads[1], "ctx", 2)
-    gates = run_kernel(
-        far_gate_kernel,
-        (streamed, short_filter, heads[0]),
-        [gate_shape] * 2,
-        staging + [pltpu.SemaphoreType.DMA((4,))],
-        [IN_HBM] * 3,
-        WIDE_LIMIT,
-    )
-    gate_third, gate_second = swapped(gates[0], "ctx", 3), swapped(gates[1], "ctx", 2)
-    near_all, own_gate, own_heads = run_kernel(
-        near_kernel,
-        (streamed, short_filter, queries, key_rows, gates[0]),
-        [((4 * rows + EDGE, own), half), gate_shape, heads_shape],
-        staging + [pltpu.SemaphoreType.DMA((8,))],
-        [IN_HBM] * 5,
-        WIDE_LIMIT,
-    )
-    near_got = swapped(near_all, "ctx", 1)
+    plain, gates = packed[:COUNT], packed[COUNT:]
+    plain = [swapped(plain[step], "ctx", step) for step in ORDER[:3]] + [plain[0]]
+    gates = [swapped(gates[step], "ctx", step) for step in ORDER[:3]] + [gates[0]]
     band, weight = run_kernel(
         ready_kernel,
         (long_filter, out_weight),
@@ -423,20 +363,29 @@
     )
     soft, totals = run_kernel(
         weights_kernel,
-        (own_heads, near_got, heads_second, heads_third),
+        plain,
         [((own // HEAD_DIM, window, window), half), ((window, HEAD_DIM), jnp.float32)],
         [pltpu.VMEM((COUNT, rows, own), half), pltpu.VMEM((window, own), half)],
     )
     third, second, values = run_kernel(
         values_kernel,
-        (own_gate, near_got, gate_second, gate_third, band, short_filter, skip_gain.reshape(1, channels), soft, totals),
+        (*plain, *gates, band, short_filter, skip_gain.reshape(1, channels), soft, totals),
         [piece, piece, ((window, own), half)],
-        [pltpu.VMEM((COUNT,) + gate_shape[0], half), pltpu.VMEM((window + rows, own), half)],
+        [
+            pltpu.VMEM((window, own), half),
+            pltpu.VMEM((COUNT, rows + EDGE, own), half),
+            pltpu.VMEM((window + rows, own), half),
+        ],
     )
     third_got, second_got = swapped(third, "ctx", 3), swapped(second, "ctx", 2)
-    near, mine = run_kernel(near_rows_kernel, (soft, totals, values), [piece] * 2)
-    attended = [mine, swapped(near, "ctx", 1), second_got, third_got]
-    return project_and_share(attended, weight)
+    upper, lower, mine = run_kernel(
+        near_rows_kernel,
+        (soft, totals, values),
+        [((rows // 2, own), half)] * 2 + [piece],
+        [pltpu.VMEM((rows, own), half)],
+    )
+    near = (swapped(upper, "ctx", 1), swapped(lower, "ctx", 1))
+    return project_and_share((third_got, second_got, *near, mine), weight)
 
 
 def projected(attended, out_weight, masks):

time: 57.4 us -> 52.8 us (0.920)
  waiting for transfers between devices: 26.4 us -> 15.9 us
  starting transfers between devices: 16.2 us -> 25.3 us
  Pallas kernels: 12.7 us -> 9.64 us
    ppermute x11 -> x13, waiting for transfers between devices: 26.4 us -> 15.9 us  [swapped(): lax.ppermute(value, axis, [(source, source ^ step) for source in range(la...]
    ppermute x11 -> x13, starting transfers between devices: 16.2 us -> 25.3 us  [swapped(): lax.ppermute(value, axis, [(source, source ^ step) for source in range(la...]
    pallas_call x9 -> x7, Pallas kernels: 12.7 us -> 9.64 us  [run_kernel(): pl.pallas_call(kernel, out_shape=[jax.ShapeDtypeStruct(shape, dtype) for...]
  transfers between devices with their start and end apart: 11 -> 13, of which waited for: 6 -> 7; matrix products, arithmetic and copies ran while one was open for 0% -> 0% of each run, Pallas kernels for 8% -> 10%
where the time goes in v6:
time: 52.8 us; the launch traced here: 52.6 us
  starting transfers between devices  25.3 us (48%)
  waiting for transfers between devices  15.9 us (30%)
  Pallas kernels  9.64 us (18%)
  other arithmetic  0.89 us (2%)
  local copies, waits for them, and re-layouts  0.73 us (1%)
    ppermute x13, starting transfers between devices, swapped(): lax.ppermute(value, axis, [(source, source ^ step) for source in range(la...  25.3 us
    ppermute x13, waiting for transfers between devices, swapped(): lax.ppermute(value, axis, [(source, source ^ step) for source in range(la...  15.9 us
    pallas_call x7, Pallas kernels, run_kernel(): pl.pallas_call(kernel, out_shape=[jax.ShapeDtypeStruct(shape, dtype) for...  9.64 us
  transfers between devices with their start and end apart: 13, of which 7 were waited for; matrix products, arithmetic and copies ran while one was open for 0% of the time, Pallas kernels for 10%

profile of v6, /device:TPU:0, one launch (start us, length us, event | category | flops | bytes accessed | tf_op | source)
XLA Modules:
  0.0 52.6 jit_solution(12740753369747736946)
XLA Ops:
  0.0 2.6 %pack_kernel.1 = (bf16[384,256]{1,0:T(8,128)(2,1)}, bf16[384,256]{1,0:T(8,128)(2,1)}, bf16[384,256]{1,0:T(8,128)(2,1)}, bf16[384,256]{1,0:T(8,128)(2,1)}, bf16[1...) custom-call(bf16[3,128,1024]{2,1,0:T(8,128)(2,1)} %bitcast.3, ...), custom_call_target="tpu_custom_call" | custom-call | flops 1000000 | bytes 1048576 | tf_op jit(solution)/shard_map/pack_kernel/pallas_call | solution.py:320
  2.6 5.1 %collective-permute-start = (bf16[384,256]{1,0:T(8,128)(2,1)}, bf16[384,256]{1,0:T(8,128)(2,1)S(1)}, u32[]{:S(2)}, u32[]{:S(2)}) collective-permute-start(bf16[384,256]{1,0:T(8,128)(2,1)} %get-tuple-element.27), channel_id=1, source_target_pairs={{0,12},{4,8},{8,4},{12,0},{1,13},{5,9},{9,5},{13,1},{2,14},{6,10},... | collective-permute-start | bytes 589832 | tf_op jit(solution)/shard_map/ppermute | solution.py:333
  7.7 0.6 %collective-permute-start.2 = (bf16[384,256]{1,0:T(8,128)(2,1)}, bf16[384,256]{1,0:T(8,128)(2,1)S(1)}, u32[]{:S(2)}, u32[]{:S(2)}) collective-permute-start(bf16[384,256]{1,0:T(8,128)(2,1)} %get-tuple-element.29), channel_id=1, source_target_pairs={{0,4},{4,0},{8,12},{12,8},{1,5},{5,1},{9,13},{13,9},{2,6},{6,2},{1... | collective-permute-start | bytes 589832 | tf_op jit(solution)/shard_map/ppermute | solution.py:333
  8.4 3.7 %collective-permute-start.3 = (bf16[144,256]{1,0:T(8,128)(2,1)}, bf16[144,256]{1,0:T(8,128)(2,1)S(1)}, u32[]{:S(2)}, u32[]{:S(2)}) collective-permute-start(bf16[144,256]{1,0:T(8,128)(2,1)} %get-tuple-element.31), channel_id=1, source_target_pairs={{0,12},{4,8},{8,4},{12,0},{1,13},{5,9},{9,5},{13,1},{2,14},{6,10},... | collective-permute-start | bytes 221192 | tf_op jit(solution)/shard_map/ppermute | solution.py:333
  12.1 1.7 %collective-permute-done.third_ref.refs_0_ = bf16[384,256]{1,0:T(8,128)(2,1)S(1)} collective-permute-done((bf16[384,256]{1,0:T(8,128)(2,1)}, bf16[384,256]{1,0:T(8,128)(2,1)S(1)}, u32[]{:S(2)}, u32[]{:S(2)}) %collective-permute-start) | collective-permute-done | bytes 196640 | tf_op jit(solution)/shard_map/ppermute | solution.py:333
  13.8 9.0 %collective-permute-start.5 = (bf16[144,256]{1,0:T(8,128)(2,1)}, bf16[144,256]{1,0:T(8,128)(2,1)S(1)}, u32[]{:S(2)}, u32[]{:S(2)}) collective-permute-start(bf16[144,256]{1,0:T(8,128)(2,1)} %get-tuple-element.33), channel_id=1, source_target_pairs={{0,4},{4,0},{8,12},{12,8},{1,5},{5,1},{9,13},{13,9},{2,6},{6,2},{1... | collective-permute-start | bytes 221192 | tf_op jit(solution)/shard_map/ppermute | solution.py:333
  22.8 0.7 %copy-done.3 = bf16[64,128]{1,0:T(8,128)(2,1)S(1)} copy-done((bf16[64,128]{1,0:T(8,128)(2,1)S(1)}, bf16[64,128]{1,0:T(8,128)(2,1)}, u32[]{:S(2)}) %copy-start.3) | copy-done | bytes 16408
  23.5 3.4 %ready_kernel.1 = (bf16[2048,256]{1,0:T(8,128)(2,1)S(1)}, bf16[1024,4096]{1,0:T(8,128)(2,1)S(1)}) custom-call(bf16[64,128]{1,0:T(8,128)(2,1)S(1)} %copy-done.3, bf16[1024,4096]{1,0:T(8,128)(2,1)} %weight_any.1), custom_call_target="tpu_custom_call" | custom-call | flops 1000000 | bytes 1048576 | tf_op jit(solution)/shard_map/ready_kernel/pallas_call | solution.py:320
  26.9 1.8 %collective-permute-done.1.second_ref.refs_1_ = bf16[384,256]{1,0:T(8,128)(2,1)S(1)} collective-permute-done((bf16[384,256]{1,0:T(8,128)(2,1)}, bf16[384,256]{1,0:T(8,128)(2,1)S(1)}, u32[]{:S(2)}, u32[]{:S(2)}) %collective-permute-start.1) | collective-permute-done | bytes 196640 | tf_op jit(solution)/shard_map/ppermute | solution.py:333
  28.8 0.7 %weights_kernel.1 = (bf16[2,512,512]{2,1,0:T(8,128)(2,1)S(1)}, f32[512,128]{1,0:T(8,128)S(1)}) custom-call(bf16[384,256]{1,0:T(8,128)(2,1)S(1)} %collective-permute-done.third_ref.refs_0_, bf16[384,256]{1,0:T(8,128)(2,1)S(1)} %collective-permute-done.1.second_ref.refs_1_, bf16[384,256]{1,0:T(8,128)(2,1)S(1)} %collective-permute-done.2.near_ref.refs_2_, ...), custom_call_target="tpu_custom_call" | custom-call | flops 1000000 | bytes 1048576 | tf_op jit(solution)/shard_map/weights_kernel/pallas_call | solution.py:320
  29.5 1.5 %collective-permute-done.4.refs_5_ = bf16[144,256]{1,0:T(8,128)(2,1)S(1)} collective-permute-done((bf16[144,256]{1,0:T(8,128)(2,1)}, bf16[144,256]{1,0:T(8,128)(2,1)S(1)}, u32[]{:S(2)}, u32[]{:S(2)}) %collective-permute-start.4) | collective-permute-done | bytes 73760 | tf_op jit(solution)/shard_map/ppermute | solution.py:333
  31.0 1.2 %values_kernel.1 = (bf16[128,256]{1,0:T(8,128)(2,1)S(1)}, bf16[128,256]{1,0:T(8,128)(2,1)S(1)}, bf16[512,256]{1,0:T(8,128)(2,1)S(1)}) custom-call(bf16[384,256]{1,0:T(8,128)(2,1)S(1)} %collective-permute-done.third_ref.refs_0_, bf16[384,256]{1,0:T(8,128)(2,1)S(1)} %collective-permute-done.1.second_ref.refs_1_, ...), custom_call_target="tpu_custom_call" | custom-call | flops 1000000 | bytes 1048576 | tf_op jit(solution)/shard_map/values_kernel/pallas_call | solution.py:320
  32.2 2.5 %collective-permute-start.6 = (bf16[128,256]{1,0:T(8,128)(2,1)S(1)}, bf16[128,256]{1,0:T(8,128)(2,1)S(1)}, u32[]{:S(2)}, u32[]{:S(2)}) collective-permute-start(bf16[128,256]{1,0:T(8,128)(2,1)S(1)} %get-tuple-element.38), channel_id=1, source_target_pairs={{0,12},{4,8},{8,4},{12,0},{1,13},{5,9},{9,5},{13,1},{2,14},{6,10},... | collective-permute-start | bytes 196616 | tf_op jit(solution)/shard_map/ppermute | solution.py:333
  34.7 0.3 near_rows_kernel.1
  35.0 2.0 %collective-permute-start.8 = (bf16[64,256]{1,0:T(8,128)(2,1)S(1)}, bf16[64,256]{1,0:T(8,128)(2,1)S(1)}, u32[]{:S(2)}, u32[]{:S(2)}) collective-permute-start(bf16[64,256]{1,0:T(8,128)(2,1)S(1)} %get-tuple-element.41), channel_id=1, source_target_pairs={{0,4},{4,0},{8,12},{12,8},{1,5},{5,1},{9,13},{13,9},{2,6},{6,2},{1... | collective-permute-start | bytes 98312 | tf_op jit(solution)/shard_map/ppermute | solution.py:333
  37.1 2.2 %collective-permute-done.8.refs_2_ = bf16[64,256]{1,0:T(8,128)(2,1)S(1)} collective-permute-done((bf16[64,256]{1,0:T(8,128)(2,1)S(1)}, bf16[64,256]{1,0:T(8,128)(2,1)S(1)}, u32[]{:S(2)}, u32[]{:S(2)}) %collective-permute-start.8) | collective-permute-done | bytes 32800 | tf_op jit(solution)/shard_map/ppermute | solution.py:333
  39.3 1.6 %collective-permute-done.9.refs_3_ = bf16[64,256]{1,0:T(8,128)(2,1)S(1)} collective-permute-done((bf16[64,256]{1,0:T(8,128)(2,1)S(1)}, bf16[64,256]{1,0:T(8,128)(2,1)S(1)}, u32[]{:S(2)}, u32[]{:S(2)}) %collective-permute-start.9) | collective-permute-done | bytes 32800 | tf_op jit(solution)/shard_map/ppermute | solution.py:333
  40.9 0.7 %project_kernel.3 = (bf16[128,1024]{1,0:T(8,128)(2,1)S(1)}, bf16[128,1024]{1,0:T(8,128)(2,1)S(1)}) custom-call(bf16[128,256]{1,0:T(8,128)(2,1)S(1)} %collective-permute-done.6.refs_0_, bf16[128,256]{1,0:T(8,128)(2,1)S(1)} %collective-permute-done.7.refs_1_, bf16[64,256]{1,0:T(8,128)(2,1)S(1)} %collective-permute-done.8.refs_2_, ...), custom_call_target="tpu_custom_call" | custom-call | flops 536870912 | bytes 1048576 | tf_op jit(solution)/shard_map/project_kernel/pallas_call | solution.py:320
  41.7 0.7 %project_kernel.2 = (bf16[128,1024]{1,0:T(8,128)(2,1)S(1)}, bf16[128,1024]{1,0:T(8,128)(2,1)S(1)}) custom-call(bf16[128,256]{1,0:T(8,128)(2,1)S(1)} %collective-permute-done.6.refs_0_, bf16[128,256]{1,0:T(8,128)(2,1)S(1)} %collective-permute-done.7.refs_1_, bf16[64,256]{1,0:T(8,128)(2,1)S(1)} %collective-permute-done.8.refs_2_, ...), custom_call_target="tpu_custom_call" | custom-call | flops 536870912 | bytes 1048576 | tf_op jit(solution)/shard_map/project_kernel/pallas_call | solution.py:320
  42.5 0.6 %collective-permute-start.10 = (bf16[128,1024]{1,0:T(8,128)(2,1)S(1)}, bf16[128,1024]{1,0:T(8,128)(2,1)S(1)}, u32[]{:S(2)}, u32[]{:S(2)}) collective-permute-start(bf16[128,1024]{1,0:T(8,128)(2,1)S(1)} %get-tuple-element.46), channel_id=1, source_target_pairs={{0,1},{1,0},{2,3},{3,2},{4,5},{5,4},{6,7},{7,6},{8,9},{9,8},{10,11... | collective-permute-start | bytes 786440 | tf_op jit(solution)/shard_map/ppermute | solution.py:333
  43.0 0.2 collective-permute-done.11
  43.3 1.6 %collective-permute-start.12 = (bf16[128,1024]{1,0:T(8,128)(2,1)S(1)}, bf16[128,1024]{1,0:T(8,128)(2,1)S(1)}, u32[]{:S(2)}, u32[]{:S(2)}) collective-permute-start(bf16[128,1024]{1,0:T(8,128)(2,1)S(1)} %add_convert_fusion.1), channel_id=1, source_target_pairs={{0,2},{1,3},{2,0},{3,1},{4,6},{5,7},{6,4},{7,5},{8,10},{9,11},{10,... | collective-permute-start | bytes 786440 | tf_op jit(solution)/shard_map/ppermute | solution.py:333
  44.9 6.8 %collective-permute-done.12 = bf16[128,1024]{1,0:T(8,128)(2,1)S(1)} collective-permute-done((bf16[128,1024]{1,0:T(8,128)(2,1)S(1)}, bf16[128,1024]{1,0:T(8,128)(2,1)S(1)}, u32[]{:S(2)}, u32[]{:S(2)}) %collective-permute-start.12) | collective-permute-done | bytes 262176 | tf_op jit(solution)/shard_map/ppermute | solution.py:333
  51.7 0.8 %add_convert_fusion = bf16[128,1024]{1,0:T(8,128)(2,1)} fusion(bf16[128,1024]{1,0:T(8,128)(2,1)S(1)} %collective-permute-done.12, bf16[128,1024]{1,0:T(8,128)(2,1)S(1)} %collective-permute-done.10, bf16[128,1024]{1,0:T(8,128)(2,1)S(1)} %get-tuple-element.45), kind=kLoop, calls=%fused_computation | loop fusion | flops 786432 | bytes 1048576 | tf_op jit(solution)/shard_map/convert_element_type | solution.py:407
  (21 shorter events, 0.3 us)
Async XLA Ops:
  0.0 31.0 %copy-start.1 = (bf16[3,3,1024]{2,1,0:T(4,128)(2,1)S(1)}, bf16[3,3,1024]{2,1,0:T(4,128)(2,1)}, u32[]{:S(2)}) copy-start(bf16[3,3,1024]{2,1,0:T(4,128)(2,1)} %refs_9_.1) | copy-start | bytes 55300
  0.0 31.0 %copy-start.4 = (f32[1024]{0:T(1024)S(1)}, f32[1024]{0:T(1024)}, u32[]{:S(2)}) copy-start(f32[1024]{0:T(1024)} %param.10) | copy-start | bytes 12292
  2.6 26.2 %copy-start = (bf16[384,256]{1,0:T(8,128)(2,1)S(1)}, bf16[384,256]{1,0:T(8,128)(2,1)}, u32[]{:S(2)}) copy-start(bf16[384,256]{1,0:T(8,128)(2,1)} %get-tuple-element.30.own_ref.refs_3_) | copy-start | bytes 589828
  2.6 28.4 %copy-start.2 = (bf16[144,256]{1,0:T(8,128)(2,1)S(1)}, bf16[144,256]{1,0:T(8,128)(2,1)}, u32[]{:S(2)}) copy-start(bf16[144,256]{1,0:T(8,128)(2,1)} %get-tuple-element.34.refs_7_) | copy-start | bytes 221188
  2.6 11.2 %collective-permute-start = (bf16[384,256]{1,0:T(8,128)(2,1)}, bf16[384,256]{1,0:T(8,128)(2,1)S(1)}, u32[]{:S(2)}, u32[]{:S(2)}) collective-permute-start(bf16[384,256]{1,0:T(8,128)(2,1)} %get-tuple-element.27), channel_id=1, source_target_pairs={{0,12},{4,8},{8,4},{12,0},{1,13},{5,9},{9,5},{13,1},{2,14},{6,10},... | collective-permute-start | bytes 589832 | tf_op jit(solution)/shard_map/ppermute | solution.py:333
  7.7 21.0 %collective-permute-start.1 = (bf16[384,256]{1,0:T(8,128)(2,1)}, bf16[384,256]{1,0:T(8,128)(2,1)S(1)}, u32[]{:S(2)}, u32[]{:S(2)}) collective-permute-start(bf16[384,256]{1,0:T(8,128)(2,1)} %get-tuple-element.28), channel_id=1, source_target_pairs={{0,8},{4,12},{8,0},{12,4},{1,9},{5,13},{9,1},{13,5},{2,10},{6,14},... | collective-permute-start | bytes 589832 | tf_op jit(solution)/shard_map/ppermute | solution.py:333
  7.7 21.0 %collective-permute-start.2 = (bf16[384,256]{1,0:T(8,128)(2,1)}, bf16[384,256]{1,0:T(8,128)(2,1)S(1)}, u32[]{:S(2)}, u32[]{:S(2)}) collective-permute-start(bf16[384,256]{1,0:T(8,128)(2,1)} %get-tuple-element.29), channel_id=1, source_target_pairs={{0,4},{4,0},{8,12},{12,8},{1,5},{5,1},{9,13},{13,9},{2,6},{6,2},{1... | collective-permute-start | bytes 589832 | tf_op jit(solution)/shard_map/ppermute | solution.py:333
  8.4 21.1 %collective-permute-start.3 = (bf16[144,256]{1,0:T(8,128)(2,1)}, bf16[144,256]{1,0:T(8,128)(2,1)S(1)}, u32[]{:S(2)}, u32[]{:S(2)}) collective-permute-start(bf16[144,256]{1,0:T(8,128)(2,1)} %get-tuple-element.31), channel_id=1, source_target_pairs={{0,12},{4,8},{8,4},{12,0},{1,13},{5,9},{9,5},{13,1},{2,14},{6,10},... | collective-permute-start | bytes 221192 | tf_op jit(solution)/shard_map/ppermute | solution.py:333
  12.1 18.8 %collective-permute-start.4 = (bf16[144,256]{1,0:T(8,128)(2,1)}, bf16[144,256]{1,0:T(8,128)(2,1)S(1)}, u32[]{:S(2)}, u32[]{:S(2)}) collective-permute-start(bf16[144,256]{1,0:T(8,128)(2,1)} %get-tuple-element.32), channel_id=1, source_target_pairs={{0,8},{4,12},{8,0},{12,4},{1,9},{5,13},{9,1},{13,5},{2,10},{6,14},... | collective-permute-start | bytes 221192 | tf_op jit(solution)/shard_map/ppermute | solution.py:333
  13.8 17.1 %collective-permute-start.5 = (bf16[144,256]{1,0:T(8,128)(2,1)}, bf16[144,256]{1,0:T(8,128)(2,1)S(1)}, u32[]{:S(2)}, u32[]{:S(2)}) collective-permute-start(bf16[144,256]{1,0:T(8,128)(2,1)} %get-tuple-element.33), channel_id=1, source_target_pairs={{0,4},{4,0},{8,12},{12,8},{1,5},{5,1},{9,13},{13,9},{2,6},{6,2},{1... | collective-permute-start | bytes 221192 | tf_op jit(solution)/shard_map/ppermute | solution.py:333
  22.8 0.7 %copy-start.3 = (bf16[64,128]{1,0:T(8,128)(2,1)S(1)}, bf16[64,128]{1,0:T(8,128)(2,1)}, u32[]{:S(2)}) copy-start(bf16[64,128]{1,0:T(8,128)(2,1)} %filter_ref.1) | copy-start | bytes 49156
  32.2 8.7 %collective-permute-start.6 = (bf16[128,256]{1,0:T(8,128)(2,1)S(1)}, bf16[128,256]{1,0:T(8,128)(2,1)S(1)}, u32[]{:S(2)}, u32[]{:S(2)}) collective-permute-start(bf16[128,256]{1,0:T(8,128)(2,1)S(1)} %get-tuple-element.38), channel_id=1, source_target_pairs={{0,12},{4,8},{8,4},{12,0},{1,13},{5,9},{9,5},{13,1},{2,14},{6,10},... | collective-permute-start | bytes 196616 | tf_op jit(solution)/shard_map/ppermute | solution.py:333
  34.7 6.2 %collective-permute-start.7 = (bf16[128,256]{1,0:T(8,128)(2,1)S(1)}, bf16[128,256]{1,0:T(8,128)(2,1)S(1)}, u32[]{:S(2)}, u32[]{:S(2)}) collective-permute-start(bf16[128,256]{1,0:T(8,128)(2,1)S(1)} %get-tuple-element.39), channel_id=1, source_target_pairs={{0,8},{4,12},{8,0},{12,4},{1,9},{5,13},{9,1},{13,5},{2,10},{6,14},... | collective-permute-start | bytes 196616 | tf_op jit(solution)/shard_map/ppermute | solution.py:333
  35.0 4.3 %collective-permute-start.8 = (bf16[64,256]{1,0:T(8,128)(2,1)S(1)}, bf16[64,256]{1,0:T(8,128)(2,1)S(1)}, u32[]{:S(2)}, u32[]{:S(2)}) collective-permute-start(bf16[64,256]{1,0:T(8,128)(2,1)S(1)} %get-tuple-element.41), channel_id=1, source_target_pairs={{0,4},{4,0},{8,12},{12,8},{1,5},{5,1},{9,13},{13,9},{2,6},{6,2},{1... | collective-permute-start | bytes 98312 | tf_op jit(solution)/shard_map/ppermute | solution.py:333
  37.0 3.9 %collective-permute-start.9 = (bf16[64,256]{1,0:T(8,128)(2,1)S(1)}, bf16[64,256]{1,0:T(8,128)(2,1)S(1)}, u32[]{:S(2)}, u32[]{:S(2)}) collective-permute-start(bf16[64,256]{1,0:T(8,128)(2,1)S(1)} %get-tuple-element.42), channel_id=1, source_target_pairs={{0,4},{4,0},{8,12},{12,8},{1,5},{5,1},{9,13},{13,9},{2,6},{6,2},{1... | collective-permute-start | bytes 98312 | tf_op jit(solution)/shard_map/ppermute | solution.py:333
  41.7 1.6 %collective-permute-start.11 = (bf16[128,1024]{1,0:T(8,128)(2,1)S(1)}, bf16[128,1024]{1,0:T(8,128)(2,1)S(1)}, u32[]{:S(2)}, u32[]{:S(2)}) collective-permute-start(bf16[128,1024]{1,0:T(8,128)(2,1)S(1)} %get-tuple-element.48), channel_id=1, source_target_pairs={{0,1},{1,0},{2,3},{3,2},{4,5},{5,4},{6,7},{7,6},{8,9},{9,8},{10,11... | collective-permute-start | bytes 786440 | tf_op jit(solution)/shard_map/ppermute | solution.py:333
  42.5 2.4 %collective-permute-start.10 = (bf16[128,1024]{1,0:T(8,128)(2,1)S(1)}, bf16[128,1024]{1,0:T(8,128)(2,1)S(1)}, u32[]{:S(2)}, u32[]{:S(2)}) collective-permute-start(bf16[128,1024]{1,0:T(8,128)(2,1)S(1)} %get-tuple-element.46), channel_id=1, source_target_pairs={{0,1},{1,0},{2,3},{3,2},{4,5},{5,4},{6,7},{7,6},{8,9},{9,8},{10,11... | collective-permute-start | bytes 786440 | tf_op jit(solution)/shard_map/ppermute | solution.py:333
  43.3 8.4 %collective-permute-start.12 = (bf16[128,1024]{1,0:T(8,128)(2,1)S(1)}, bf16[128,1024]{1,0:T(8,128)(2,1)S(1)}, u32[]{:S(2)}, u32[]{:S(2)}) collective-permute-start(bf16[128,1024]{1,0:T(8,128)(2,1)S(1)} %add_convert_fusion.1), channel_id=1, source_target_pairs={{0,2},{1,3},{2,0},{3,1},{4,6},{5,7},{6,4},{7,5},{8,10},{9,11},{10,... | collective-permute-start | bytes 786440 | tf_op jit(solution)/shard_map/ppermute | solution.py:333

commit v7 on v6

--- a/solution.py
+++ b/solution.py
@@ -132,33 +132,41 @@
     out_ref[rows : rows + EDGE] = jnp.concatenate(edges, axis=0).astype(jnp.bfloat16)
 
 
-def pack_kernel(inputs_any, short_any, queries_any, keys_any, *refs):
-    plain_refs, gate_refs = refs[:COUNT], refs[COUNT : 2 * COUNT]
-    signal_s, short_s, sems = refs[2 * COUNT :]
-    rows, own = inputs_any.shape[1], plain_refs[0].shape[1]
-    position = lax.axis_index("ctx")
-    loads = [
+def plain_kernel(inputs_any, queries_any, keys_any, *refs):
+    out_refs, sems = refs[:COUNT], refs[COUNT]
+    rows, own = queries_any.shape[0], out_refs[0].shape[1]
+    position = lax.axis_index("ctx")
+    copies = []
+    for step in ORDER:
+        columns = columns_of(position ^ step, own)
+        for index, source in enumerate((queries_any, keys_any, inputs_any.at[0])):
+            target = out_refs[step].at[index * rows : (index + 1) * rows]
+            copies.append(pltpu.make_async_copy(source.at[:, columns], target, sems.at[len(copies)]))
+    for copy in copies:
+        copy.start()
+    for copy in copies:
+        copy.wait()
+
+
+def gate_kernel(inputs_any, short_any, *refs):
+    out_refs, (signal_s, short_s, sems) = refs[:COUNT], refs[COUNT:]
+    own = out_refs[0].shape[1]
+    position = lax.axis_index("ctx")
+    copies = [
         pltpu.make_async_copy(short_any, short_s, sems.at[0]),
         pltpu.make_async_copy(inputs_any.at[1:3], signal_s, sems.at[1]),
     ]
-    for step in ORDER:
-        columns = columns_of(position ^ step, own)
-        for index, source in enumerate((queries_any, keys_any, inputs_any.at[0])):
-            target = plain_refs[step].at[index * rows : (index + 1) * rows]
-            loads.append(pltpu.make_async_copy(source.at[:, columns], target, sems.at[len(loads)]))
-    for load in loads:
-        load.start()
-    for load in loads[:2]:
-        load.wait()
+    for copy in copies:
+        copy.start()
+    for copy in copies:
+        copy.wait()
     for step in ORDER:
         columns = columns_of(position ^ step, own)
         signals = [signal_s[stream, :, columns].astype(jnp.float32) for stream in range(2)]
         taps = [
             [short_s[lag, stream : stream + 1, columns].astype(jnp.float32) for lag in range(3)] for stream in (1, 2)
         ]
-        write_gate(signals, taps, gate_refs[step])
-    for load in loads[2:]:
-        load.wait()
+        write_gate(signals, taps, out_refs[step])
 
 
 def ready_kernel(filter_ref, weight_any, band_ref, weight_ref, sem):
@@ -311,7 +319,8 @@
 
 
 VMEM_LIMIT = 40 * 1024 * 1024
-WIDE_LIMIT = 60 * 1024 * 1024
+PLAIN_LIMIT = 53 * 1024 * 1024
+GATE_LIMIT = 60 * 1024 * 1024
 IN_HBM = pl.BlockSpec(memory_space=pltpu.HBM)
 IN_VMEM = pl.BlockSpec(memory_space=pltpu.VMEM)
 
@@ -339,19 +348,27 @@
     groups, taps = long_filter.shape
     half = jnp.bfloat16
     piece, window = ((rows, own), half), COUNT * rows
-    packed = run_kernel(
-        pack_kernel,
-        (jnp.transpose(inputs, (1, 0, 2)), short_filter, queries, key_rows),
-        [((3 * rows, own), half)] * COUNT + [((rows + EDGE, own), half)] * COUNT,
+    streamed = jnp.transpose(inputs, (1, 0, 2))
+    plain = run_kernel(
+        plain_kernel,
+        (streamed, queries, key_rows),
+        [((3 * rows, own), half)] * COUNT,
+        [pltpu.SemaphoreType.DMA((3 * COUNT,))],
+        [IN_HBM] * 3,
+        PLAIN_LIMIT,
+    )
+    gates = run_kernel(
+        gate_kernel,
+        (streamed, short_filter),
+        [((rows + EDGE, own), half)] * COUNT,
         [
             pltpu.VMEM((2, rows, channels), half),
             pltpu.VMEM(short_filter.shape, half),
-            pltpu.SemaphoreType.DMA((3 * COUNT + 2,)),
+            pltpu.SemaphoreType.DMA((2,)),
         ],
-        [IN_HBM] * 4,
-        WIDE_LIMIT,
-    )
-    plain, gates = packed[:COUNT], packed[COUNT:]
+        [IN_HBM] * 2,
+        GATE_LIMIT,
+    )
     plain = [swapped(plain[step], "ctx", step) for step in ORDER[:3]] + [plain[0]]
     gates = [swapped(gates[step], "ctx", step) for step in ORDER[:3]] + [gates[0]]
     band, weight = run_kernel(

time: 52.8 us -> 51.3 us (0.972)
  waiting for transfers between devices: 15.9 us -> 14.2 us
  Pallas kernels: 9.64 us -> 10.4 us
  starting transfers between devices: 25.3 us -> 24.6 us
    ppermute x13, waiting for transfers between devices: 15.9 us -> 14.2 us  [swapped(): lax.ppermute(value, axis, [(source, source ^ step) for source in range(la...]
    pallas_call x7 -> x8, Pallas kernels: 9.64 us -> 10.4 us  [run_kernel(): pl.pallas_call(kernel, out_shape=[jax.ShapeDtypeStruct(shape, dtype) for...]
    ppermute x13, starting transfers between devices: 25.3 us -> 24.6 us  [swapped(): lax.ppermute(value, axis, [(source, source ^ step) for source in range(la...]
  transfers between devices with their start and end apart: 13 -> 13, of which waited for: 7 -> 6; matrix products, arithmetic and copies ran while one was open for 0% -> 0% of each run, Pallas kernels for 10% -> 14%
where the time goes in v7:
time: 51.3 us; the launch traced here: 51 us
  starting transfers between devices  24.6 us (48%)
  waiting for transfers between devices  14.2 us (28%)
  Pallas kernels  10.4 us (20%)
  other arithmetic  0.89 us (2%)
  local copies, waits for them, and re-layouts  0.73 us (1%)
    ppermute x13, starting transfers between devices, swapped(): lax.ppermute(value, axis, [(source, source ^ step) for source in range(la...  24.6 us
    ppermute x13, waiting for transfers between devices, swapped(): lax.ppermute(value, axis, [(source, source ^ step) for source in range(la...  14.2 us
    pallas_call x8, Pallas kernels, run_kernel(): pl.pallas_call(kernel, out_shape=[jax.ShapeDtypeStruct(shape, dtype) for...  10.4 us
  transfers between devices with their start and end apart: 13, of which 6 were waited for; matrix products, arithmetic and copies ran while one was open for 0% of the time, Pallas kernels for 14%

profile of v7, /device:TPU:0, one launch (start us, length us, event | category | flops | bytes accessed | tf_op | source)
XLA Modules:
  0.0 51.0 jit_solution(15418379520908462149)
XLA Ops:
  0.0 1.3 %plain_kernel.1 = (bf16[384,256]{1,0:T(8,128)(2,1)S(1)}, bf16[384,256]{1,0:T(8,128)(2,1)S(1)}, bf16[384,256]{1,0:T(8,128)(2,1)S(1)}, bf16[384,256]{1,0:T(8,128)(2,1)S(1)}) custom-call(bf16[3,128,1024]{2,1,0:T(8,128)(2,1)} %bitcast.3, bf16[128,1024]{1,0:T(8,128)(2,1)} %queries_any.1, bf16[128,1024]{1,0:T(8,128)(2,1)} %keys_any.1), custom_call_target="tpu_custom_call" | custom-call | flops 1000000 | bytes 1048576 | tf_op jit(solution)/shard_map/plain_kernel/pallas_call | solution.py:329
  1.3 5.1 %collective-permute-start = (bf16[384,256]{1,0:T(8,128)(2,1)S(1)}, bf16[384,256]{1,0:T(8,128)(2,1)S(1)}, u32[]{:S(2)}, u32[]{:S(2)}) collective-permute-start(bf16[384,256]{1,0:T(8,128)(2,1)S(1)} %get-tuple-element.27), channel_id=1, source_target_pairs={{0,12},{4,8},{8,4},{12,0},{1,13},{5,9},{9,5},{13,1},{2,14},{6,10},... | collective-permute-start | bytes 589832 | tf_op jit(solution)/shard_map/ppermute | solution.py:342
  6.4 0.6 %collective-permute-start.2 = (bf16[384,256]{1,0:T(8,128)(2,1)S(1)}, bf16[384,256]{1,0:T(8,128)(2,1)S(1)}, u32[]{:S(2)}, u32[]{:S(2)}) collective-permute-start(bf16[384,256]{1,0:T(8,128)(2,1)S(1)} %get-tuple-element.29), channel_id=1, source_target_pairs={{0,4},{4,0},{8,12},{12,8},{1,5},{5,1},{9,13},{13,9},{2,6},{6,2},{1... | collective-permute-start | bytes 589832 | tf_op jit(solution)/shard_map/ppermute | solution.py:342
  7.0 2.1 %gate_kernel.1 = (bf16[144,256]{1,0:T(8,128)(2,1)}, bf16[144,256]{1,0:T(8,128)(2,1)}, bf16[144,256]{1,0:T(8,128)(2,1)}, bf16[144,256]{1,0:T(8,128)(2,1)}) custom-call(bf16[3,128,1024]{2,1,0:T(8,128)(2,1)} %bitcast.4, bf16[3,3,1024]{2,1,0:T(4,128)(2,1)} %refs_9_.1), custom_call_target="tpu_custom_call" | custom-call | flops 1000000 | bytes 1048576 | tf_op jit(solution)/shard_map/gate_kernel/pallas_call | solution.py:329
  9.2 3.8 %collective-permute-start.3 = (bf16[144,256]{1,0:T(8,128)(2,1)}, bf16[144,256]{1,0:T(8,128)(2,1)S(1)}, u32[]{:S(2)}, u32[]{:S(2)}) collective-permute-start(bf16[144,256]{1,0:T(8,128)(2,1)} %get-tuple-element.31), channel_id=1, source_target_pairs={{0,12},{4,8},{8,4},{12,0},{1,13},{5,9},{9,5},{13,1},{2,14},{6,10},... | collective-permute-start | bytes 221192 | tf_op jit(solution)/shard_map/ppermute | solution.py:342
  13.0 8.3 %collective-permute-start.5 = (bf16[144,256]{1,0:T(8,128)(2,1)}, bf16[144,256]{1,0:T(8,128)(2,1)S(1)}, u32[]{:S(2)}, u32[]{:S(2)}) collective-permute-start(bf16[144,256]{1,0:T(8,128)(2,1)} %get-tuple-element.33), channel_id=1, source_target_pairs={{0,4},{4,0},{8,12},{12,8},{1,5},{5,1},{9,13},{13,9},{2,6},{6,2},{1... | collective-permute-start | bytes 221192 | tf_op jit(solution)/shard_map/ppermute | solution.py:342
  21.2 0.7 %copy-done.2 = bf16[64,128]{1,0:T(8,128)(2,1)S(1)} copy-done((bf16[64,128]{1,0:T(8,128)(2,1)S(1)}, bf16[64,128]{1,0:T(8,128)(2,1)}, u32[]{:S(2)}) %copy-start.2) | copy-done | bytes 16408
  22.0 3.4 %ready_kernel.1 = (bf16[2048,256]{1,0:T(8,128)(2,1)S(1)}, bf16[1024,4096]{1,0:T(8,128)(2,1)S(1)}) custom-call(bf16[64,128]{1,0:T(8,128)(2,1)S(1)} %copy-done.2, bf16[1024,4096]{1,0:T(8,128)(2,1)} %weight_any.1), custom_call_target="tpu_custom_call" | custom-call | flops 1000000 | bytes 1048576 | tf_op jit(solution)/shard_map/ready_kernel/pallas_call | solution.py:329
  25.4 1.8 %collective-permute-done.1.second_ref.refs_1_ = bf16[384,256]{1,0:T(8,128)(2,1)S(1)} collective-permute-done((bf16[384,256]{1,0:T(8,128)(2,1)S(1)}, bf16[384,256]{1,0:T(8,128)(2,1)S(1)}, u32[]{:S(2)}, u32[]{:S(2)}) %collective-permute-start.1) | collective-permute-done | bytes 196640 | tf_op jit(solution)/shard_map/ppermute | solution.py:342
  27.2 0.7 %weights_kernel.1 = (bf16[2,512,512]{2,1,0:T(8,128)(2,1)S(1)}, f32[512,128]{1,0:T(8,128)S(1)}) custom-call(bf16[384,256]{1,0:T(8,128)(2,1)S(1)} %collective-permute-done.third_ref.refs_0_, bf16[384,256]{1,0:T(8,128)(2,1)S(1)} %collective-permute-done.1.second_ref.refs_1_, bf16[384,256]{1,0:T(8,128)(2,1)S(1)} %collective-permute-done.2.near_ref.refs_2_, ...), custom_call_target="tpu_custom_call" | custom-call | flops 1000000 | bytes 1048576 | tf_op jit(solution)/shard_map/weights_kernel/pallas_call | solution.py:329
  27.9 1.5 %collective-permute-done.4.refs_5_ = bf16[144,256]{1,0:T(8,128)(2,1)S(1)} collective-permute-done((bf16[144,256]{1,0:T(8,128)(2,1)}, bf16[144,256]{1,0:T(8,128)(2,1)S(1)}, u32[]{:S(2)}, u32[]{:S(2)}) %collective-permute-start.4) | collective-permute-done | bytes 73760 | tf_op jit(solution)/shard_map/ppermute | solution.py:342
  29.4 1.2 %values_kernel.1 = (bf16[128,256]{1,0:T(8,128)(2,1)S(1)}, bf16[128,256]{1,0:T(8,128)(2,1)S(1)}, bf16[512,256]{1,0:T(8,128)(2,1)S(1)}) custom-call(bf16[384,256]{1,0:T(8,128)(2,1)S(1)} %collective-permute-done.third_ref.refs_0_, bf16[384,256]{1,0:T(8,128)(2,1)S(1)} %collective-permute-done.1.second_ref.refs_1_, ...), custom_call_target="tpu_custom_call" | custom-call | flops 1000000 | bytes 1048576 | tf_op jit(solution)/shard_map/values_kernel/pallas_call | solution.py:329
  30.6 2.5 %collective-permute-start.6 = (bf16[128,256]{1,0:T(8,128)(2,1)S(1)}, bf16[128,256]{1,0:T(8,128)(2,1)S(1)}, u32[]{:S(2)}, u32[]{:S(2)}) collective-permute-start(bf16[128,256]{1,0:T(8,128)(2,1)S(1)} %get-tuple-element.38), channel_id=1, source_target_pairs={{0,12},{4,8},{8,4},{12,0},{1,13},{5,9},{9,5},{13,1},{2,14},{6,10},... | collective-permute-start | bytes 196616 | tf_op jit(solution)/shard_map/ppermute | solution.py:342
  33.2 0.3 near_rows_kernel.1
  33.5 2.0 %collective-permute-start.8 = (bf16[64,256]{1,0:T(8,128)(2,1)S(1)}, bf16[64,256]{1,0:T(8,128)(2,1)S(1)}, u32[]{:S(2)}, u32[]{:S(2)}) collective-permute-start(bf16[64,256]{1,0:T(8,128)(2,1)S(1)} %get-tuple-element.41), channel_id=1, source_target_pairs={{0,4},{4,0},{8,12},{12,8},{1,5},{5,1},{9,13},{13,9},{2,6},{6,2},{1... | collective-permute-start | bytes 98312 | tf_op jit(solution)/shard_map/ppermute | solution.py:342
  35.6 2.2 %collective-permute-done.8.refs_2_ = bf16[64,256]{1,0:T(8,128)(2,1)S(1)} collective-permute-done((bf16[64,256]{1,0:T(8,128)(2,1)S(1)}, bf16[64,256]{1,0:T(8,128)(2,1)S(1)}, u32[]{:S(2)}, u32[]{:S(2)}) %collective-permute-start.8) | collective-permute-done | bytes 32800 | tf_op jit(solution)/shard_map/ppermute | solution.py:342
  37.7 1.6 %collective-permute-done.9.refs_3_ = bf16[64,256]{1,0:T(8,128)(2,1)S(1)} collective-permute-done((bf16[64,256]{1,0:T(8,128)(2,1)S(1)}, bf16[64,256]{1,0:T(8,128)(2,1)S(1)}, u32[]{:S(2)}, u32[]{:S(2)}) %collective-permute-start.9) | collective-permute-done | bytes 32800 | tf_op jit(solution)/shard_map/ppermute | solution.py:342
  39.4 0.7 %project_kernel.3 = (bf16[128,1024]{1,0:T(8,128)(2,1)S(1)}, bf16[128,1024]{1,0:T(8,128)(2,1)S(1)}) custom-call(bf16[128,256]{1,0:T(8,128)(2,1)S(1)} %collective-permute-done.6.refs_0_, bf16[128,256]{1,0:T(8,128)(2,1)S(1)} %collective-permute-done.7.refs_1_, bf16[64,256]{1,0:T(8,128)(2,1)S(1)} %collective-permute-done.8.refs_2_, ...), custom_call_target="tpu_custom_call" | custom-call | flops 536870912 | bytes 1048576 | tf_op jit(solution)/shard_map/project_kernel/pallas_call | solution.py:329
  40.2 0.7 %project_kernel.2 = (bf16[128,1024]{1,0:T(8,128)(2,1)S(1)}, bf16[128,1024]{1,0:T(8,128)(2,1)S(1)}) custom-call(bf16[128,256]{1,0:T(8,128)(2,1)S(1)} %collective-permute-done.6.refs_0_, bf16[128,256]{1,0:T(8,128)(2,1)S(1)} %collective-permute-done.7.refs_1_, bf16[64,256]{1,0:T(8,128)(2,1)S(1)} %collective-permute-done.8.refs_2_, ...), custom_call_target="tpu_custom_call" | custom-call | flops 536870912 | bytes 1048576 | tf_op jit(solution)/shard_map/project_kernel/pallas_call | solution.py:329
  40.9 0.6 %collective-permute-start.10 = (bf16[128,1024]{1,0:T(8,128)(2,1)S(1)}, bf16[128,1024]{1,0:T(8,128)(2,1)S(1)}, u32[]{:S(2)}, u32[]{:S(2)}) collective-permute-start(bf16[128,1024]{1,0:T(8,128)(2,1)S(1)} %get-tuple-element.46), channel_id=1, source_target_pairs={{0,1},{1,0},{2,3},{3,2},{4,5},{5,4},{6,7},{7,6},{8,9},{9,8},{10,11... | collective-permute-start | bytes 786440 | tf_op jit(solution)/shard_map/ppermute | solution.py:342
  41.5 0.2 collective-permute-done.11
  41.8 1.6 %collective-permute-start.12 = (bf16[128,1024]{1,0:T(8,128)(2,1)S(1)}, bf16[128,1024]{1,0:T(8,128)(2,1)S(1)}, u32[]{:S(2)}, u32[]{:S(2)}) collective-permute-start(bf16[128,1024]{1,0:T(8,128)(2,1)S(1)} %add_convert_fusion.1), channel_id=1, source_target_pairs={{0,2},{1,3},{2,0},{3,1},{4,6},{5,7},{6,4},{7,5},{8,10},{9,11},{10,... | collective-permute-start | bytes 786440 | tf_op jit(solution)/shard_map/ppermute | solution.py:342
  43.3 6.9 %collective-permute-done.12 = bf16[128,1024]{1,0:T(8,128)(2,1)S(1)} collective-permute-done((bf16[128,1024]{1,0:T(8,128)(2,1)S(1)}, bf16[128,1024]{1,0:T(8,128)(2,1)S(1)}, u32[]{:S(2)}, u32[]{:S(2)}) %collective-permute-start.12) | collective-permute-done | bytes 262176 | tf_op jit(solution)/shard_map/ppermute | solution.py:342
  50.2 0.8 %add_convert_fusion = bf16[128,1024]{1,0:T(8,128)(2,1)} fusion(bf16[128,1024]{1,0:T(8,128)(2,1)S(1)} %collective-permute-done.12, bf16[128,1024]{1,0:T(8,128)(2,1)S(1)} %collective-permute-done.10, bf16[128,1024]{1,0:T(8,128)(2,1)S(1)} %get-tuple-element.45), kind=kLoop, calls=%fused_computation | loop fusion | flops 786432 | bytes 1048576 | tf_op jit(solution)/shard_map/convert_element_type | solution.py:424
  (20 shorter events, 0.3 us)
Async XLA Ops:
  0.0 29.4 %copy-start = (bf16[3,3,1024]{2,1,0:T(4,128)(2,1)S(1)}, bf16[3,3,1024]{2,1,0:T(4,128)(2,1)}, u32[]{:S(2)}) copy-start(bf16[3,3,1024]{2,1,0:T(4,128)(2,1)} %refs_9_.1) | copy-start | bytes 55300
  0.0 29.4 %copy-start.3 = (f32[1024]{0:T(1024)S(1)}, f32[1024]{0:T(1024)}, u32[]{:S(2)}) copy-start(f32[1024]{0:T(1024)} %param.10) | copy-start | bytes 12292
  1.3 11.7 %collective-permute-start = (bf16[384,256]{1,0:T(8,128)(2,1)S(1)}, bf16[384,256]{1,0:T(8,128)(2,1)S(1)}, u32[]{:S(2)}, u32[]{:S(2)}) collective-permute-start(bf16[384,256]{1,0:T(8,128)(2,1)S(1)} %get-tuple-element.27), channel_id=1, source_target_pairs={{0,12},{4,8},{8,4},{12,0},{1,13},{5,9},{9,5},{13,1},{2,14},{6,10},... | collective-permute-start | bytes 589832 | tf_op jit(solution)/shard_map/ppermute | solution.py:342
  6.4 20.8 %collective-permute-start.1 = (bf16[384,256]{1,0:T(8,128)(2,1)S(1)}, bf16[384,256]{1,0:T(8,128)(2,1)S(1)}, u32[]{:S(2)}, u32[]{:S(2)}) collective-permute-start(bf16[384,256]{1,0:T(8,128)(2,1)S(1)} %get-tuple-element.28), channel_id=1, source_target_pairs={{0,8},{4,12},{8,0},{12,4},{1,9},{5,13},{9,1},{13,5},{2,10},{6,14},... | collective-permute-start | bytes 589832 | tf_op jit(solution)/shard_map/ppermute | solution.py:342
  6.4 20.8 %collective-permute-start.2 = (bf16[384,256]{1,0:T(8,128)(2,1)S(1)}, bf16[384,256]{1,0:T(8,128)(2,1)S(1)}, u32[]{:S(2)}, u32[]{:S(2)}) collective-permute-start(bf16[384,256]{1,0:T(8,128)(2,1)S(1)} %get-tuple-element.29), channel_id=1, source_target_pairs={{0,4},{4,0},{8,12},{12,8},{1,5},{5,1},{9,13},{13,9},{2,6},{6,2},{1... | collective-permute-start | bytes 589832 | tf_op jit(solution)/shard_map/ppermute | solution.py:342
  9.2 20.3 %copy-start.1 = (bf16[144,256]{1,0:T(8,128)(2,1)S(1)}, bf16[144,256]{1,0:T(8,128)(2,1)}, u32[]{:S(2)}) copy-start(bf16[144,256]{1,0:T(8,128)(2,1)} %get-tuple-element.34.refs_7_) | copy-start | bytes 221188
  9.2 18.7 %collective-permute-start.3 = (bf16[144,256]{1,0:T(8,128)(2,1)}, bf16[144,256]{1,0:T(8,128)(2,1)S(1)}, u32[]{:S(2)}, u32[]{:S(2)}) collective-permute-start(bf16[144,256]{1,0:T(8,128)(2,1)} %get-tuple-element.31), channel_id=1, source_target_pairs={{0,12},{4,8},{8,4},{12,0},{1,13},{5,9},{9,5},{13,1},{2,14},{6,10},... | collective-permute-start | bytes 221192 | tf_op jit(solution)/shard_map/ppermute | solution.py:342
  13.0 16.4 %collective-permute-start.4 = (bf16[144,256]{1,0:T(8,128)(2,1)}, bf16[144,256]{1,0:T(8,128)(2,1)S(1)}, u32[]{:S(2)}, u32[]{:S(2)}) collective-permute-start(bf16[144,256]{1,0:T(8,128)(2,1)} %get-tuple-element.32), channel_id=1, source_target_pairs={{0,8},{4,12},{8,0},{12,4},{1,9},{5,13},{9,1},{13,5},{2,10},{6,14},... | collective-permute-start | bytes 221192 | tf_op jit(solution)/shard_map/ppermute | solution.py:342
  13.0 16.4 %collective-permute-start.5 = (bf16[144,256]{1,0:T(8,128)(2,1)}, bf16[144,256]{1,0:T(8,128)(2,1)S(1)}, u32[]{:S(2)}, u32[]{:S(2)}) collective-permute-start(bf16[144,256]{1,0:T(8,128)(2,1)} %get-tuple-element.33), channel_id=1, source_target_pairs={{0,4},{4,0},{8,12},{12,8},{1,5},{5,1},{9,13},{13,9},{2,6},{6,2},{1... | collective-permute-start | bytes 221192 | tf_op jit(solution)/shard_map/ppermute | solution.py:342
  21.2 0.7 %copy-start.2 = (bf16[64,128]{1,0:T(8,128)(2,1)S(1)}, bf16[64,128]{1,0:T(8,128)(2,1)}, u32[]{:S(2)}) copy-start(bf16[64,128]{1,0:T(8,128)(2,1)} %filter_ref.1) | copy-start | bytes 49156
  30.6 8.7 %collective-permute-start.6 = (bf16[128,256]{1,0:T(8,128)(2,1)S(1)}, bf16[128,256]{1,0:T(8,128)(2,1)S(1)}, u32[]{:S(2)}, u32[]{:S(2)}) collective-permute-start(bf16[128,256]{1,0:T(8,128)(2,1)S(1)} %get-tuple-element.38), channel_id=1, source_target_pairs={{0,12},{4,8},{8,4},{12,0},{1,13},{5,9},{9,5},{13,1},{2,14},{6,10},... | collective-permute-start | bytes 196616 | tf_op jit(solution)/shard_map/ppermute | solution.py:342
  33.2 6.2 %collective-permute-start.7 = (bf16[128,256]{1,0:T(8,128)(2,1)S(1)}, bf16[128,256]{1,0:T(8,128)(2,1)S(1)}, u32[]{:S(2)}, u32[]{:S(2)}) collective-permute-start(bf16[128,256]{1,0:T(8,128)(2,1)S(1)} %get-tuple-element.39), channel_id=1, source_target_pairs={{0,8},{4,12},{8,0},{12,4},{1,9},{5,13},{9,1},{13,5},{2,10},{6,14},... | collective-permute-start | bytes 196616 | tf_op jit(solution)/shard_map/ppermute | solution.py:342
  33.5 4.3 %collective-permute-start.8 = (bf16[64,256]{1,0:T(8,128)(2,1)S(1)}, bf16[64,256]{1,0:T(8,128)(2,1)S(1)}, u32[]{:S(2)}, u32[]{:S(2)}) collective-permute-start(bf16[64,256]{1,0:T(8,128)(2,1)S(1)} %get-tuple-element.41), channel_id=1, source_target_pairs={{0,4},{4,0},{8,12},{12,8},{1,5},{5,1},{9,13},{13,9},{2,6},{6,2},{1... | collective-permute-start | bytes 98312 | tf_op jit(solution)/shard_map/ppermute | solution.py:342
  35.4 3.9 %collective-permute-start.9 = (bf16[64,256]{1,0:T(8,128)(2,1)S(1)}, bf16[64,256]{1,0:T(8,128)(2,1)S(1)}, u32[]{:S(2)}, u32[]{:S(2)}) collective-permute-start(bf16[64,256]{1,0:T(8,128)(2,1)S(1)} %get-tuple-element.42), channel_id=1, source_target_pairs={{0,4},{4,0},{8,12},{12,8},{1,5},{5,1},{9,13},{13,9},{2,6},{6,2},{1... | collective-permute-start | bytes 98312 | tf_op jit(solution)/shard_map/ppermute | solution.py:342
  40.1 1.6 %collective-permute-start.11 = (bf16[128,1024]{1,0:T(8,128)(2,1)S(1)}, bf16[128,1024]{1,0:T(8,128)(2,1)S(1)}, u32[]{:S(2)}, u32[]{:S(2)}) collective-permute-start(bf16[128,1024]{1,0:T(8,128)(2,1)S(1)} %get-tuple-element.48), channel_id=1, source_target_pairs={{0,1},{1,0},{2,3},{3,2},{4,5},{5,4},{6,7},{7,6},{8,9},{9,8},{10,11... | collective-permute-start | bytes 786440 | tf_op jit(solution)/shard_map/ppermute | solution.py:342
  40.9 2.4 %collective-permute-start.10 = (bf16[128,1024]{1,0:T(8,128)(2,1)S(1)}, bf16[128,1024]{1,0:T(8,128)(2,1)S(1)}, u32[]{:S(2)}, u32[]{:S(2)}) collective-permute-start(bf16[128,1024]{1,0:T(8,128)(2,1)S(1)} %get-tuple-element.46), channel_id=1, source_target_pairs={{0,1},{1,0},{2,3},{3,2},{4,5},{5,4},{6,7},{7,6},{8,9},{9,8},{10,11... | collective-permute-start | bytes 786440 | tf_op jit(solution)/shard_map/ppermute | solution.py:342
  41.8 8.4 %collective-permute-start.12 = (bf16[128,1024]{1,0:T(8,128)(2,1)S(1)}, bf16[128,1024]{1,0:T(8,128)(2,1)S(1)}, u32[]{:S(2)}, u32[]{:S(2)}) collective-permute-start(bf16[128,1024]{1,0:T(8,128)(2,1)S(1)} %add_convert_fusion.1), channel_id=1, source_target_pairs={{0,2},{1,3},{2,0},{3,1},{4,6},{5,7},{6,4},{7,5},{8,10},{9,11},{10,... | collective-permute-start | bytes 786440 | tf_op jit(solution)/shard_map/ppermute | solution.py:342

commit v8 on v7

--- a/solution.py
+++ b/solution.py
@@ -301,11 +301,11 @@
 
 def project_kernel(masks, *refs):
     given, weight_ref = refs[:5], refs[5]
-    out_refs, attended_s = refs[6:-1], refs[-1]
+    out_refs, attended_s = refs[-1 - len(masks) : -1], refs[-1]
     own = given[0].shape[1]
     width = out_refs[0].shape[1]
     position, here = lax.axis_index("ctx"), lax.axis_index("mp")
-    third, second, upper, lower, mine = given
+    second, third, upper, lower, mine = given
     half = upper.shape[0]
     attended_s[0:half, columns_of(position ^ 1, own)] = upper[...]
     attended_s[half:, columns_of(position ^ 1, own)] = lower[...]
@@ -323,6 +323,7 @@
 GATE_LIMIT = 60 * 1024 * 1024
 IN_HBM = pl.BlockSpec(memory_space=pltpu.HBM)
 IN_VMEM = pl.BlockSpec(memory_space=pltpu.VMEM)
+ANYWHERE = pl.BlockSpec(memory_space=pl.ANY)
 
 
 def run_kernel(kernel, operands, outputs, scratch=(), spaces=None, limit=VMEM_LIMIT, cost=10**6):
@@ -402,17 +403,18 @@
         [pltpu.VMEM((rows, own), half)],
     )
     near = (swapped(upper, "ctx", 1), swapped(lower, "ctx", 1))
-    return project_and_share((third_got, second_got, *near, mine), weight)
-
-
-def projected(attended, out_weight, masks):
+    return project_and_share((second_got, third_got, *near, mine), weight)
+
+
+def projected(attended, out_weight, masks, after=()):
     rows = attended[0].shape[0]
     width = out_weight.shape[1] // lax.axis_size("mp")
     return run_kernel(
         functools.partial(project_kernel, masks),
-        (*attended, out_weight),
+        (*attended, out_weight, *after),
         [((rows, width), jnp.bfloat16)] * len(masks),
         [pltpu.VMEM((rows, out_weight.shape[0]), jnp.bfloat16)],
+        [IN_VMEM] * (len(attended) + 1) + [ANYWHERE] * len(after),
         cost=2 * rows * out_weight.shape[0] * width * len(masks),
     )
 
@@ -425,11 +427,13 @@
 
 
 def project_and_share(attended, out_weight):
-    far_given, far_kept = projected(attended, out_weight, (3, 2))
+    (far_given,) = projected(attended, out_weight, (3,))
     far_got = swapped(far_given, "mp", 1)
-    near_given, near_kept = projected(attended, out_weight, (1, 0))
+    (far_kept,) = projected(attended, out_weight, (2,))
     far_sum = added(far_kept, far_got)
-    near_got = swapped(near_given, "mp", 1)
+    near_given, near_kept = projected(attended, out_weight, (1, 0), (far_sum,))
+    half = near_given.shape[0] // 2
+    near_got = jnp.concatenate([swapped(near_given[:half], "mp", 1), swapped(near_given[half:], "mp", 1)])
     return added(near_kept, near_got, swapped(far_sum, "mp", 2))
 
 

time: 51.3 us -> 50.1 us (0.977)
  waiting for transfers between devices: 14.2 us -> 12.7 us
    ppermute x13 -> x14, waiting for transfers between devices: 14.2 us -> 12.7 us  [swapped(): lax.ppermute(value, axis, [(source, source ^ step) for source in range(la...]
    pallas_call x8 -> x9, Pallas kernels: 10.4 us -> 10.6 us  [run_kernel(): pl.pallas_call(kernel, out_shape=[jax.ShapeDtypeStruct(shape, dtype) for...]
    ppermute x13 -> x14, starting transfers between devices: 24.6 us -> 24.7 us  [swapped(): lax.ppermute(value, axis, [(source, source ^ step) for source in range(la...]
  transfers between devices with their start and end apart: 13 -> 14, of which waited for: 6 -> 8; matrix products, arithmetic and copies ran while one was open for 0% -> 0% of each run, Pallas kernels for 14% -> 15%
where the time goes in v8:
time: 50.1 us; the launch traced here: 49.8 us
  starting transfers between devices  24.7 us (49%)
  waiting for transfers between devices  12.7 us (25%)
  Pallas kernels  10.6 us (21%)
  other arithmetic  0.89 us (2%)
  local copies, waits for them, and re-layouts  0.75 us (1%)
    ppermute x14, starting transfers between devices, swapped(): lax.ppermute(value, axis, [(source, source ^ step) for source in range(la...  24.7 us
    ppermute x14, waiting for transfers between devices, swapped(): lax.ppermute(value, axis, [(source, source ^ step) for source in range(la...  12.7 us
    pallas_call x9, Pallas kernels, run_kernel(): pl.pallas_call(kernel, out_shape=[jax.ShapeDtypeStruct(shape, dtype) for...  10.6 us
  transfers between devices with their start and end apart: 14, of which 8 were waited for; matrix products, arithmetic and copies ran while one was open for 0% of the time, Pallas kernels for 15%

profile of v8, /device:TPU:0, one launch (start us, length us, event | category | flops | bytes accessed | tf_op | source)
XLA Modules:
  0.0 49.8 jit_solution(15506748959667889959)
XLA Ops:
  0.0 1.3 %plain_kernel.1 = (bf16[384,256]{1,0:T(8,128)(2,1)S(1)}, bf16[384,256]{1,0:T(8,128)(2,1)S(1)}, bf16[384,256]{1,0:T(8,128)(2,1)S(1)}, bf16[384,256]{1,0:T(8,128)(2,1)S(1)}) custom-call(bf16[3,128,1024]{2,1,0:T(8,128)(2,1)} %bitcast.3, bf16[128,1024]{1,0:T(8,128)(2,1)} %queries_any.1, bf16[128,1024]{1,0:T(8,128)(2,1)} %keys_any.1), custom_call_target="tpu_custom_call" | custom-call | flops 1000000 | bytes 1048576 | tf_op jit(solution)/shard_map/plain_kernel/pallas_call | solution.py:330
  1.3 5.1 %collective-permute-start = (bf16[384,256]{1,0:T(8,128)(2,1)S(1)}, bf16[384,256]{1,0:T(8,128)(2,1)S(1)}, u32[]{:S(2)}, u32[]{:S(2)}) collective-permute-start(bf16[384,256]{1,0:T(8,128)(2,1)S(1)} %get-tuple-element.25), channel_id=1, source_target_pairs={{0,12},{4,8},{8,4},{12,0},{1,13},{5,9},{9,5},{13,1},{2,14},{6,10},... | collective-permute-start | bytes 589832 | tf_op jit(solution)/shard_map/ppermute | solution.py:343
  6.4 0.6 %collective-permute-start.2 = (bf16[384,256]{1,0:T(8,128)(2,1)S(1)}, bf16[384,256]{1,0:T(8,128)(2,1)S(1)}, u32[]{:S(2)}, u32[]{:S(2)}) collective-permute-start(bf16[384,256]{1,0:T(8,128)(2,1)S(1)} %get-tuple-element.27), channel_id=1, source_target_pairs={{0,4},{4,0},{8,12},{12,8},{1,5},{5,1},{9,13},{13,9},{2,6},{6,2},{1... | collective-permute-start | bytes 589832 | tf_op jit(solution)/shard_map/ppermute | solution.py:343
  7.0 2.1 %gate_kernel.1 = (bf16[144,256]{1,0:T(8,128)(2,1)}, bf16[144,256]{1,0:T(8,128)(2,1)}, bf16[144,256]{1,0:T(8,128)(2,1)}, bf16[144,256]{1,0:T(8,128)(2,1)}) custom-call(bf16[3,128,1024]{2,1,0:T(8,128)(2,1)} %bitcast.4, bf16[3,3,1024]{2,1,0:T(4,128)(2,1)} %refs_9_.1), custom_call_target="tpu_custom_call" | custom-call | flops 1000000 | bytes 1048576 | tf_op jit(solution)/shard_map/gate_kernel/pallas_call | solution.py:330
  9.2 3.8 %collective-permute-start.3 = (bf16[144,256]{1,0:T(8,128)(2,1)}, bf16[144,256]{1,0:T(8,128)(2,1)S(1)}, u32[]{:S(2)}, u32[]{:S(2)}) collective-permute-start(bf16[144,256]{1,0:T(8,128)(2,1)} %get-tuple-element.29), channel_id=1, source_target_pairs={{0,12},{4,8},{8,4},{12,0},{1,13},{5,9},{9,5},{13,1},{2,14},{6,10},... | collective-permute-start | bytes 221192 | tf_op jit(solution)/shard_map/ppermute | solution.py:343
  13.0 8.3 %collective-permute-start.5 = (bf16[144,256]{1,0:T(8,128)(2,1)}, bf16[144,256]{1,0:T(8,128)(2,1)S(1)}, u32[]{:S(2)}, u32[]{:S(2)}) collective-permute-start(bf16[144,256]{1,0:T(8,128)(2,1)} %get-tuple-element.31), channel_id=1, source_target_pairs={{0,4},{4,0},{8,12},{12,8},{1,5},{5,1},{9,13},{13,9},{2,6},{6,2},{1... | collective-permute-start | bytes 221192 | tf_op jit(solution)/shard_map/ppermute | solution.py:343
  21.2 0.7 %copy-done.2 = bf16[64,128]{1,0:T(8,128)(2,1)S(1)} copy-done((bf16[64,128]{1,0:T(8,128)(2,1)S(1)}, bf16[64,128]{1,0:T(8,128)(2,1)}, u32[]{:S(2)}) %copy-start.2) | copy-done | bytes 16408
  22.0 3.4 %ready_kernel.1 = (bf16[2048,256]{1,0:T(8,128)(2,1)S(1)}, bf16[1024,4096]{1,0:T(8,128)(2,1)S(1)}) custom-call(bf16[64,128]{1,0:T(8,128)(2,1)S(1)} %copy-done.2, bf16[1024,4096]{1,0:T(8,128)(2,1)} %weight_any.1), custom_call_target="tpu_custom_call" | custom-call | flops 1000000 | bytes 1048576 | tf_op jit(solution)/shard_map/ready_kernel/pallas_call | solution.py:330
  25.4 1.8 %collective-permute-done.1.second_ref.refs_1_ = bf16[384,256]{1,0:T(8,128)(2,1)S(1)} collective-permute-done((bf16[384,256]{1,0:T(8,128)(2,1)S(1)}, bf16[384,256]{1,0:T(8,128)(2,1)S(1)}, u32[]{:S(2)}, u32[]{:S(2)}) %collective-permute-start.1) | collective-permute-done | bytes 196640 | tf_op jit(solution)/shard_map/ppermute | solution.py:343
  27.2 0.7 %weights_kernel.1 = (bf16[2,512,512]{2,1,0:T(8,128)(2,1)S(1)}, f32[512,128]{1,0:T(8,128)S(1)}) custom-call(bf16[384,256]{1,0:T(8,128)(2,1)S(1)} %collective-permute-done.third_ref.refs_0_, bf16[384,256]{1,0:T(8,128)(2,1)S(1)} %collective-permute-done.1.second_ref.refs_1_, bf16[384,256]{1,0:T(8,128)(2,1)S(1)} %collective-permute-done.2.near_ref.refs_2_, ...), custom_call_target="tpu_custom_call" | custom-call | flops 1000000 | bytes 1048576 | tf_op jit(solution)/shard_map/weights_kernel/pallas_call | solution.py:330
  27.9 1.5 %collective-permute-done.4.refs_5_ = bf16[144,256]{1,0:T(8,128)(2,1)S(1)} collective-permute-done((bf16[144,256]{1,0:T(8,128)(2,1)}, bf16[144,256]{1,0:T(8,128)(2,1)S(1)}, u32[]{:S(2)}, u32[]{:S(2)}) %collective-permute-start.4) | collective-permute-done | bytes 73760 | tf_op jit(solution)/shard_map/ppermute | solution.py:343
  29.4 1.2 %values_kernel.1 = (bf16[128,256]{1,0:T(8,128)(2,1)S(1)}, bf16[128,256]{1,0:T(8,128)(2,1)S(1)}, bf16[512,256]{1,0:T(8,128)(2,1)S(1)}) custom-call(bf16[384,256]{1,0:T(8,128)(2,1)S(1)} %collective-permute-done.third_ref.refs_0_, bf16[384,256]{1,0:T(8,128)(2,1)S(1)} %collective-permute-done.1.second_ref.refs_1_, ...), custom_call_target="tpu_custom_call" | custom-call | flops 1000000 | bytes 1048576 | tf_op jit(solution)/shard_map/values_kernel/pallas_call | solution.py:330
  30.6 0.9 %collective-permute-start.6 = (bf16[128,256]{1,0:T(8,128)(2,1)S(1)}, bf16[128,256]{1,0:T(8,128)(2,1)S(1)}, u32[]{:S(2)}, u32[]{:S(2)}) collective-permute-start(bf16[128,256]{1,0:T(8,128)(2,1)S(1)} %get-tuple-element.36), channel_id=1, source_target_pairs={{0,8},{4,12},{8,0},{12,4},{1,9},{5,13},{9,1},{13,5},{2,10},{6,14},... | collective-permute-start | bytes 196616 | tf_op jit(solution)/shard_map/ppermute | solution.py:343
  31.5 1.8 %collective-permute-start.7 = (bf16[128,256]{1,0:T(8,128)(2,1)S(1)}, bf16[128,256]{1,0:T(8,128)(2,1)S(1)}, u32[]{:S(2)}, u32[]{:S(2)}) collective-permute-start(bf16[128,256]{1,0:T(8,128)(2,1)S(1)} %get-tuple-element.37), channel_id=1, source_target_pairs={{0,12},{4,8},{8,4},{12,0},{1,13},{5,9},{9,5},{13,1},{2,14},{6,10},... | collective-permute-start | bytes 196616 | tf_op jit(solution)/shard_map/ppermute | solution.py:343
  33.5 1.0 %collective-permute-start.8 = (bf16[64,256]{1,0:T(8,128)(2,1)S(1)}, bf16[64,256]{1,0:T(8,128)(2,1)S(1)}, u32[]{:S(2)}, u32[]{:S(2)}) collective-permute-start(bf16[64,256]{1,0:T(8,128)(2,1)S(1)} %get-tuple-element.39), channel_id=1, source_target_pairs={{0,4},{4,0},{8,12},{12,8},{1,5},{5,1},{9,13},{13,9},{2,6},{6,2},{1... | collective-permute-start | bytes 98312 | tf_op jit(solution)/shard_map/ppermute | solution.py:343
  34.5 1.1 %collective-permute-start.9 = (bf16[64,256]{1,0:T(8,128)(2,1)S(1)}, bf16[64,256]{1,0:T(8,128)(2,1)S(1)}, u32[]{:S(2)}, u32[]{:S(2)}) collective-permute-start(bf16[64,256]{1,0:T(8,128)(2,1)S(1)} %get-tuple-element.40), channel_id=1, source_target_pairs={{0,4},{4,0},{8,12},{12,8},{1,5},{5,1},{9,13},{13,9},{2,6},{6,2},{1... | collective-permute-start | bytes 98312 | tf_op jit(solution)/shard_map/ppermute | solution.py:343
  35.6 2.4 %collective-permute-done.8.refs_2_ = bf16[64,256]{1,0:T(8,128)(2,1)S(1)} collective-permute-done((bf16[64,256]{1,0:T(8,128)(2,1)S(1)}, bf16[64,256]{1,0:T(8,128)(2,1)S(1)}, u32[]{:S(2)}, u32[]{:S(2)}) %collective-permute-start.8) | collective-permute-done | bytes 32800 | tf_op jit(solution)/shard_map/ppermute | solution.py:343
  39.5 1.0 %collective-permute-done.10 = bf16[128,1024]{1,0:T(8,128)(2,1)S(1)} collective-permute-done((bf16[128,1024]{1,0:T(8,128)(2,1)S(1)}, bf16[128,1024]{1,0:T(8,128)(2,1)S(1)}, u32[]{:S(2)}, u32[]{:S(2)}) %collective-permute-start.10) | collective-permute-done | bytes 262176 | tf_op jit(solution)/shard_map/ppermute | solution.py:343
  40.6 1.6 %collective-permute-start.13 = (bf16[128,1024]{1,0:T(8,128)(2,1)S(1)}, bf16[128,1024]{1,0:T(8,128)(2,1)S(1)}, u32[]{:S(2)}, u32[]{:S(2)}) collective-permute-start(bf16[128,1024]{1,0:T(8,128)(2,1)S(1)} %add_convert_fusion.1.refs_6_), channel_id=1, source_target_pairs={{0,2},{1,3},{2,0},{3,1},{4,6},{5,7},{6,4},{7,5},{8,10},{9,11},{10,... | collective-permute-start | bytes 786440 | tf_op jit(solution)/shard_map/ppermute | solution.py:343
  42.2 0.7 %project_kernel.5 = (bf16[128,1024]{1,0:T(8,128)(2,1)S(1)}, bf16[128,1024]{1,0:T(8,128)(2,1)S(1)}) custom-call(bf16[128,256]{1,0:T(8,128)(2,1)S(1)} %collective-permute-done.6.refs_0_, bf16[128,256]{1,0:T(8,128)(2,1)S(1)} %collective-permute-done.7.refs_1_, bf16[64,256]{1,0:T(8,128)(2,1)S(1)} %collective-permute-done.8.refs_2_, ...), custom_call_target="tpu_custom_call" | custom-call | flops 536870912 | bytes 1048576 | tf_op jit(solution)/shard_map/project_kernel/pallas_call | solution.py:330
  43.0 0.5 collective-permute-start.12
  43.5 0.8 %collective-permute-done.11 = bf16[64,1024]{1,0:T(8,128)(2,1)S(1)} collective-permute-done((bf16[64,1024]{1,0:T(8,128)(2,1)S(1)}, bf16[64,1024]{1,0:T(8,128)(2,1)S(1)}, u32[]{:S(2)}, u32[]{:S(2)}) %collective-permute-start.11) | collective-permute-done | bytes 131104 | tf_op jit(solution)/shard_map/ppermute | solution.py:343
  44.5 4.5 %collective-permute-done.13 = bf16[128,1024]{1,0:T(8,128)(2,1)S(1)} collective-permute-done((bf16[128,1024]{1,0:T(8,128)(2,1)S(1)}, bf16[128,1024]{1,0:T(8,128)(2,1)S(1)}, u32[]{:S(2)}, u32[]{:S(2)}) %collective-permute-start.13) | collective-permute-done | bytes 262176 | tf_op jit(solution)/shard_map/ppermute | solution.py:343
  49.0 0.8 %add_convert_fusion = bf16[128,1024]{1,0:T(8,128)(2,1)} fusion(bf16[128,1024]{1,0:T(8,128)(2,1)S(1)} %collective-permute-done.13, bf16[128,1024]{1,0:T(8,128)(2,1)S(1)} %get-tuple-element.43, bf16[64,1024]{1,0:T(8,128)(2,1)S(1)} %collective-permute-done.12, bf16[64,1024]{1,0:T(8,128)(2,1)S(1)} %collective-permute-done.11), kind=kLoop, calls=%fused_computation | loop fusion | flops 1179648 | bytes 1048576 | tf_op jit(solution)/shard_map/convert_element_type | solution.py:426
  (24 shorter events, 2.2 us)
Async XLA Ops:
  0.0 29.4 %copy-start = (bf16[3,3,1024]{2,1,0:T(4,128)(2,1)S(1)}, bf16[3,3,1024]{2,1,0:T(4,128)(2,1)}, u32[]{:S(2)}) copy-start(bf16[3,3,1024]{2,1,0:T(4,128)(2,1)} %refs_9_.1) | copy-start | bytes 55300
  0.0 29.4 %copy-start.3 = (f32[1024]{0:T(1024)S(1)}, f32[1024]{0:T(1024)}, u32[]{:S(2)}) copy-start(f32[1024]{0:T(1024)} %param.10) | copy-start | bytes 12292
  1.3 11.7 %collective-permute-start = (bf16[384,256]{1,0:T(8,128)(2,1)S(1)}, bf16[384,256]{1,0:T(8,128)(2,1)S(1)}, u32[]{:S(2)}, u32[]{:S(2)}) collective-permute-start(bf16[384,256]{1,0:T(8,128)(2,1)S(1)} %get-tuple-element.25), channel_id=1, source_target_pairs={{0,12},{4,8},{8,4},{12,0},{1,13},{5,9},{9,5},{13,1},{2,14},{6,10},... | collective-permute-start | bytes 589832 | tf_op jit(solution)/shard_map/ppermute | solution.py:343
  6.4 20.8 %collective-permute-start.1 = (bf16[384,256]{1,0:T(8,128)(2,1)S(1)}, bf16[384,256]{1,0:T(8,128)(2,1)S(1)}, u32[]{:S(2)}, u32[]{:S(2)}) collective-permute-start(bf16[384,256]{1,0:T(8,128)(2,1)S(1)} %get-tuple-element.26), channel_id=1, source_target_pairs={{0,8},{4,12},{8,0},{12,4},{1,9},{5,13},{9,1},{13,5},{2,10},{6,14},... | collective-permute-start | bytes 589832 | tf_op jit(solution)/shard_map/ppermute | solution.py:343
  6.4 20.8 %collective-permute-start.2 = (bf16[384,256]{1,0:T(8,128)(2,1)S(1)}, bf16[384,256]{1,0:T(8,128)(2,1)S(1)}, u32[]{:S(2)}, u32[]{:S(2)}) collective-permute-start(bf16[384,256]{1,0:T(8,128)(2,1)S(1)} %get-tuple-element.27), channel_id=1, source_target_pairs={{0,4},{4,0},{8,12},{12,8},{1,5},{5,1},{9,13},{13,9},{2,6},{6,2},{1... | collective-permute-start | bytes 589832 | tf_op jit(solution)/shard_map/ppermute | solution.py:343
  9.2 20.3 %copy-start.1 = (bf16[144,256]{1,0:T(8,128)(2,1)S(1)}, bf16[144,256]{1,0:T(8,128)(2,1)}, u32[]{:S(2)}) copy-start(bf16[144,256]{1,0:T(8,128)(2,1)} %get-tuple-element.32.refs_7_) | copy-start | bytes 221188
  9.2 18.7 %collective-permute-start.3 = (bf16[144,256]{1,0:T(8,128)(2,1)}, bf16[144,256]{1,0:T(8,128)(2,1)S(1)}, u32[]{:S(2)}, u32[]{:S(2)}) collective-permute-start(bf16[144,256]{1,0:T(8,128)(2,1)} %get-tuple-element.29), channel_id=1, source_target_pairs={{0,12},{4,8},{8,4},{12,0},{1,13},{5,9},{9,5},{13,1},{2,14},{6,10},... | collective-permute-start | bytes 221192 | tf_op jit(solution)/shard_map/ppermute | solution.py:343
  13.0 16.4 %collective-permute-start.4 = (bf16[144,256]{1,0:T(8,128)(2,1)}, bf16[144,256]{1,0:T(8,128)(2,1)S(1)}, u32[]{:S(2)}, u32[]{:S(2)}) collective-permute-start(bf16[144,256]{1,0:T(8,128)(2,1)} %get-tuple-element.30), channel_id=1, source_target_pairs={{0,8},{4,12},{8,0},{12,4},{1,9},{5,13},{9,1},{13,5},{2,10},{6,14},... | collective-permute-start | bytes 221192 | tf_op jit(solution)/shard_map/ppermute | solution.py:343
  13.0 16.4 %collective-permute-start.5 = (bf16[144,256]{1,0:T(8,128)(2,1)}, bf16[144,256]{1,0:T(8,128)(2,1)S(1)}, u32[]{:S(2)}, u32[]{:S(2)}) collective-permute-start(bf16[144,256]{1,0:T(8,128)(2,1)} %get-tuple-element.31), channel_id=1, source_target_pairs={{0,4},{4,0},{8,12},{12,8},{1,5},{5,1},{9,13},{13,9},{2,6},{6,2},{1... | collective-permute-start | bytes 221192 | tf_op jit(solution)/shard_map/ppermute | solution.py:343
  21.2 0.7 %copy-start.2 = (bf16[64,128]{1,0:T(8,128)(2,1)S(1)}, bf16[64,128]{1,0:T(8,128)(2,1)}, u32[]{:S(2)}) copy-start(bf16[64,128]{1,0:T(8,128)(2,1)} %filter_ref.1) | copy-start | bytes 49156
  30.6 7.8 %collective-permute-start.6 = (bf16[128,256]{1,0:T(8,128)(2,1)S(1)}, bf16[128,256]{1,0:T(8,128)(2,1)S(1)}, u32[]{:S(2)}, u32[]{:S(2)}) collective-permute-start(bf16[128,256]{1,0:T(8,128)(2,1)S(1)} %get-tuple-element.36), channel_id=1, source_target_pairs={{0,8},{4,12},{8,0},{12,4},{1,9},{5,13},{9,1},{13,5},{2,10},{6,14},... | collective-permute-start | bytes 196616 | tf_op jit(solution)/shard_map/ppermute | solution.py:343
  31.5 7.0 %collective-permute-start.7 = (bf16[128,256]{1,0:T(8,128)(2,1)S(1)}, bf16[128,256]{1,0:T(8,128)(2,1)S(1)}, u32[]{:S(2)}, u32[]{:S(2)}) collective-permute-start(bf16[128,256]{1,0:T(8,128)(2,1)S(1)} %get-tuple-element.37), channel_id=1, source_target_pairs={{0,12},{4,8},{8,4},{12,0},{1,13},{5,9},{9,5},{13,1},{2,14},{6,10},... | collective-permute-start | bytes 196616 | tf_op jit(solution)/shard_map/ppermute | solution.py:343
  33.5 4.5 %collective-permute-start.8 = (bf16[64,256]{1,0:T(8,128)(2,1)S(1)}, bf16[64,256]{1,0:T(8,128)(2,1)S(1)}, u32[]{:S(2)}, u32[]{:S(2)}) collective-permute-start(bf16[64,256]{1,0:T(8,128)(2,1)S(1)} %get-tuple-element.39), channel_id=1, source_target_pairs={{0,4},{4,0},{8,12},{12,8},{1,5},{5,1},{9,13},{13,9},{2,6},{6,2},{1... | collective-permute-start | bytes 98312 | tf_op jit(solution)/shard_map/ppermute | solution.py:343
  34.5 3.9 %collective-permute-start.9 = (bf16[64,256]{1,0:T(8,128)(2,1)S(1)}, bf16[64,256]{1,0:T(8,128)(2,1)S(1)}, u32[]{:S(2)}, u32[]{:S(2)}) collective-permute-start(bf16[64,256]{1,0:T(8,128)(2,1)S(1)} %get-tuple-element.40), channel_id=1, source_target_pairs={{0,4},{4,0},{8,12},{12,8},{1,5},{5,1},{9,13},{13,9},{2,6},{6,2},{1... | collective-permute-start | bytes 98312 | tf_op jit(solution)/shard_map/ppermute | solution.py:343
  38.9 1.6 %collective-permute-start.10 = (bf16[128,1024]{1,0:T(8,128)(2,1)S(1)}, bf16[128,1024]{1,0:T(8,128)(2,1)S(1)}, u32[]{:S(2)}, u32[]{:S(2)}) collective-permute-start(bf16[128,1024]{1,0:T(8,128)(2,1)S(1)} %project_kernel.4), channel_id=1, source_target_pairs={{0,1},{1,0},{2,3},{3,2},{4,5},{5,4},{6,7},{7,6},{8,9},{9,8},{10,11... | collective-permute-start | bytes 786440 | tf_op jit(solution)/shard_map/ppermute | solution.py:343
  40.6 8.4 %collective-permute-start.13 = (bf16[128,1024]{1,0:T(8,128)(2,1)S(1)}, bf16[128,1024]{1,0:T(8,128)(2,1)S(1)}, u32[]{:S(2)}, u32[]{:S(2)}) collective-permute-start(bf16[128,1024]{1,0:T(8,128)(2,1)S(1)} %add_convert_fusion.1.refs_6_), channel_id=1, source_target_pairs={{0,2},{1,3},{2,0},{3,1},{4,6},{5,7},{6,4},{7,5},{8,10},{9,11},{10,... | collective-permute-start | bytes 786440 | tf_op jit(solution)/shard_map/ppermute | solution.py:343
  42.9 1.4 %collective-permute-start.11 = (bf16[64,1024]{1,0:T(8,128)(2,1)S(1)}, bf16[64,1024]{1,0:T(8,128)(2,1)S(1)}, u32[]{:S(2)}, u32[]{:S(2)}) collective-permute-start(bf16[64,1024]{1,0:T(8,128)(2,1)S(1)} %get-tuple-element.45), channel_id=1, source_target_pairs={{0,1},{1,0},{2,3},{3,2},{4,5},{5,4},{6,7},{7,6},{8,9},{9,8},{10,11... | collective-permute-start | bytes 393224 | tf_op jit(solution)/shard_map/ppermute | solution.py:343
  43.0 1.5 %collective-permute-start.12 = (bf16[64,1024]{1,0:T(8,128)(2,1)S(1)}, bf16[64,1024]{1,0:T(8,128)(2,1)S(1)}, u32[]{:S(2)}, u32[]{:S(2)}) collective-permute-start(bf16[64,1024]{1,0:T(8,128)(2,1)S(1)} %get-tuple-element.46), channel_id=1, source_target_pairs={{0,1},{1,0},{2,3},{3,2},{4,5},{5,4},{6,7},{7,6},{8,9},{9,8},{10,11... | collective-permute-start | bytes 393224 | tf_op jit(solution)/shard_map/ppermute | solution.py:343

commit v9 on v8

--- a/solution.py
+++ b/solution.py
@@ -10,6 +10,7 @@
 HEAD_DIM = 128
 COUNT = 4
 ORDER = (3, 2, 1, 0)
+BACK = (2, 3, 1, 0)
 EDGE = 16
 
 
@@ -215,22 +216,27 @@
                 weight_ref[head, here, seen:] = jnp.zeros((rows, count * rows - seen), jnp.bfloat16)
 
 
-def mix_rows(block, weight_ref, total_ref, value_ref, out_ref):
-    rows = out_ref.shape[0]
+def mix_rows(block, weight_ref, total_ref, value_ref, out_refs):
+    rows = sum(out_ref.shape[0] for out_ref in out_refs)
+    own = value_ref.shape[1]
     here = columns_of(block, rows)
-    for head in range(out_ref.shape[1] // HEAD_DIM):
+    for head in range(own // HEAD_DIM):
         columns = slice(head * HEAD_DIM, (head + 1) * HEAD_DIM)
         mixed = jnp.dot(weight_ref[head, here], value_ref[:, columns], preferred_element_type=jnp.float32)
-        out_ref[:, columns] = (mixed / total_ref[here, head : head + 1]).astype(jnp.bfloat16)
+        mixed = (mixed / total_ref[here, head : head + 1]).astype(jnp.bfloat16)
+        start = 0
+        for out_ref in out_refs:
+            out_ref[:, columns] = mixed[start : start + out_ref.shape[0]]
+            start += out_ref.shape[0]
 
 
 def values_kernel(*refs):
     count = COUNT
     plain, gates = refs[:count], refs[count : 2 * count]
     band_ref, short_ref, gain_ref, weight_ref, total_ref = refs[2 * count : 2 * count + 5]
-    third_ref, second_ref, value_ref = refs[2 * count + 5 : 2 * count + 8]
-    signal_s, gates_s, gate_s = refs[2 * count + 8 :]
-    rows, own = second_ref.shape
+    third_refs, second_refs = refs[2 * count + 5 : 2 * count + 7], refs[2 * count + 7 : 2 * count + 9]
+    value_ref, signal_s, gates_s, gate_s = refs[2 * count + 9 :]
+    rows, own = plain[0].shape[0] // 3, plain[0].shape[1]
     per_group = own * rows // band_ref.shape[0]
     position = lax.axis_index("ctx")
     mine = columns_of(position, own)
@@ -285,36 +291,32 @@
                 value_ref[here, columns] = (
                     feature[here, columns] * (part + gain[:, columns] * gate)
                 ).astype(jnp.bfloat16)
-    for step, out_ref in ((3, third_ref), (2, second_ref)):
-        mix_rows(position ^ step, weight_ref, total_ref, value_ref, out_ref)
+    for step, out_refs in ((3, third_refs), (2, second_refs)):
+        mix_rows(position ^ step, weight_ref, total_ref, value_ref, out_refs)
 
 
 def near_rows_kernel(weight_ref, total_ref, value_ref, *refs):
-    upper_ref, lower_ref, own_ref, near_s = refs
-    half = upper_ref.shape[0]
-    position = lax.axis_index("ctx")
-    mix_rows(position ^ 1, weight_ref, total_ref, value_ref, near_s)
-    upper_ref[...] = near_s[0:half]
-    lower_ref[...] = near_s[half:]
-    mix_rows(position, weight_ref, total_ref, value_ref, own_ref)
+    position = lax.axis_index("ctx")
+    mix_rows(position ^ 1, weight_ref, total_ref, value_ref, refs[0:2])
+    mix_rows(position, weight_ref, total_ref, value_ref, refs[2:4])
 
 
 def project_kernel(masks, *refs):
-    given, weight_ref = refs[:5], refs[5]
-    out_refs, attended_s = refs[-1 - len(masks) : -1], refs[-1]
-    own = given[0].shape[1]
+    outs = len(masks)
+    out_refs, attended_s = refs[-outs - 1 : -1], refs[-1]
+    own = refs[0].shape[1]
+    count = sum(ref.shape[1] == own for ref in refs)
+    given, weight_ref = refs[:count], refs[count]
     width = out_refs[0].shape[1]
     position, here = lax.axis_index("ctx"), lax.axis_index("mp")
-    second, third, upper, lower, mine = given
-    half = upper.shape[0]
-    attended_s[0:half, columns_of(position ^ 1, own)] = upper[...]
-    attended_s[half:, columns_of(position ^ 1, own)] = lower[...]
-    for step, piece in ((0, mine), (2, second), (3, third)):
-        attended_s[:, columns_of(position ^ step, own)] = piece[...]
+    start = 0
+    for index, piece in enumerate(given):
+        rows = piece.shape[0]
+        attended_s[start : start + rows, columns_of(position ^ BACK[index % COUNT], own)] = piece[...]
+        start += rows if index % COUNT == COUNT - 1 else 0
     for mask, out_ref in zip(masks, out_refs):
-        columns = pl.ds(pl.multiple_of((here ^ mask) * width, width), width)
         out_ref[...] = jnp.dot(
-            attended_s[...], weight_ref[:, columns], preferred_element_type=jnp.float32
+            attended_s[...], weight_ref[:, columns_of(here ^ mask, width)], preferred_element_type=jnp.float32
         ).astype(jnp.bfloat16)
 
 
@@ -334,7 +336,7 @@
         out_specs=[IN_VMEM] * len(outputs),
         scratch_shapes=scratch,
         compiler_params=pltpu.CompilerParams(vmem_limit_bytes=limit),
-        cost_estimate=pl.CostEstimate(flops=cost, bytes_accessed=2**20, transcendentals=0),
+        cost_estimate=pl.CostEstimate(flops=cost, bytes_accessed=min(2**20, cost), transcendentals=0),
         name=getattr(kernel, "func", kernel).__name__,
     )(*operands)
 
@@ -385,29 +387,27 @@
         [((own // HEAD_DIM, window, window), half), ((window, HEAD_DIM), jnp.float32)],
         [pltpu.VMEM((COUNT, rows, own), half), pltpu.VMEM((window, own), half)],
     )
-    third, second, values = run_kernel(
+    sides = [((rows // 2, own), half), ((rows // 2, own), half)]
+    *far, values = run_kernel(
         values_kernel,
         (*plain, *gates, band, short_filter, skip_gain.reshape(1, channels), soft, totals),
-        [piece, piece, ((window, own), half)],
+        sides * 2 + [((window, own), half)],
         [
             pltpu.VMEM((window, own), half),
             pltpu.VMEM((COUNT, rows + EDGE, own), half),
             pltpu.VMEM((window + rows, own), half),
         ],
     )
-    third_got, second_got = swapped(third, "ctx", 3), swapped(second, "ctx", 2)
-    upper, lower, mine = run_kernel(
-        near_rows_kernel,
-        (soft, totals, values),
-        [((rows // 2, own), half)] * 2 + [piece],
-        [pltpu.VMEM((rows, own), half)],
-    )
-    near = (swapped(upper, "ctx", 1), swapped(lower, "ctx", 1))
-    return project_and_share((second_got, third_got, *near, mine), weight)
-
-
-def projected(attended, out_weight, masks, after=()):
-    rows = attended[0].shape[0]
+    near = run_kernel(near_rows_kernel, (soft, totals, values), sides * 2)
+    halves = [
+        [swapped(far[2 + side], "ctx", 2), swapped(far[side], "ctx", 3), swapped(near[side], "ctx", 1), near[2 + side]]
+        for side in range(2)
+    ]
+    return project_and_share(halves, weight)
+
+
+def projected(attended, out_weight, masks, after, cost):
+    rows = sum(piece.shape[0] for piece in attended) // COUNT
     width = out_weight.shape[1] // lax.axis_size("mp")
     return run_kernel(
         functools.partial(project_kernel, masks),
@@ -415,8 +415,11 @@
         [((rows, width), jnp.bfloat16)] * len(masks),
         [pltpu.VMEM((rows, out_weight.shape[0]), jnp.bfloat16)],
         [IN_VMEM] * (len(attended) + 1) + [ANYWHERE] * len(after),
-        cost=2 * rows * out_weight.shape[0] * width * len(masks),
-    )
+        cost=cost,
+    )
+
+
+FAR_COST, NEAR_COST = 10**10, 10**3
 
 
 def added(*terms):
@@ -426,15 +429,19 @@
     return total.astype(jnp.bfloat16)
 
 
-def project_and_share(attended, out_weight):
-    (far_given,) = projected(attended, out_weight, (3,))
-    far_got = swapped(far_given, "mp", 1)
-    (far_kept,) = projected(attended, out_weight, (2,))
-    far_sum = added(far_kept, far_got)
-    near_given, near_kept = projected(attended, out_weight, (1, 0), (far_sum,))
+def project_and_share(halves, out_weight):
+    crossed, after = [], ()
+    for pieces in halves:
+        (given,) = projected(pieces, out_weight, (3,), after, FAR_COST)
+        got = swapped(given, "mp", 1)
+        (kept,) = projected(pieces, out_weight, (2,), after, FAR_COST)
+        far_sum = added(kept, got)
+        after = (far_sum,)
+        crossed.append(swapped(far_sum, "mp", 2))
+    near_given, near_kept = projected(halves[0] + halves[1], out_weight, (1, 0), after, NEAR_COST)
     half = near_given.shape[0] // 2
-    near_got = jnp.concatenate([swapped(near_given[:half], "mp", 1), swapped(near_given[half:], "mp", 1)])
-    return added(near_kept, near_got, swapped(far_sum, "mp", 2))
+    near_got = [swapped(near_given[:half], "mp", 1), swapped(near_given[half:], "mp", 1)]
+    return added(near_kept, jnp.concatenate(near_got), jnp.concatenate(crossed))
 
 
 def per_device(inputs, short_filter, long_filter, skip_gain, queries, key_rows, out_weight):

time: 50.1 us -> 52 us (1.038)
  starting transfers between devices: 24.7 us -> 29.7 us
  waiting for transfers between devices: 12.7 us -> 8.6 us
  Pallas kernels: 10.6 us -> 11.6 us
    ppermute x14 -> x18, starting transfers between devices: 24.7 us -> 29.7 us  [swapped(): lax.ppermute(value, axis, [(source, source ^ step) for source in range(la...]
    ppermute x14 -> x18, waiting for transfers between devices: 12.7 us -> 8.6 us  [swapped(): lax.ppermute(value, axis, [(source, source ^ step) for source in range(la...]
    pallas_call x9 -> x11, Pallas kernels: 10.6 us -> 11.6 us  [run_kernel(): pl.pallas_call(kernel, out_shape=[jax.ShapeDtypeStruct(shape, dtype) for...]
  transfers between devices with their start and end apart: 14 -> 18, of which waited for: 8 -> 6; matrix products, arithmetic and copies ran while one was open for 0% -> 0% of each run, Pallas kernels for 15% -> 18%
where the time goes in v9:
time: 52 us; the launch traced here: 51.7 us
  starting transfers between devices  29.7 us (57%)
  Pallas kernels  11.6 us (22%)
  waiting for transfers between devices  8.6 us (17%)
  other arithmetic  0.89 us (2%)
  local copies, waits for them, and re-layouts  0.75 us (1%)
    ppermute x18, starting transfers between devices, swapped(): lax.ppermute(value, axis, [(source, source ^ step) for source in range(la...  29.7 us
    pallas_call x11, Pallas kernels, run_kernel(): pl.pallas_call(kernel, out_shape=[jax.ShapeDtypeStruct(shape, dtype) for...  11.6 us
    ppermute x18, waiting for transfers between devices, swapped(): lax.ppermute(value, axis, [(source, source ^ step) for source in range(la...  8.6 us
  transfers between devices with their start and end apart: 18, of which 6 were waited for; matrix products, arithmetic and copies ran while one was open for 0% of the time, Pallas kernels for 18%

profile of v9, /device:TPU:0, one launch (start us, length us, event | category | flops | bytes accessed | tf_op | source)
XLA Modules:
  0.0 51.7 jit_solution(1183380468808830633)
XLA Ops:
  0.0 1.3 %plain_kernel.1 = (bf16[384,256]{1,0:T(8,128)(2,1)S(1)}, bf16[384,256]{1,0:T(8,128)(2,1)S(1)}, bf16[384,256]{1,0:T(8,128)(2,1)S(1)}, bf16[384,256]{1,0:T(8,128)(2,1)S(1)}) custom-call(bf16[3,128,1024]{2,1,0:T(8,128)(2,1)} %bitcast.3, bf16[128,1024]{1,0:T(8,128)(2,1)} %queries_any.1, bf16[128,1024]{1,0:T(8,128)(2,1)} %keys_any.1), custom_call_target="tpu_custom_call" | custom-call | flops 1000000 | bytes 1000000 | tf_op jit(solution)/shard_map/plain_kernel/pallas_call | solution.py:332
  1.3 5.1 %collective-permute-start = (bf16[384,256]{1,0:T(8,128)(2,1)S(1)}, bf16[384,256]{1,0:T(8,128)(2,1)S(1)}, u32[]{:S(2)}, u32[]{:S(2)}) collective-permute-start(bf16[384,256]{1,0:T(8,128)(2,1)S(1)} %get-tuple-element.28), channel_id=1, source_target_pairs={{0,12},{4,8},{8,4},{12,0},{1,13},{5,9},{9,5},{13,1},{2,14},{6,10},... | collective-permute-start | bytes 589832 | tf_op jit(solution)/shard_map/ppermute | solution.py:345
  7.0 2.1 %gate_kernel.1 = (bf16[144,256]{1,0:T(8,128)(2,1)}, bf16[144,256]{1,0:T(8,128)(2,1)}, bf16[144,256]{1,0:T(8,128)(2,1)}, bf16[144,256]{1,0:T(8,128)(2,1)}) custom-call(bf16[3,128,1024]{2,1,0:T(8,128)(2,1)} %bitcast.4, bf16[3,3,1024]{2,1,0:T(4,128)(2,1)} %refs_9_.1), custom_call_target="tpu_custom_call" | custom-call | flops 1000000 | bytes 1000000 | tf_op jit(solution)/shard_map/gate_kernel/pallas_call | solution.py:332
  9.2 3.8 %collective-permute-start.3 = (bf16[144,256]{1,0:T(8,128)(2,1)}, bf16[144,256]{1,0:T(8,128)(2,1)S(1)}, u32[]{:S(2)}, u32[]{:S(2)}) collective-permute-start(bf16[144,256]{1,0:T(8,128)(2,1)} %get-tuple-element.32), channel_id=1, source_target_pairs={{0,12},{4,8},{8,4},{12,0},{1,13},{5,9},{9,5},{13,1},{2,14},{6,10},... | collective-permute-start | bytes 221192 | tf_op jit(solution)/shard_map/ppermute | solution.py:345
  13.0 8.3 %collective-permute-start.5 = (bf16[144,256]{1,0:T(8,128)(2,1)}, bf16[144,256]{1,0:T(8,128)(2,1)S(1)}, u32[]{:S(2)}, u32[]{:S(2)}) collective-permute-start(bf16[144,256]{1,0:T(8,128)(2,1)} %get-tuple-element.34), channel_id=1, source_target_pairs={{0,4},{4,0},{8,12},{12,8},{1,5},{5,1},{9,13},{13,9},{2,6},{6,2},{1... | collective-permute-start | bytes 221192 | tf_op jit(solution)/shard_map/ppermute | solution.py:345
  21.2 0.7 %copy-done.2 = bf16[64,128]{1,0:T(8,128)(2,1)S(1)} copy-done((bf16[64,128]{1,0:T(8,128)(2,1)S(1)}, bf16[64,128]{1,0:T(8,128)(2,1)}, u32[]{:S(2)}) %copy-start.2) | copy-done | bytes 16408
  22.0 3.4 %ready_kernel.1 = (bf16[2048,256]{1,0:T(8,128)(2,1)S(1)}, bf16[1024,4096]{1,0:T(8,128)(2,1)S(1)}) custom-call(bf16[64,128]{1,0:T(8,128)(2,1)S(1)} %copy-done.2, bf16[1024,4096]{1,0:T(8,128)(2,1)} %weight_any.1), custom_call_target="tpu_custom_call" | custom-call | flops 1000000 | bytes 1000000 | tf_op jit(solution)/shard_map/ready_kernel/pallas_call | solution.py:332
  25.4 1.8 %collective-permute-done.1.second_ref.refs_1_ = bf16[384,256]{1,0:T(8,128)(2,1)S(1)} collective-permute-done((bf16[384,256]{1,0:T(8,128)(2,1)S(1)}, bf16[384,256]{1,0:T(8,128)(2,1)S(1)}, u32[]{:S(2)}, u32[]{:S(2)}) %collective-permute-start.1) | collective-permute-done | bytes 196640 | tf_op jit(solution)/shard_map/ppermute | solution.py:345
  27.9 1.5 %collective-permute-done.4.refs_5_ = bf16[144,256]{1,0:T(8,128)(2,1)S(1)} collective-permute-done((bf16[144,256]{1,0:T(8,128)(2,1)}, bf16[144,256]{1,0:T(8,128)(2,1)S(1)}, u32[]{:S(2)}, u32[]{:S(2)}) %collective-permute-start.4) | collective-permute-done | bytes 73760 | tf_op jit(solution)/shard_map/ppermute | solution.py:345
  29.4 1.2 %values_kernel.1 = (bf16[64,256]{1,0:T(8,128)(2,1)S(1)}, bf16[64,256]{1,0:T(8,128)(2,1)S(1)}, bf16[64,256]{1,0:T(8,128)(2,1)S(1)}, bf16[64,256]{1,0:T(8,128)(2,1)S(1)}, bf16[512,256]{1,0:T(8,128)(2,1)S(1)}) custom-call(bf16[384,256]{1,0:T(8,128)(2,1)S(1)} %collective-permute-done.third_ref.refs_0_, ...), custom_call_target="tpu_custom_call" | custom-call | flops 1000000 | bytes 1000000 | tf_op jit(solution)/shard_map/values_kernel/pallas_call | solution.py:332
  30.6 0.9 %collective-permute-start.6 = (bf16[64,256]{1,0:T(8,128)(2,1)S(1)}, bf16[64,256]{1,0:T(8,128)(2,1)S(1)}, u32[]{:S(2)}, u32[]{:S(2)}) collective-permute-start(bf16[64,256]{1,0:T(8,128)(2,1)S(1)} %get-tuple-element.39), channel_id=1, source_target_pairs={{0,8},{4,12},{8,0},{12,4},{1,9},{5,13},{9,1},{13,5},{2,10},{6,14},... | collective-permute-start | bytes 98312 | tf_op jit(solution)/shard_map/ppermute | solution.py:345
  31.5 1.8 %collective-permute-start.7 = (bf16[64,256]{1,0:T(8,128)(2,1)S(1)}, bf16[64,256]{1,0:T(8,128)(2,1)S(1)}, u32[]{:S(2)}, u32[]{:S(2)}) collective-permute-start(bf16[64,256]{1,0:T(8,128)(2,1)S(1)} %get-tuple-element.40), channel_id=1, source_target_pairs={{0,12},{4,8},{8,4},{12,0},{1,13},{5,9},{9,5},{13,1},{2,14},{6,10},... | collective-permute-start | bytes 98312 | tf_op jit(solution)/shard_map/ppermute | solution.py:345
  33.5 1.0 %collective-permute-start.8 = (bf16[64,256]{1,0:T(8,128)(2,1)S(1)}, bf16[64,256]{1,0:T(8,128)(2,1)S(1)}, u32[]{:S(2)}, u32[]{:S(2)}) collective-permute-start(bf16[64,256]{1,0:T(8,128)(2,1)S(1)} %get-tuple-element.42), channel_id=1, source_target_pairs={{0,4},{4,0},{8,12},{12,8},{1,5},{5,1},{9,13},{13,9},{2,6},{6,2},{1... | collective-permute-start | bytes 98312 | tf_op jit(solution)/shard_map/ppermute | solution.py:345
  34.5 1.1 %collective-permute-start.11 = (bf16[64,256]{1,0:T(8,128)(2,1)S(1)}, bf16[64,256]{1,0:T(8,128)(2,1)S(1)}, u32[]{:S(2)}, u32[]{:S(2)}) collective-permute-start(bf16[64,256]{1,0:T(8,128)(2,1)S(1)} %get-tuple-element.46), channel_id=1, source_target_pairs={{0,4},{4,0},{8,12},{12,8},{1,5},{5,1},{9,13},{13,9},{2,6},{6,2},{1... | collective-permute-start | bytes 98312 | tf_op jit(solution)/shard_map/ppermute | solution.py:345
  35.6 1.9 %collective-permute-start.9 = (bf16[64,256]{1,0:T(8,128)(2,1)S(1)}, bf16[64,256]{1,0:T(8,128)(2,1)S(1)}, u32[]{:S(2)}, u32[]{:S(2)}) collective-permute-start(bf16[64,256]{1,0:T(8,128)(2,1)S(1)} %get-tuple-element.44), channel_id=1, source_target_pairs={{0,8},{4,12},{8,0},{12,4},{1,9},{5,13},{9,1},{13,5},{2,10},{6,14},... | collective-permute-start | bytes 98312 | tf_op jit(solution)/shard_map/ppermute | solution.py:345
  37.6 1.4 %collective-permute-start.10 = (bf16[64,256]{1,0:T(8,128)(2,1)S(1)}, bf16[64,256]{1,0:T(8,128)(2,1)S(1)}, u32[]{:S(2)}, u32[]{:S(2)}) collective-permute-start(bf16[64,256]{1,0:T(8,128)(2,1)S(1)} %get-tuple-element.45), channel_id=1, source_target_pairs={{0,12},{4,8},{8,4},{12,0},{1,13},{5,9},{9,5},{13,1},{2,14},{6,10},... | collective-permute-start | bytes 98312 | tf_op jit(solution)/shard_map/ppermute | solution.py:345
  40.0 0.8 %collective-permute-done.12 = bf16[64,1024]{1,0:T(8,128)(2,1)S(1)} collective-permute-done((bf16[64,1024]{1,0:T(8,128)(2,1)S(1)}, bf16[64,1024]{1,0:T(8,128)(2,1)S(1)}, u32[]{:S(2)}, u32[]{:S(2)}) %collective-permute-start.12) | collective-permute-done | bytes 131104 | tf_op jit(solution)/shard_map/ppermute | solution.py:345
  40.9 1.6 %collective-permute-start.16 = (bf16[64,1024]{1,0:T(8,128)(2,1)S(1)}, bf16[64,1024]{1,0:T(8,128)(2,1)S(1)}, u32[]{:S(2)}, u32[]{:S(2)}) collective-permute-start(bf16[64,1024]{1,0:T(8,128)(2,1)S(1)} %add_convert_fusion.2.refs_5_), channel_id=1, source_target_pairs={{0,2},{1,3},{2,0},{3,1},{4,6},{5,7},{6,4},{7,5},{8,10},{9,11},{10,... | collective-permute-start | bytes 393224 | tf_op jit(solution)/shard_map/ppermute | solution.py:345
  42.4 0.8 %collective-permute-done.10.refs_1_.refs_5_ = bf16[64,256]{1,0:T(8,128)(2,1)S(1)} collective-permute-done((bf16[64,256]{1,0:T(8,128)(2,1)S(1)}, bf16[64,256]{1,0:T(8,128)(2,1)S(1)}, u32[]{:S(2)}, u32[]{:S(2)}) %collective-permute-start.10) | collective-permute-done | bytes 32800 | tf_op jit(solution)/shard_map/ppermute | solution.py:345
  44.4 0.8 %collective-permute-done.13 = bf16[64,1024]{1,0:T(8,128)(2,1)S(1)} collective-permute-done((bf16[64,1024]{1,0:T(8,128)(2,1)S(1)}, bf16[64,1024]{1,0:T(8,128)(2,1)S(1)}, u32[]{:S(2)}, u32[]{:S(2)}) %collective-permute-start.13) | collective-permute-done | bytes 131104 | tf_op jit(solution)/shard_map/ppermute | solution.py:345
  45.2 1.6 %collective-permute-start.17 = (bf16[64,1024]{1,0:T(8,128)(2,1)S(1)}, bf16[64,1024]{1,0:T(8,128)(2,1)S(1)}, u32[]{:S(2)}, u32[]{:S(2)}) collective-permute-start(bf16[64,1024]{1,0:T(8,128)(2,1)S(1)} %add_convert_fusion.1.refs_9_), channel_id=1, source_target_pairs={{0,2},{1,3},{2,0},{3,1},{4,6},{5,7},{6,4},{7,5},{8,10},{9,11},{10,... | collective-permute-start | bytes 393224 | tf_op jit(solution)/shard_map/ppermute | solution.py:345
  46.8 0.7 %project_kernel.9 = (bf16[128,1024]{1,0:T(8,128)(2,1)S(1)}, bf16[128,1024]{1,0:T(8,128)(2,1)S(1)}) custom-call(bf16[64,256]{1,0:T(8,128)(2,1)S(1)} %collective-permute-done.6.refs_0_, bf16[64,256]{1,0:T(8,128)(2,1)S(1)} %collective-permute-done.7.refs_1_, bf16[64,256]{1,0:T(8,128)(2,1)S(1)} %collective-permute-done.8.refs_2_, ...), custom_call_target="tpu_custom_call" | custom-call | flops 1000 | bytes 1000 | tf_op jit(solution)/shard_map/project_kernel/pallas_call | solution.py:332
  48.1 2.7 %collective-permute-done.17 = bf16[64,1024]{1,0:T(8,128)(2,1)S(1)} collective-permute-done((bf16[64,1024]{1,0:T(8,128)(2,1)S(1)}, bf16[64,1024]{1,0:T(8,128)(2,1)S(1)}, u32[]{:S(2)}, u32[]{:S(2)}) %collective-permute-start.17) | collective-permute-done | bytes 131104 | tf_op jit(solution)/shard_map/ppermute | solution.py:345
  50.8 0.8 %add_convert_fusion = bf16[128,1024]{1,0:T(8,128)(2,1)} fusion(bf16[128,1024]{1,0:T(8,128)(2,1)S(1)} %get-tuple-element.49, bf16[64,1024]{1,0:T(8,128)(2,1)S(1)} %collective-permute-done.15, bf16[64,1024]{1,0:T(8,128)(2,1)S(1)} %collective-permute-done.14, bf16[64,1024]{1,0:T(8,128)(2,1)S(1)} %collective-permute-done.17, ...), kind=kLoop, calls=%fused_computation | loop fusion | flops 1572864 | bytes 1048576 | tf_op jit(solution)/shard_map/convert_element_type | solution.py:429
  (35 shorter events, 4.4 us)
Async XLA Ops:
  0.0 29.4 %copy-start = (bf16[3,3,1024]{2,1,0:T(4,128)(2,1)S(1)}, bf16[3,3,1024]{2,1,0:T(4,128)(2,1)}, u32[]{:S(2)}) copy-start(bf16[3,3,1024]{2,1,0:T(4,128)(2,1)} %refs_9_.1) | copy-start | bytes 55300
  0.0 29.4 %copy-start.3 = (f32[1024]{0:T(1024)S(1)}, f32[1024]{0:T(1024)}, u32[]{:S(2)}) copy-start(f32[1024]{0:T(1024)} %param.10) | copy-start | bytes 12292
  1.3 11.7 %collective-permute-start = (bf16[384,256]{1,0:T(8,128)(2,1)S(1)}, bf16[384,256]{1,0:T(8,128)(2,1)S(1)}, u32[]{:S(2)}, u32[]{:S(2)}) collective-permute-start(bf16[384,256]{1,0:T(8,128)(2,1)S(1)} %get-tuple-element.28), channel_id=1, source_target_pairs={{0,12},{4,8},{8,4},{12,0},{1,13},{5,9},{9,5},{13,1},{2,14},{6,10},... | collective-permute-start | bytes 589832 | tf_op jit(solution)/shard_map/ppermute | solution.py:345
  6.4 20.8 %collective-permute-start.1 = (bf16[384,256]{1,0:T(8,128)(2,1)S(1)}, bf16[384,256]{1,0:T(8,128)(2,1)S(1)}, u32[]{:S(2)}, u32[]{:S(2)}) collective-permute-start(bf16[384,256]{1,0:T(8,128)(2,1)S(1)} %get-tuple-element.29), channel_id=1, source_target_pairs={{0,8},{4,12},{8,0},{12,4},{1,9},{5,13},{9,1},{13,5},{2,10},{6,14},... | collective-permute-start | bytes 589832 | tf_op jit(solution)/shard_map/ppermute | solution.py:345
  6.4 20.8 %collective-permute-start.2 = (bf16[384,256]{1,0:T(8,128)(2,1)S(1)}, bf16[384,256]{1,0:T(8,128)(2,1)S(1)}, u32[]{:S(2)}, u32[]{:S(2)}) collective-permute-start(bf16[384,256]{1,0:T(8,128)(2,1)S(1)} %get-tuple-element.30), channel_id=1, source_target_pairs={{0,4},{4,0},{8,12},{12,8},{1,5},{5,1},{9,13},{13,9},{2,6},{6,2},{1... | collective-permute-start | bytes 589832 | tf_op jit(solution)/shard_map/ppermute | solution.py:345
  9.2 20.3 %copy-start.1 = (bf16[144,256]{1,0:T(8,128)(2,1)S(1)}, bf16[144,256]{1,0:T(8,128)(2,1)}, u32[]{:S(2)}) copy-start(bf16[144,256]{1,0:T(8,128)(2,1)} %get-tuple-element.35.refs_7_) | copy-start | bytes 221188
  9.2 18.7 %collective-permute-start.3 = (bf16[144,256]{1,0:T(8,128)(2,1)}, bf16[144,256]{1,0:T(8,128)(2,1)S(1)}, u32[]{:S(2)}, u32[]{:S(2)}) collective-permute-start(bf16[144,256]{1,0:T(8,128)(2,1)} %get-tuple-element.32), channel_id=1, source_target_pairs={{0,12},{4,8},{8,4},{12,0},{1,13},{5,9},{9,5},{13,1},{2,14},{6,10},... | collective-permute-start | bytes 221192 | tf_op jit(solution)/shard_map/ppermute | solution.py:345
  13.0 16.4 %collective-permute-start.4 = (bf16[144,256]{1,0:T(8,128)(2,1)}, bf16[144,256]{1,0:T(8,128)(2,1)S(1)}, u32[]{:S(2)}, u32[]{:S(2)}) collective-permute-start(bf16[144,256]{1,0:T(8,128)(2,1)} %get-tuple-element.33), channel_id=1, source_target_pairs={{0,8},{4,12},{8,0},{12,4},{1,9},{5,13},{9,1},{13,5},{2,10},{6,14},... | collective-permute-start | bytes 221192 | tf_op jit(solution)/shard_map/ppermute | solution.py:345
  13.0 16.4 %collective-permute-start.5 = (bf16[144,256]{1,0:T(8,128)(2,1)}, bf16[144,256]{1,0:T(8,128)(2,1)S(1)}, u32[]{:S(2)}, u32[]{:S(2)}) collective-permute-start(bf16[144,256]{1,0:T(8,128)(2,1)} %get-tuple-element.34), channel_id=1, source_target_pairs={{0,4},{4,0},{8,12},{12,8},{1,5},{5,1},{9,13},{13,9},{2,6},{6,2},{1... | collective-permute-start | bytes 221192 | tf_op jit(solution)/shard_map/ppermute | solution.py:345
  21.2 0.7 %copy-start.2 = (bf16[64,128]{1,0:T(8,128)(2,1)S(1)}, bf16[64,128]{1,0:T(8,128)(2,1)}, u32[]{:S(2)}) copy-start(bf16[64,128]{1,0:T(8,128)(2,1)} %filter_ref.1) | copy-start | bytes 49156
  30.6 6.9 %collective-permute-start.6 = (bf16[64,256]{1,0:T(8,128)(2,1)S(1)}, bf16[64,256]{1,0:T(8,128)(2,1)S(1)}, u32[]{:S(2)}, u32[]{:S(2)}) collective-permute-start(bf16[64,256]{1,0:T(8,128)(2,1)S(1)} %get-tuple-element.39), channel_id=1, source_target_pairs={{0,8},{4,12},{8,0},{12,4},{1,9},{5,13},{9,1},{13,5},{2,10},{6,14},... | collective-permute-start | bytes 98312 | tf_op jit(solution)/shard_map/ppermute | solution.py:345
  31.5 7.5 %collective-permute-start.7 = (bf16[64,256]{1,0:T(8,128)(2,1)S(1)}, bf16[64,256]{1,0:T(8,128)(2,1)S(1)}, u32[]{:S(2)}, u32[]{:S(2)}) collective-permute-start(bf16[64,256]{1,0:T(8,128)(2,1)S(1)} %get-tuple-element.40), channel_id=1, source_target_pairs={{0,12},{4,8},{8,4},{12,0},{1,13},{5,9},{9,5},{13,1},{2,14},{6,10},... | collective-permute-start | bytes 98312 | tf_op jit(solution)/shard_map/ppermute | solution.py:345
  33.5 5.4 %collective-permute-start.8 = (bf16[64,256]{1,0:T(8,128)(2,1)S(1)}, bf16[64,256]{1,0:T(8,128)(2,1)S(1)}, u32[]{:S(2)}, u32[]{:S(2)}) collective-permute-start(bf16[64,256]{1,0:T(8,128)(2,1)S(1)} %get-tuple-element.42), channel_id=1, source_target_pairs={{0,4},{4,0},{8,12},{12,8},{1,5},{5,1},{9,13},{13,9},{2,6},{6,2},{1... | collective-permute-start | bytes 98312 | tf_op jit(solution)/shard_map/ppermute | solution.py:345
  34.5 7.9 %collective-permute-start.11 = (bf16[64,256]{1,0:T(8,128)(2,1)S(1)}, bf16[64,256]{1,0:T(8,128)(2,1)S(1)}, u32[]{:S(2)}, u32[]{:S(2)}) collective-permute-start(bf16[64,256]{1,0:T(8,128)(2,1)S(1)} %get-tuple-element.46), channel_id=1, source_target_pairs={{0,4},{4,0},{8,12},{12,8},{1,5},{5,1},{9,13},{13,9},{2,6},{6,2},{1... | collective-permute-start | bytes 98312 | tf_op jit(solution)/shard_map/ppermute | solution.py:345
  35.6 6.8 %collective-permute-start.9 = (bf16[64,256]{1,0:T(8,128)(2,1)S(1)}, bf16[64,256]{1,0:T(8,128)(2,1)S(1)}, u32[]{:S(2)}, u32[]{:S(2)}) collective-permute-start(bf16[64,256]{1,0:T(8,128)(2,1)S(1)} %get-tuple-element.44), channel_id=1, source_target_pairs={{0,8},{4,12},{8,0},{12,4},{1,9},{5,13},{9,1},{13,5},{2,10},{6,14},... | collective-permute-start | bytes 98312 | tf_op jit(solution)/shard_map/ppermute | solution.py:345
  37.6 5.7 %collective-permute-start.10 = (bf16[64,256]{1,0:T(8,128)(2,1)S(1)}, bf16[64,256]{1,0:T(8,128)(2,1)S(1)}, u32[]{:S(2)}, u32[]{:S(2)}) collective-permute-start(bf16[64,256]{1,0:T(8,128)(2,1)S(1)} %get-tuple-element.45), channel_id=1, source_target_pairs={{0,12},{4,8},{8,4},{12,0},{1,13},{5,9},{9,5},{13,1},{2,14},{6,10},... | collective-permute-start | bytes 98312 | tf_op jit(solution)/shard_map/ppermute | solution.py:345
  39.4 1.4 %collective-permute-start.12 = (bf16[64,1024]{1,0:T(8,128)(2,1)S(1)}, bf16[64,1024]{1,0:T(8,128)(2,1)S(1)}, u32[]{:S(2)}, u32[]{:S(2)}) collective-permute-start(bf16[64,1024]{1,0:T(8,128)(2,1)S(1)} %project_kernel.6), channel_id=1, source_target_pairs={{0,1},{1,0},{2,3},{3,2},{4,5},{5,4},{6,7},{7,6},{8,9},{9,8},{10,11... | collective-permute-start | bytes 393224 | tf_op jit(solution)/shard_map/ppermute | solution.py:345
  40.9 7.3 %collective-permute-start.16 = (bf16[64,1024]{1,0:T(8,128)(2,1)S(1)}, bf16[64,1024]{1,0:T(8,128)(2,1)S(1)}, u32[]{:S(2)}, u32[]{:S(2)}) collective-permute-start(bf16[64,1024]{1,0:T(8,128)(2,1)S(1)} %add_convert_fusion.2.refs_5_), channel_id=1, source_target_pairs={{0,2},{1,3},{2,0},{3,1},{4,6},{5,7},{6,4},{7,5},{8,10},{9,11},{10,... | collective-permute-start | bytes 393224 | tf_op jit(solution)/shard_map/ppermute | solution.py:345
  43.8 1.4 %collective-permute-start.13 = (bf16[64,1024]{1,0:T(8,128)(2,1)S(1)}, bf16[64,1024]{1,0:T(8,128)(2,1)S(1)}, u32[]{:S(2)}, u32[]{:S(2)}) collective-permute-start(bf16[64,1024]{1,0:T(8,128)(2,1)S(1)} %project_kernel.8), channel_id=1, source_target_pairs={{0,1},{1,0},{2,3},{3,2},{4,5},{5,4},{6,7},{7,6},{8,9},{9,8},{10,11... | collective-permute-start | bytes 393224 | tf_op jit(solution)/shard_map/ppermute | solution.py:345
  45.2 5.6 %collective-permute-start.17 = (bf16[64,1024]{1,0:T(8,128)(2,1)S(1)}, bf16[64,1024]{1,0:T(8,128)(2,1)S(1)}, u32[]{:S(2)}, u32[]{:S(2)}) collective-permute-start(bf16[64,1024]{1,0:T(8,128)(2,1)S(1)} %add_convert_fusion.1.refs_9_), channel_id=1, source_target_pairs={{0,2},{1,3},{2,0},{3,1},{4,6},{5,7},{6,4},{7,5},{8,10},{9,11},{10,... | collective-permute-start | bytes 393224 | tf_op jit(solution)/shard_map/ppermute | solution.py:345
  47.6 3.3 %collective-permute-start.14 = (bf16[64,1024]{1,0:T(8,128)(2,1)S(1)}, bf16[64,1024]{1,0:T(8,128)(2,1)S(1)}, u32[]{:S(2)}, u32[]{:S(2)}) collective-permute-start(bf16[64,1024]{1,0:T(8,128)(2,1)S(1)} %get-tuple-element.51), channel_id=1, source_target_pairs={{0,1},{1,0},{2,3},{3,2},{4,5},{5,4},{6,7},{7,6},{8,9},{9,8},{10,11... | collective-permute-start | bytes 393224 | tf_op jit(solution)/shard_map/ppermute | solution.py:345
  47.6 3.2 %collective-permute-start.15 = (bf16[64,1024]{1,0:T(8,128)(2,1)S(1)}, bf16[64,1024]{1,0:T(8,128)(2,1)S(1)}, u32[]{:S(2)}, u32[]{:S(2)}) collective-permute-start(bf16[64,1024]{1,0:T(8,128)(2,1)S(1)} %get-tuple-element.52), channel_id=1, source_target_pairs={{0,1},{1,0},{2,3},{3,2},{4,5},{5,4},{6,7},{7,6},{8,9},{9,8},{10,11... | collective-permute-start | bytes 393224 | tf_op jit(solution)/shard_map/ppermute | solution.py:345

commit v10 on v8

--- a/solution.py
+++ b/solution.py
@@ -187,13 +187,16 @@
     weights.wait()
 
 
-def weights_kernel(third_ref, second_ref, near_ref, own_ref, weight_ref, total_ref, query_s, key_s):
+def weights_kernel(third_ref, second_ref, near_ref, own_ref, short_ref, weight_ref, total_ref, feature_ref, query_s, key_s, signal_s):
     count = COUNT
     rows, own = query_s.shape[1:]
     position = lax.axis_index("ctx")
     for step, given in zip(ORDER, (third_ref, second_ref, near_ref, own_ref)):
         query_s[position ^ step] = given[0:rows]
         key_s[columns_of(position ^ step, rows)] = given[rows : 2 * rows]
+        signal_s[columns_of(position ^ step, rows)] = given[2 * rows :]
+    taps = [short_ref[lag, 0:1, columns_of(position, own)].astype(jnp.float32) for lag in range(3)]
+    feature_ref[...] = featured(signal_s[...].astype(jnp.float32), taps)
     causal = lax.broadcasted_iota(jnp.int32, (rows, rows), 1) <= lax.broadcasted_iota(jnp.int32, (rows, rows), 0)
     for head in range(own // HEAD_DIM):
         columns = slice(head * HEAD_DIM, (head + 1) * HEAD_DIM)
@@ -226,16 +229,15 @@
 
 def values_kernel(*refs):
     count = COUNT
-    plain, gates = refs[:count], refs[count : 2 * count]
-    band_ref, short_ref, gain_ref, weight_ref, total_ref = refs[2 * count : 2 * count + 5]
-    third_ref, second_ref, value_ref = refs[2 * count + 5 : 2 * count + 8]
-    signal_s, gates_s, gate_s = refs[2 * count + 8 :]
+    gates, feature_ref = refs[:count], refs[count]
+    band_ref, short_ref, gain_ref, weight_ref, total_ref = refs[count + 1 : count + 6]
+    third_ref, second_ref, value_ref = refs[count + 6 : count + 9]
+    gates_s, gate_s = refs[count + 9 :]
     rows, own = second_ref.shape
     per_group = own * rows // band_ref.shape[0]
     position = lax.axis_index("ctx")
     mine = columns_of(position, own)
-    for step, given, gate in zip(ORDER, plain, gates):
-        signal_s[columns_of(position ^ step, rows)] = given[2 * rows :]
+    for step, gate in zip(ORDER, gates):
         gates_s[position ^ step] = gate[...]
     taps = [
         [short_ref[lag, stream : stream + 1, mine].astype(jnp.float32) for lag in range(3)] for stream in range(3)
@@ -262,7 +264,6 @@
         head = gates_s[block, 0:16].astype(jnp.float32)
         head = jnp.where(head_row < 2, jnp.concatenate([fixed, fixed], axis=0), head)
         gate_s[(block + 1) * rows : (block + 1) * rows + 16] = head.astype(jnp.bfloat16)
-    feature = featured(signal_s[...].astype(jnp.float32), taps[0])
     gain = gain_ref[:, mine]
     per_tile = HEAD_DIM // per_group
     lane = lax.broadcasted_iota(jnp.int32, (rows, 2 * HEAD_DIM), 1) % HEAD_DIM // per_group
@@ -283,7 +284,7 @@
                 gate = gate_s[(block + index + 1) * rows : (block + index + 2) * rows, columns].astype(jnp.float32)
                 part = filtered[:, index * HEAD_DIM : (index + 1) * HEAD_DIM]
                 value_ref[here, columns] = (
-                    feature[here, columns] * (part + gain[:, columns] * gate)
+                    feature_ref[here, columns] * (part + gain[:, columns] * gate)
                 ).astype(jnp.bfloat16)
     for step, out_ref in ((3, third_ref), (2, second_ref)):
         mix_rows(position ^ step, weight_ref, total_ref, value_ref, out_ref)
@@ -299,20 +300,19 @@
     mix_rows(position, weight_ref, total_ref, value_ref, own_ref)
 
 
-def project_kernel(masks, *refs):
+def project_kernel(spans, *refs):
     given, weight_ref = refs[:5], refs[5]
-    out_refs, attended_s = refs[-1 - len(masks) : -1], refs[-1]
-    own = given[0].shape[1]
-    width = out_refs[0].shape[1]
-    position, here = lax.axis_index("ctx"), lax.axis_index("mp")
+    out_refs, attended_s = refs[-1 - len(spans) : -1], refs[-1]
     second, third, upper, lower, mine = given
     half = upper.shape[0]
+    rows, own = mine.shape
+    position, here = lax.axis_index("ctx"), lax.axis_index("mp")
     attended_s[0:half, columns_of(position ^ 1, own)] = upper[...]
     attended_s[half:, columns_of(position ^ 1, own)] = lower[...]
     for step, piece in ((0, mine), (2, second), (3, third)):
         attended_s[:, columns_of(position ^ step, own)] = piece[...]
-    for mask, out_ref in zip(masks, out_refs):
-        columns = pl.ds(pl.multiple_of((here ^ mask) * width, width), width)
+    for (mask, part, parts), out_ref in zip(spans, out_refs):
+        columns = columns_of((here ^ mask) * parts + part, out_ref.shape[1])
         out_ref[...] = jnp.dot(
             attended_s[...], weight_ref[:, columns], preferred_element_type=jnp.float32
         ).astype(jnp.bfloat16)
@@ -379,18 +379,25 @@
         [pltpu.SemaphoreType.DMA],
         [IN_VMEM, IN_HBM],
     )
-    soft, totals = run_kernel(
+    soft, totals, feature = run_kernel(
         weights_kernel,
-        plain,
-        [((own // HEAD_DIM, window, window), half), ((window, HEAD_DIM), jnp.float32)],
-        [pltpu.VMEM((COUNT, rows, own), half), pltpu.VMEM((window, own), half)],
+        (*plain, short_filter),
+        [
+            ((own // HEAD_DIM, window, window), half),
+            ((window, HEAD_DIM), jnp.float32),
+            ((window, own), jnp.float32),
+        ],
+        [
+            pltpu.VMEM((COUNT, rows, own), half),
+            pltpu.VMEM((window, own), half),
+            pltpu.VMEM((window, own), half),
+        ],
     )
     third, second, values = run_kernel(
         values_kernel,
-        (*plain, *gates, band, short_filter, skip_gain.reshape(1, channels), soft, totals),
+        (*gates, feature, band, short_filter, skip_gain.reshape(1, channels), soft, totals),
         [piece, piece, ((window, own), half)],
         [
-            pltpu.VMEM((window, own), half),
             pltpu.VMEM((COUNT, rows + EDGE, own), half),
             pltpu.VMEM((window + rows, own), half),
         ],
@@ -406,17 +413,20 @@
     return project_and_share((second_got, third_got, *near, mine), weight)
 
 
-def projected(attended, out_weight, masks, after=()):
-    rows = attended[0].shape[0]
+def projected(attended, out_weight, spans, after=(), cost=10**6):
+    rows = attended[-1].shape[0]
     width = out_weight.shape[1] // lax.axis_size("mp")
     return run_kernel(
-        functools.partial(project_kernel, masks),
+        functools.partial(project_kernel, spans),
         (*attended, out_weight, *after),
-        [((rows, width), jnp.bfloat16)] * len(masks),
+        [((rows, width // parts), jnp.bfloat16) for _, _, parts in spans],
         [pltpu.VMEM((rows, out_weight.shape[0]), jnp.bfloat16)],
         [IN_VMEM] * (len(attended) + 1) + [ANYWHERE] * len(after),
-        cost=2 * rows * out_weight.shape[0] * width * len(masks),
-    )
+        cost=cost,
+    )
+
+
+FAR_COST, NEAR_COST = 10**6, 10**6
 
 
 def added(*terms):
@@ -427,14 +437,16 @@
 
 
 def project_and_share(attended, out_weight):
-    (far_given,) = projected(attended, out_weight, (3,))
-    far_got = swapped(far_given, "mp", 1)
-    (far_kept,) = projected(attended, out_weight, (2,))
-    far_sum = added(far_kept, far_got)
-    near_given, near_kept = projected(attended, out_weight, (1, 0), (far_sum,))
+    crossed, after = [], ()
+    for part in range(2):
+        given, kept = projected(attended, out_weight, ((3, part, 2), (2, part, 2)), after, FAR_COST)
+        after = (given,)
+        far_sum = added(kept, swapped(given, "mp", 1))
+        crossed.append(swapped(far_sum, "mp", 2))
+    near_given, near_kept = projected(attended, out_weight, ((1, 0, 1), (0, 0, 1)), (far_sum,), NEAR_COST)
     half = near_given.shape[0] // 2
     near_got = jnp.concatenate([swapped(near_given[:half], "mp", 1), swapped(near_given[half:], "mp", 1)])
-    return added(near_kept, near_got, swapped(far_sum, "mp", 2))
+    return added(near_kept, near_got, jnp.concatenate(crossed, axis=1))
 
 
 def per_device(inputs, short_filter, long_filter, skip_gain, queries, key_rows, out_weight):

time: 50.1 us -> 49.8 us (level)
  waiting for transfers between devices: 12.7 us -> 11 us
  starting transfers between devices: 24.7 us -> 26 us
    ppermute x14 -> x16, waiting for transfers between devices: 12.7 us -> 11 us  [swapped(): lax.ppermute(value, axis, [(source, source ^ step) for source in range(la...]
    ppermute x14 -> x16, starting transfers between devices: 24.7 us -> 26 us  [swapped(): lax.ppermute(value, axis, [(source, source ^ step) for source in range(la...]
  transfers between devices with their start and end apart: 14 -> 16, of which waited for: 8 -> 7; matrix products, arithmetic and copies ran while one was open for 0% -> 0% of each run, Pallas kernels for 15% -> 16%
where the time goes in v10:
time: 49.8 us; the launch traced here: 49.5 us
  starting transfers between devices  26 us (52%)
  waiting for transfers between devices  11 us (22%)
  Pallas kernels  10.8 us (22%)
  other arithmetic  0.88 us (2%)
  local copies, waits for them, and re-layouts  0.75 us (2%)
    ppermute x16, starting transfers between devices, swapped(): lax.ppermute(value, axis, [(source, source ^ step) for source in range(la...  26 us
    ppermute x16, waiting for transfers between devices, swapped(): lax.ppermute(value, axis, [(source, source ^ step) for source in range(la...  11 us
    pallas_call x9, Pallas kernels, run_kernel(): pl.pallas_call(kernel, out_shape=[jax.ShapeDtypeStruct(shape, dtype) for...  10.8 us
  transfers between devices with their start and end apart: 16, of which 7 were waited for; matrix products, arithmetic and copies ran while one was open for 0% of the time, Pallas kernels for 16%

profile of v10, /device:TPU:0, one launch (start us, length us, event | category | flops | bytes accessed | tf_op | source)
XLA Modules:
  0.0 49.5 jit_solution(7084285433768999012)
XLA Ops:
  0.0 1.3 %plain_kernel.1 = (bf16[384,256]{1,0:T(8,128)(2,1)S(1)}, bf16[384,256]{1,0:T(8,128)(2,1)S(1)}, bf16[384,256]{1,0:T(8,128)(2,1)S(1)}, bf16[384,256]{1,0:T(8,128)(2,1)S(1)}) custom-call(bf16[3,128,1024]{2,1,0:T(8,128)(2,1)} %bitcast.3, bf16[128,1024]{1,0:T(8,128)(2,1)} %queries_any.1, bf16[128,1024]{1,0:T(8,128)(2,1)} %keys_any.1), custom_call_target="tpu_custom_call" | custom-call | flops 1000000 | bytes 1048576 | tf_op jit(solution)/shard_map/plain_kernel/pallas_call | solution.py:330
  1.3 5.1 %collective-permute-start.3 = (bf16[384,256]{1,0:T(8,128)(2,1)S(1)}, bf16[384,256]{1,0:T(8,128)(2,1)S(1)}, u32[]{:S(2)}, u32[]{:S(2)}) collective-permute-start(bf16[384,256]{1,0:T(8,128)(2,1)S(1)} %get-tuple-element.34), channel_id=1, source_target_pairs={{0,12},{4,8},{8,4},{12,0},{1,13},{5,9},{9,5},{13,1},{2,14},{6,10},... | collective-permute-start | bytes 589832 | tf_op jit(solution)/shard_map/ppermute | solution.py:343
  6.4 0.6 %collective-permute-start.5 = (bf16[384,256]{1,0:T(8,128)(2,1)S(1)}, bf16[384,256]{1,0:T(8,128)(2,1)S(1)}, u32[]{:S(2)}, u32[]{:S(2)}) collective-permute-start(bf16[384,256]{1,0:T(8,128)(2,1)S(1)} %get-tuple-element.36), channel_id=1, source_target_pairs={{0,4},{4,0},{8,12},{12,8},{1,5},{5,1},{9,13},{13,9},{2,6},{6,2},{1... | collective-permute-start | bytes 589832 | tf_op jit(solution)/shard_map/ppermute | solution.py:343
  7.0 2.1 %gate_kernel.1 = (bf16[144,256]{1,0:T(8,128)(2,1)}, bf16[144,256]{1,0:T(8,128)(2,1)}, bf16[144,256]{1,0:T(8,128)(2,1)}, bf16[144,256]{1,0:T(8,128)(2,1)}) custom-call(bf16[3,128,1024]{2,1,0:T(8,128)(2,1)} %bitcast.4, bf16[3,3,1024]{2,1,0:T(4,128)(2,1)} %refs_6_.1), custom_call_target="tpu_custom_call" | custom-call | flops 1000000 | bytes 1048576 | tf_op jit(solution)/shard_map/gate_kernel/pallas_call | solution.py:330
  9.2 3.8 %collective-permute-start = (bf16[144,256]{1,0:T(8,128)(2,1)}, bf16[144,256]{1,0:T(8,128)(2,1)S(1)}, u32[]{:S(2)}, u32[]{:S(2)}) collective-permute-start(bf16[144,256]{1,0:T(8,128)(2,1)} %get-tuple-element.30), channel_id=1, source_target_pairs={{0,12},{4,8},{8,4},{12,0},{1,13},{5,9},{9,5},{13,1},{2,14},{6,10},... | collective-permute-start | bytes 221192 | tf_op jit(solution)/shard_map/ppermute | solution.py:343
  13.0 8.3 %collective-permute-start.2 = (bf16[144,256]{1,0:T(8,128)(2,1)}, bf16[144,256]{1,0:T(8,128)(2,1)S(1)}, u32[]{:S(2)}, u32[]{:S(2)}) collective-permute-start(bf16[144,256]{1,0:T(8,128)(2,1)} %get-tuple-element.32), channel_id=1, source_target_pairs={{0,4},{4,0},{8,12},{12,8},{1,5},{5,1},{9,13},{13,9},{2,6},{6,2},{1... | collective-permute-start | bytes 221192 | tf_op jit(solution)/shard_map/ppermute | solution.py:343
  21.2 0.7 %copy-done.2 = bf16[64,128]{1,0:T(8,128)(2,1)S(1)} copy-done((bf16[64,128]{1,0:T(8,128)(2,1)S(1)}, bf16[64,128]{1,0:T(8,128)(2,1)}, u32[]{:S(2)}) %copy-start.2) | copy-done | bytes 16408
  22.0 3.4 %ready_kernel.1 = (bf16[2048,256]{1,0:T(8,128)(2,1)S(1)}, bf16[1024,4096]{1,0:T(8,128)(2,1)S(1)}) custom-call(bf16[64,128]{1,0:T(8,128)(2,1)S(1)} %copy-done.2, bf16[1024,4096]{1,0:T(8,128)(2,1)} %weight_any.1), custom_call_target="tpu_custom_call" | custom-call | flops 1000000 | bytes 1048576 | tf_op jit(solution)/shard_map/ready_kernel/pallas_call | solution.py:330
  25.4 1.8 %collective-permute-done.4.second_ref = bf16[384,256]{1,0:T(8,128)(2,1)S(1)} collective-permute-done((bf16[384,256]{1,0:T(8,128)(2,1)S(1)}, bf16[384,256]{1,0:T(8,128)(2,1)S(1)}, u32[]{:S(2)}, u32[]{:S(2)}) %collective-permute-start.4) | collective-permute-done | bytes 196640 | tf_op jit(solution)/shard_map/ppermute | solution.py:343
  27.2 0.9 %weights_kernel.1 = (bf16[2,512,512]{2,1,0:T(8,128)(2,1)S(1)}, f32[512,128]{1,0:T(8,128)S(1)}, f32[512,256]{1,0:T(8,128)S(1)}) custom-call(bf16[384,256]{1,0:T(8,128)(2,1)S(1)} %collective-permute-done.3.third_ref, bf16[384,256]{1,0:T(8,128)(2,1)S(1)} %collective-permute-done.4.second_ref, bf16[384,256]{1,0:T(8,128)(2,1)S(1)} %collective-permute-done.5.near_ref, ...), custom_call_target="tpu_custom_call" | custom-call | flops 1000000 | bytes 1048576 | tf_op jit(solution)/shard_map/weights_kernel/pallas_call | solution.py:330
  28.2 1.2 %collective-permute-done.1.refs_1_ = bf16[144,256]{1,0:T(8,128)(2,1)S(1)} collective-permute-done((bf16[144,256]{1,0:T(8,128)(2,1)}, bf16[144,256]{1,0:T(8,128)(2,1)S(1)}, u32[]{:S(2)}, u32[]{:S(2)}) %collective-permute-start.1) | collective-permute-done | bytes 73760 | tf_op jit(solution)/shard_map/ppermute | solution.py:343
  29.4 1.1 %values_kernel.1 = (bf16[128,256]{1,0:T(8,128)(2,1)S(1)}, bf16[128,256]{1,0:T(8,128)(2,1)S(1)}, bf16[512,256]{1,0:T(8,128)(2,1)S(1)}) custom-call(bf16[144,256]{1,0:T(8,128)(2,1)S(1)} %collective-permute-done.refs_0_, bf16[144,256]{1,0:T(8,128)(2,1)S(1)} %collective-permute-done.1.refs_1_, bf16[144,256]{1,0:T(8,128)(2,1)S(1)} %collective-permute-done.2.refs_2_, ...), custom_call_target="tpu_custom_call" | custom-call | flops 1000000 | bytes 1048576 | tf_op jit(solution)/shard_map/values_kernel/pallas_call | solution.py:330
  30.5 0.9 %collective-permute-start.6 = (bf16[128,256]{1,0:T(8,128)(2,1)S(1)}, bf16[128,256]{1,0:T(8,128)(2,1)S(1)}, u32[]{:S(2)}, u32[]{:S(2)}) collective-permute-start(bf16[128,256]{1,0:T(8,128)(2,1)S(1)} %get-tuple-element.42), channel_id=1, source_target_pairs={{0,8},{4,12},{8,0},{12,4},{1,9},{5,13},{9,1},{13,5},{2,10},{6,14},... | collective-permute-start | bytes 196616 | tf_op jit(solution)/shard_map/ppermute | solution.py:343
  31.4 1.8 %collective-permute-start.7 = (bf16[128,256]{1,0:T(8,128)(2,1)S(1)}, bf16[128,256]{1,0:T(8,128)(2,1)S(1)}, u32[]{:S(2)}, u32[]{:S(2)}) collective-permute-start(bf16[128,256]{1,0:T(8,128)(2,1)S(1)} %get-tuple-element.43), channel_id=1, source_target_pairs={{0,12},{4,8},{8,4},{12,0},{1,13},{5,9},{9,5},{13,1},{2,14},{6,10},... | collective-permute-start | bytes 196616 | tf_op jit(solution)/shard_map/ppermute | solution.py:343
  33.4 1.0 %collective-permute-start.8 = (bf16[64,256]{1,0:T(8,128)(2,1)S(1)}, bf16[64,256]{1,0:T(8,128)(2,1)S(1)}, u32[]{:S(2)}, u32[]{:S(2)}) collective-permute-start(bf16[64,256]{1,0:T(8,128)(2,1)S(1)} %get-tuple-element.45), channel_id=1, source_target_pairs={{0,4},{4,0},{8,12},{12,8},{1,5},{5,1},{9,13},{13,9},{2,6},{6,2},{1... | collective-permute-start | bytes 98312 | tf_op jit(solution)/shard_map/ppermute | solution.py:343
  34.4 1.1 %collective-permute-start.9 = (bf16[64,256]{1,0:T(8,128)(2,1)S(1)}, bf16[64,256]{1,0:T(8,128)(2,1)S(1)}, u32[]{:S(2)}, u32[]{:S(2)}) collective-permute-start(bf16[64,256]{1,0:T(8,128)(2,1)S(1)} %get-tuple-element.46), channel_id=1, source_target_pairs={{0,4},{4,0},{8,12},{12,8},{1,5},{5,1},{9,13},{13,9},{2,6},{6,2},{1... | collective-permute-start | bytes 98312 | tf_op jit(solution)/shard_map/ppermute | solution.py:343
  35.5 2.4 %collective-permute-done.8.refs_2_ = bf16[64,256]{1,0:T(8,128)(2,1)S(1)} collective-permute-done((bf16[64,256]{1,0:T(8,128)(2,1)S(1)}, bf16[64,256]{1,0:T(8,128)(2,1)S(1)}, u32[]{:S(2)}, u32[]{:S(2)}) %collective-permute-start.8) | collective-permute-done | bytes 32800 | tf_op jit(solution)/shard_map/ppermute | solution.py:343
  39.4 0.6 %collective-permute-start.10 = (bf16[128,512]{1,0:T(8,128)(2,1)S(1)}, bf16[128,512]{1,0:T(8,128)(2,1)S(1)}, u32[]{:S(2)}, u32[]{:S(2)}) collective-permute-start(bf16[128,512]{1,0:T(8,128)(2,1)S(1)} %get-tuple-element.51), channel_id=1, source_target_pairs={{0,1},{1,0},{2,3},{3,2},{4,5},{5,4},{6,7},{7,6},{8,9},{9,8},{10,11... | collective-permute-start | bytes 393224 | tf_op jit(solution)/shard_map/ppermute | solution.py:343
  40.3 1.6 %collective-permute-start.14 = (bf16[128,512]{1,0:T(8,128)(2,1)S(1)}, bf16[128,512]{1,0:T(8,128)(2,1)S(1)}, u32[]{:S(2)}, u32[]{:S(2)}) collective-permute-start(bf16[128,512]{1,0:T(8,128)(2,1)S(1)} %add_convert_fusion.1), channel_id=1, source_target_pairs={{0,2},{1,3},{2,0},{3,1},{4,6},{5,7},{6,4},{7,5},{8,10},{9,11},{10,... | collective-permute-start | bytes 393224 | tf_op jit(solution)/shard_map/ppermute | solution.py:343
  41.9 0.7 %collective-permute-start.15 = (bf16[128,512]{1,0:T(8,128)(2,1)S(1)}, bf16[128,512]{1,0:T(8,128)(2,1)S(1)}, u32[]{:S(2)}, u32[]{:S(2)}) collective-permute-start(bf16[128,512]{1,0:T(8,128)(2,1)S(1)} %add_convert_fusion.2.refs_6_), channel_id=1, source_target_pairs={{0,2},{1,3},{2,0},{3,1},{4,6},{5,7},{6,4},{7,5},{8,10},{9,11},{10,... | collective-permute-start | bytes 393224 | tf_op jit(solution)/shard_map/ppermute | solution.py:343
  42.6 0.7 %project_kernel.5 = (bf16[128,1024]{1,0:T(8,128)(2,1)S(1)}, bf16[128,1024]{1,0:T(8,128)(2,1)S(1)}) custom-call(bf16[128,256]{1,0:T(8,128)(2,1)S(1)} %collective-permute-done.6.refs_0_, bf16[128,256]{1,0:T(8,128)(2,1)S(1)} %collective-permute-done.7.refs_1_, bf16[64,256]{1,0:T(8,128)(2,1)S(1)} %collective-permute-done.8.refs_2_, ...), custom_call_target="tpu_custom_call" | custom-call | flops 1000000 | bytes 1048576 | tf_op jit(solution)/shard_map/project_kernel/pallas_call | solution.py:330
  43.9 2.8 %collective-permute-done.14 = bf16[128,512]{1,0:T(8,128)(2,1)S(1)} collective-permute-done((bf16[128,512]{1,0:T(8,128)(2,1)S(1)}, bf16[128,512]{1,0:T(8,128)(2,1)S(1)}, u32[]{:S(2)}, u32[]{:S(2)}) %collective-permute-start.14) | collective-permute-done | bytes 131104 | tf_op jit(solution)/shard_map/ppermute | solution.py:343
  46.7 2.0 %collective-permute-done.15 = bf16[128,512]{1,0:T(8,128)(2,1)S(1)} collective-permute-done((bf16[128,512]{1,0:T(8,128)(2,1)S(1)}, bf16[128,512]{1,0:T(8,128)(2,1)S(1)}, u32[]{:S(2)}, u32[]{:S(2)}) %collective-permute-start.15) | collective-permute-done | bytes 131104 | tf_op jit(solution)/shard_map/ppermute | solution.py:343
  48.7 0.8 %add_convert_fusion = bf16[128,1024]{1,0:T(8,128)(2,1)} fusion(bf16[128,1024]{1,0:T(8,128)(2,1)S(1)} %get-tuple-element.52, bf16[64,1024]{1,0:T(8,128)(2,1)S(1)} %collective-permute-done.12, bf16[64,1024]{1,0:T(8,128)(2,1)S(1)} %collective-permute-done.11, bf16[128,512]{1,0:T(8,128)(2,1)S(1)} %collective-permute-done.15, ...), kind=kLoop, calls=%fused_computation | loop fusion | flops 1572864 | bytes 1048576 | tf_op jit(solution)/shard_map/convert_element_type | solution.py:436
  (29 shorter events, 2.8 us)
Async XLA Ops:
  0.0 27.2 %copy-start = (bf16[3,3,1024]{2,1,0:T(4,128)(2,1)S(1)}, bf16[3,3,1024]{2,1,0:T(4,128)(2,1)}, u32[]{:S(2)}) copy-start(bf16[3,3,1024]{2,1,0:T(4,128)(2,1)} %refs_6_.1) | copy-start | bytes 55300
  0.0 29.4 %copy-start.3 = (f32[1024]{0:T(1024)S(1)}, f32[1024]{0:T(1024)}, u32[]{:S(2)}) copy-start(f32[1024]{0:T(1024)} %param.10) | copy-start | bytes 12292
  1.3 11.7 %collective-permute-start.3 = (bf16[384,256]{1,0:T(8,128)(2,1)S(1)}, bf16[384,256]{1,0:T(8,128)(2,1)S(1)}, u32[]{:S(2)}, u32[]{:S(2)}) collective-permute-start(bf16[384,256]{1,0:T(8,128)(2,1)S(1)} %get-tuple-element.34), channel_id=1, source_target_pairs={{0,12},{4,8},{8,4},{12,0},{1,13},{5,9},{9,5},{13,1},{2,14},{6,10},... | collective-permute-start | bytes 589832 | tf_op jit(solution)/shard_map/ppermute | solution.py:343
  6.4 20.8 %collective-permute-start.4 = (bf16[384,256]{1,0:T(8,128)(2,1)S(1)}, bf16[384,256]{1,0:T(8,128)(2,1)S(1)}, u32[]{:S(2)}, u32[]{:S(2)}) collective-permute-start(bf16[384,256]{1,0:T(8,128)(2,1)S(1)} %get-tuple-element.35), channel_id=1, source_target_pairs={{0,8},{4,12},{8,0},{12,4},{1,9},{5,13},{9,1},{13,5},{2,10},{6,14},... | collective-permute-start | bytes 589832 | tf_op jit(solution)/shard_map/ppermute | solution.py:343
  6.4 20.8 %collective-permute-start.5 = (bf16[384,256]{1,0:T(8,128)(2,1)S(1)}, bf16[384,256]{1,0:T(8,128)(2,1)S(1)}, u32[]{:S(2)}, u32[]{:S(2)}) collective-permute-start(bf16[384,256]{1,0:T(8,128)(2,1)S(1)} %get-tuple-element.36), channel_id=1, source_target_pairs={{0,4},{4,0},{8,12},{12,8},{1,5},{5,1},{9,13},{13,9},{2,6},{6,2},{1... | collective-permute-start | bytes 589832 | tf_op jit(solution)/shard_map/ppermute | solution.py:343
  9.2 20.3 %copy-start.1 = (bf16[144,256]{1,0:T(8,128)(2,1)S(1)}, bf16[144,256]{1,0:T(8,128)(2,1)}, u32[]{:S(2)}) copy-start(bf16[144,256]{1,0:T(8,128)(2,1)} %get-tuple-element.33.refs_3_) | copy-start | bytes 221188
  9.2 19.0 %collective-permute-start = (bf16[144,256]{1,0:T(8,128)(2,1)}, bf16[144,256]{1,0:T(8,128)(2,1)S(1)}, u32[]{:S(2)}, u32[]{:S(2)}) collective-permute-start(bf16[144,256]{1,0:T(8,128)(2,1)} %get-tuple-element.30), channel_id=1, source_target_pairs={{0,12},{4,8},{8,4},{12,0},{1,13},{5,9},{9,5},{13,1},{2,14},{6,10},... | collective-permute-start | bytes 221192 | tf_op jit(solution)/shard_map/ppermute | solution.py:343
  13.0 16.4 %collective-permute-start.1 = (bf16[144,256]{1,0:T(8,128)(2,1)}, bf16[144,256]{1,0:T(8,128)(2,1)S(1)}, u32[]{:S(2)}, u32[]{:S(2)}) collective-permute-start(bf16[144,256]{1,0:T(8,128)(2,1)} %get-tuple-element.31), channel_id=1, source_target_pairs={{0,8},{4,12},{8,0},{12,4},{1,9},{5,13},{9,1},{13,5},{2,10},{6,14},... | collective-permute-start | bytes 221192 | tf_op jit(solution)/shard_map/ppermute | solution.py:343
  13.0 16.4 %collective-permute-start.2 = (bf16[144,256]{1,0:T(8,128)(2,1)}, bf16[144,256]{1,0:T(8,128)(2,1)S(1)}, u32[]{:S(2)}, u32[]{:S(2)}) collective-permute-start(bf16[144,256]{1,0:T(8,128)(2,1)} %get-tuple-element.32), channel_id=1, source_target_pairs={{0,4},{4,0},{8,12},{12,8},{1,5},{5,1},{9,13},{13,9},{2,6},{6,2},{1... | collective-permute-start | bytes 221192 | tf_op jit(solution)/shard_map/ppermute | solution.py:343
  21.2 0.7 %copy-start.2 = (bf16[64,128]{1,0:T(8,128)(2,1)S(1)}, bf16[64,128]{1,0:T(8,128)(2,1)}, u32[]{:S(2)}) copy-start(bf16[64,128]{1,0:T(8,128)(2,1)} %filter_ref.1) | copy-start | bytes 49156
  30.5 7.8 %collective-permute-start.6 = (bf16[128,256]{1,0:T(8,128)(2,1)S(1)}, bf16[128,256]{1,0:T(8,128)(2,1)S(1)}, u32[]{:S(2)}, u32[]{:S(2)}) collective-permute-start(bf16[128,256]{1,0:T(8,128)(2,1)S(1)} %get-tuple-element.42), channel_id=1, source_target_pairs={{0,8},{4,12},{8,0},{12,4},{1,9},{5,13},{9,1},{13,5},{2,10},{6,14},... | collective-permute-start | bytes 196616 | tf_op jit(solution)/shard_map/ppermute | solution.py:343
  31.4 7.0 %collective-permute-start.7 = (bf16[128,256]{1,0:T(8,128)(2,1)S(1)}, bf16[128,256]{1,0:T(8,128)(2,1)S(1)}, u32[]{:S(2)}, u32[]{:S(2)}) collective-permute-start(bf16[128,256]{1,0:T(8,128)(2,1)S(1)} %get-tuple-element.43), channel_id=1, source_target_pairs={{0,12},{4,8},{8,4},{12,0},{1,13},{5,9},{9,5},{13,1},{2,14},{6,10},... | collective-permute-start | bytes 196616 | tf_op jit(solution)/shard_map/ppermute | solution.py:343
  33.4 4.5 %collective-permute-start.8 = (bf16[64,256]{1,0:T(8,128)(2,1)S(1)}, bf16[64,256]{1,0:T(8,128)(2,1)S(1)}, u32[]{:S(2)}, u32[]{:S(2)}) collective-permute-start(bf16[64,256]{1,0:T(8,128)(2,1)S(1)} %get-tuple-element.45), channel_id=1, source_target_pairs={{0,4},{4,0},{8,12},{12,8},{1,5},{5,1},{9,13},{13,9},{2,6},{6,2},{1... | collective-permute-start | bytes 98312 | tf_op jit(solution)/shard_map/ppermute | solution.py:343
  34.4 3.9 %collective-permute-start.9 = (bf16[64,256]{1,0:T(8,128)(2,1)S(1)}, bf16[64,256]{1,0:T(8,128)(2,1)S(1)}, u32[]{:S(2)}, u32[]{:S(2)}) collective-permute-start(bf16[64,256]{1,0:T(8,128)(2,1)S(1)} %get-tuple-element.46), channel_id=1, source_target_pairs={{0,4},{4,0},{8,12},{12,8},{1,5},{5,1},{9,13},{13,9},{2,6},{6,2},{1... | collective-permute-start | bytes 98312 | tf_op jit(solution)/shard_map/ppermute | solution.py:343
  38.8 1.4 %collective-permute-start.13 = (bf16[128,512]{1,0:T(8,128)(2,1)S(1)}, bf16[128,512]{1,0:T(8,128)(2,1)S(1)}, u32[]{:S(2)}, u32[]{:S(2)}) collective-permute-start(bf16[128,512]{1,0:T(8,128)(2,1)S(1)} %get-tuple-element.49.refs_6_), channel_id=1, source_target_pairs={{0,1},{1,0},{2,3},{3,2},{4,5},{5,4},{6,7},{7,6},{8,9},{9,8},{10,11... | collective-permute-start | bytes 393224 | tf_op jit(solution)/shard_map/ppermute | solution.py:343
  39.4 2.4 %collective-permute-start.10 = (bf16[128,512]{1,0:T(8,128)(2,1)S(1)}, bf16[128,512]{1,0:T(8,128)(2,1)S(1)}, u32[]{:S(2)}, u32[]{:S(2)}) collective-permute-start(bf16[128,512]{1,0:T(8,128)(2,1)S(1)} %get-tuple-element.51), channel_id=1, source_target_pairs={{0,1},{1,0},{2,3},{3,2},{4,5},{5,4},{6,7},{7,6},{8,9},{9,8},{10,11... | collective-permute-start | bytes 393224 | tf_op jit(solution)/shard_map/ppermute | solution.py:343
  40.3 6.4 %collective-permute-start.14 = (bf16[128,512]{1,0:T(8,128)(2,1)S(1)}, bf16[128,512]{1,0:T(8,128)(2,1)S(1)}, u32[]{:S(2)}, u32[]{:S(2)}) collective-permute-start(bf16[128,512]{1,0:T(8,128)(2,1)S(1)} %add_convert_fusion.1), channel_id=1, source_target_pairs={{0,2},{1,3},{2,0},{3,1},{4,6},{5,7},{6,4},{7,5},{8,10},{9,11},{10,... | collective-permute-start | bytes 393224 | tf_op jit(solution)/shard_map/ppermute | solution.py:343
  41.9 6.8 %collective-permute-start.15 = (bf16[128,512]{1,0:T(8,128)(2,1)S(1)}, bf16[128,512]{1,0:T(8,128)(2,1)S(1)}, u32[]{:S(2)}, u32[]{:S(2)}) collective-permute-start(bf16[128,512]{1,0:T(8,128)(2,1)S(1)} %add_convert_fusion.2.refs_6_), channel_id=1, source_target_pairs={{0,2},{1,3},{2,0},{3,1},{4,6},{5,7},{6,4},{7,5},{8,10},{9,11},{10,... | collective-permute-start | bytes 393224 | tf_op jit(solution)/shard_map/ppermute | solution.py:343
  43.3 5.4 %collective-permute-start.11 = (bf16[64,1024]{1,0:T(8,128)(2,1)S(1)}, bf16[64,1024]{1,0:T(8,128)(2,1)S(1)}, u32[]{:S(2)}, u32[]{:S(2)}) collective-permute-start(bf16[64,1024]{1,0:T(8,128)(2,1)S(1)} %get-tuple-element.55), channel_id=1, source_target_pairs={{0,1},{1,0},{2,3},{3,2},{4,5},{5,4},{6,7},{7,6},{8,9},{9,8},{10,11... | collective-permute-start | bytes 393224 | tf_op jit(solution)/shard_map/ppermute | solution.py:343
  43.5 5.3 %collective-permute-start.12 = (bf16[64,1024]{1,0:T(8,128)(2,1)S(1)}, bf16[64,1024]{1,0:T(8,128)(2,1)S(1)}, u32[]{:S(2)}, u32[]{:S(2)}) collective-permute-start(bf16[64,1024]{1,0:T(8,128)(2,1)S(1)} %get-tuple-element.56), channel_id=1, source_target_pairs={{0,1},{1,0},{2,3},{3,2},{4,5},{5,4},{6,7},{7,6},{8,9},{9,8},{10,11... | collective-permute-start | bytes 393224 | tf_op jit(solution)/shard_map/ppermute | solution.py:343

commit v11 on v10

--- a/solution.py
+++ b/solution.py
@@ -132,24 +132,28 @@
     out_ref[rows : rows + EDGE] = jnp.concatenate(edges, axis=0).astype(jnp.bfloat16)
 
 
-def plain_kernel(inputs_any, queries_any, keys_any, *refs):
-    out_refs, sems = refs[:COUNT], refs[COUNT]
-    rows, own = queries_any.shape[0], out_refs[0].shape[1]
+def plain_copies(sources, out_refs, steps, sems):
+    rows, own = sources[0].shape[0], out_refs[0].shape[1]
     position = lax.axis_index("ctx")
     copies = []
-    for step in ORDER:
+    for step, out_ref in zip(steps, out_refs):
         columns = columns_of(position ^ step, own)
-        for index, source in enumerate((queries_any, keys_any, inputs_any.at[0])):
-            target = out_refs[step].at[index * rows : (index + 1) * rows]
+        for index, source in enumerate(sources):
+            target = out_ref.at[index * rows : (index + 1) * rows]
             copies.append(pltpu.make_async_copy(source.at[:, columns], target, sems.at[len(copies)]))
     for copy in copies:
         copy.start()
-    for copy in copies:
+    return copies
+
+
+def plain_kernel(inputs_any, queries_any, keys_any, *refs):
+    for copy in plain_copies((queries_any, keys_any, inputs_any.at[0]), refs[:2], ORDER[:2], refs[2]):
         copy.wait()
 
 
-def gate_kernel(inputs_any, short_any, *refs):
-    out_refs, (signal_s, short_s, sems) = refs[:COUNT], refs[COUNT:]
+def gate_kernel(inputs_any, short_any, queries_any, keys_any, *refs):
+    out_refs, plain_refs = refs[:COUNT], refs[COUNT : COUNT + 2]
+    signal_s, short_s, sems, plain_sems = refs[COUNT + 2 :]
     own = out_refs[0].shape[1]
     position = lax.axis_index("ctx")
     copies = [
@@ -158,6 +162,7 @@
     ]
     for copy in copies:
         copy.start()
+    plain = plain_copies((queries_any, keys_any, inputs_any.at[0]), plain_refs, ORDER[2:], plain_sems)
     for copy in copies:
         copy.wait()
     for step in ORDER:
@@ -167,6 +172,8 @@
             [short_s[lag, stream : stream + 1, columns].astype(jnp.float32) for lag in range(3)] for stream in (1, 2)
         ]
         write_gate(signals, taps, out_refs[step])
+    for copy in plain:
+        copy.wait()
 
 
 def ready_kernel(filter_ref, weight_any, band_ref, weight_ref, sem):
@@ -232,7 +239,7 @@
     gates, feature_ref = refs[:count], refs[count]
     band_ref, short_ref, gain_ref, weight_ref, total_ref = refs[count + 1 : count + 6]
     third_ref, second_ref, value_ref = refs[count + 6 : count + 9]
-    gates_s, gate_s = refs[count + 9 :]
+    gates_s, gate_s, filtered_s = refs[count + 9 :]
     rows, own = second_ref.shape
     per_group = own * rows // band_ref.shape[0]
     position = lax.axis_index("ctx")
@@ -265,27 +272,25 @@
         head = jnp.where(head_row < 2, jnp.concatenate([fixed, fixed], axis=0), head)
         gate_s[(block + 1) * rows : (block + 1) * rows + 16] = head.astype(jnp.bfloat16)
     gain = gain_ref[:, mine]
-    per_tile = HEAD_DIM // per_group
-    lane = lax.broadcasted_iota(jnp.int32, (rows, 2 * HEAD_DIM), 1) % HEAD_DIM // per_group
-    for tile in range(own // HEAD_DIM):
-        columns = slice(tile * HEAD_DIM, (tile + 1) * HEAD_DIM)
-        for block in range(0, count, 2):
-            windows = [gate_s[other * rows : (other + 2) * rows, columns] for other in (block, block + 1)]
-            mixed = jnp.dot(
-                band_ref[tile * per_tile * rows : (tile + 1) * per_tile * rows],
-                jnp.concatenate(windows, axis=1),
-                preferred_element_type=jnp.float32,
-            )
-            filtered = mixed[:rows]
-            for group in range(1, per_tile):
-                filtered = jnp.where(lane == group, mixed[group * rows : (group + 1) * rows], filtered)
-            for index in range(2):
-                here = slice((block + index) * rows, (block + index + 1) * rows)
-                gate = gate_s[(block + index + 1) * rows : (block + index + 2) * rows, columns].astype(jnp.float32)
-                part = filtered[:, index * HEAD_DIM : (index + 1) * HEAD_DIM]
-                value_ref[here, columns] = (
-                    feature_ref[here, columns] * (part + gain[:, columns] * gate)
-                ).astype(jnp.bfloat16)
+    chunk = 2 * HEAD_DIM // count
+    in_chunk = chunk // per_group
+    lane = lax.broadcasted_iota(jnp.int32, (rows, 2 * HEAD_DIM), 1) % chunk // per_group
+    for part in range(own // chunk):
+        columns = slice(part * chunk, (part + 1) * chunk)
+        windows = [gate_s[block * rows : (block + 2) * rows, columns] for block in range(count)]
+        mixed = jnp.dot(
+            band_ref[part * in_chunk * rows : (part + 1) * in_chunk * rows],
+            jnp.concatenate(windows, axis=1),
+            preferred_element_type=jnp.float32,
+        )
+        filtered = mixed[:rows]
+        for group in range(1, in_chunk):
+            filtered = jnp.where(lane == group, mixed[group * rows : (group + 1) * rows], filtered)
+        for block in range(count):
+            filtered_s[block * rows : (block + 1) * rows, columns] = filtered[:, block * chunk : (block + 1) * chunk]
+    value_ref[...] = (
+        feature_ref[...] * (filtered_s[...] + gain * gate_s[rows:].astype(jnp.float32))
+    ).astype(jnp.bfloat16)
     for step, out_ref in ((3, third_ref), (2, second_ref)):
         mix_rows(position ^ step, weight_ref, total_ref, value_ref, out_ref)
 
@@ -319,7 +324,7 @@
 
 
 VMEM_LIMIT = 40 * 1024 * 1024
-PLAIN_LIMIT = 53 * 1024 * 1024
+PLAIN_LIMIT = 53 * 1024 * 1024 + 400 * 1024
 GATE_LIMIT = 60 * 1024 * 1024
 IN_HBM = pl.BlockSpec(memory_space=pltpu.HBM)
 IN_VMEM = pl.BlockSpec(memory_space=pltpu.VMEM)
@@ -350,26 +355,28 @@
     half = jnp.bfloat16
     piece, window = ((rows, own), half), COUNT * rows
     streamed = jnp.transpose(inputs, (1, 0, 2))
-    plain = run_kernel(
+    far_plain = run_kernel(
         plain_kernel,
         (streamed, queries, key_rows),
-        [((3 * rows, own), half)] * COUNT,
-        [pltpu.SemaphoreType.DMA((3 * COUNT,))],
+        [((3 * rows, own), half)] * 2,
+        [pltpu.SemaphoreType.DMA((6,))],
         [IN_HBM] * 3,
         PLAIN_LIMIT,
     )
-    gates = run_kernel(
+    *gates, near_plain, own_plain = run_kernel(
         gate_kernel,
-        (streamed, short_filter),
-        [((rows + EDGE, own), half)] * COUNT,
+        (streamed, short_filter, queries, key_rows),
+        [((rows + EDGE, own), half)] * COUNT + [((3 * rows, own), half)] * 2,
         [
             pltpu.VMEM((2, rows, channels), half),
             pltpu.VMEM(short_filter.shape, half),
             pltpu.SemaphoreType.DMA((2,)),
+            pltpu.SemaphoreType.DMA((6,)),
         ],
-        [IN_HBM] * 2,
+        [IN_HBM] * 4,
         GATE_LIMIT,
     )
+    plain = [own_plain, near_plain, far_plain[1], far_plain[0]]
     plain = [swapped(plain[step], "ctx", step) for step in ORDER[:3]] + [plain[0]]
     gates = [swapped(gates[step], "ctx", step) for step in ORDER[:3]] + [gates[0]]
     band, weight = run_kernel(
@@ -400,6 +407,7 @@
         [
             pltpu.VMEM((COUNT, rows + EDGE, own), half),
             pltpu.VMEM((window + rows, own), half),
+            pltpu.VMEM((window, own), jnp.float32),
         ],
     )
     third_got, second_got = swapped(third, "ctx", 3), swapped(second, "ctx", 2)

time: 49.8 us -> 49.6 us (level)
  starting transfers between devices: 26 us -> 25.5 us
  transfers between devices with their start and end apart: 16 -> 16, of which waited for: 7 -> 7; matrix products, arithmetic and copies ran while one was open for 0% -> 0% of each run, Pallas kernels for 16% -> 17%
where the time goes in v11:
time: 49.6 us; the launch traced here: 49.3 us
  starting transfers between devices  25.5 us (51%)
  Pallas kernels  11 us (22%)
  waiting for transfers between devices  11 us (22%)
  other arithmetic  0.88 us (2%)
  local copies, waits for them, and re-layouts  0.75 us (2%)
    ppermute x16, starting transfers between devices, swapped(): lax.ppermute(value, axis, [(source, source ^ step) for source in range(la...  25.5 us
    ppermute x16, waiting for transfers between devices, swapped(): lax.ppermute(value, axis, [(source, source ^ step) for source in range(la...  11 us
    pallas_call x9, Pallas kernels, run_kernel(): pl.pallas_call(kernel, out_shape=[jax.ShapeDtypeStruct(shape, dtype) for...  11 us
  transfers between devices with their start and end apart: 16, of which 7 were waited for; matrix products, arithmetic and copies ran while one was open for 0% of the time, Pallas kernels for 17%

profile of v11, /device:TPU:0, one launch (start us, length us, event | category | flops | bytes accessed | tf_op | source)
XLA Modules:
  0.0 49.3 jit_solution(14842268199867300709)
XLA Ops:
  0.0 1.1 %plain_kernel.1 = (bf16[384,256]{1,0:T(8,128)(2,1)S(1)}, bf16[384,256]{1,0:T(8,128)(2,1)S(1)}) custom-call(bf16[3,128,1024]{2,1,0:T(8,128)(2,1)} %bitcast.3, bf16[128,1024]{1,0:T(8,128)(2,1)} %queries_any.3, bf16[128,1024]{1,0:T(8,128)(2,1)} %keys_any.3), custom_call_target="tpu_custom_call" | custom-call | flops 1000000 | bytes 1048576 | tf_op jit(solution)/shard_map/plain_kernel/pallas_call | solution.py:335
  1.1 5.1 %collective-permute-start.3 = (bf16[384,256]{1,0:T(8,128)(2,1)S(1)}, bf16[384,256]{1,0:T(8,128)(2,1)S(1)}, u32[]{:S(2)}, u32[]{:S(2)}) collective-permute-start(bf16[384,256]{1,0:T(8,128)(2,1)S(1)} %get-tuple-element.34), channel_id=1, source_target_pairs={{0,12},{4,8},{8,4},{12,0},{1,13},{5,9},{9,5},{13,1},{2,14},{6,10},... | collective-permute-start | bytes 589832 | tf_op jit(solution)/shard_map/ppermute | solution.py:348
  6.2 2.6 %gate_kernel.1 = (bf16[144,256]{1,0:T(8,128)(2,1)}, bf16[144,256]{1,0:T(8,128)(2,1)}, bf16[144,256]{1,0:T(8,128)(2,1)}, bf16[144,256]{1,0:T(8,128)(2,1)}, bf16[3...) custom-call(bf16[3,128,1024]{2,1,0:T(8,128)(2,1)} %bitcast.4, bf16[3,3,1024]{2,1,0:T(4,128)(2,1)} %refs_6_.1, ...), custom_call_target="tpu_custom_call" | custom-call | flops 1000000 | bytes 1048576 | tf_op jit(solution)/shard_map/gate_kernel/pallas_call | solution.py:335
  8.8 0.7 %collective-permute-start.5 = (bf16[384,256]{1,0:T(8,128)(2,1)}, bf16[384,256]{1,0:T(8,128)(2,1)S(1)}, u32[]{:S(2)}, u32[]{:S(2)}) collective-permute-start(bf16[384,256]{1,0:T(8,128)(2,1)} %get-tuple-element.36), channel_id=1, source_target_pairs={{0,4},{4,0},{8,12},{12,8},{1,5},{5,1},{9,13},{13,9},{2,6},{6,2},{1... | collective-permute-start | bytes 589832 | tf_op jit(solution)/shard_map/ppermute | solution.py:348
  9.5 3.7 %collective-permute-start = (bf16[144,256]{1,0:T(8,128)(2,1)}, bf16[144,256]{1,0:T(8,128)(2,1)S(1)}, u32[]{:S(2)}, u32[]{:S(2)}) collective-permute-start(bf16[144,256]{1,0:T(8,128)(2,1)} %get-tuple-element.30), channel_id=1, source_target_pairs={{0,12},{4,8},{8,4},{12,0},{1,13},{5,9},{9,5},{13,1},{2,14},{6,10},... | collective-permute-start | bytes 221192 | tf_op jit(solution)/shard_map/ppermute | solution.py:348
  13.2 7.8 %collective-permute-start.2 = (bf16[144,256]{1,0:T(8,128)(2,1)}, bf16[144,256]{1,0:T(8,128)(2,1)S(1)}, u32[]{:S(2)}, u32[]{:S(2)}) collective-permute-start(bf16[144,256]{1,0:T(8,128)(2,1)} %get-tuple-element.32), channel_id=1, source_target_pairs={{0,4},{4,0},{8,12},{12,8},{1,5},{5,1},{9,13},{13,9},{2,6},{6,2},{1... | collective-permute-start | bytes 221192 | tf_op jit(solution)/shard_map/ppermute | solution.py:348
  21.0 0.7 %copy-done.3 = bf16[64,128]{1,0:T(8,128)(2,1)S(1)} copy-done((bf16[64,128]{1,0:T(8,128)(2,1)S(1)}, bf16[64,128]{1,0:T(8,128)(2,1)}, u32[]{:S(2)}) %copy-start.3) | copy-done | bytes 16408
  21.7 3.4 %ready_kernel.1 = (bf16[2048,256]{1,0:T(8,128)(2,1)S(1)}, bf16[1024,4096]{1,0:T(8,128)(2,1)S(1)}) custom-call(bf16[64,128]{1,0:T(8,128)(2,1)S(1)} %copy-done.3, bf16[1024,4096]{1,0:T(8,128)(2,1)} %weight_any.1), custom_call_target="tpu_custom_call" | custom-call | flops 1000000 | bytes 1048576 | tf_op jit(solution)/shard_map/ready_kernel/pallas_call | solution.py:335
  25.2 1.8 %collective-permute-done.4.second_ref = bf16[384,256]{1,0:T(8,128)(2,1)S(1)} collective-permute-done((bf16[384,256]{1,0:T(8,128)(2,1)S(1)}, bf16[384,256]{1,0:T(8,128)(2,1)S(1)}, u32[]{:S(2)}, u32[]{:S(2)}) %collective-permute-start.4) | collective-permute-done | bytes 196640 | tf_op jit(solution)/shard_map/ppermute | solution.py:348
  27.0 0.9 %weights_kernel.1 = (bf16[2,512,512]{2,1,0:T(8,128)(2,1)S(1)}, f32[512,128]{1,0:T(8,128)S(1)}, f32[512,256]{1,0:T(8,128)S(1)}) custom-call(bf16[384,256]{1,0:T(8,128)(2,1)S(1)} %collective-permute-done.3.third_ref, bf16[384,256]{1,0:T(8,128)(2,1)S(1)} %collective-permute-done.4.second_ref, bf16[384,256]{1,0:T(8,128)(2,1)S(1)} %collective-permute-done.5.near_ref, ...), custom_call_target="tpu_custom_call" | custom-call | flops 1000000 | bytes 1048576 | tf_op jit(solution)/shard_map/weights_kernel/pallas_call | solution.py:335
  28.0 1.2 %collective-permute-done.1.refs_1_ = bf16[144,256]{1,0:T(8,128)(2,1)S(1)} collective-permute-done((bf16[144,256]{1,0:T(8,128)(2,1)}, bf16[144,256]{1,0:T(8,128)(2,1)S(1)}, u32[]{:S(2)}, u32[]{:S(2)}) %collective-permute-start.1) | collective-permute-done | bytes 73760 | tf_op jit(solution)/shard_map/ppermute | solution.py:348
  29.2 1.1 %values_kernel.1 = (bf16[128,256]{1,0:T(8,128)(2,1)S(1)}, bf16[128,256]{1,0:T(8,128)(2,1)S(1)}, bf16[512,256]{1,0:T(8,128)(2,1)S(1)}) custom-call(bf16[144,256]{1,0:T(8,128)(2,1)S(1)} %collective-permute-done.refs_0_, bf16[144,256]{1,0:T(8,128)(2,1)S(1)} %collective-permute-done.1.refs_1_, bf16[144,256]{1,0:T(8,128)(2,1)S(1)} %collective-permute-done.2.refs_2_, ...), custom_call_target="tpu_custom_call" | custom-call | flops 1000000 | bytes 1048576 | tf_op jit(solution)/shard_map/values_kernel/pallas_call | solution.py:335
  30.3 0.9 %collective-permute-start.6 = (bf16[128,256]{1,0:T(8,128)(2,1)S(1)}, bf16[128,256]{1,0:T(8,128)(2,1)S(1)}, u32[]{:S(2)}, u32[]{:S(2)}) collective-permute-start(bf16[128,256]{1,0:T(8,128)(2,1)S(1)} %get-tuple-element.42), channel_id=1, source_target_pairs={{0,8},{4,12},{8,0},{12,4},{1,9},{5,13},{9,1},{13,5},{2,10},{6,14},... | collective-permute-start | bytes 196616 | tf_op jit(solution)/shard_map/ppermute | solution.py:348
  31.1 1.8 %collective-permute-start.7 = (bf16[128,256]{1,0:T(8,128)(2,1)S(1)}, bf16[128,256]{1,0:T(8,128)(2,1)S(1)}, u32[]{:S(2)}, u32[]{:S(2)}) collective-permute-start(bf16[128,256]{1,0:T(8,128)(2,1)S(1)} %get-tuple-element.43), channel_id=1, source_target_pairs={{0,12},{4,8},{8,4},{12,0},{1,13},{5,9},{9,5},{13,1},{2,14},{6,10},... | collective-permute-start | bytes 196616 | tf_op jit(solution)/shard_map/ppermute | solution.py:348
  33.2 1.0 %collective-permute-start.8 = (bf16[64,256]{1,0:T(8,128)(2,1)S(1)}, bf16[64,256]{1,0:T(8,128)(2,1)S(1)}, u32[]{:S(2)}, u32[]{:S(2)}) collective-permute-start(bf16[64,256]{1,0:T(8,128)(2,1)S(1)} %get-tuple-element.45), channel_id=1, source_target_pairs={{0,4},{4,0},{8,12},{12,8},{1,5},{5,1},{9,13},{13,9},{2,6},{6,2},{1... | collective-permute-start | bytes 98312 | tf_op jit(solution)/shard_map/ppermute | solution.py:348
  34.2 1.1 %collective-permute-start.9 = (bf16[64,256]{1,0:T(8,128)(2,1)S(1)}, bf16[64,256]{1,0:T(8,128)(2,1)S(1)}, u32[]{:S(2)}, u32[]{:S(2)}) collective-permute-start(bf16[64,256]{1,0:T(8,128)(2,1)S(1)} %get-tuple-element.46), channel_id=1, source_target_pairs={{0,4},{4,0},{8,12},{12,8},{1,5},{5,1},{9,13},{13,9},{2,6},{6,2},{1... | collective-permute-start | bytes 98312 | tf_op jit(solution)/shard_map/ppermute | solution.py:348
  35.3 2.4 %collective-permute-done.8.refs_2_ = bf16[64,256]{1,0:T(8,128)(2,1)S(1)} collective-permute-done((bf16[64,256]{1,0:T(8,128)(2,1)S(1)}, bf16[64,256]{1,0:T(8,128)(2,1)S(1)}, u32[]{:S(2)}, u32[]{:S(2)}) %collective-permute-start.8) | collective-permute-done | bytes 32800 | tf_op jit(solution)/shard_map/ppermute | solution.py:348
  39.2 0.5 %collective-permute-start.10 = (bf16[128,512]{1,0:T(8,128)(2,1)S(1)}, bf16[128,512]{1,0:T(8,128)(2,1)S(1)}, u32[]{:S(2)}, u32[]{:S(2)}) collective-permute-start(bf16[128,512]{1,0:T(8,128)(2,1)S(1)} %get-tuple-element.51), channel_id=1, source_target_pairs={{0,1},{1,0},{2,3},{3,2},{4,5},{5,4},{6,7},{7,6},{8,9},{9,8},{10,11... | collective-permute-start | bytes 393224 | tf_op jit(solution)/shard_map/ppermute | solution.py:348
  40.0 1.6 %collective-permute-start.14 = (bf16[128,512]{1,0:T(8,128)(2,1)S(1)}, bf16[128,512]{1,0:T(8,128)(2,1)S(1)}, u32[]{:S(2)}, u32[]{:S(2)}) collective-permute-start(bf16[128,512]{1,0:T(8,128)(2,1)S(1)} %add_convert_fusion.1), channel_id=1, source_target_pairs={{0,2},{1,3},{2,0},{3,1},{4,6},{5,7},{6,4},{7,5},{8,10},{9,11},{10,... | collective-permute-start | bytes 393224 | tf_op jit(solution)/shard_map/ppermute | solution.py:348
  41.6 0.7 %collective-permute-start.15 = (bf16[128,512]{1,0:T(8,128)(2,1)S(1)}, bf16[128,512]{1,0:T(8,128)(2,1)S(1)}, u32[]{:S(2)}, u32[]{:S(2)}) collective-permute-start(bf16[128,512]{1,0:T(8,128)(2,1)S(1)} %add_convert_fusion.2.refs_6_), channel_id=1, source_target_pairs={{0,2},{1,3},{2,0},{3,1},{4,6},{5,7},{6,4},{7,5},{8,10},{9,11},{10,... | collective-permute-start | bytes 393224 | tf_op jit(solution)/shard_map/ppermute | solution.py:348
  42.3 0.7 %project_kernel.5 = (bf16[128,1024]{1,0:T(8,128)(2,1)S(1)}, bf16[128,1024]{1,0:T(8,128)(2,1)S(1)}) custom-call(bf16[128,256]{1,0:T(8,128)(2,1)S(1)} %collective-permute-done.6.refs_0_, bf16[128,256]{1,0:T(8,128)(2,1)S(1)} %collective-permute-done.7.refs_1_, bf16[64,256]{1,0:T(8,128)(2,1)S(1)} %collective-permute-done.8.refs_2_, ...), custom_call_target="tpu_custom_call" | custom-call | flops 1000000 | bytes 1048576 | tf_op jit(solution)/shard_map/project_kernel/pallas_call | solution.py:335
  43.7 2.8 %collective-permute-done.14 = bf16[128,512]{1,0:T(8,128)(2,1)S(1)} collective-permute-done((bf16[128,512]{1,0:T(8,128)(2,1)S(1)}, bf16[128,512]{1,0:T(8,128)(2,1)S(1)}, u32[]{:S(2)}, u32[]{:S(2)}) %collective-permute-start.14) | collective-permute-done | bytes 131104 | tf_op jit(solution)/shard_map/ppermute | solution.py:348
  46.5 2.0 %collective-permute-done.15 = bf16[128,512]{1,0:T(8,128)(2,1)S(1)} collective-permute-done((bf16[128,512]{1,0:T(8,128)(2,1)S(1)}, bf16[128,512]{1,0:T(8,128)(2,1)S(1)}, u32[]{:S(2)}, u32[]{:S(2)}) %collective-permute-start.15) | collective-permute-done | bytes 131104 | tf_op jit(solution)/shard_map/ppermute | solution.py:348
  48.5 0.8 %add_convert_fusion = bf16[128,1024]{1,0:T(8,128)(2,1)} fusion(bf16[128,1024]{1,0:T(8,128)(2,1)S(1)} %get-tuple-element.52, bf16[64,1024]{1,0:T(8,128)(2,1)S(1)} %collective-permute-done.12, bf16[64,1024]{1,0:T(8,128)(2,1)S(1)} %collective-permute-done.11, bf16[128,512]{1,0:T(8,128)(2,1)S(1)} %collective-permute-done.15, ...), kind=kLoop, calls=%fused_computation | loop fusion | flops 1572864 | bytes 1048576 | tf_op jit(solution)/shard_map/convert_element_type | solution.py:444
  (31 shorter events, 2.8 us)
Async XLA Ops:
  0.0 27.0 %copy-start = (bf16[3,3,1024]{2,1,0:T(4,128)(2,1)S(1)}, bf16[3,3,1024]{2,1,0:T(4,128)(2,1)}, u32[]{:S(2)}) copy-start(bf16[3,3,1024]{2,1,0:T(4,128)(2,1)} %refs_6_.1) | copy-start | bytes 55300
  0.0 29.2 %copy-start.4 = (f32[1024]{0:T(1024)S(1)}, f32[1024]{0:T(1024)}, u32[]{:S(2)}) copy-start(f32[1024]{0:T(1024)} %param.10) | copy-start | bytes 12292
  1.1 12.2 %collective-permute-start.3 = (bf16[384,256]{1,0:T(8,128)(2,1)S(1)}, bf16[384,256]{1,0:T(8,128)(2,1)S(1)}, u32[]{:S(2)}, u32[]{:S(2)}) collective-permute-start(bf16[384,256]{1,0:T(8,128)(2,1)S(1)} %get-tuple-element.34), channel_id=1, source_target_pairs={{0,12},{4,8},{8,4},{12,0},{1,13},{5,9},{9,5},{13,1},{2,14},{6,10},... | collective-permute-start | bytes 589832 | tf_op jit(solution)/shard_map/ppermute | solution.py:348
  6.2 20.8 %collective-permute-start.4 = (bf16[384,256]{1,0:T(8,128)(2,1)S(1)}, bf16[384,256]{1,0:T(8,128)(2,1)S(1)}, u32[]{:S(2)}, u32[]{:S(2)}) collective-permute-start(bf16[384,256]{1,0:T(8,128)(2,1)S(1)} %get-tuple-element.35), channel_id=1, source_target_pairs={{0,8},{4,12},{8,0},{12,4},{1,9},{5,13},{9,1},{13,5},{2,10},{6,14},... | collective-permute-start | bytes 589832 | tf_op jit(solution)/shard_map/ppermute | solution.py:348
  8.8 18.3 %copy-start.1 = (bf16[384,256]{1,0:T(8,128)(2,1)S(1)}, bf16[384,256]{1,0:T(8,128)(2,1)}, u32[]{:S(2)}) copy-start(bf16[384,256]{1,0:T(8,128)(2,1)} %get-tuple-element.37.own_ref) | copy-start | bytes 589828
  8.8 20.4 %copy-start.2 = (bf16[144,256]{1,0:T(8,128)(2,1)S(1)}, bf16[144,256]{1,0:T(8,128)(2,1)}, u32[]{:S(2)}) copy-start(bf16[144,256]{1,0:T(8,128)(2,1)} %get-tuple-element.33.refs_3_) | copy-start | bytes 221188
  8.8 18.2 %collective-permute-start.5 = (bf16[384,256]{1,0:T(8,128)(2,1)}, bf16[384,256]{1,0:T(8,128)(2,1)S(1)}, u32[]{:S(2)}, u32[]{:S(2)}) collective-permute-start(bf16[384,256]{1,0:T(8,128)(2,1)} %get-tuple-element.36), channel_id=1, source_target_pairs={{0,4},{4,0},{8,12},{12,8},{1,5},{5,1},{9,13},{13,9},{2,6},{6,2},{1... | collective-permute-start | bytes 589832 | tf_op jit(solution)/shard_map/ppermute | solution.py:348
  9.5 18.5 %collective-permute-start = (bf16[144,256]{1,0:T(8,128)(2,1)}, bf16[144,256]{1,0:T(8,128)(2,1)S(1)}, u32[]{:S(2)}, u32[]{:S(2)}) collective-permute-start(bf16[144,256]{1,0:T(8,128)(2,1)} %get-tuple-element.30), channel_id=1, source_target_pairs={{0,12},{4,8},{8,4},{12,0},{1,13},{5,9},{9,5},{13,1},{2,14},{6,10},... | collective-permute-start | bytes 221192 | tf_op jit(solution)/shard_map/ppermute | solution.py:348
  13.2 16.0 %collective-permute-start.1 = (bf16[144,256]{1,0:T(8,128)(2,1)}, bf16[144,256]{1,0:T(8,128)(2,1)S(1)}, u32[]{:S(2)}, u32[]{:S(2)}) collective-permute-start(bf16[144,256]{1,0:T(8,128)(2,1)} %get-tuple-element.31), channel_id=1, source_target_pairs={{0,8},{4,12},{8,0},{12,4},{1,9},{5,13},{9,1},{13,5},{2,10},{6,14},... | collective-permute-start | bytes 221192 | tf_op jit(solution)/shard_map/ppermute | solution.py:348
  13.2 16.0 %collective-permute-start.2 = (bf16[144,256]{1,0:T(8,128)(2,1)}, bf16[144,256]{1,0:T(8,128)(2,1)S(1)}, u32[]{:S(2)}, u32[]{:S(2)}) collective-permute-start(bf16[144,256]{1,0:T(8,128)(2,1)} %get-tuple-element.32), channel_id=1, source_target_pairs={{0,4},{4,0},{8,12},{12,8},{1,5},{5,1},{9,13},{13,9},{2,6},{6,2},{1... | collective-permute-start | bytes 221192 | tf_op jit(solution)/shard_map/ppermute | solution.py:348
  21.0 0.7 %copy-start.3 = (bf16[64,128]{1,0:T(8,128)(2,1)S(1)}, bf16[64,128]{1,0:T(8,128)(2,1)}, u32[]{:S(2)}) copy-start(bf16[64,128]{1,0:T(8,128)(2,1)} %filter_ref.1) | copy-start | bytes 49156
  30.3 7.8 %collective-permute-start.6 = (bf16[128,256]{1,0:T(8,128)(2,1)S(1)}, bf16[128,256]{1,0:T(8,128)(2,1)S(1)}, u32[]{:S(2)}, u32[]{:S(2)}) collective-permute-start(bf16[128,256]{1,0:T(8,128)(2,1)S(1)} %get-tuple-element.42), channel_id=1, source_target_pairs={{0,8},{4,12},{8,0},{12,4},{1,9},{5,13},{9,1},{13,5},{2,10},{6,14},... | collective-permute-start | bytes 196616 | tf_op jit(solution)/shard_map/ppermute | solution.py:348
  31.1 7.0 %collective-permute-start.7 = (bf16[128,256]{1,0:T(8,128)(2,1)S(1)}, bf16[128,256]{1,0:T(8,128)(2,1)S(1)}, u32[]{:S(2)}, u32[]{:S(2)}) collective-permute-start(bf16[128,256]{1,0:T(8,128)(2,1)S(1)} %get-tuple-element.43), channel_id=1, source_target_pairs={{0,12},{4,8},{8,4},{12,0},{1,13},{5,9},{9,5},{13,1},{2,14},{6,10},... | collective-permute-start | bytes 196616 | tf_op jit(solution)/shard_map/ppermute | solution.py:348
  33.2 4.5 %collective-permute-start.8 = (bf16[64,256]{1,0:T(8,128)(2,1)S(1)}, bf16[64,256]{1,0:T(8,128)(2,1)S(1)}, u32[]{:S(2)}, u32[]{:S(2)}) collective-permute-start(bf16[64,256]{1,0:T(8,128)(2,1)S(1)} %get-tuple-element.45), channel_id=1, source_target_pairs={{0,4},{4,0},{8,12},{12,8},{1,5},{5,1},{9,13},{13,9},{2,6},{6,2},{1... | collective-permute-start | bytes 98312 | tf_op jit(solution)/shard_map/ppermute | solution.py:348
  34.2 3.9 %collective-permute-start.9 = (bf16[64,256]{1,0:T(8,128)(2,1)S(1)}, bf16[64,256]{1,0:T(8,128)(2,1)S(1)}, u32[]{:S(2)}, u32[]{:S(2)}) collective-permute-start(bf16[64,256]{1,0:T(8,128)(2,1)S(1)} %get-tuple-element.46), channel_id=1, source_target_pairs={{0,4},{4,0},{8,12},{12,8},{1,5},{5,1},{9,13},{13,9},{2,6},{6,2},{1... | collective-permute-start | bytes 98312 | tf_op jit(solution)/shard_map/ppermute | solution.py:348
  38.6 1.4 %collective-permute-start.13 = (bf16[128,512]{1,0:T(8,128)(2,1)S(1)}, bf16[128,512]{1,0:T(8,128)(2,1)S(1)}, u32[]{:S(2)}, u32[]{:S(2)}) collective-permute-start(bf16[128,512]{1,0:T(8,128)(2,1)S(1)} %get-tuple-element.49.refs_6_), channel_id=1, source_target_pairs={{0,1},{1,0},{2,3},{3,2},{4,5},{5,4},{6,7},{7,6},{8,9},{9,8},{10,11... | collective-permute-start | bytes 393224 | tf_op jit(solution)/shard_map/ppermute | solution.py:348
  39.2 2.4 %collective-permute-start.10 = (bf16[128,512]{1,0:T(8,128)(2,1)S(1)}, bf16[128,512]{1,0:T(8,128)(2,1)S(1)}, u32[]{:S(2)}, u32[]{:S(2)}) collective-permute-start(bf16[128,512]{1,0:T(8,128)(2,1)S(1)} %get-tuple-element.51), channel_id=1, source_target_pairs={{0,1},{1,0},{2,3},{3,2},{4,5},{5,4},{6,7},{7,6},{8,9},{9,8},{10,11... | collective-permute-start | bytes 393224 | tf_op jit(solution)/shard_map/ppermute | solution.py:348
  40.0 6.4 %collective-permute-start.14 = (bf16[128,512]{1,0:T(8,128)(2,1)S(1)}, bf16[128,512]{1,0:T(8,128)(2,1)S(1)}, u32[]{:S(2)}, u32[]{:S(2)}) collective-permute-start(bf16[128,512]{1,0:T(8,128)(2,1)S(1)} %add_convert_fusion.1), channel_id=1, source_target_pairs={{0,2},{1,3},{2,0},{3,1},{4,6},{5,7},{6,4},{7,5},{8,10},{9,11},{10,... | collective-permute-start | bytes 393224 | tf_op jit(solution)/shard_map/ppermute | solution.py:348
  41.6 6.8 %collective-permute-start.15 = (bf16[128,512]{1,0:T(8,128)(2,1)S(1)}, bf16[128,512]{1,0:T(8,128)(2,1)S(1)}, u32[]{:S(2)}, u32[]{:S(2)}) collective-permute-start(bf16[128,512]{1,0:T(8,128)(2,1)S(1)} %add_convert_fusion.2.refs_6_), channel_id=1, source_target_pairs={{0,2},{1,3},{2,0},{3,1},{4,6},{5,7},{6,4},{7,5},{8,10},{9,11},{10,... | collective-permute-start | bytes 393224 | tf_op jit(solution)/shard_map/ppermute | solution.py:348
  43.1 5.4 %collective-permute-start.11 = (bf16[64,1024]{1,0:T(8,128)(2,1)S(1)}, bf16[64,1024]{1,0:T(8,128)(2,1)S(1)}, u32[]{:S(2)}, u32[]{:S(2)}) collective-permute-start(bf16[64,1024]{1,0:T(8,128)(2,1)S(1)} %get-tuple-element.55), channel_id=1, source_target_pairs={{0,1},{1,0},{2,3},{3,2},{4,5},{5,4},{6,7},{7,6},{8,9},{9,8},{10,11... | collective-permute-start | bytes 393224 | tf_op jit(solution)/shard_map/ppermute | solution.py:348
  43.2 5.3 %collective-permute-start.12 = (bf16[64,1024]{1,0:T(8,128)(2,1)S(1)}, bf16[64,1024]{1,0:T(8,128)(2,1)S(1)}, u32[]{:S(2)}, u32[]{:S(2)}) collective-permute-start(bf16[64,1024]{1,0:T(8,128)(2,1)S(1)} %get-tuple-element.56), channel_id=1, source_target_pairs={{0,1},{1,0},{2,3},{3,2},{4,5},{5,4},{6,7},{7,6},{8,9},{9,8},{10,11... | collective-permute-start | bytes 393224 | tf_op jit(solution)/shard_map/ppermute | solution.py:348

commit v12 on v11

--- a/solution.py
+++ b/solution.py
@@ -9,7 +9,7 @@
 
 HEAD_DIM = 128
 COUNT = 4
-ORDER = (3, 2, 1, 0)
+ORDER = (2, 3, 1, 0)
 EDGE = 16
 
 
@@ -194,11 +194,11 @@
     weights.wait()
 
 
-def weights_kernel(third_ref, second_ref, near_ref, own_ref, short_ref, weight_ref, total_ref, feature_ref, query_s, key_s, signal_s):
+def weights_kernel(second_ref, third_ref, near_ref, own_ref, short_ref, weight_ref, total_ref, feature_ref, query_s, key_s, signal_s):
     count = COUNT
     rows, own = query_s.shape[1:]
     position = lax.axis_index("ctx")
-    for step, given in zip(ORDER, (third_ref, second_ref, near_ref, own_ref)):
+    for step, given in zip(ORDER, (second_ref, third_ref, near_ref, own_ref)):
         query_s[position ^ step] = given[0:rows]
         key_s[columns_of(position ^ step, rows)] = given[rows : 2 * rows]
         signal_s[columns_of(position ^ step, rows)] = given[2 * rows :]
@@ -376,7 +376,7 @@
         [IN_HBM] * 4,
         GATE_LIMIT,
     )
-    plain = [own_plain, near_plain, far_plain[1], far_plain[0]]
+    plain = [own_plain, near_plain, *far_plain]
     plain = [swapped(plain[step], "ctx", step) for step in ORDER[:3]] + [plain[0]]
     gates = [swapped(gates[step], "ctx", step) for step in ORDER[:3]] + [gates[0]]
     band, weight = run_kernel(

time: 49.6 us -> 50.8 us (1.024)
  waiting for transfers between devices: 11 us -> 18.3 us
  starting transfers between devices: 25.5 us -> 19.5 us
    ppermute x16, waiting for transfers between devices: 11 us -> 18.3 us  [swapped(): lax.ppermute(value, axis, [(source, source ^ step) for source in range(la...]
    ppermute x16, starting transfers between devices: 25.5 us -> 19.5 us  [swapped(): lax.ppermute(value, axis, [(source, source ^ step) for source in range(la...]
  transfers between devices with their start and end apart: 16 -> 16, of which waited for: 7 -> 8; matrix products, arithmetic and copies ran while one was open for 0% -> 0% of each run, Pallas kernels for 17% -> 17%
where the time goes in v12:
time: 50.8 us; the launch traced here: 50.5 us
  starting transfers between devices  19.5 us (38%)
  waiting for transfers between devices  18.3 us (36%)
  Pallas kernels  11 us (22%)
  other arithmetic  0.88 us (2%)
  local copies, waits for them, and re-layouts  0.75 us (1%)
    ppermute x16, starting transfers between devices, swapped(): lax.ppermute(value, axis, [(source, source ^ step) for source in range(la...  19.5 us
    ppermute x16, waiting for transfers between devices, swapped(): lax.ppermute(value, axis, [(source, source ^ step) for source in range(la...  18.3 us
    pallas_call x9, Pallas kernels, run_kernel(): pl.pallas_call(kernel, out_shape=[jax.ShapeDtypeStruct(shape, dtype) for...  11 us
  transfers between devices with their start and end apart: 16, of which 8 were waited for; matrix products, arithmetic and copies ran while one was open for 0% of the time, Pallas kernels for 17%

profile of v12, /device:TPU:0, one launch (start us, length us, event | category | flops | bytes accessed | tf_op | source)
XLA Modules:
  0.0 50.5 jit_solution(2995594085990484177)
XLA Ops:
  0.0 1.1 %plain_kernel.1 = (bf16[384,256]{1,0:T(8,128)(2,1)S(1)}, bf16[384,256]{1,0:T(8,128)(2,1)S(1)}) custom-call(bf16[3,128,1024]{2,1,0:T(8,128)(2,1)} %bitcast.3, bf16[128,1024]{1,0:T(8,128)(2,1)} %queries_any.3, bf16[128,1024]{1,0:T(8,128)(2,1)} %keys_any.3), custom_call_target="tpu_custom_call" | custom-call | flops 1000000 | bytes 1048576 | tf_op jit(solution)/shard_map/plain_kernel/pallas_call | solution.py:335
  1.1 4.1 %collective-permute-start.3 = (bf16[384,256]{1,0:T(8,128)(2,1)S(1)}, bf16[384,256]{1,0:T(8,128)(2,1)S(1)}, u32[]{:S(2)}, u32[]{:S(2)}) collective-permute-start(bf16[384,256]{1,0:T(8,128)(2,1)S(1)} %get-tuple-element.34), channel_id=1, source_target_pairs={{0,8},{4,12},{8,0},{12,4},{1,9},{5,13},{9,1},{13,5},{2,10},{6,14},... | collective-permute-start | bytes 589832 | tf_op jit(solution)/shard_map/ppermute | solution.py:348
  5.2 1.3 %collective-permute-start.4 = (bf16[384,256]{1,0:T(8,128)(2,1)S(1)}, bf16[384,256]{1,0:T(8,128)(2,1)S(1)}, u32[]{:S(2)}, u32[]{:S(2)}) collective-permute-start(bf16[384,256]{1,0:T(8,128)(2,1)S(1)} %get-tuple-element.35), channel_id=1, source_target_pairs={{0,12},{4,8},{8,4},{12,0},{1,13},{5,9},{9,5},{13,1},{2,14},{6,10},... | collective-permute-start | bytes 589832 | tf_op jit(solution)/shard_map/ppermute | solution.py:348
  6.5 2.6 %gate_kernel.1 = (bf16[144,256]{1,0:T(8,128)(2,1)}, bf16[144,256]{1,0:T(8,128)(2,1)}, bf16[144,256]{1,0:T(8,128)(2,1)}, bf16[144,256]{1,0:T(8,128)(2,1)}, bf16[3...) custom-call(bf16[3,128,1024]{2,1,0:T(8,128)(2,1)} %bitcast.4, bf16[3,3,1024]{2,1,0:T(4,128)(2,1)} %refs_6_.1, ...), custom_call_target="tpu_custom_call" | custom-call | flops 1000000 | bytes 1048576 | tf_op jit(solution)/shard_map/gate_kernel/pallas_call | solution.py:335
  9.4 2.8 %collective-permute-start = (bf16[144,256]{1,0:T(8,128)(2,1)}, bf16[144,256]{1,0:T(8,128)(2,1)S(1)}, u32[]{:S(2)}, u32[]{:S(2)}) collective-permute-start(bf16[144,256]{1,0:T(8,128)(2,1)} %get-tuple-element.30), channel_id=1, source_target_pairs={{0,8},{4,12},{8,0},{12,4},{1,9},{5,13},{9,1},{13,5},{2,10},{6,14},... | collective-permute-start | bytes 221192 | tf_op jit(solution)/shard_map/ppermute | solution.py:348
  12.2 1.3 %collective-permute-start.1 = (bf16[144,256]{1,0:T(8,128)(2,1)}, bf16[144,256]{1,0:T(8,128)(2,1)S(1)}, u32[]{:S(2)}, u32[]{:S(2)}) collective-permute-start(bf16[144,256]{1,0:T(8,128)(2,1)} %get-tuple-element.31), channel_id=1, source_target_pairs={{0,12},{4,8},{8,4},{12,0},{1,13},{5,9},{9,5},{13,1},{2,14},{6,10},... | collective-permute-start | bytes 221192 | tf_op jit(solution)/shard_map/ppermute | solution.py:348
  13.6 6.6 %collective-permute-done.3.second_ref = bf16[384,256]{1,0:T(8,128)(2,1)S(1)} collective-permute-done((bf16[384,256]{1,0:T(8,128)(2,1)S(1)}, bf16[384,256]{1,0:T(8,128)(2,1)S(1)}, u32[]{:S(2)}, u32[]{:S(2)}) %collective-permute-start.3) | collective-permute-done | bytes 196640 | tf_op jit(solution)/shard_map/ppermute | solution.py:348
  20.2 0.7 %copy-done.3 = bf16[64,128]{1,0:T(8,128)(2,1)S(1)} copy-done((bf16[64,128]{1,0:T(8,128)(2,1)S(1)}, bf16[64,128]{1,0:T(8,128)(2,1)}, u32[]{:S(2)}) %copy-start.3) | copy-done | bytes 16408
  21.0 3.4 %ready_kernel.1 = (bf16[2048,256]{1,0:T(8,128)(2,1)S(1)}, bf16[1024,4096]{1,0:T(8,128)(2,1)S(1)}) custom-call(bf16[64,128]{1,0:T(8,128)(2,1)S(1)} %copy-done.3, bf16[1024,4096]{1,0:T(8,128)(2,1)} %weight_any.1), custom_call_target="tpu_custom_call" | custom-call | flops 1000000 | bytes 1048576 | tf_op jit(solution)/shard_map/ready_kernel/pallas_call | solution.py:335
  24.5 0.9 %weights_kernel.1 = (bf16[2,512,512]{2,1,0:T(8,128)(2,1)S(1)}, f32[512,128]{1,0:T(8,128)S(1)}, f32[512,256]{1,0:T(8,128)S(1)}) custom-call(bf16[384,256]{1,0:T(8,128)(2,1)S(1)} %collective-permute-done.3.second_ref, bf16[384,256]{1,0:T(8,128)(2,1)S(1)} %collective-permute-done.4.third_ref, bf16[384,256]{1,0:T(8,128)(2,1)S(1)} %collective-permute-done.5.near_ref, ...), custom_call_target="tpu_custom_call" | custom-call | flops 1000000 | bytes 1048576 | tf_op jit(solution)/shard_map/weights_kernel/pallas_call | solution.py:335
  25.4 2.9 %collective-permute-done.refs_0_ = bf16[144,256]{1,0:T(8,128)(2,1)S(1)} collective-permute-done((bf16[144,256]{1,0:T(8,128)(2,1)}, bf16[144,256]{1,0:T(8,128)(2,1)S(1)}, u32[]{:S(2)}, u32[]{:S(2)}) %collective-permute-start) | collective-permute-done | bytes 73760 | tf_op jit(solution)/shard_map/ppermute | solution.py:348
  28.3 1.1 %values_kernel.1 = (bf16[128,256]{1,0:T(8,128)(2,1)S(1)}, bf16[128,256]{1,0:T(8,128)(2,1)S(1)}, bf16[512,256]{1,0:T(8,128)(2,1)S(1)}) custom-call(bf16[144,256]{1,0:T(8,128)(2,1)S(1)} %collective-permute-done.refs_0_, bf16[144,256]{1,0:T(8,128)(2,1)S(1)} %collective-permute-done.1.refs_1_, bf16[144,256]{1,0:T(8,128)(2,1)S(1)} %collective-permute-done.2.refs_2_, ...), custom_call_target="tpu_custom_call" | custom-call | flops 1000000 | bytes 1048576 | tf_op jit(solution)/shard_map/values_kernel/pallas_call | solution.py:335
  29.4 3.5 %collective-permute-start.6 = (bf16[128,256]{1,0:T(8,128)(2,1)S(1)}, bf16[128,256]{1,0:T(8,128)(2,1)S(1)}, u32[]{:S(2)}, u32[]{:S(2)}) collective-permute-start(bf16[128,256]{1,0:T(8,128)(2,1)S(1)} %get-tuple-element.42), channel_id=1, source_target_pairs={{0,8},{4,12},{8,0},{12,4},{1,9},{5,13},{9,1},{13,5},{2,10},{6,14},... | collective-permute-start | bytes 196616 | tf_op jit(solution)/shard_map/ppermute | solution.py:348
  32.9 0.5 %collective-permute-start.7 = (bf16[128,256]{1,0:T(8,128)(2,1)S(1)}, bf16[128,256]{1,0:T(8,128)(2,1)S(1)}, u32[]{:S(2)}, u32[]{:S(2)}) collective-permute-start(bf16[128,256]{1,0:T(8,128)(2,1)S(1)} %get-tuple-element.43), channel_id=1, source_target_pairs={{0,12},{4,8},{8,4},{12,0},{1,13},{5,9},{9,5},{13,1},{2,14},{6,10},... | collective-permute-start | bytes 196616 | tf_op jit(solution)/shard_map/ppermute | solution.py:348
  33.9 1.9 %collective-permute-start.9 = (bf16[64,256]{1,0:T(8,128)(2,1)S(1)}, bf16[64,256]{1,0:T(8,128)(2,1)S(1)}, u32[]{:S(2)}, u32[]{:S(2)}) collective-permute-start(bf16[64,256]{1,0:T(8,128)(2,1)S(1)} %get-tuple-element.46), channel_id=1, source_target_pairs={{0,4},{4,0},{8,12},{12,8},{1,5},{5,1},{9,13},{13,9},{2,6},{6,2},{1... | collective-permute-start | bytes 98312 | tf_op jit(solution)/shard_map/ppermute | solution.py:348
  35.8 3.1 %collective-permute-done.8.refs_2_ = bf16[64,256]{1,0:T(8,128)(2,1)S(1)} collective-permute-done((bf16[64,256]{1,0:T(8,128)(2,1)S(1)}, bf16[64,256]{1,0:T(8,128)(2,1)S(1)}, u32[]{:S(2)}, u32[]{:S(2)}) %collective-permute-start.8) | collective-permute-done | bytes 32800 | tf_op jit(solution)/shard_map/ppermute | solution.py:348
  39.9 0.5 project_kernel.4
  40.4 0.6 %collective-permute-start.10 = (bf16[128,512]{1,0:T(8,128)(2,1)S(1)}, bf16[128,512]{1,0:T(8,128)(2,1)S(1)}, u32[]{:S(2)}, u32[]{:S(2)}) collective-permute-start(bf16[128,512]{1,0:T(8,128)(2,1)S(1)} %get-tuple-element.51), channel_id=1, source_target_pairs={{0,1},{1,0},{2,3},{3,2},{4,5},{5,4},{6,7},{7,6},{8,9},{9,8},{10,11... | collective-permute-start | bytes 393224 | tf_op jit(solution)/shard_map/ppermute | solution.py:348
  41.3 1.6 %collective-permute-start.14 = (bf16[128,512]{1,0:T(8,128)(2,1)S(1)}, bf16[128,512]{1,0:T(8,128)(2,1)S(1)}, u32[]{:S(2)}, u32[]{:S(2)}) collective-permute-start(bf16[128,512]{1,0:T(8,128)(2,1)S(1)} %add_convert_fusion.1), channel_id=1, source_target_pairs={{0,2},{1,3},{2,0},{3,1},{4,6},{5,7},{6,4},{7,5},{8,10},{9,11},{10,... | collective-permute-start | bytes 393224 | tf_op jit(solution)/shard_map/ppermute | solution.py:348
  42.9 0.7 %collective-permute-start.15 = (bf16[128,512]{1,0:T(8,128)(2,1)S(1)}, bf16[128,512]{1,0:T(8,128)(2,1)S(1)}, u32[]{:S(2)}, u32[]{:S(2)}) collective-permute-start(bf16[128,512]{1,0:T(8,128)(2,1)S(1)} %add_convert_fusion.2.refs_6_), channel_id=1, source_target_pairs={{0,2},{1,3},{2,0},{3,1},{4,6},{5,7},{6,4},{7,5},{8,10},{9,11},{10,... | collective-permute-start | bytes 393224 | tf_op jit(solution)/shard_map/ppermute | solution.py:348
  43.5 0.7 %project_kernel.5 = (bf16[128,1024]{1,0:T(8,128)(2,1)S(1)}, bf16[128,1024]{1,0:T(8,128)(2,1)S(1)}) custom-call(bf16[128,256]{1,0:T(8,128)(2,1)S(1)} %collective-permute-done.6.refs_0_, bf16[128,256]{1,0:T(8,128)(2,1)S(1)} %collective-permute-done.7.refs_1_, bf16[64,256]{1,0:T(8,128)(2,1)S(1)} %collective-permute-done.8.refs_2_, ...), custom_call_target="tpu_custom_call" | custom-call | flops 1000000 | bytes 1048576 | tf_op jit(solution)/shard_map/project_kernel/pallas_call | solution.py:335
  44.9 2.8 %collective-permute-done.14 = bf16[128,512]{1,0:T(8,128)(2,1)S(1)} collective-permute-done((bf16[128,512]{1,0:T(8,128)(2,1)S(1)}, bf16[128,512]{1,0:T(8,128)(2,1)S(1)}, u32[]{:S(2)}, u32[]{:S(2)}) %collective-permute-start.14) | collective-permute-done | bytes 131104 | tf_op jit(solution)/shard_map/ppermute | solution.py:348
  47.7 2.0 %collective-permute-done.15 = bf16[128,512]{1,0:T(8,128)(2,1)S(1)} collective-permute-done((bf16[128,512]{1,0:T(8,128)(2,1)S(1)}, bf16[128,512]{1,0:T(8,128)(2,1)S(1)}, u32[]{:S(2)}, u32[]{:S(2)}) %collective-permute-start.15) | collective-permute-done | bytes 131104 | tf_op jit(solution)/shard_map/ppermute | solution.py:348
  49.7 0.8 %add_convert_fusion = bf16[128,1024]{1,0:T(8,128)(2,1)} fusion(bf16[128,1024]{1,0:T(8,128)(2,1)S(1)} %get-tuple-element.52, bf16[64,1024]{1,0:T(8,128)(2,1)S(1)} %collective-permute-done.12, bf16[64,1024]{1,0:T(8,128)(2,1)S(1)} %collective-permute-done.11, bf16[128,512]{1,0:T(8,128)(2,1)S(1)} %collective-permute-done.15, ...), kind=kLoop, calls=%fused_computation | loop fusion | flops 1572864 | bytes 1048576 | tf_op jit(solution)/shard_map/convert_element_type | solution.py:444
  (31 shorter events, 2.8 us)
Async XLA Ops:
  0.0 24.5 %copy-start = (bf16[3,3,1024]{2,1,0:T(4,128)(2,1)S(1)}, bf16[3,3,1024]{2,1,0:T(4,128)(2,1)}, u32[]{:S(2)}) copy-start(bf16[3,3,1024]{2,1,0:T(4,128)(2,1)} %refs_6_.1) | copy-start | bytes 55300
  0.0 28.3 %copy-start.4 = (f32[1024]{0:T(1024)S(1)}, f32[1024]{0:T(1024)}, u32[]{:S(2)}) copy-start(f32[1024]{0:T(1024)} %param.10) | copy-start | bytes 12292
  1.1 19.1 %collective-permute-start.3 = (bf16[384,256]{1,0:T(8,128)(2,1)S(1)}, bf16[384,256]{1,0:T(8,128)(2,1)S(1)}, u32[]{:S(2)}, u32[]{:S(2)}) collective-permute-start(bf16[384,256]{1,0:T(8,128)(2,1)S(1)} %get-tuple-element.34), channel_id=1, source_target_pairs={{0,8},{4,12},{8,0},{12,4},{1,9},{5,13},{9,1},{13,5},{2,10},{6,14},... | collective-permute-start | bytes 589832 | tf_op jit(solution)/shard_map/ppermute | solution.py:348
  5.2 19.2 %collective-permute-start.4 = (bf16[384,256]{1,0:T(8,128)(2,1)S(1)}, bf16[384,256]{1,0:T(8,128)(2,1)S(1)}, u32[]{:S(2)}, u32[]{:S(2)}) collective-permute-start(bf16[384,256]{1,0:T(8,128)(2,1)S(1)} %get-tuple-element.35), channel_id=1, source_target_pairs={{0,12},{4,8},{8,4},{12,0},{1,13},{5,9},{9,5},{13,1},{2,14},{6,10},... | collective-permute-start | bytes 589832 | tf_op jit(solution)/shard_map/ppermute | solution.py:348
  9.1 15.4 %copy-start.1 = (bf16[384,256]{1,0:T(8,128)(2,1)S(1)}, bf16[384,256]{1,0:T(8,128)(2,1)}, u32[]{:S(2)}) copy-start(bf16[384,256]{1,0:T(8,128)(2,1)} %get-tuple-element.37.own_ref) | copy-start | bytes 589828
  9.1 19.2 %copy-start.2 = (bf16[144,256]{1,0:T(8,128)(2,1)S(1)}, bf16[144,256]{1,0:T(8,128)(2,1)}, u32[]{:S(2)}) copy-start(bf16[144,256]{1,0:T(8,128)(2,1)} %get-tuple-element.33.refs_3_) | copy-start | bytes 221188
  9.1 15.3 %collective-permute-start.5 = (bf16[384,256]{1,0:T(8,128)(2,1)}, bf16[384,256]{1,0:T(8,128)(2,1)S(1)}, u32[]{:S(2)}, u32[]{:S(2)}) collective-permute-start(bf16[384,256]{1,0:T(8,128)(2,1)} %get-tuple-element.36), channel_id=1, source_target_pairs={{0,4},{4,0},{8,12},{12,8},{1,5},{5,1},{9,13},{13,9},{2,6},{6,2},{1... | collective-permute-start | bytes 589832 | tf_op jit(solution)/shard_map/ppermute | solution.py:348
  9.4 18.9 %collective-permute-start = (bf16[144,256]{1,0:T(8,128)(2,1)}, bf16[144,256]{1,0:T(8,128)(2,1)S(1)}, u32[]{:S(2)}, u32[]{:S(2)}) collective-permute-start(bf16[144,256]{1,0:T(8,128)(2,1)} %get-tuple-element.30), channel_id=1, source_target_pairs={{0,8},{4,12},{8,0},{12,4},{1,9},{5,13},{9,1},{13,5},{2,10},{6,14},... | collective-permute-start | bytes 221192 | tf_op jit(solution)/shard_map/ppermute | solution.py:348
  12.2 16.1 %collective-permute-start.1 = (bf16[144,256]{1,0:T(8,128)(2,1)}, bf16[144,256]{1,0:T(8,128)(2,1)S(1)}, u32[]{:S(2)}, u32[]{:S(2)}) collective-permute-start(bf16[144,256]{1,0:T(8,128)(2,1)} %get-tuple-element.31), channel_id=1, source_target_pairs={{0,12},{4,8},{8,4},{12,0},{1,13},{5,9},{9,5},{13,1},{2,14},{6,10},... | collective-permute-start | bytes 221192 | tf_op jit(solution)/shard_map/ppermute | solution.py:348
  20.2 8.1 %collective-permute-start.2 = (bf16[144,256]{1,0:T(8,128)(2,1)}, bf16[144,256]{1,0:T(8,128)(2,1)S(1)}, u32[]{:S(2)}, u32[]{:S(2)}) collective-permute-start(bf16[144,256]{1,0:T(8,128)(2,1)} %get-tuple-element.32), channel_id=1, source_target_pairs={{0,4},{4,0},{8,12},{12,8},{1,5},{5,1},{9,13},{13,9},{2,6},{6,2},{1... | collective-permute-start | bytes 221192 | tf_op jit(solution)/shard_map/ppermute | solution.py:348
  20.2 0.7 %copy-start.3 = (bf16[64,128]{1,0:T(8,128)(2,1)S(1)}, bf16[64,128]{1,0:T(8,128)(2,1)}, u32[]{:S(2)}) copy-start(bf16[64,128]{1,0:T(8,128)(2,1)} %filter_ref.1) | copy-start | bytes 49156
  29.4 10.0 %collective-permute-start.6 = (bf16[128,256]{1,0:T(8,128)(2,1)S(1)}, bf16[128,256]{1,0:T(8,128)(2,1)S(1)}, u32[]{:S(2)}, u32[]{:S(2)}) collective-permute-start(bf16[128,256]{1,0:T(8,128)(2,1)S(1)} %get-tuple-element.42), channel_id=1, source_target_pairs={{0,8},{4,12},{8,0},{12,4},{1,9},{5,13},{9,1},{13,5},{2,10},{6,14},... | collective-permute-start | bytes 196616 | tf_op jit(solution)/shard_map/ppermute | solution.py:348
  32.9 6.5 %collective-permute-start.7 = (bf16[128,256]{1,0:T(8,128)(2,1)S(1)}, bf16[128,256]{1,0:T(8,128)(2,1)S(1)}, u32[]{:S(2)}, u32[]{:S(2)}) collective-permute-start(bf16[128,256]{1,0:T(8,128)(2,1)S(1)} %get-tuple-element.43), channel_id=1, source_target_pairs={{0,12},{4,8},{8,4},{12,0},{1,13},{5,9},{9,5},{13,1},{2,14},{6,10},... | collective-permute-start | bytes 196616 | tf_op jit(solution)/shard_map/ppermute | solution.py:348
  33.7 5.2 %collective-permute-start.8 = (bf16[64,256]{1,0:T(8,128)(2,1)S(1)}, bf16[64,256]{1,0:T(8,128)(2,1)S(1)}, u32[]{:S(2)}, u32[]{:S(2)}) collective-permute-start(bf16[64,256]{1,0:T(8,128)(2,1)S(1)} %get-tuple-element.45), channel_id=1, source_target_pairs={{0,4},{4,0},{8,12},{12,8},{1,5},{5,1},{9,13},{13,9},{2,6},{6,2},{1... | collective-permute-start | bytes 98312 | tf_op jit(solution)/shard_map/ppermute | solution.py:348
  33.9 5.5 %collective-permute-start.9 = (bf16[64,256]{1,0:T(8,128)(2,1)S(1)}, bf16[64,256]{1,0:T(8,128)(2,1)S(1)}, u32[]{:S(2)}, u32[]{:S(2)}) collective-permute-start(bf16[64,256]{1,0:T(8,128)(2,1)S(1)} %get-tuple-element.46), channel_id=1, source_target_pairs={{0,4},{4,0},{8,12},{12,8},{1,5},{5,1},{9,13},{13,9},{2,6},{6,2},{1... | collective-permute-start | bytes 98312 | tf_op jit(solution)/shard_map/ppermute | solution.py:348
  39.8 1.4 %collective-permute-start.13 = (bf16[128,512]{1,0:T(8,128)(2,1)S(1)}, bf16[128,512]{1,0:T(8,128)(2,1)S(1)}, u32[]{:S(2)}, u32[]{:S(2)}) collective-permute-start(bf16[128,512]{1,0:T(8,128)(2,1)S(1)} %get-tuple-element.49.refs_6_), channel_id=1, source_target_pairs={{0,1},{1,0},{2,3},{3,2},{4,5},{5,4},{6,7},{7,6},{8,9},{9,8},{10,11... | collective-permute-start | bytes 393224 | tf_op jit(solution)/shard_map/ppermute | solution.py:348
  40.4 2.4 %collective-permute-start.10 = (bf16[128,512]{1,0:T(8,128)(2,1)S(1)}, bf16[128,512]{1,0:T(8,128)(2,1)S(1)}, u32[]{:S(2)}, u32[]{:S(2)}) collective-permute-start(bf16[128,512]{1,0:T(8,128)(2,1)S(1)} %get-tuple-element.51), channel_id=1, source_target_pairs={{0,1},{1,0},{2,3},{3,2},{4,5},{5,4},{6,7},{7,6},{8,9},{9,8},{10,11... | collective-permute-start | bytes 393224 | tf_op jit(solution)/shard_map/ppermute | solution.py:348
  41.3 6.4 %collective-permute-start.14 = (bf16[128,512]{1,0:T(8,128)(2,1)S(1)}, bf16[128,512]{1,0:T(8,128)(2,1)S(1)}, u32[]{:S(2)}, u32[]{:S(2)}) collective-permute-start(bf16[128,512]{1,0:T(8,128)(2,1)S(1)} %add_convert_fusion.1), channel_id=1, source_target_pairs={{0,2},{1,3},{2,0},{3,1},{4,6},{5,7},{6,4},{7,5},{8,10},{9,11},{10,... | collective-permute-start | bytes 393224 | tf_op jit(solution)/shard_map/ppermute | solution.py:348
  42.9 6.8 %collective-permute-start.15 = (bf16[128,512]{1,0:T(8,128)(2,1)S(1)}, bf16[128,512]{1,0:T(8,128)(2,1)S(1)}, u32[]{:S(2)}, u32[]{:S(2)}) collective-permute-start(bf16[128,512]{1,0:T(8,128)(2,1)S(1)} %add_convert_fusion.2.refs_6_), channel_id=1, source_target_pairs={{0,2},{1,3},{2,0},{3,1},{4,6},{5,7},{6,4},{7,5},{8,10},{9,11},{10,... | collective-permute-start | bytes 393224 | tf_op jit(solution)/shard_map/ppermute | solution.py:348
  44.3 5.4 %collective-permute-start.11 = (bf16[64,1024]{1,0:T(8,128)(2,1)S(1)}, bf16[64,1024]{1,0:T(8,128)(2,1)S(1)}, u32[]{:S(2)}, u32[]{:S(2)}) collective-permute-start(bf16[64,1024]{1,0:T(8,128)(2,1)S(1)} %get-tuple-element.55), channel_id=1, source_target_pairs={{0,1},{1,0},{2,3},{3,2},{4,5},{5,4},{6,7},{7,6},{8,9},{9,8},{10,11... | collective-permute-start | bytes 393224 | tf_op jit(solution)/shard_map/ppermute | solution.py:348
  44.4 5.3 %collective-permute-start.12 = (bf16[64,1024]{1,0:T(8,128)(2,1)S(1)}, bf16[64,1024]{1,0:T(8,128)(2,1)S(1)}, u32[]{:S(2)}, u32[]{:S(2)}) collective-permute-start(bf16[64,1024]{1,0:T(8,128)(2,1)S(1)} %get-tuple-element.56), channel_id=1, source_target_pairs={{0,1},{1,0},{2,3},{3,2},{4,5},{5,4},{6,7},{7,6},{8,9},{9,8},{10,11... | collective-permute-start | bytes 393224 | tf_op jit(solution)/shard_map/ppermute | solution.py:348

commit v13 on v11

--- a/solution.py
+++ b/solution.py
@@ -10,6 +10,7 @@
 HEAD_DIM = 128
 COUNT = 4
 ORDER = (3, 2, 1, 0)
+GATE_ORDER = (2, 3, 1, 0)
 EDGE = 16
 
 
@@ -244,7 +245,7 @@
     per_group = own * rows // band_ref.shape[0]
     position = lax.axis_index("ctx")
     mine = columns_of(position, own)
-    for step, gate in zip(ORDER, gates):
+    for step, gate in zip(GATE_ORDER, gates):
         gates_s[position ^ step] = gate[...]
     taps = [
         [short_ref[lag, stream : stream + 1, mine].astype(jnp.float32) for lag in range(3)] for stream in range(3)
@@ -378,7 +379,7 @@
     )
     plain = [own_plain, near_plain, far_plain[1], far_plain[0]]
     plain = [swapped(plain[step], "ctx", step) for step in ORDER[:3]] + [plain[0]]
-    gates = [swapped(gates[step], "ctx", step) for step in ORDER[:3]] + [gates[0]]
+    gates = [swapped(gates[step], "ctx", step) for step in GATE_ORDER[:3]] + [gates[0]]
     band, weight = run_kernel(
         ready_kernel,
         (long_filter, out_weight),

time: 49.6 us -> 50.1 us (1.010)
  starting transfers between devices: 25.5 us -> 26.6 us
  waiting for transfers between devices: 11 us -> 10.4 us
    ppermute x16, starting transfers between devices: 25.5 us -> 26.6 us  [swapped(): lax.ppermute(value, axis, [(source, source ^ step) for source in range(la...]
    ppermute x16, waiting for transfers between devices: 11 us -> 10.4 us  [swapped(): lax.ppermute(value, axis, [(source, source ^ step) for source in range(la...]
where the time goes in v13:
time: 50.1 us; the launch traced here: 49.8 us
  starting transfers between devices  26.6 us (53%)
  Pallas kernels  11 us (22%)
  waiting for transfers between devices  10.4 us (21%)
  other arithmetic  0.88 us (2%)
  local copies, waits for them, and re-layouts  0.75 us (1%)
    ppermute x16, starting transfers between devices, swapped(): lax.ppermute(value, axis, [(source, source ^ step) for source in range(la...  26.6 us
    pallas_call x9, Pallas kernels, run_kernel(): pl.pallas_call(kernel, out_shape=[jax.ShapeDtypeStruct(shape, dtype) for...  11 us
    ppermute x16, waiting for transfers between devices, swapped(): lax.ppermute(value, axis, [(source, source ^ step) for source in range(la...  10.4 us
  transfers between devices with their start and end apart: 16, of which 7 were waited for; matrix products, arithmetic and copies ran while one was open for 0% of the time, Pallas kernels for 17%

profile of v13, /device:TPU:0, one launch (start us, length us, event | category | flops | bytes accessed | tf_op | source)
XLA Modules:
  0.0 49.8 jit_solution(17919664723755967656)
XLA Ops:
  0.0 1.1 %plain_kernel.1 = (bf16[384,256]{1,0:T(8,128)(2,1)S(1)}, bf16[384,256]{1,0:T(8,128)(2,1)S(1)}) custom-call(bf16[3,128,1024]{2,1,0:T(8,128)(2,1)} %bitcast.3, bf16[128,1024]{1,0:T(8,128)(2,1)} %queries_any.3, bf16[128,1024]{1,0:T(8,128)(2,1)} %keys_any.3), custom_call_target="tpu_custom_call" | custom-call | flops 1000000 | bytes 1048576 | tf_op jit(solution)/shard_map/plain_kernel/pallas_call | solution.py:336
  1.1 5.1 %collective-permute-start.3 = (bf16[384,256]{1,0:T(8,128)(2,1)S(1)}, bf16[384,256]{1,0:T(8,128)(2,1)S(1)}, u32[]{:S(2)}, u32[]{:S(2)}) collective-permute-start(bf16[384,256]{1,0:T(8,128)(2,1)S(1)} %get-tuple-element.34), channel_id=1, source_target_pairs={{0,12},{4,8},{8,4},{12,0},{1,13},{5,9},{9,5},{13,1},{2,14},{6,10},... | collective-permute-start | bytes 589832 | tf_op jit(solution)/shard_map/ppermute | solution.py:349
  6.2 2.6 %gate_kernel.1 = (bf16[144,256]{1,0:T(8,128)(2,1)}, bf16[144,256]{1,0:T(8,128)(2,1)}, bf16[144,256]{1,0:T(8,128)(2,1)}, bf16[144,256]{1,0:T(8,128)(2,1)}, bf16[3...) custom-call(bf16[3,128,1024]{2,1,0:T(8,128)(2,1)} %bitcast.4, bf16[3,3,1024]{2,1,0:T(4,128)(2,1)} %refs_6_.1, ...), custom_call_target="tpu_custom_call" | custom-call | flops 1000000 | bytes 1048576 | tf_op jit(solution)/shard_map/gate_kernel/pallas_call | solution.py:336
  8.8 0.7 %collective-permute-start.5 = (bf16[384,256]{1,0:T(8,128)(2,1)}, bf16[384,256]{1,0:T(8,128)(2,1)S(1)}, u32[]{:S(2)}, u32[]{:S(2)}) collective-permute-start(bf16[384,256]{1,0:T(8,128)(2,1)} %get-tuple-element.36), channel_id=1, source_target_pairs={{0,4},{4,0},{8,12},{12,8},{1,5},{5,1},{9,13},{13,9},{2,6},{6,2},{1... | collective-permute-start | bytes 589832 | tf_op jit(solution)/shard_map/ppermute | solution.py:349
  9.5 2.4 %collective-permute-start = (bf16[144,256]{1,0:T(8,128)(2,1)}, bf16[144,256]{1,0:T(8,128)(2,1)S(1)}, u32[]{:S(2)}, u32[]{:S(2)}) collective-permute-start(bf16[144,256]{1,0:T(8,128)(2,1)} %get-tuple-element.30), channel_id=1, source_target_pairs={{0,8},{4,12},{8,0},{12,4},{1,9},{5,13},{9,1},{13,5},{2,10},{6,14},... | collective-permute-start | bytes 221192 | tf_op jit(solution)/shard_map/ppermute | solution.py:349
  11.8 1.4 %collective-permute-start.1 = (bf16[144,256]{1,0:T(8,128)(2,1)}, bf16[144,256]{1,0:T(8,128)(2,1)S(1)}, u32[]{:S(2)}, u32[]{:S(2)}) collective-permute-start(bf16[144,256]{1,0:T(8,128)(2,1)} %get-tuple-element.31), channel_id=1, source_target_pairs={{0,12},{4,8},{8,4},{12,0},{1,13},{5,9},{9,5},{13,1},{2,14},{6,10},... | collective-permute-start | bytes 221192 | tf_op jit(solution)/shard_map/ppermute | solution.py:349
  13.2 7.8 %collective-permute-start.2 = (bf16[144,256]{1,0:T(8,128)(2,1)}, bf16[144,256]{1,0:T(8,128)(2,1)S(1)}, u32[]{:S(2)}, u32[]{:S(2)}) collective-permute-start(bf16[144,256]{1,0:T(8,128)(2,1)} %get-tuple-element.32), channel_id=1, source_target_pairs={{0,4},{4,0},{8,12},{12,8},{1,5},{5,1},{9,13},{13,9},{2,6},{6,2},{1... | collective-permute-start | bytes 221192 | tf_op jit(solution)/shard_map/ppermute | solution.py:349
  21.0 0.7 %copy-done.3 = bf16[64,128]{1,0:T(8,128)(2,1)S(1)} copy-done((bf16[64,128]{1,0:T(8,128)(2,1)S(1)}, bf16[64,128]{1,0:T(8,128)(2,1)}, u32[]{:S(2)}) %copy-start.3) | copy-done | bytes 16408
  21.7 3.4 %ready_kernel.1 = (bf16[2048,256]{1,0:T(8,128)(2,1)S(1)}, bf16[1024,4096]{1,0:T(8,128)(2,1)S(1)}) custom-call(bf16[64,128]{1,0:T(8,128)(2,1)S(1)} %copy-done.3, bf16[1024,4096]{1,0:T(8,128)(2,1)} %weight_any.1), custom_call_target="tpu_custom_call" | custom-call | flops 1000000 | bytes 1048576 | tf_op jit(solution)/shard_map/ready_kernel/pallas_call | solution.py:336
  25.2 1.8 %collective-permute-done.4.second_ref = bf16[384,256]{1,0:T(8,128)(2,1)S(1)} collective-permute-done((bf16[384,256]{1,0:T(8,128)(2,1)S(1)}, bf16[384,256]{1,0:T(8,128)(2,1)S(1)}, u32[]{:S(2)}, u32[]{:S(2)}) %collective-permute-start.4) | collective-permute-done | bytes 196640 | tf_op jit(solution)/shard_map/ppermute | solution.py:349
  27.0 0.9 %weights_kernel.1 = (bf16[2,512,512]{2,1,0:T(8,128)(2,1)S(1)}, f32[512,128]{1,0:T(8,128)S(1)}, f32[512,256]{1,0:T(8,128)S(1)}) custom-call(bf16[384,256]{1,0:T(8,128)(2,1)S(1)} %collective-permute-done.3.third_ref, bf16[384,256]{1,0:T(8,128)(2,1)S(1)} %collective-permute-done.4.second_ref, bf16[384,256]{1,0:T(8,128)(2,1)S(1)} %collective-permute-done.5.near_ref, ...), custom_call_target="tpu_custom_call" | custom-call | flops 1000000 | bytes 1048576 | tf_op jit(solution)/shard_map/weights_kernel/pallas_call | solution.py:336
  28.4 1.1 %values_kernel.1 = (bf16[128,256]{1,0:T(8,128)(2,1)S(1)}, bf16[128,256]{1,0:T(8,128)(2,1)S(1)}, bf16[512,256]{1,0:T(8,128)(2,1)S(1)}) custom-call(bf16[144,256]{1,0:T(8,128)(2,1)S(1)} %collective-permute-done.refs_0_, bf16[144,256]{1,0:T(8,128)(2,1)S(1)} %collective-permute-done.1.refs_1_, bf16[144,256]{1,0:T(8,128)(2,1)S(1)} %collective-permute-done.2.refs_2_, ...), custom_call_target="tpu_custom_call" | custom-call | flops 1000000 | bytes 1048576 | tf_op jit(solution)/shard_map/values_kernel/pallas_call | solution.py:336
  29.5 2.5 %collective-permute-start.6 = (bf16[128,256]{1,0:T(8,128)(2,1)S(1)}, bf16[128,256]{1,0:T(8,128)(2,1)S(1)}, u32[]{:S(2)}, u32[]{:S(2)}) collective-permute-start(bf16[128,256]{1,0:T(8,128)(2,1)S(1)} %get-tuple-element.42), channel_id=1, source_target_pairs={{0,8},{4,12},{8,0},{12,4},{1,9},{5,13},{9,1},{13,5},{2,10},{6,14},... | collective-permute-start | bytes 196616 | tf_op jit(solution)/shard_map/ppermute | solution.py:349
  32.0 1.3 %collective-permute-start.7 = (bf16[128,256]{1,0:T(8,128)(2,1)S(1)}, bf16[128,256]{1,0:T(8,128)(2,1)S(1)}, u32[]{:S(2)}, u32[]{:S(2)}) collective-permute-start(bf16[128,256]{1,0:T(8,128)(2,1)S(1)} %get-tuple-element.43), channel_id=1, source_target_pairs={{0,12},{4,8},{8,4},{12,0},{1,13},{5,9},{9,5},{13,1},{2,14},{6,10},... | collective-permute-start | bytes 196616 | tf_op jit(solution)/shard_map/ppermute | solution.py:349
  33.6 2.0 %collective-permute-start.9 = (bf16[64,256]{1,0:T(8,128)(2,1)S(1)}, bf16[64,256]{1,0:T(8,128)(2,1)S(1)}, u32[]{:S(2)}, u32[]{:S(2)}) collective-permute-start(bf16[64,256]{1,0:T(8,128)(2,1)S(1)} %get-tuple-element.46), channel_id=1, source_target_pairs={{0,4},{4,0},{8,12},{12,8},{1,5},{5,1},{9,13},{13,9},{2,6},{6,2},{1... | collective-permute-start | bytes 98312 | tf_op jit(solution)/shard_map/ppermute | solution.py:349
  35.7 2.6 %collective-permute-done.8.refs_2_ = bf16[64,256]{1,0:T(8,128)(2,1)S(1)} collective-permute-done((bf16[64,256]{1,0:T(8,128)(2,1)S(1)}, bf16[64,256]{1,0:T(8,128)(2,1)S(1)}, u32[]{:S(2)}, u32[]{:S(2)}) %collective-permute-start.8) | collective-permute-done | bytes 32800 | tf_op jit(solution)/shard_map/ppermute | solution.py:349
  39.2 0.5 project_kernel.4
  39.6 0.6 %collective-permute-start.10 = (bf16[128,512]{1,0:T(8,128)(2,1)S(1)}, bf16[128,512]{1,0:T(8,128)(2,1)S(1)}, u32[]{:S(2)}, u32[]{:S(2)}) collective-permute-start(bf16[128,512]{1,0:T(8,128)(2,1)S(1)} %get-tuple-element.51), channel_id=1, source_target_pairs={{0,1},{1,0},{2,3},{3,2},{4,5},{5,4},{6,7},{7,6},{8,9},{9,8},{10,11... | collective-permute-start | bytes 393224 | tf_op jit(solution)/shard_map/ppermute | solution.py:349
  40.5 1.6 %collective-permute-start.14 = (bf16[128,512]{1,0:T(8,128)(2,1)S(1)}, bf16[128,512]{1,0:T(8,128)(2,1)S(1)}, u32[]{:S(2)}, u32[]{:S(2)}) collective-permute-start(bf16[128,512]{1,0:T(8,128)(2,1)S(1)} %add_convert_fusion.1), channel_id=1, source_target_pairs={{0,2},{1,3},{2,0},{3,1},{4,6},{5,7},{6,4},{7,5},{8,10},{9,11},{10,... | collective-permute-start | bytes 393224 | tf_op jit(solution)/shard_map/ppermute | solution.py:349
  42.1 0.7 %collective-permute-start.15 = (bf16[128,512]{1,0:T(8,128)(2,1)S(1)}, bf16[128,512]{1,0:T(8,128)(2,1)S(1)}, u32[]{:S(2)}, u32[]{:S(2)}) collective-permute-start(bf16[128,512]{1,0:T(8,128)(2,1)S(1)} %add_convert_fusion.2.refs_6_), channel_id=1, source_target_pairs={{0,2},{1,3},{2,0},{3,1},{4,6},{5,7},{6,4},{7,5},{8,10},{9,11},{10,... | collective-permute-start | bytes 393224 | tf_op jit(solution)/shard_map/ppermute | solution.py:349
  42.8 0.7 %project_kernel.5 = (bf16[128,1024]{1,0:T(8,128)(2,1)S(1)}, bf16[128,1024]{1,0:T(8,128)(2,1)S(1)}) custom-call(bf16[128,256]{1,0:T(8,128)(2,1)S(1)} %collective-permute-done.6.refs_0_, bf16[128,256]{1,0:T(8,128)(2,1)S(1)} %collective-permute-done.7.refs_1_, bf16[64,256]{1,0:T(8,128)(2,1)S(1)} %collective-permute-done.8.refs_2_, ...), custom_call_target="tpu_custom_call" | custom-call | flops 1000000 | bytes 1048576 | tf_op jit(solution)/shard_map/project_kernel/pallas_call | solution.py:336
  44.1 2.8 %collective-permute-done.14 = bf16[128,512]{1,0:T(8,128)(2,1)S(1)} collective-permute-done((bf16[128,512]{1,0:T(8,128)(2,1)S(1)}, bf16[128,512]{1,0:T(8,128)(2,1)S(1)}, u32[]{:S(2)}, u32[]{:S(2)}) %collective-permute-start.14) | collective-permute-done | bytes 131104 | tf_op jit(solution)/shard_map/ppermute | solution.py:349
  46.9 2.0 %collective-permute-done.15 = bf16[128,512]{1,0:T(8,128)(2,1)S(1)} collective-permute-done((bf16[128,512]{1,0:T(8,128)(2,1)S(1)}, bf16[128,512]{1,0:T(8,128)(2,1)S(1)}, u32[]{:S(2)}, u32[]{:S(2)}) %collective-permute-start.15) | collective-permute-done | bytes 131104 | tf_op jit(solution)/shard_map/ppermute | solution.py:349
  49.0 0.8 %add_convert_fusion = bf16[128,1024]{1,0:T(8,128)(2,1)} fusion(bf16[128,1024]{1,0:T(8,128)(2,1)S(1)} %get-tuple-element.52, bf16[64,1024]{1,0:T(8,128)(2,1)S(1)} %collective-permute-done.12, bf16[64,1024]{1,0:T(8,128)(2,1)S(1)} %collective-permute-done.11, bf16[128,512]{1,0:T(8,128)(2,1)S(1)} %collective-permute-done.15, ...), kind=kLoop, calls=%fused_computation | loop fusion | flops 1572864 | bytes 1048576 | tf_op jit(solution)/shard_map/convert_element_type | solution.py:445
  (31 shorter events, 2.7 us)
Async XLA Ops:
  0.0 27.0 %copy-start = (bf16[3,3,1024]{2,1,0:T(4,128)(2,1)S(1)}, bf16[3,3,1024]{2,1,0:T(4,128)(2,1)}, u32[]{:S(2)}) copy-start(bf16[3,3,1024]{2,1,0:T(4,128)(2,1)} %refs_6_.1) | copy-start | bytes 55300
  0.0 28.4 %copy-start.4 = (f32[1024]{0:T(1024)S(1)}, f32[1024]{0:T(1024)}, u32[]{:S(2)}) copy-start(f32[1024]{0:T(1024)} %param.10) | copy-start | bytes 12292
  1.1 12.2 %collective-permute-start.3 = (bf16[384,256]{1,0:T(8,128)(2,1)S(1)}, bf16[384,256]{1,0:T(8,128)(2,1)S(1)}, u32[]{:S(2)}, u32[]{:S(2)}) collective-permute-start(bf16[384,256]{1,0:T(8,128)(2,1)S(1)} %get-tuple-element.34), channel_id=1, source_target_pairs={{0,12},{4,8},{8,4},{12,0},{1,13},{5,9},{9,5},{13,1},{2,14},{6,10},... | collective-permute-start | bytes 589832 | tf_op jit(solution)/shard_map/ppermute | solution.py:349
  6.2 20.8 %collective-permute-start.4 = (bf16[384,256]{1,0:T(8,128)(2,1)S(1)}, bf16[384,256]{1,0:T(8,128)(2,1)S(1)}, u32[]{:S(2)}, u32[]{:S(2)}) collective-permute-start(bf16[384,256]{1,0:T(8,128)(2,1)S(1)} %get-tuple-element.35), channel_id=1, source_target_pairs={{0,8},{4,12},{8,0},{12,4},{1,9},{5,13},{9,1},{13,5},{2,10},{6,14},... | collective-permute-start | bytes 589832 | tf_op jit(solution)/shard_map/ppermute | solution.py:349
  8.8 18.3 %copy-start.1 = (bf16[384,256]{1,0:T(8,128)(2,1)S(1)}, bf16[384,256]{1,0:T(8,128)(2,1)}, u32[]{:S(2)}) copy-start(bf16[384,256]{1,0:T(8,128)(2,1)} %get-tuple-element.37.own_ref) | copy-start | bytes 589828
  8.8 19.7 %copy-start.2 = (bf16[144,256]{1,0:T(8,128)(2,1)S(1)}, bf16[144,256]{1,0:T(8,128)(2,1)}, u32[]{:S(2)}) copy-start(bf16[144,256]{1,0:T(8,128)(2,1)} %get-tuple-element.33.refs_3_) | copy-start | bytes 221188
  8.8 18.2 %collective-permute-start.5 = (bf16[384,256]{1,0:T(8,128)(2,1)}, bf16[384,256]{1,0:T(8,128)(2,1)S(1)}, u32[]{:S(2)}, u32[]{:S(2)}) collective-permute-start(bf16[384,256]{1,0:T(8,128)(2,1)} %get-tuple-element.36), channel_id=1, source_target_pairs={{0,4},{4,0},{8,12},{12,8},{1,5},{5,1},{9,13},{13,9},{2,6},{6,2},{1... | collective-permute-start | bytes 589832 | tf_op jit(solution)/shard_map/ppermute | solution.py:349
  9.5 18.9 %collective-permute-start = (bf16[144,256]{1,0:T(8,128)(2,1)}, bf16[144,256]{1,0:T(8,128)(2,1)S(1)}, u32[]{:S(2)}, u32[]{:S(2)}) collective-permute-start(bf16[144,256]{1,0:T(8,128)(2,1)} %get-tuple-element.30), channel_id=1, source_target_pairs={{0,8},{4,12},{8,0},{12,4},{1,9},{5,13},{9,1},{13,5},{2,10},{6,14},... | collective-permute-start | bytes 221192 | tf_op jit(solution)/shard_map/ppermute | solution.py:349
  11.8 16.6 %collective-permute-start.1 = (bf16[144,256]{1,0:T(8,128)(2,1)}, bf16[144,256]{1,0:T(8,128)(2,1)S(1)}, u32[]{:S(2)}, u32[]{:S(2)}) collective-permute-start(bf16[144,256]{1,0:T(8,128)(2,1)} %get-tuple-element.31), channel_id=1, source_target_pairs={{0,12},{4,8},{8,4},{12,0},{1,13},{5,9},{9,5},{13,1},{2,14},{6,10},... | collective-permute-start | bytes 221192 | tf_op jit(solution)/shard_map/ppermute | solution.py:349
  13.2 15.2 %collective-permute-start.2 = (bf16[144,256]{1,0:T(8,128)(2,1)}, bf16[144,256]{1,0:T(8,128)(2,1)S(1)}, u32[]{:S(2)}, u32[]{:S(2)}) collective-permute-start(bf16[144,256]{1,0:T(8,128)(2,1)} %get-tuple-element.32), channel_id=1, source_target_pairs={{0,4},{4,0},{8,12},{12,8},{1,5},{5,1},{9,13},{13,9},{2,6},{6,2},{1... | collective-permute-start | bytes 221192 | tf_op jit(solution)/shard_map/ppermute | solution.py:349
  21.0 0.7 %copy-start.3 = (bf16[64,128]{1,0:T(8,128)(2,1)S(1)}, bf16[64,128]{1,0:T(8,128)(2,1)}, u32[]{:S(2)}) copy-start(bf16[64,128]{1,0:T(8,128)(2,1)} %filter_ref.1) | copy-start | bytes 49156
  29.5 9.1 %collective-permute-start.6 = (bf16[128,256]{1,0:T(8,128)(2,1)S(1)}, bf16[128,256]{1,0:T(8,128)(2,1)S(1)}, u32[]{:S(2)}, u32[]{:S(2)}) collective-permute-start(bf16[128,256]{1,0:T(8,128)(2,1)S(1)} %get-tuple-element.42), channel_id=1, source_target_pairs={{0,8},{4,12},{8,0},{12,4},{1,9},{5,13},{9,1},{13,5},{2,10},{6,14},... | collective-permute-start | bytes 196616 | tf_op jit(solution)/shard_map/ppermute | solution.py:349
  32.0 6.6 %collective-permute-start.7 = (bf16[128,256]{1,0:T(8,128)(2,1)S(1)}, bf16[128,256]{1,0:T(8,128)(2,1)S(1)}, u32[]{:S(2)}, u32[]{:S(2)}) collective-permute-start(bf16[128,256]{1,0:T(8,128)(2,1)S(1)} %get-tuple-element.43), channel_id=1, source_target_pairs={{0,12},{4,8},{8,4},{12,0},{1,13},{5,9},{9,5},{13,1},{2,14},{6,10},... | collective-permute-start | bytes 196616 | tf_op jit(solution)/shard_map/ppermute | solution.py:349
  33.6 4.7 %collective-permute-start.8 = (bf16[64,256]{1,0:T(8,128)(2,1)S(1)}, bf16[64,256]{1,0:T(8,128)(2,1)S(1)}, u32[]{:S(2)}, u32[]{:S(2)}) collective-permute-start(bf16[64,256]{1,0:T(8,128)(2,1)S(1)} %get-tuple-element.45), channel_id=1, source_target_pairs={{0,4},{4,0},{8,12},{12,8},{1,5},{5,1},{9,13},{13,9},{2,6},{6,2},{1... | collective-permute-start | bytes 98312 | tf_op jit(solution)/shard_map/ppermute | solution.py:349
  33.6 5.0 %collective-permute-start.9 = (bf16[64,256]{1,0:T(8,128)(2,1)S(1)}, bf16[64,256]{1,0:T(8,128)(2,1)S(1)}, u32[]{:S(2)}, u32[]{:S(2)}) collective-permute-start(bf16[64,256]{1,0:T(8,128)(2,1)S(1)} %get-tuple-element.46), channel_id=1, source_target_pairs={{0,4},{4,0},{8,12},{12,8},{1,5},{5,1},{9,13},{13,9},{2,6},{6,2},{1... | collective-permute-start | bytes 98312 | tf_op jit(solution)/shard_map/ppermute | solution.py:349
  39.1 1.4 %collective-permute-start.13 = (bf16[128,512]{1,0:T(8,128)(2,1)S(1)}, bf16[128,512]{1,0:T(8,128)(2,1)S(1)}, u32[]{:S(2)}, u32[]{:S(2)}) collective-permute-start(bf16[128,512]{1,0:T(8,128)(2,1)S(1)} %get-tuple-element.49.refs_6_), channel_id=1, source_target_pairs={{0,1},{1,0},{2,3},{3,2},{4,5},{5,4},{6,7},{7,6},{8,9},{9,8},{10,11... | collective-permute-start | bytes 393224 | tf_op jit(solution)/shard_map/ppermute | solution.py:349
  39.6 2.4 %collective-permute-start.10 = (bf16[128,512]{1,0:T(8,128)(2,1)S(1)}, bf16[128,512]{1,0:T(8,128)(2,1)S(1)}, u32[]{:S(2)}, u32[]{:S(2)}) collective-permute-start(bf16[128,512]{1,0:T(8,128)(2,1)S(1)} %get-tuple-element.51), channel_id=1, source_target_pairs={{0,1},{1,0},{2,3},{3,2},{4,5},{5,4},{6,7},{7,6},{8,9},{9,8},{10,11... | collective-permute-start | bytes 393224 | tf_op jit(solution)/shard_map/ppermute | solution.py:349
  40.5 6.4 %collective-permute-start.14 = (bf16[128,512]{1,0:T(8,128)(2,1)S(1)}, bf16[128,512]{1,0:T(8,128)(2,1)S(1)}, u32[]{:S(2)}, u32[]{:S(2)}) collective-permute-start(bf16[128,512]{1,0:T(8,128)(2,1)S(1)} %add_convert_fusion.1), channel_id=1, source_target_pairs={{0,2},{1,3},{2,0},{3,1},{4,6},{5,7},{6,4},{7,5},{8,10},{9,11},{10,... | collective-permute-start | bytes 393224 | tf_op jit(solution)/shard_map/ppermute | solution.py:349
  42.1 6.8 %collective-permute-start.15 = (bf16[128,512]{1,0:T(8,128)(2,1)S(1)}, bf16[128,512]{1,0:T(8,128)(2,1)S(1)}, u32[]{:S(2)}, u32[]{:S(2)}) collective-permute-start(bf16[128,512]{1,0:T(8,128)(2,1)S(1)} %add_convert_fusion.2.refs_6_), channel_id=1, source_target_pairs={{0,2},{1,3},{2,0},{3,1},{4,6},{5,7},{6,4},{7,5},{8,10},{9,11},{10,... | collective-permute-start | bytes 393224 | tf_op jit(solution)/shard_map/ppermute | solution.py:349
  43.6 5.4 %collective-permute-start.11 = (bf16[64,1024]{1,0:T(8,128)(2,1)S(1)}, bf16[64,1024]{1,0:T(8,128)(2,1)S(1)}, u32[]{:S(2)}, u32[]{:S(2)}) collective-permute-start(bf16[64,1024]{1,0:T(8,128)(2,1)S(1)} %get-tuple-element.55), channel_id=1, source_target_pairs={{0,1},{1,0},{2,3},{3,2},{4,5},{5,4},{6,7},{7,6},{8,9},{9,8},{10,11... | collective-permute-start | bytes 393224 | tf_op jit(solution)/shard_map/ppermute | solution.py:349
  43.7 5.3 %collective-permute-start.12 = (bf16[64,1024]{1,0:T(8,128)(2,1)S(1)}, bf16[64,1024]{1,0:T(8,128)(2,1)S(1)}, u32[]{:S(2)}, u32[]{:S(2)}) collective-permute-start(bf16[64,1024]{1,0:T(8,128)(2,1)S(1)} %get-tuple-element.56), channel_id=1, source_target_pairs={{0,1},{1,0},{2,3},{3,2},{4,5},{5,4},{6,7},{7,6},{8,9},{9,8},{10,11... | collective-permute-start | bytes 393224 | tf_op jit(solution)/shard_map/ppermute | solution.py:349

commit v14 on v11

--- a/solution.py
+++ b/solution.py
@@ -323,6 +323,25 @@
         ).astype(jnp.bfloat16)
 
 
+def total_kernel(kept_ref, upper_ref, lower_ref, first_ref, second_ref, out_any, total_s, sems):
+    half, cut = upper_ref.shape[0], first_ref.shape[1]
+    copies = []
+    for index, near_ref in enumerate((upper_ref, lower_ref)):
+        here = slice(index * half, (index + 1) * half)
+        for columns, crossed_ref in ((slice(0, cut), first_ref), (slice(cut, 2 * cut), second_ref)):
+            total = (
+                kept_ref[here, columns].astype(jnp.float32)
+                + near_ref[:, columns].astype(jnp.float32)
+                + crossed_ref[here].astype(jnp.float32)
+            )
+            total_s[here, columns] = total.astype(jnp.bfloat16)
+        copy = pltpu.make_async_copy(total_s.at[here], out_any.at[here], sems.at[index])
+        copy.start()
+        copies.append(copy)
+    for copy in copies:
+        copy.wait()
+
+
 VMEM_LIMIT = 40 * 1024 * 1024
 PLAIN_LIMIT = 53 * 1024 * 1024 + 400 * 1024
 GATE_LIMIT = 60 * 1024 * 1024
@@ -331,12 +350,12 @@
 ANYWHERE = pl.BlockSpec(memory_space=pl.ANY)
 
 
-def run_kernel(kernel, operands, outputs, scratch=(), spaces=None, limit=VMEM_LIMIT, cost=10**6):
+def run_kernel(kernel, operands, outputs, scratch=(), spaces=None, limit=VMEM_LIMIT, cost=10**6, targets=None):
     return pl.pallas_call(
         kernel,
         out_shape=[jax.ShapeDtypeStruct(shape, dtype) for shape, dtype in outputs],
         in_specs=spaces or [IN_VMEM] * len(operands),
-        out_specs=[IN_VMEM] * len(outputs),
+        out_specs=targets or [IN_VMEM] * len(outputs),
         scratch_shapes=scratch,
         compiler_params=pltpu.CompilerParams(vmem_limit_bytes=limit),
         cost_estimate=pl.CostEstimate(flops=cost, bytes_accessed=2**20, transcendentals=0),
@@ -453,8 +472,15 @@
         crossed.append(swapped(far_sum, "mp", 2))
     near_given, near_kept = projected(attended, out_weight, ((1, 0, 1), (0, 0, 1)), (far_sum,), NEAR_COST)
     half = near_given.shape[0] // 2
-    near_got = jnp.concatenate([swapped(near_given[:half], "mp", 1), swapped(near_given[half:], "mp", 1)])
-    return added(near_kept, near_got, jnp.concatenate(crossed, axis=1))
+    near_got = [swapped(near_given[:half], "mp", 1), swapped(near_given[half:], "mp", 1)]
+    (total,) = run_kernel(
+        total_kernel,
+        (near_kept, *near_got, *crossed),
+        [(near_kept.shape, near_kept.dtype)],
+        [pltpu.VMEM(near_kept.shape, near_kept.dtype), pltpu.SemaphoreType.DMA((2,))],
+        targets=[IN_HBM],
+    )
+    return total
 
 
 def per_device(inputs, short_filter, long_filter, skip_gain, queries, key_rows, out_weight):

time: 49.6 us -> 49.5 us (level)
  other arithmetic: 0.88 us -> 0.07 us
  Pallas kernels: 11 us -> 11.8 us
    convert_element_type x3 -> x2, other arithmetic: 0.88 us -> 0.07 us  [added(): return total.astype(jnp.bfloat16)]
    pallas_call x9 -> x10, Pallas kernels: 11 us -> 11.8 us  [run_kernel(): pl.pallas_call(kernel, out_shape=[jax.ShapeDtypeStruct(shape, dtype) for...]
where the time goes in v14:
time: 49.5 us; the launch traced here: 49.2 us
  starting transfers between devices  25.5 us (52%)
  Pallas kernels  11.8 us (24%)
  waiting for transfers between devices  11 us (22%)
  local copies, waits for them, and re-layouts  0.75 us (2%)
    ppermute x16, starting transfers between devices, swapped(): lax.ppermute(value, axis, [(source, source ^ step) for source in range(la...  25.5 us
    pallas_call x10, Pallas kernels, run_kernel(): pl.pallas_call(kernel, out_shape=[jax.ShapeDtypeStruct(shape, dtype) for...  11.8 us
    ppermute x16, waiting for transfers between devices, swapped(): lax.ppermute(value, axis, [(source, source ^ step) for source in range(la...  11 us
  transfers between devices with their start and end apart: 16, of which 7 were waited for; matrix products, arithmetic and copies ran while one was open for 0% of the time, Pallas kernels for 17%

profile of v14, /device:TPU:0, one launch (start us, length us, event | category | flops | bytes accessed | tf_op | source)
XLA Modules:
  0.0 49.2 jit_solution(17817022297597218777)
XLA Ops:
  0.0 1.1 %plain_kernel.1 = (bf16[384,256]{1,0:T(8,128)(2,1)S(1)}, bf16[384,256]{1,0:T(8,128)(2,1)S(1)}) custom-call(bf16[3,128,1024]{2,1,0:T(8,128)(2,1)} %bitcast.3, bf16[128,1024]{1,0:T(8,128)(2,1)} %queries_any.3, bf16[128,1024]{1,0:T(8,128)(2,1)} %keys_any.3), custom_call_target="tpu_custom_call" | custom-call | flops 1000000 | bytes 1048576 | tf_op jit(solution)/shard_map/plain_kernel/pallas_call | solution.py:354
  1.1 5.1 %collective-permute-start.3 = (bf16[384,256]{1,0:T(8,128)(2,1)S(1)}, bf16[384,256]{1,0:T(8,128)(2,1)S(1)}, u32[]{:S(2)}, u32[]{:S(2)}) collective-permute-start(bf16[384,256]{1,0:T(8,128)(2,1)S(1)} %get-tuple-element.34), channel_id=1, source_target_pairs={{0,12},{4,8},{8,4},{12,0},{1,13},{5,9},{9,5},{13,1},{2,14},{6,10},... | collective-permute-start | bytes 589832 | tf_op jit(solution)/shard_map/ppermute | solution.py:367
  6.2 2.6 %gate_kernel.1 = (bf16[144,256]{1,0:T(8,128)(2,1)}, bf16[144,256]{1,0:T(8,128)(2,1)}, bf16[144,256]{1,0:T(8,128)(2,1)}, bf16[144,256]{1,0:T(8,128)(2,1)}, bf16[3...) custom-call(bf16[3,128,1024]{2,1,0:T(8,128)(2,1)} %bitcast.4, bf16[3,3,1024]{2,1,0:T(4,128)(2,1)} %refs_6_.1, ...), custom_call_target="tpu_custom_call" | custom-call | flops 1000000 | bytes 1048576 | tf_op jit(solution)/shard_map/gate_kernel/pallas_call | solution.py:354
  8.8 0.7 %collective-permute-start.5 = (bf16[384,256]{1,0:T(8,128)(2,1)}, bf16[384,256]{1,0:T(8,128)(2,1)S(1)}, u32[]{:S(2)}, u32[]{:S(2)}) collective-permute-start(bf16[384,256]{1,0:T(8,128)(2,1)} %get-tuple-element.36), channel_id=1, source_target_pairs={{0,4},{4,0},{8,12},{12,8},{1,5},{5,1},{9,13},{13,9},{2,6},{6,2},{1... | collective-permute-start | bytes 589832 | tf_op jit(solution)/shard_map/ppermute | solution.py:367
  9.5 3.7 %collective-permute-start = (bf16[144,256]{1,0:T(8,128)(2,1)}, bf16[144,256]{1,0:T(8,128)(2,1)S(1)}, u32[]{:S(2)}, u32[]{:S(2)}) collective-permute-start(bf16[144,256]{1,0:T(8,128)(2,1)} %get-tuple-element.30), channel_id=1, source_target_pairs={{0,12},{4,8},{8,4},{12,0},{1,13},{5,9},{9,5},{13,1},{2,14},{6,10},... | collective-permute-start | bytes 221192 | tf_op jit(solution)/shard_map/ppermute | solution.py:367
  13.2 7.8 %collective-permute-start.2 = (bf16[144,256]{1,0:T(8,128)(2,1)}, bf16[144,256]{1,0:T(8,128)(2,1)S(1)}, u32[]{:S(2)}, u32[]{:S(2)}) collective-permute-start(bf16[144,256]{1,0:T(8,128)(2,1)} %get-tuple-element.32), channel_id=1, source_target_pairs={{0,4},{4,0},{8,12},{12,8},{1,5},{5,1},{9,13},{13,9},{2,6},{6,2},{1... | collective-permute-start | bytes 221192 | tf_op jit(solution)/shard_map/ppermute | solution.py:367
  21.0 0.7 %copy-done.3 = bf16[64,128]{1,0:T(8,128)(2,1)S(1)} copy-done((bf16[64,128]{1,0:T(8,128)(2,1)S(1)}, bf16[64,128]{1,0:T(8,128)(2,1)}, u32[]{:S(2)}) %copy-start.3) | copy-done | bytes 16408
  21.7 3.4 %ready_kernel.1 = (bf16[2048,256]{1,0:T(8,128)(2,1)S(1)}, bf16[1024,4096]{1,0:T(8,128)(2,1)S(1)}) custom-call(bf16[64,128]{1,0:T(8,128)(2,1)S(1)} %copy-done.3, bf16[1024,4096]{1,0:T(8,128)(2,1)} %weight_any.1), custom_call_target="tpu_custom_call" | custom-call | flops 1000000 | bytes 1048576 | tf_op jit(solution)/shard_map/ready_kernel/pallas_call | solution.py:354
  25.2 1.8 %collective-permute-done.4.second_ref = bf16[384,256]{1,0:T(8,128)(2,1)S(1)} collective-permute-done((bf16[384,256]{1,0:T(8,128)(2,1)S(1)}, bf16[384,256]{1,0:T(8,128)(2,1)S(1)}, u32[]{:S(2)}, u32[]{:S(2)}) %collective-permute-start.4) | collective-permute-done | bytes 196640 | tf_op jit(solution)/shard_map/ppermute | solution.py:367
  27.0 0.9 %weights_kernel.1 = (bf16[2,512,512]{2,1,0:T(8,128)(2,1)S(1)}, f32[512,128]{1,0:T(8,128)S(1)}, f32[512,256]{1,0:T(8,128)S(1)}) custom-call(bf16[384,256]{1,0:T(8,128)(2,1)S(1)} %collective-permute-done.3.third_ref, bf16[384,256]{1,0:T(8,128)(2,1)S(1)} %collective-permute-done.4.second_ref, bf16[384,256]{1,0:T(8,128)(2,1)S(1)} %collective-permute-done.5.near_ref, ...), custom_call_target="tpu_custom_call" | custom-call | flops 1000000 | bytes 1048576 | tf_op jit(solution)/shard_map/weights_kernel/pallas_call | solution.py:354
  28.0 1.2 %collective-permute-done.1.refs_1_ = bf16[144,256]{1,0:T(8,128)(2,1)S(1)} collective-permute-done((bf16[144,256]{1,0:T(8,128)(2,1)}, bf16[144,256]{1,0:T(8,128)(2,1)S(1)}, u32[]{:S(2)}, u32[]{:S(2)}) %collective-permute-start.1) | collective-permute-done | bytes 73760 | tf_op jit(solution)/shard_map/ppermute | solution.py:367
  29.2 1.1 %values_kernel.1 = (bf16[128,256]{1,0:T(8,128)(2,1)S(1)}, bf16[128,256]{1,0:T(8,128)(2,1)S(1)}, bf16[512,256]{1,0:T(8,128)(2,1)S(1)}) custom-call(bf16[144,256]{1,0:T(8,128)(2,1)S(1)} %collective-permute-done.refs_0_, bf16[144,256]{1,0:T(8,128)(2,1)S(1)} %collective-permute-done.1.refs_1_, bf16[144,256]{1,0:T(8,128)(2,1)S(1)} %collective-permute-done.2.refs_2_, ...), custom_call_target="tpu_custom_call" | custom-call | flops 1000000 | bytes 1048576 | tf_op jit(solution)/shard_map/values_kernel/pallas_call | solution.py:354
  30.3 0.9 %collective-permute-start.6 = (bf16[128,256]{1,0:T(8,128)(2,1)S(1)}, bf16[128,256]{1,0:T(8,128)(2,1)S(1)}, u32[]{:S(2)}, u32[]{:S(2)}) collective-permute-start(bf16[128,256]{1,0:T(8,128)(2,1)S(1)} %get-tuple-element.42), channel_id=1, source_target_pairs={{0,8},{4,12},{8,0},{12,4},{1,9},{5,13},{9,1},{13,5},{2,10},{6,14},... | collective-permute-start | bytes 196616 | tf_op jit(solution)/shard_map/ppermute | solution.py:367
  31.1 1.8 %collective-permute-start.7 = (bf16[128,256]{1,0:T(8,128)(2,1)S(1)}, bf16[128,256]{1,0:T(8,128)(2,1)S(1)}, u32[]{:S(2)}, u32[]{:S(2)}) collective-permute-start(bf16[128,256]{1,0:T(8,128)(2,1)S(1)} %get-tuple-element.43), channel_id=1, source_target_pairs={{0,12},{4,8},{8,4},{12,0},{1,13},{5,9},{9,5},{13,1},{2,14},{6,10},... | collective-permute-start | bytes 196616 | tf_op jit(solution)/shard_map/ppermute | solution.py:367
  33.2 1.0 %collective-permute-start.8 = (bf16[64,256]{1,0:T(8,128)(2,1)S(1)}, bf16[64,256]{1,0:T(8,128)(2,1)S(1)}, u32[]{:S(2)}, u32[]{:S(2)}) collective-permute-start(bf16[64,256]{1,0:T(8,128)(2,1)S(1)} %get-tuple-element.45), channel_id=1, source_target_pairs={{0,4},{4,0},{8,12},{12,8},{1,5},{5,1},{9,13},{13,9},{2,6},{6,2},{1... | collective-permute-start | bytes 98312 | tf_op jit(solution)/shard_map/ppermute | solution.py:367
  34.2 1.1 %collective-permute-start.9 = (bf16[64,256]{1,0:T(8,128)(2,1)S(1)}, bf16[64,256]{1,0:T(8,128)(2,1)S(1)}, u32[]{:S(2)}, u32[]{:S(2)}) collective-permute-start(bf16[64,256]{1,0:T(8,128)(2,1)S(1)} %get-tuple-element.46), channel_id=1, source_target_pairs={{0,4},{4,0},{8,12},{12,8},{1,5},{5,1},{9,13},{13,9},{2,6},{6,2},{1... | collective-permute-start | bytes 98312 | tf_op jit(solution)/shard_map/ppermute | solution.py:367
  35.3 2.4 %collective-permute-done.8.refs_2_ = bf16[64,256]{1,0:T(8,128)(2,1)S(1)} collective-permute-done((bf16[64,256]{1,0:T(8,128)(2,1)S(1)}, bf16[64,256]{1,0:T(8,128)(2,1)S(1)}, u32[]{:S(2)}, u32[]{:S(2)}) %collective-permute-start.8) | collective-permute-done | bytes 32800 | tf_op jit(solution)/shard_map/ppermute | solution.py:367
  39.2 0.5 %collective-permute-start.10 = (bf16[128,512]{1,0:T(8,128)(2,1)S(1)}, bf16[128,512]{1,0:T(8,128)(2,1)S(1)}, u32[]{:S(2)}, u32[]{:S(2)}) collective-permute-start(bf16[128,512]{1,0:T(8,128)(2,1)S(1)} %get-tuple-element.51), channel_id=1, source_target_pairs={{0,1},{1,0},{2,3},{3,2},{4,5},{5,4},{6,7},{7,6},{8,9},{9,8},{10,11... | collective-permute-start | bytes 393224 | tf_op jit(solution)/shard_map/ppermute | solution.py:367
  40.0 1.6 %collective-permute-start.14 = (bf16[128,512]{1,0:T(8,128)(2,1)S(1)}, bf16[128,512]{1,0:T(8,128)(2,1)S(1)}, u32[]{:S(2)}, u32[]{:S(2)}) collective-permute-start(bf16[128,512]{1,0:T(8,128)(2,1)S(1)} %add_convert_fusion), channel_id=1, source_target_pairs={{0,2},{1,3},{2,0},{3,1},{4,6},{5,7},{6,4},{7,5},{8,10},{9,11},{10,... | collective-permute-start | bytes 393224 | tf_op jit(solution)/shard_map/ppermute | solution.py:367
  41.6 0.7 %collective-permute-start.15 = (bf16[128,512]{1,0:T(8,128)(2,1)S(1)}, bf16[128,512]{1,0:T(8,128)(2,1)S(1)}, u32[]{:S(2)}, u32[]{:S(2)}) collective-permute-start(bf16[128,512]{1,0:T(8,128)(2,1)S(1)} %add_convert_fusion.1.refs_6_), channel_id=1, source_target_pairs={{0,2},{1,3},{2,0},{3,1},{4,6},{5,7},{6,4},{7,5},{8,10},{9,11},{10,... | collective-permute-start | bytes 393224 | tf_op jit(solution)/shard_map/ppermute | solution.py:367
  42.3 0.7 %project_kernel.5 = (bf16[128,1024]{1,0:T(8,128)(2,1)S(1)}, bf16[128,1024]{1,0:T(8,128)(2,1)S(1)}) custom-call(bf16[128,256]{1,0:T(8,128)(2,1)S(1)} %collective-permute-done.6.refs_0_, bf16[128,256]{1,0:T(8,128)(2,1)S(1)} %collective-permute-done.7.refs_1_, bf16[64,256]{1,0:T(8,128)(2,1)S(1)} %collective-permute-done.8.refs_2_, ...), custom_call_target="tpu_custom_call" | custom-call | flops 1000000 | bytes 1048576 | tf_op jit(solution)/shard_map/project_kernel/pallas_call | solution.py:354
  43.7 2.8 %collective-permute-done.14.first_ref = bf16[128,512]{1,0:T(8,128)(2,1)S(1)} collective-permute-done((bf16[128,512]{1,0:T(8,128)(2,1)S(1)}, bf16[128,512]{1,0:T(8,128)(2,1)S(1)}, u32[]{:S(2)}, u32[]{:S(2)}) %collective-permute-start.14) | collective-permute-done | bytes 131104 | tf_op jit(solution)/shard_map/ppermute | solution.py:367
  46.5 2.0 %collective-permute-done.15.second_ref = bf16[128,512]{1,0:T(8,128)(2,1)S(1)} collective-permute-done((bf16[128,512]{1,0:T(8,128)(2,1)S(1)}, bf16[128,512]{1,0:T(8,128)(2,1)S(1)}, u32[]{:S(2)}, u32[]{:S(2)}) %collective-permute-start.15) | collective-permute-done | bytes 131104 | tf_op jit(solution)/shard_map/ppermute | solution.py:367
  48.5 0.8 %total_kernel.1 = bf16[128,1024]{1,0:T(8,128)(2,1)} custom-call(bf16[128,1024]{1,0:T(8,128)(2,1)S(1)} %get-tuple-element.52.kept_ref, bf16[64,1024]{1,0:T(8,128)(2,1)S(1)} %collective-permute-done.11.upper_ref, bf16[64,1024]{1,0:T(8,128)(2,1)S(1)} %collective-permute-done.12.lower_ref, bf16[128,512]{1,0:T(8,128)(2,1)S(1)} %collective-permute-done.14.first_ref, ...), custom_call_target="tpu_custom_call" | custom-call | flops 1000000 | bytes 1048576 | tf_op jit(solution)/shard_map/total_kernel/pallas_call | solution.py:354
  (31 shorter events, 2.8 us)
Async XLA Ops:
  0.0 27.0 %copy-start = (bf16[3,3,1024]{2,1,0:T(4,128)(2,1)S(1)}, bf16[3,3,1024]{2,1,0:T(4,128)(2,1)}, u32[]{:S(2)}) copy-start(bf16[3,3,1024]{2,1,0:T(4,128)(2,1)} %refs_6_.1) | copy-start | bytes 55300
  0.0 29.2 %copy-start.4 = (f32[1024]{0:T(1024)S(1)}, f32[1024]{0:T(1024)}, u32[]{:S(2)}) copy-start(f32[1024]{0:T(1024)} %param.10) | copy-start | bytes 12292
  1.1 12.2 %collective-permute-start.3 = (bf16[384,256]{1,0:T(8,128)(2,1)S(1)}, bf16[384,256]{1,0:T(8,128)(2,1)S(1)}, u32[]{:S(2)}, u32[]{:S(2)}) collective-permute-start(bf16[384,256]{1,0:T(8,128)(2,1)S(1)} %get-tuple-element.34), channel_id=1, source_target_pairs={{0,12},{4,8},{8,4},{12,0},{1,13},{5,9},{9,5},{13,1},{2,14},{6,10},... | collective-permute-start | bytes 589832 | tf_op jit(solution)/shard_map/ppermute | solution.py:367
  6.2 20.8 %collective-permute-start.4 = (bf16[384,256]{1,0:T(8,128)(2,1)S(1)}, bf16[384,256]{1,0:T(8,128)(2,1)S(1)}, u32[]{:S(2)}, u32[]{:S(2)}) collective-permute-start(bf16[384,256]{1,0:T(8,128)(2,1)S(1)} %get-tuple-element.35), channel_id=1, source_target_pairs={{0,8},{4,12},{8,0},{12,4},{1,9},{5,13},{9,1},{13,5},{2,10},{6,14},... | collective-permute-start | bytes 589832 | tf_op jit(solution)/shard_map/ppermute | solution.py:367
  8.8 18.3 %copy-start.1 = (bf16[384,256]{1,0:T(8,128)(2,1)S(1)}, bf16[384,256]{1,0:T(8,128)(2,1)}, u32[]{:S(2)}) copy-start(bf16[384,256]{1,0:T(8,128)(2,1)} %get-tuple-element.37.own_ref) | copy-start | bytes 589828
  8.8 20.4 %copy-start.2 = (bf16[144,256]{1,0:T(8,128)(2,1)S(1)}, bf16[144,256]{1,0:T(8,128)(2,1)}, u32[]{:S(2)}) copy-start(bf16[144,256]{1,0:T(8,128)(2,1)} %get-tuple-element.33.refs_3_) | copy-start | bytes 221188
  8.8 18.2 %collective-permute-start.5 = (bf16[384,256]{1,0:T(8,128)(2,1)}, bf16[384,256]{1,0:T(8,128)(2,1)S(1)}, u32[]{:S(2)}, u32[]{:S(2)}) collective-permute-start(bf16[384,256]{1,0:T(8,128)(2,1)} %get-tuple-element.36), channel_id=1, source_target_pairs={{0,4},{4,0},{8,12},{12,8},{1,5},{5,1},{9,13},{13,9},{2,6},{6,2},{1... | collective-permute-start | bytes 589832 | tf_op jit(solution)/shard_map/ppermute | solution.py:367
  9.5 18.5 %collective-permute-start = (bf16[144,256]{1,0:T(8,128)(2,1)}, bf16[144,256]{1,0:T(8,128)(2,1)S(1)}, u32[]{:S(2)}, u32[]{:S(2)}) collective-permute-start(bf16[144,256]{1,0:T(8,128)(2,1)} %get-tuple-element.30), channel_id=1, source_target_pairs={{0,12},{4,8},{8,4},{12,0},{1,13},{5,9},{9,5},{13,1},{2,14},{6,10},... | collective-permute-start | bytes 221192 | tf_op jit(solution)/shard_map/ppermute | solution.py:367
  13.2 16.0 %collective-permute-start.1 = (bf16[144,256]{1,0:T(8,128)(2,1)}, bf16[144,256]{1,0:T(8,128)(2,1)S(1)}, u32[]{:S(2)}, u32[]{:S(2)}) collective-permute-start(bf16[144,256]{1,0:T(8,128)(2,1)} %get-tuple-element.31), channel_id=1, source_target_pairs={{0,8},{4,12},{8,0},{12,4},{1,9},{5,13},{9,1},{13,5},{2,10},{6,14},... | collective-permute-start | bytes 221192 | tf_op jit(solution)/shard_map/ppermute | solution.py:367
  13.2 16.0 %collective-permute-start.2 = (bf16[144,256]{1,0:T(8,128)(2,1)}, bf16[144,256]{1,0:T(8,128)(2,1)S(1)}, u32[]{:S(2)}, u32[]{:S(2)}) collective-permute-start(bf16[144,256]{1,0:T(8,128)(2,1)} %get-tuple-element.32), channel_id=1, source_target_pairs={{0,4},{4,0},{8,12},{12,8},{1,5},{5,1},{9,13},{13,9},{2,6},{6,2},{1... | collective-permute-start | bytes 221192 | tf_op jit(solution)/shard_map/ppermute | solution.py:367
  21.0 0.7 %copy-start.3 = (bf16[64,128]{1,0:T(8,128)(2,1)S(1)}, bf16[64,128]{1,0:T(8,128)(2,1)}, u32[]{:S(2)}) copy-start(bf16[64,128]{1,0:T(8,128)(2,1)} %filter_ref.1) | copy-start | bytes 49156
  30.3 7.8 %collective-permute-start.6 = (bf16[128,256]{1,0:T(8,128)(2,1)S(1)}, bf16[128,256]{1,0:T(8,128)(2,1)S(1)}, u32[]{:S(2)}, u32[]{:S(2)}) collective-permute-start(bf16[128,256]{1,0:T(8,128)(2,1)S(1)} %get-tuple-element.42), channel_id=1, source_target_pairs={{0,8},{4,12},{8,0},{12,4},{1,9},{5,13},{9,1},{13,5},{2,10},{6,14},... | collective-permute-start | bytes 196616 | tf_op jit(solution)/shard_map/ppermute | solution.py:367
  31.1 7.0 %collective-permute-start.7 = (bf16[128,256]{1,0:T(8,128)(2,1)S(1)}, bf16[128,256]{1,0:T(8,128)(2,1)S(1)}, u32[]{:S(2)}, u32[]{:S(2)}) collective-permute-start(bf16[128,256]{1,0:T(8,128)(2,1)S(1)} %get-tuple-element.43), channel_id=1, source_target_pairs={{0,12},{4,8},{8,4},{12,0},{1,13},{5,9},{9,5},{13,1},{2,14},{6,10},... | collective-permute-start | bytes 196616 | tf_op jit(solution)/shard_map/ppermute | solution.py:367
  33.2 4.5 %collective-permute-start.8 = (bf16[64,256]{1,0:T(8,128)(2,1)S(1)}, bf16[64,256]{1,0:T(8,128)(2,1)S(1)}, u32[]{:S(2)}, u32[]{:S(2)}) collective-permute-start(bf16[64,256]{1,0:T(8,128)(2,1)S(1)} %get-tuple-element.45), channel_id=1, source_target_pairs={{0,4},{4,0},{8,12},{12,8},{1,5},{5,1},{9,13},{13,9},{2,6},{6,2},{1... | collective-permute-start | bytes 98312 | tf_op jit(solution)/shard_map/ppermute | solution.py:367
  34.2 3.9 %collective-permute-start.9 = (bf16[64,256]{1,0:T(8,128)(2,1)S(1)}, bf16[64,256]{1,0:T(8,128)(2,1)S(1)}, u32[]{:S(2)}, u32[]{:S(2)}) collective-permute-start(bf16[64,256]{1,0:T(8,128)(2,1)S(1)} %get-tuple-element.46), channel_id=1, source_target_pairs={{0,4},{4,0},{8,12},{12,8},{1,5},{5,1},{9,13},{13,9},{2,6},{6,2},{1... | collective-permute-start | bytes 98312 | tf_op jit(solution)/shard_map/ppermute | solution.py:367
  38.6 1.4 %collective-permute-start.13 = (bf16[128,512]{1,0:T(8,128)(2,1)S(1)}, bf16[128,512]{1,0:T(8,128)(2,1)S(1)}, u32[]{:S(2)}, u32[]{:S(2)}) collective-permute-start(bf16[128,512]{1,0:T(8,128)(2,1)S(1)} %get-tuple-element.49.refs_6_), channel_id=1, source_target_pairs={{0,1},{1,0},{2,3},{3,2},{4,5},{5,4},{6,7},{7,6},{8,9},{9,8},{10,11... | collective-permute-start | bytes 393224 | tf_op jit(solution)/shard_map/ppermute | solution.py:367
  39.2 2.4 %collective-permute-start.10 = (bf16[128,512]{1,0:T(8,128)(2,1)S(1)}, bf16[128,512]{1,0:T(8,128)(2,1)S(1)}, u32[]{:S(2)}, u32[]{:S(2)}) collective-permute-start(bf16[128,512]{1,0:T(8,128)(2,1)S(1)} %get-tuple-element.51), channel_id=1, source_target_pairs={{0,1},{1,0},{2,3},{3,2},{4,5},{5,4},{6,7},{7,6},{8,9},{9,8},{10,11... | collective-permute-start | bytes 393224 | tf_op jit(solution)/shard_map/ppermute | solution.py:367
  40.0 6.4 %collective-permute-start.14 = (bf16[128,512]{1,0:T(8,128)(2,1)S(1)}, bf16[128,512]{1,0:T(8,128)(2,1)S(1)}, u32[]{:S(2)}, u32[]{:S(2)}) collective-permute-start(bf16[128,512]{1,0:T(8,128)(2,1)S(1)} %add_convert_fusion), channel_id=1, source_target_pairs={{0,2},{1,3},{2,0},{3,1},{4,6},{5,7},{6,4},{7,5},{8,10},{9,11},{10,... | collective-permute-start | bytes 393224 | tf_op jit(solution)/shard_map/ppermute | solution.py:367
  41.6 6.8 %collective-permute-start.15 = (bf16[128,512]{1,0:T(8,128)(2,1)S(1)}, bf16[128,512]{1,0:T(8,128)(2,1)S(1)}, u32[]{:S(2)}, u32[]{:S(2)}) collective-permute-start(bf16[128,512]{1,0:T(8,128)(2,1)S(1)} %add_convert_fusion.1.refs_6_), channel_id=1, source_target_pairs={{0,2},{1,3},{2,0},{3,1},{4,6},{5,7},{6,4},{7,5},{8,10},{9,11},{10,... | collective-permute-start | bytes 393224 | tf_op jit(solution)/shard_map/ppermute | solution.py:367
  43.1 5.4 %collective-permute-start.12 = (bf16[64,1024]{1,0:T(8,128)(2,1)S(1)}, bf16[64,1024]{1,0:T(8,128)(2,1)S(1)}, u32[]{:S(2)}, u32[]{:S(2)}) collective-permute-start(bf16[64,1024]{1,0:T(8,128)(2,1)S(1)} %get-tuple-element.55), channel_id=1, source_target_pairs={{0,1},{1,0},{2,3},{3,2},{4,5},{5,4},{6,7},{7,6},{8,9},{9,8},{10,11... | collective-permute-start | bytes 393224 | tf_op jit(solution)/shard_map/ppermute | solution.py:367
  43.2 5.3 %collective-permute-start.11 = (bf16[64,1024]{1,0:T(8,128)(2,1)S(1)}, bf16[64,1024]{1,0:T(8,128)(2,1)S(1)}, u32[]{:S(2)}, u32[]{:S(2)}) collective-permute-start(bf16[64,1024]{1,0:T(8,128)(2,1)S(1)} %get-tuple-element.56), channel_id=1, source_target_pairs={{0,1},{1,0},{2,3},{3,2},{4,5},{5,4},{6,7},{7,6},{8,9},{9,8},{10,11... | collective-permute-start | bytes 393224 | tf_op jit(solution)/shard_map/ppermute | solution.py:367

commit v15 on v14

--- a/solution.py
+++ b/solution.py
@@ -323,6 +323,36 @@
         ).astype(jnp.bfloat16)
 
 
+def partial_kernel(second_ref, mine_ref, weight_ref, out_ref):
+    own, width = mine_ref.shape[1], out_ref.shape[1] // 2
+    position, here = lax.axis_index("ctx"), lax.axis_index("mp")
+    for index, mask in enumerate((3, 2)):
+        columns = columns_of(here ^ mask, width)
+        out_ref[:, index * width : (index + 1) * width] = jnp.dot(
+            mine_ref[...], weight_ref[columns_of(position, own), columns], preferred_element_type=jnp.float32
+        ) + jnp.dot(
+            second_ref[...], weight_ref[columns_of(position ^ 2, own), columns], preferred_element_type=jnp.float32
+        )
+
+
+def project_far_kernel(part, third_ref, upper_ref, lower_ref, partial_ref, weight_ref, *refs):
+    given_ref, kept_ref = refs[-2:]
+    own, size = third_ref.shape[1], given_ref.shape[1]
+    width = partial_ref.shape[1] // 2
+    position, here = lax.axis_index("ctx"), lax.axis_index("mp")
+    near = jnp.concatenate([upper_ref[...], lower_ref[...]], axis=0)
+    for index, (mask, out_ref) in enumerate(((3, given_ref), (2, kept_ref))):
+        columns = columns_of((here ^ mask) * (width // size) + part, size)
+        start = index * width + part * size
+        total = partial_ref[:, start : start + size] + jnp.dot(
+            third_ref[...], weight_ref[columns_of(position ^ 3, own), columns], preferred_element_type=jnp.float32
+        )
+        total = total + jnp.dot(
+            near, weight_ref[columns_of(position ^ 1, own), columns], preferred_element_type=jnp.float32
+        )
+        out_ref[...] = total.astype(jnp.bfloat16)
+
+
 def total_kernel(kept_ref, upper_ref, lower_ref, first_ref, second_ref, out_any, total_s, sems):
     half, cut = upper_ref.shape[0], first_ref.shape[1]
     copies = []
@@ -453,7 +483,7 @@
     )
 
 
-FAR_COST, NEAR_COST = 10**6, 10**6
+NEAR_COST = 10**6
 
 
 def added(*terms):
@@ -464,10 +494,17 @@
 
 
 def project_and_share(attended, out_weight):
-    crossed, after = [], ()
+    second, third, upper, lower, mine = attended
+    rows = mine.shape[0]
+    width = out_weight.shape[1] // lax.axis_size("mp")
+    (partial,) = run_kernel(partial_kernel, (second, mine, out_weight), [((rows, 2 * width), jnp.float32)])
+    crossed = []
     for part in range(2):
-        given, kept = projected(attended, out_weight, ((3, part, 2), (2, part, 2)), after, FAR_COST)
-        after = (given,)
+        given, kept = run_kernel(
+            functools.partial(project_far_kernel, part),
+            (third, upper, lower, partial, out_weight),
+            [((rows, width // 2), jnp.bfloat16)] * 2,
+        )
         far_sum = added(kept, swapped(given, "mp", 1))
         crossed.append(swapped(far_sum, "mp", 2))
     near_given, near_kept = projected(attended, out_weight, ((1, 0, 1), (0, 0, 1)), (far_sum,), NEAR_COST)

time: 49.5 us -> 49.4 us (level)
    pallas_call x10 -> x11, Pallas kernels: 11.8 us -> 11.9 us  [run_kernel(): pl.pallas_call(kernel, out_shape=[jax.ShapeDtypeStruct(shape, dtype) for...]
  transfers between devices with their start and end apart: 16 -> 16, of which waited for: 7 -> 8; matrix products, arithmetic and copies ran while one was open for 0% -> 0% of each run, Pallas kernels for 17% -> 18%
where the time goes in v15:
time: 49.4 us; the launch traced here: 49.1 us
  starting transfers between devices  25.4 us (51%)
  Pallas kernels  11.9 us (24%)
  waiting for transfers between devices  10.8 us (22%)
  local copies, waits for them, and re-layouts  0.75 us (2%)
    ppermute x16, starting transfers between devices, swapped(): lax.ppermute(value, axis, [(source, source ^ step) for source in range(la...  25.4 us
    pallas_call x11, Pallas kernels, run_kernel(): pl.pallas_call(kernel, out_shape=[jax.ShapeDtypeStruct(shape, dtype) for...  11.9 us
    ppermute x16, waiting for transfers between devices, swapped(): lax.ppermute(value, axis, [(source, source ^ step) for source in range(la...  10.8 us
  transfers between devices with their start and end apart: 16, of which 8 were waited for; matrix products, arithmetic and copies ran while one was open for 0% of the time, Pallas kernels for 18%

profile of v15, /device:TPU:0, one launch (start us, length us, event | category | flops | bytes accessed | tf_op | source)
XLA Modules:
  0.0 49.1 jit_solution(6377466257366939808)
XLA Ops:
  0.0 1.1 %plain_kernel.1 = (bf16[384,256]{1,0:T(8,128)(2,1)S(1)}, bf16[384,256]{1,0:T(8,128)(2,1)S(1)}) custom-call(bf16[3,128,1024]{2,1,0:T(8,128)(2,1)} %bitcast.3, bf16[128,1024]{1,0:T(8,128)(2,1)} %queries_any.3, bf16[128,1024]{1,0:T(8,128)(2,1)} %keys_any.3), custom_call_target="tpu_custom_call" | custom-call | flops 1000000 | bytes 1048576 | tf_op jit(solution)/shard_map/plain_kernel/pallas_call | solution.py:384
  1.1 5.1 %collective-permute-start.3 = (bf16[384,256]{1,0:T(8,128)(2,1)S(1)}, bf16[384,256]{1,0:T(8,128)(2,1)S(1)}, u32[]{:S(2)}, u32[]{:S(2)}) collective-permute-start(bf16[384,256]{1,0:T(8,128)(2,1)S(1)} %get-tuple-element.34), channel_id=1, source_target_pairs={{0,12},{4,8},{8,4},{12,0},{1,13},{5,9},{9,5},{13,1},{2,14},{6,10},... | collective-permute-start | bytes 589832 | tf_op jit(solution)/shard_map/ppermute | solution.py:397
  6.2 2.6 %gate_kernel.1 = (bf16[144,256]{1,0:T(8,128)(2,1)}, bf16[144,256]{1,0:T(8,128)(2,1)}, bf16[144,256]{1,0:T(8,128)(2,1)}, bf16[144,256]{1,0:T(8,128)(2,1)}, bf16[3...) custom-call(bf16[3,128,1024]{2,1,0:T(8,128)(2,1)} %bitcast.4, bf16[3,3,1024]{2,1,0:T(4,128)(2,1)} %refs_6_.1, ...), custom_call_target="tpu_custom_call" | custom-call | flops 1000000 | bytes 1048576 | tf_op jit(solution)/shard_map/gate_kernel/pallas_call | solution.py:384
  8.8 0.7 %collective-permute-start.5 = (bf16[384,256]{1,0:T(8,128)(2,1)}, bf16[384,256]{1,0:T(8,128)(2,1)S(1)}, u32[]{:S(2)}, u32[]{:S(2)}) collective-permute-start(bf16[384,256]{1,0:T(8,128)(2,1)} %get-tuple-element.36), channel_id=1, source_target_pairs={{0,4},{4,0},{8,12},{12,8},{1,5},{5,1},{9,13},{13,9},{2,6},{6,2},{1... | collective-permute-start | bytes 589832 | tf_op jit(solution)/shard_map/ppermute | solution.py:397
  9.5 3.7 %collective-permute-start = (bf16[144,256]{1,0:T(8,128)(2,1)}, bf16[144,256]{1,0:T(8,128)(2,1)S(1)}, u32[]{:S(2)}, u32[]{:S(2)}) collective-permute-start(bf16[144,256]{1,0:T(8,128)(2,1)} %get-tuple-element.30), channel_id=1, source_target_pairs={{0,12},{4,8},{8,4},{12,0},{1,13},{5,9},{9,5},{13,1},{2,14},{6,10},... | collective-permute-start | bytes 221192 | tf_op jit(solution)/shard_map/ppermute | solution.py:397
  13.2 7.8 %collective-permute-start.2 = (bf16[144,256]{1,0:T(8,128)(2,1)}, bf16[144,256]{1,0:T(8,128)(2,1)S(1)}, u32[]{:S(2)}, u32[]{:S(2)}) collective-permute-start(bf16[144,256]{1,0:T(8,128)(2,1)} %get-tuple-element.32), channel_id=1, source_target_pairs={{0,4},{4,0},{8,12},{12,8},{1,5},{5,1},{9,13},{13,9},{2,6},{6,2},{1... | collective-permute-start | bytes 221192 | tf_op jit(solution)/shard_map/ppermute | solution.py:397
  21.0 0.7 %copy-done.3 = bf16[64,128]{1,0:T(8,128)(2,1)S(1)} copy-done((bf16[64,128]{1,0:T(8,128)(2,1)S(1)}, bf16[64,128]{1,0:T(8,128)(2,1)}, u32[]{:S(2)}) %copy-start.3) | copy-done | bytes 16408
  21.7 3.4 %ready_kernel.1 = (bf16[2048,256]{1,0:T(8,128)(2,1)S(1)}, bf16[1024,4096]{1,0:T(8,128)(2,1)S(1)}) custom-call(bf16[64,128]{1,0:T(8,128)(2,1)S(1)} %copy-done.3, bf16[1024,4096]{1,0:T(8,128)(2,1)} %weight_any.1), custom_call_target="tpu_custom_call" | custom-call | flops 1000000 | bytes 1048576 | tf_op jit(solution)/shard_map/ready_kernel/pallas_call | solution.py:384
  25.2 1.8 %collective-permute-done.4.second_ref = bf16[384,256]{1,0:T(8,128)(2,1)S(1)} collective-permute-done((bf16[384,256]{1,0:T(8,128)(2,1)S(1)}, bf16[384,256]{1,0:T(8,128)(2,1)S(1)}, u32[]{:S(2)}, u32[]{:S(2)}) %collective-permute-start.4) | collective-permute-done | bytes 196640 | tf_op jit(solution)/shard_map/ppermute | solution.py:397
  27.0 0.9 %weights_kernel.1 = (bf16[2,512,512]{2,1,0:T(8,128)(2,1)S(1)}, f32[512,128]{1,0:T(8,128)S(1)}, f32[512,256]{1,0:T(8,128)S(1)}) custom-call(bf16[384,256]{1,0:T(8,128)(2,1)S(1)} %collective-permute-done.3.third_ref, bf16[384,256]{1,0:T(8,128)(2,1)S(1)} %collective-permute-done.4.second_ref, bf16[384,256]{1,0:T(8,128)(2,1)S(1)} %collective-permute-done.5.near_ref, ...), custom_call_target="tpu_custom_call" | custom-call | flops 1000000 | bytes 1048576 | tf_op jit(solution)/shard_map/weights_kernel/pallas_call | solution.py:384
  28.0 1.2 %collective-permute-done.1.refs_1_ = bf16[144,256]{1,0:T(8,128)(2,1)S(1)} collective-permute-done((bf16[144,256]{1,0:T(8,128)(2,1)}, bf16[144,256]{1,0:T(8,128)(2,1)S(1)}, u32[]{:S(2)}, u32[]{:S(2)}) %collective-permute-start.1) | collective-permute-done | bytes 73760 | tf_op jit(solution)/shard_map/ppermute | solution.py:397
  29.2 1.1 %values_kernel.1 = (bf16[128,256]{1,0:T(8,128)(2,1)S(1)}, bf16[128,256]{1,0:T(8,128)(2,1)S(1)}, bf16[512,256]{1,0:T(8,128)(2,1)S(1)}) custom-call(bf16[144,256]{1,0:T(8,128)(2,1)S(1)} %collective-permute-done.refs_0_, bf16[144,256]{1,0:T(8,128)(2,1)S(1)} %collective-permute-done.1.refs_1_, bf16[144,256]{1,0:T(8,128)(2,1)S(1)} %collective-permute-done.2.refs_2_, ...), custom_call_target="tpu_custom_call" | custom-call | flops 1000000 | bytes 1048576 | tf_op jit(solution)/shard_map/values_kernel/pallas_call | solution.py:384
  30.3 0.9 %collective-permute-start.6 = (bf16[128,256]{1,0:T(8,128)(2,1)S(1)}, bf16[128,256]{1,0:T(8,128)(2,1)S(1)}, u32[]{:S(2)}, u32[]{:S(2)}) collective-permute-start(bf16[128,256]{1,0:T(8,128)(2,1)S(1)} %get-tuple-element.42), channel_id=1, source_target_pairs={{0,8},{4,12},{8,0},{12,4},{1,9},{5,13},{9,1},{13,5},{2,10},{6,14},... | collective-permute-start | bytes 196616 | tf_op jit(solution)/shard_map/ppermute | solution.py:397
  31.1 1.8 %collective-permute-start.7 = (bf16[128,256]{1,0:T(8,128)(2,1)S(1)}, bf16[128,256]{1,0:T(8,128)(2,1)S(1)}, u32[]{:S(2)}, u32[]{:S(2)}) collective-permute-start(bf16[128,256]{1,0:T(8,128)(2,1)S(1)} %get-tuple-element.43), channel_id=1, source_target_pairs={{0,12},{4,8},{8,4},{12,0},{1,13},{5,9},{9,5},{13,1},{2,14},{6,10},... | collective-permute-start | bytes 196616 | tf_op jit(solution)/shard_map/ppermute | solution.py:397
  33.2 1.0 %collective-permute-start.8 = (bf16[64,256]{1,0:T(8,128)(2,1)S(1)}, bf16[64,256]{1,0:T(8,128)(2,1)S(1)}, u32[]{:S(2)}, u32[]{:S(2)}) collective-permute-start(bf16[64,256]{1,0:T(8,128)(2,1)S(1)} %get-tuple-element.45), channel_id=1, source_target_pairs={{0,4},{4,0},{8,12},{12,8},{1,5},{5,1},{9,13},{13,9},{2,6},{6,2},{1... | collective-permute-start | bytes 98312 | tf_op jit(solution)/shard_map/ppermute | solution.py:397
  34.2 1.1 %collective-permute-start.9 = (bf16[64,256]{1,0:T(8,128)(2,1)S(1)}, bf16[64,256]{1,0:T(8,128)(2,1)S(1)}, u32[]{:S(2)}, u32[]{:S(2)}) collective-permute-start(bf16[64,256]{1,0:T(8,128)(2,1)S(1)} %get-tuple-element.46), channel_id=1, source_target_pairs={{0,4},{4,0},{8,12},{12,8},{1,5},{5,1},{9,13},{13,9},{2,6},{6,2},{1... | collective-permute-start | bytes 98312 | tf_op jit(solution)/shard_map/ppermute | solution.py:397
  35.3 1.3 %collective-permute-done.6.second_ref.refs_0_ = bf16[128,256]{1,0:T(8,128)(2,1)S(1)} collective-permute-done((bf16[128,256]{1,0:T(8,128)(2,1)S(1)}, bf16[128,256]{1,0:T(8,128)(2,1)S(1)}, u32[]{:S(2)}, u32[]{:S(2)}) %collective-permute-start.6) | collective-permute-done | bytes 65568 | tf_op jit(solution)/shard_map/ppermute | solution.py:397
  37.0 0.6 %collective-permute-done.8.upper_ref.refs_2_ = bf16[64,256]{1,0:T(8,128)(2,1)S(1)} collective-permute-done((bf16[64,256]{1,0:T(8,128)(2,1)S(1)}, bf16[64,256]{1,0:T(8,128)(2,1)S(1)}, u32[]{:S(2)}, u32[]{:S(2)}) %collective-permute-start.8) | collective-permute-done | bytes 32800 | tf_op jit(solution)/shard_map/ppermute | solution.py:397
  39.9 1.6 %collective-permute-start.14 = (bf16[128,512]{1,0:T(8,128)(2,1)S(1)}, bf16[128,512]{1,0:T(8,128)(2,1)S(1)}, u32[]{:S(2)}, u32[]{:S(2)}) collective-permute-start(bf16[128,512]{1,0:T(8,128)(2,1)S(1)} %add_convert_fusion), channel_id=1, source_target_pairs={{0,2},{1,3},{2,0},{3,1},{4,6},{5,7},{6,4},{7,5},{8,10},{9,11},{10,... | collective-permute-start | bytes 393224 | tf_op jit(solution)/shard_map/ppermute | solution.py:397
  41.5 0.6 %collective-permute-start.15 = (bf16[128,512]{1,0:T(8,128)(2,1)S(1)}, bf16[128,512]{1,0:T(8,128)(2,1)S(1)}, u32[]{:S(2)}, u32[]{:S(2)}) collective-permute-start(bf16[128,512]{1,0:T(8,128)(2,1)S(1)} %add_convert_fusion.1.refs_6_), channel_id=1, source_target_pairs={{0,2},{1,3},{2,0},{3,1},{4,6},{5,7},{6,4},{7,5},{8,10},{9,11},{10,... | collective-permute-start | bytes 393224 | tf_op jit(solution)/shard_map/ppermute | solution.py:397
  42.1 0.7 %project_kernel.1 = (bf16[128,1024]{1,0:T(8,128)(2,1)S(1)}, bf16[128,1024]{1,0:T(8,128)(2,1)S(1)}) custom-call(bf16[128,256]{1,0:T(8,128)(2,1)S(1)} %collective-permute-done.6.second_ref.refs_0_, bf16[128,256]{1,0:T(8,128)(2,1)S(1)} %collective-permute-done.7.third_ref.refs_1_, bf16[64,256]{1,0:T(8,128)(2,1)S(1)} %collective-permute-done.8.upper_ref.refs_2_, ...), custom_call_target="tpu_custom_call" | custom-call | flops 1000000 | bytes 1048576 | tf_op jit(solution)/shard_map/project_kernel/pallas_call | solution.py:384
  43.4 2.9 %collective-permute-done.14.first_ref = bf16[128,512]{1,0:T(8,128)(2,1)S(1)} collective-permute-done((bf16[128,512]{1,0:T(8,128)(2,1)S(1)}, bf16[128,512]{1,0:T(8,128)(2,1)S(1)}, u32[]{:S(2)}, u32[]{:S(2)}) %collective-permute-start.14) | collective-permute-done | bytes 131104 | tf_op jit(solution)/shard_map/ppermute | solution.py:397
  46.3 2.0 %collective-permute-done.15.second_ref = bf16[128,512]{1,0:T(8,128)(2,1)S(1)} collective-permute-done((bf16[128,512]{1,0:T(8,128)(2,1)S(1)}, bf16[128,512]{1,0:T(8,128)(2,1)S(1)}, u32[]{:S(2)}, u32[]{:S(2)}) %collective-permute-start.15) | collective-permute-done | bytes 131104 | tf_op jit(solution)/shard_map/ppermute | solution.py:397
  48.3 0.8 %total_kernel.1 = bf16[128,1024]{1,0:T(8,128)(2,1)} custom-call(bf16[128,1024]{1,0:T(8,128)(2,1)S(1)} %get-tuple-element.51.kept_ref, bf16[64,1024]{1,0:T(8,128)(2,1)S(1)} %collective-permute-done.11.upper_ref, bf16[64,1024]{1,0:T(8,128)(2,1)S(1)} %collective-permute-done.12.lower_ref, bf16[128,512]{1,0:T(8,128)(2,1)S(1)} %collective-permute-done.14.first_ref, ...), custom_call_target="tpu_custom_call" | custom-call | flops 1000000 | bytes 1048576 | tf_op jit(solution)/shard_map/total_kernel/pallas_call | solution.py:384
  (32 shorter events, 3.6 us)
Async XLA Ops:
  0.0 27.0 %copy-start = (bf16[3,3,1024]{2,1,0:T(4,128)(2,1)S(1)}, bf16[3,3,1024]{2,1,0:T(4,128)(2,1)}, u32[]{:S(2)}) copy-start(bf16[3,3,1024]{2,1,0:T(4,128)(2,1)} %refs_6_.1) | copy-start | bytes 55300
  0.0 29.2 %copy-start.4 = (f32[1024]{0:T(1024)S(1)}, f32[1024]{0:T(1024)}, u32[]{:S(2)}) copy-start(f32[1024]{0:T(1024)} %param.10) | copy-start | bytes 12292
  1.1 12.2 %collective-permute-start.3 = (bf16[384,256]{1,0:T(8,128)(2,1)S(1)}, bf16[384,256]{1,0:T(8,128)(2,1)S(1)}, u32[]{:S(2)}, u32[]{:S(2)}) collective-permute-start(bf16[384,256]{1,0:T(8,128)(2,1)S(1)} %get-tuple-element.34), channel_id=1, source_target_pairs={{0,12},{4,8},{8,4},{12,0},{1,13},{5,9},{9,5},{13,1},{2,14},{6,10},... | collective-permute-start | bytes 589832 | tf_op jit(solution)/shard_map/ppermute | solution.py:397
  6.2 20.8 %collective-permute-start.4 = (bf16[384,256]{1,0:T(8,128)(2,1)S(1)}, bf16[384,256]{1,0:T(8,128)(2,1)S(1)}, u32[]{:S(2)}, u32[]{:S(2)}) collective-permute-start(bf16[384,256]{1,0:T(8,128)(2,1)S(1)} %get-tuple-element.35), channel_id=1, source_target_pairs={{0,8},{4,12},{8,0},{12,4},{1,9},{5,13},{9,1},{13,5},{2,10},{6,14},... | collective-permute-start | bytes 589832 | tf_op jit(solution)/shard_map/ppermute | solution.py:397
  8.8 18.3 %copy-start.1 = (bf16[384,256]{1,0:T(8,128)(2,1)S(1)}, bf16[384,256]{1,0:T(8,128)(2,1)}, u32[]{:S(2)}) copy-start(bf16[384,256]{1,0:T(8,128)(2,1)} %get-tuple-element.37.own_ref) | copy-start | bytes 589828
  8.8 20.4 %copy-start.2 = (bf16[144,256]{1,0:T(8,128)(2,1)S(1)}, bf16[144,256]{1,0:T(8,128)(2,1)}, u32[]{:S(2)}) copy-start(bf16[144,256]{1,0:T(8,128)(2,1)} %get-tuple-element.33.refs_3_) | copy-start | bytes 221188
  8.8 18.2 %collective-permute-start.5 = (bf16[384,256]{1,0:T(8,128)(2,1)}, bf16[384,256]{1,0:T(8,128)(2,1)S(1)}, u32[]{:S(2)}, u32[]{:S(2)}) collective-permute-start(bf16[384,256]{1,0:T(8,128)(2,1)} %get-tuple-element.36), channel_id=1, source_target_pairs={{0,4},{4,0},{8,12},{12,8},{1,5},{5,1},{9,13},{13,9},{2,6},{6,2},{1... | collective-permute-start | bytes 589832 | tf_op jit(solution)/shard_map/ppermute | solution.py:397
  9.5 18.5 %collective-permute-start = (bf16[144,256]{1,0:T(8,128)(2,1)}, bf16[144,256]{1,0:T(8,128)(2,1)S(1)}, u32[]{:S(2)}, u32[]{:S(2)}) collective-permute-start(bf16[144,256]{1,0:T(8,128)(2,1)} %get-tuple-element.30), channel_id=1, source_target_pairs={{0,12},{4,8},{8,4},{12,0},{1,13},{5,9},{9,5},{13,1},{2,14},{6,10},... | collective-permute-start | bytes 221192 | tf_op jit(solution)/shard_map/ppermute | solution.py:397
  13.2 16.0 %collective-permute-start.1 = (bf16[144,256]{1,0:T(8,128)(2,1)}, bf16[144,256]{1,0:T(8,128)(2,1)S(1)}, u32[]{:S(2)}, u32[]{:S(2)}) collective-permute-start(bf16[144,256]{1,0:T(8,128)(2,1)} %get-tuple-element.31), channel_id=1, source_target_pairs={{0,8},{4,12},{8,0},{12,4},{1,9},{5,13},{9,1},{13,5},{2,10},{6,14},... | collective-permute-start | bytes 221192 | tf_op jit(solution)/shard_map/ppermute | solution.py:397
  13.2 16.0 %collective-permute-start.2 = (bf16[144,256]{1,0:T(8,128)(2,1)}, bf16[144,256]{1,0:T(8,128)(2,1)S(1)}, u32[]{:S(2)}, u32[]{:S(2)}) collective-permute-start(bf16[144,256]{1,0:T(8,128)(2,1)} %get-tuple-element.32), channel_id=1, source_target_pairs={{0,4},{4,0},{8,12},{12,8},{1,5},{5,1},{9,13},{13,9},{2,6},{6,2},{1... | collective-permute-start | bytes 221192 | tf_op jit(solution)/shard_map/ppermute | solution.py:397
  21.0 0.7 %copy-start.3 = (bf16[64,128]{1,0:T(8,128)(2,1)S(1)}, bf16[64,128]{1,0:T(8,128)(2,1)}, u32[]{:S(2)}) copy-start(bf16[64,128]{1,0:T(8,128)(2,1)} %filter_ref.1) | copy-start | bytes 49156
  30.3 6.3 %collective-permute-start.6 = (bf16[128,256]{1,0:T(8,128)(2,1)S(1)}, bf16[128,256]{1,0:T(8,128)(2,1)S(1)}, u32[]{:S(2)}, u32[]{:S(2)}) collective-permute-start(bf16[128,256]{1,0:T(8,128)(2,1)S(1)} %get-tuple-element.42), channel_id=1, source_target_pairs={{0,8},{4,12},{8,0},{12,4},{1,9},{5,13},{9,1},{13,5},{2,10},{6,14},... | collective-permute-start | bytes 196616 | tf_op jit(solution)/shard_map/ppermute | solution.py:397
  31.1 7.0 %collective-permute-start.7 = (bf16[128,256]{1,0:T(8,128)(2,1)S(1)}, bf16[128,256]{1,0:T(8,128)(2,1)S(1)}, u32[]{:S(2)}, u32[]{:S(2)}) collective-permute-start(bf16[128,256]{1,0:T(8,128)(2,1)S(1)} %get-tuple-element.43), channel_id=1, source_target_pairs={{0,12},{4,8},{8,4},{12,0},{1,13},{5,9},{9,5},{13,1},{2,14},{6,10},... | collective-permute-start | bytes 196616 | tf_op jit(solution)/shard_map/ppermute | solution.py:397
  33.2 4.5 %collective-permute-start.8 = (bf16[64,256]{1,0:T(8,128)(2,1)S(1)}, bf16[64,256]{1,0:T(8,128)(2,1)S(1)}, u32[]{:S(2)}, u32[]{:S(2)}) collective-permute-start(bf16[64,256]{1,0:T(8,128)(2,1)S(1)} %get-tuple-element.45), channel_id=1, source_target_pairs={{0,4},{4,0},{8,12},{12,8},{1,5},{5,1},{9,13},{13,9},{2,6},{6,2},{1... | collective-permute-start | bytes 98312 | tf_op jit(solution)/shard_map/ppermute | solution.py:397
  34.2 3.9 %collective-permute-start.9 = (bf16[64,256]{1,0:T(8,128)(2,1)S(1)}, bf16[64,256]{1,0:T(8,128)(2,1)S(1)}, u32[]{:S(2)}, u32[]{:S(2)}) collective-permute-start(bf16[64,256]{1,0:T(8,128)(2,1)S(1)} %get-tuple-element.46), channel_id=1, source_target_pairs={{0,4},{4,0},{8,12},{12,8},{1,5},{5,1},{9,13},{13,9},{2,6},{6,2},{1... | collective-permute-start | bytes 98312 | tf_op jit(solution)/shard_map/ppermute | solution.py:397
  38.4 1.4 %collective-permute-start.13 = (bf16[128,512]{1,0:T(8,128)(2,1)S(1)}, bf16[128,512]{1,0:T(8,128)(2,1)S(1)}, u32[]{:S(2)}, u32[]{:S(2)}) collective-permute-start(bf16[128,512]{1,0:T(8,128)(2,1)S(1)} %get-tuple-element.54), channel_id=1, source_target_pairs={{0,1},{1,0},{2,3},{3,2},{4,5},{5,4},{6,7},{7,6},{8,9},{9,8},{10,11... | collective-permute-start | bytes 393224 | tf_op jit(solution)/shard_map/ppermute | solution.py:397
  38.9 2.6 %collective-permute-start.10 = (bf16[128,512]{1,0:T(8,128)(2,1)S(1)}, bf16[128,512]{1,0:T(8,128)(2,1)S(1)}, u32[]{:S(2)}, u32[]{:S(2)}) collective-permute-start(bf16[128,512]{1,0:T(8,128)(2,1)S(1)} %get-tuple-element.50), channel_id=1, source_target_pairs={{0,1},{1,0},{2,3},{3,2},{4,5},{5,4},{6,7},{7,6},{8,9},{9,8},{10,11... | collective-permute-start | bytes 393224 | tf_op jit(solution)/shard_map/ppermute | solution.py:397
  39.9 6.4 %collective-permute-start.14 = (bf16[128,512]{1,0:T(8,128)(2,1)S(1)}, bf16[128,512]{1,0:T(8,128)(2,1)S(1)}, u32[]{:S(2)}, u32[]{:S(2)}) collective-permute-start(bf16[128,512]{1,0:T(8,128)(2,1)S(1)} %add_convert_fusion), channel_id=1, source_target_pairs={{0,2},{1,3},{2,0},{3,1},{4,6},{5,7},{6,4},{7,5},{8,10},{9,11},{10,... | collective-permute-start | bytes 393224 | tf_op jit(solution)/shard_map/ppermute | solution.py:397
  41.5 6.8 %collective-permute-start.15 = (bf16[128,512]{1,0:T(8,128)(2,1)S(1)}, bf16[128,512]{1,0:T(8,128)(2,1)S(1)}, u32[]{:S(2)}, u32[]{:S(2)}) collective-permute-start(bf16[128,512]{1,0:T(8,128)(2,1)S(1)} %add_convert_fusion.1.refs_6_), channel_id=1, source_target_pairs={{0,2},{1,3},{2,0},{3,1},{4,6},{5,7},{6,4},{7,5},{8,10},{9,11},{10,... | collective-permute-start | bytes 393224 | tf_op jit(solution)/shard_map/ppermute | solution.py:397
  42.9 5.5 %collective-permute-start.12 = (bf16[64,1024]{1,0:T(8,128)(2,1)S(1)}, bf16[64,1024]{1,0:T(8,128)(2,1)S(1)}, u32[]{:S(2)}, u32[]{:S(2)}) collective-permute-start(bf16[64,1024]{1,0:T(8,128)(2,1)S(1)} %get-tuple-element.55), channel_id=1, source_target_pairs={{0,1},{1,0},{2,3},{3,2},{4,5},{5,4},{6,7},{7,6},{8,9},{9,8},{10,11... | collective-permute-start | bytes 393224 | tf_op jit(solution)/shard_map/ppermute | solution.py:397
  42.9 5.4 %collective-permute-start.11 = (bf16[64,1024]{1,0:T(8,128)(2,1)S(1)}, bf16[64,1024]{1,0:T(8,128)(2,1)S(1)}, u32[]{:S(2)}, u32[]{:S(2)}) collective-permute-start(bf16[64,1024]{1,0:T(8,128)(2,1)S(1)} %get-tuple-element.56), channel_id=1, source_target_pairs={{0,1},{1,0},{2,3},{3,2},{4,5},{5,4},{6,7},{7,6},{8,9},{9,8},{10,11... | collective-permute-start | bytes 393224 | tf_op jit(solution)/shard_map/ppermute | solution.py:397

commit v16 on v15

--- a/solution.py
+++ b/solution.py
@@ -10,7 +10,7 @@
 HEAD_DIM = 128
 COUNT = 4
 ORDER = (3, 2, 1, 0)
-EDGE = 16
+EDGE = 8
 
 
 masked_score = -1e30
@@ -122,14 +122,20 @@
 
 def write_gate(signals, taps, out_ref):
     rows, own = signals[0].shape
-    edge_row = lax.broadcasted_iota(jnp.int32, (8, own), 0)
+    tiles = [slice(start, start + HEAD_DIM) for start in range(0, own, HEAD_DIM)]
+    edge_row = lax.broadcasted_iota(jnp.int32, (EDGE, own), 0)
     features = [featured(signal, tap) for signal, tap in zip(signals, taps)]
-    edges = [
-        jnp.where(edge_row < 2, signal[:8], jnp.where(edge_row < 4, pltpu.roll(signal[rows - 8 :], 4, 0), 0.0))
-        for signal in signals
+    gate = (features[0] * features[1]).astype(jnp.bfloat16)
+    first, second = [
+        jnp.where(
+            edge_row % 4 < 2, pltpu.roll(signal[:EDGE], turn, 0), pltpu.roll(signal[rows - EDGE :], 4 - turn, 0)
+        )
+        for signal, turn in zip(signals, (0, 4))
     ]
-    out_ref[0:rows] = (features[0] * features[1]).astype(jnp.bfloat16)
-    out_ref[rows : rows + EDGE] = jnp.concatenate(edges, axis=0).astype(jnp.bfloat16)
+    edges = jnp.where(edge_row < 4, first, second)
+    for index, tile in enumerate(tiles):
+        out_ref[index * rows : (index + 1) * rows] = gate[:, tile]
+    out_ref[len(tiles) * rows :] = jnp.concatenate([edges[:, tile] for tile in tiles], axis=0).astype(jnp.bfloat16)
 
 
 def plain_copies(sources, out_refs, steps, sems):
@@ -154,7 +160,7 @@
 def gate_kernel(inputs_any, short_any, queries_any, keys_any, *refs):
     out_refs, plain_refs = refs[:COUNT], refs[COUNT : COUNT + 2]
     signal_s, short_s, sems, plain_sems = refs[COUNT + 2 :]
-    own = out_refs[0].shape[1]
+    own = plain_refs[0].shape[1]
     position = lax.axis_index("ctx")
     copies = [
         pltpu.make_async_copy(short_any, short_s, sems.at[0]),
@@ -239,38 +245,38 @@
     gates, feature_ref = refs[:count], refs[count]
     band_ref, short_ref, gain_ref, weight_ref, total_ref = refs[count + 1 : count + 6]
     third_ref, second_ref, value_ref = refs[count + 6 : count + 9]
-    gates_s, gate_s, filtered_s = refs[count + 9 :]
+    edge_s, gate_s, filtered_s = refs[count + 9 :]
     rows, own = second_ref.shape
     per_group = own * rows // band_ref.shape[0]
     position = lax.axis_index("ctx")
     mine = columns_of(position, own)
+    tiles = [slice(start, start + HEAD_DIM) for start in range(0, own, HEAD_DIM)]
+    gate_s[0:rows] = jnp.zeros((rows, own), jnp.bfloat16)
     for step, gate in zip(ORDER, gates):
-        gates_s[position ^ step] = gate[...]
+        for index, tile in enumerate(tiles):
+            gate_s[columns_of((position ^ step) + 1, rows), tile] = gate[index * rows : (index + 1) * rows]
+        edges = gate[len(tiles) * rows :].astype(jnp.float32)
+        for index, tile in enumerate(tiles):
+            edge_s[position ^ step, :, tile] = edges[index * EDGE : (index + 1) * EDGE]
     taps = [
         [short_ref[lag, stream : stream + 1, mine].astype(jnp.float32) for lag in range(3)] for stream in range(3)
     ]
-    gate_s[0:rows] = jnp.zeros((rows, own), jnp.bfloat16)
-    edge_row = lax.broadcasted_iota(jnp.int32, (8, own), 0)
-    head_row = lax.broadcasted_iota(jnp.int32, (16, own), 0)
-    for block in range(count):
-        gate_s[(block + 1) * rows : (block + 2) * rows] = gates_s[block, 0:rows]
-        if block == 0:
-            continue
+    edge_row = lax.broadcasted_iota(jnp.int32, (EDGE, own), 0)
+    head_row = lax.broadcasted_iota(jnp.int32, (2 * EDGE, own), 0)
+    for block in range(1, count):
         fixed = 1.0
-        before = gates_s[block - 1, rows:].astype(jnp.float32)
-        here = gates_s[block, rows:].astype(jnp.float32)
-        for which, stream in enumerate((1, 2)):
-            old = pltpu.roll(before[8 * which : 8 * which + 8], 6, 0)
-            new = pltpu.roll(here[8 * which : 8 * which + 8], 2, 0)
-            joined = jnp.where(edge_row < 2, old, new)
+        for stream, back, on in ((1, 6, 2), (2, 2, 6)):
+            joined = jnp.where(
+                edge_row < 2, pltpu.roll(edge_s[block - 1], back, 0), pltpu.roll(edge_s[block], on, 0)
+            )
             fixed = fixed * (
                 taps[stream][0] * pltpu.roll(joined, 6, 0)
                 + taps[stream][1] * pltpu.roll(joined, 7, 0)
                 + taps[stream][2] * joined
             )
-        head = gates_s[block, 0:16].astype(jnp.float32)
-        head = jnp.where(head_row < 2, jnp.concatenate([fixed, fixed], axis=0), head)
-        gate_s[(block + 1) * rows : (block + 1) * rows + 16] = head.astype(jnp.bfloat16)
+        here = slice((block + 1) * rows, (block + 1) * rows + 2 * EDGE)
+        head = jnp.where(head_row < 2, jnp.concatenate([fixed, fixed], axis=0), gate_s[here].astype(jnp.float32))
+        gate_s[here] = head.astype(jnp.bfloat16)
     gain = gain_ref[:, mine]
     chunk = 2 * HEAD_DIM // count
     in_chunk = chunk // per_group
@@ -415,7 +421,7 @@
     *gates, near_plain, own_plain = run_kernel(
         gate_kernel,
         (streamed, short_filter, queries, key_rows),
-        [((rows + EDGE, own), half)] * COUNT + [((3 * rows, own), half)] * 2,
+        [((own // HEAD_DIM * (rows + EDGE), HEAD_DIM), half)] * COUNT + [((3 * rows, own), half)] * 2,
         [
             pltpu.VMEM((2, rows, channels), half),
             pltpu.VMEM(short_filter.shape, half),
@@ -454,7 +460,7 @@
         (*gates, feature, band, short_filter, skip_gain.reshape(1, channels), soft, totals),
         [piece, piece, ((window, own), half)],
         [
-            pltpu.VMEM((COUNT, rows + EDGE, own), half),
+            pltpu.VMEM((COUNT, EDGE, own), jnp.float32),
             pltpu.VMEM((window + rows, own), half),
             pltpu.VMEM((window, own), jnp.float32),
         ],

time: 49.4 us -> 49 us (level)
  no operation moved by 1% of the time
where the time goes in v16:
time: 49 us; the launch traced here: 48.7 us
  starting transfers between devices  25.4 us (52%)
  Pallas kernels  11.9 us (24%)
  waiting for transfers between devices  10.4 us (21%)
  local copies, waits for them, and re-layouts  0.75 us (2%)
    ppermute x16, starting transfers between devices, swapped(): lax.ppermute(value, axis, [(source, source ^ step) for source in range(la...  25.4 us
    pallas_call x11, Pallas kernels, run_kernel(): pl.pallas_call(kernel, out_shape=[jax.ShapeDtypeStruct(shape, dtype) for...  11.9 us
    ppermute x16, waiting for transfers between devices, swapped(): lax.ppermute(value, axis, [(source, source ^ step) for source in range(la...  10.4 us
  transfers between devices with their start and end apart: 16, of which 8 were waited for; matrix products, arithmetic and copies ran while one was open for 0% of the time, Pallas kernels for 18%

profile of v16, /device:TPU:0, one launch (start us, length us, event | category | flops | bytes accessed | tf_op | source)
XLA Modules:
  0.0 48.7 jit_solution(8452312296601799490)
XLA Ops:
  0.0 1.1 %plain_kernel.1 = (bf16[384,256]{1,0:T(8,128)(2,1)S(1)}, bf16[384,256]{1,0:T(8,128)(2,1)S(1)}) custom-call(bf16[3,128,1024]{2,1,0:T(8,128)(2,1)} %bitcast.3, bf16[128,1024]{1,0:T(8,128)(2,1)} %queries_any.3, bf16[128,1024]{1,0:T(8,128)(2,1)} %keys_any.3), custom_call_target="tpu_custom_call" | custom-call | flops 1000000 | bytes 1048576 | tf_op jit(solution)/shard_map/plain_kernel/pallas_call | solution.py:390
  1.1 5.1 %collective-permute-start.3 = (bf16[384,256]{1,0:T(8,128)(2,1)S(1)}, bf16[384,256]{1,0:T(8,128)(2,1)S(1)}, u32[]{:S(2)}, u32[]{:S(2)}) collective-permute-start(bf16[384,256]{1,0:T(8,128)(2,1)S(1)} %get-tuple-element.34), channel_id=1, source_target_pairs={{0,12},{4,8},{8,4},{12,0},{1,13},{5,9},{9,5},{13,1},{2,14},{6,10},... | collective-permute-start | bytes 589832 | tf_op jit(solution)/shard_map/ppermute | solution.py:403
  6.2 2.5 %gate_kernel.1 = (bf16[272,128]{1,0:T(8,128)(2,1)}, bf16[272,128]{1,0:T(8,128)(2,1)}, bf16[272,128]{1,0:T(8,128)(2,1)}, bf16[272,128]{1,0:T(8,128)(2,1)}, bf16[3...) custom-call(bf16[3,128,1024]{2,1,0:T(8,128)(2,1)} %bitcast.4, bf16[3,3,1024]{2,1,0:T(4,128)(2,1)} %refs_6_.1, ...), custom_call_target="tpu_custom_call" | custom-call | flops 1000000 | bytes 1048576 | tf_op jit(solution)/shard_map/gate_kernel/pallas_call | solution.py:390
  8.8 0.7 %collective-permute-start.5 = (bf16[384,256]{1,0:T(8,128)(2,1)}, bf16[384,256]{1,0:T(8,128)(2,1)S(1)}, u32[]{:S(2)}, u32[]{:S(2)}) collective-permute-start(bf16[384,256]{1,0:T(8,128)(2,1)} %get-tuple-element.36), channel_id=1, source_target_pairs={{0,4},{4,0},{8,12},{12,8},{1,5},{5,1},{9,13},{13,9},{2,6},{6,2},{1... | collective-permute-start | bytes 589832 | tf_op jit(solution)/shard_map/ppermute | solution.py:403
  9.5 3.7 %collective-permute-start = (bf16[272,128]{1,0:T(8,128)(2,1)}, bf16[272,128]{1,0:T(8,128)(2,1)S(1)}, u32[]{:S(2)}, u32[]{:S(2)}) collective-permute-start(bf16[272,128]{1,0:T(8,128)(2,1)} %get-tuple-element.30), channel_id=1, source_target_pairs={{0,12},{4,8},{8,4},{12,0},{1,13},{5,9},{9,5},{13,1},{2,14},{6,10},... | collective-permute-start | bytes 208904 | tf_op jit(solution)/shard_map/ppermute | solution.py:403
  13.2 7.8 %collective-permute-start.2 = (bf16[272,128]{1,0:T(8,128)(2,1)}, bf16[272,128]{1,0:T(8,128)(2,1)S(1)}, u32[]{:S(2)}, u32[]{:S(2)}) collective-permute-start(bf16[272,128]{1,0:T(8,128)(2,1)} %get-tuple-element.32), channel_id=1, source_target_pairs={{0,4},{4,0},{8,12},{12,8},{1,5},{5,1},{9,13},{13,9},{2,6},{6,2},{1... | collective-permute-start | bytes 208904 | tf_op jit(solution)/shard_map/ppermute | solution.py:403
  21.0 0.7 %copy-done.3 = bf16[64,128]{1,0:T(8,128)(2,1)S(1)} copy-done((bf16[64,128]{1,0:T(8,128)(2,1)S(1)}, bf16[64,128]{1,0:T(8,128)(2,1)}, u32[]{:S(2)}) %copy-start.3) | copy-done | bytes 16408
  21.7 3.4 %ready_kernel.1 = (bf16[2048,256]{1,0:T(8,128)(2,1)S(1)}, bf16[1024,4096]{1,0:T(8,128)(2,1)S(1)}) custom-call(bf16[64,128]{1,0:T(8,128)(2,1)S(1)} %copy-done.3, bf16[1024,4096]{1,0:T(8,128)(2,1)} %weight_any.1), custom_call_target="tpu_custom_call" | custom-call | flops 1000000 | bytes 1048576 | tf_op jit(solution)/shard_map/ready_kernel/pallas_call | solution.py:390
  25.2 1.7 %collective-permute-done.4.second_ref = bf16[384,256]{1,0:T(8,128)(2,1)S(1)} collective-permute-done((bf16[384,256]{1,0:T(8,128)(2,1)S(1)}, bf16[384,256]{1,0:T(8,128)(2,1)S(1)}, u32[]{:S(2)}, u32[]{:S(2)}) %collective-permute-start.4) | collective-permute-done | bytes 196640 | tf_op jit(solution)/shard_map/ppermute | solution.py:403
  26.8 0.9 %weights_kernel.1 = (bf16[2,512,512]{2,1,0:T(8,128)(2,1)S(1)}, f32[512,128]{1,0:T(8,128)S(1)}, f32[512,256]{1,0:T(8,128)S(1)}) custom-call(bf16[384,256]{1,0:T(8,128)(2,1)S(1)} %collective-permute-done.3.third_ref, bf16[384,256]{1,0:T(8,128)(2,1)S(1)} %collective-permute-done.4.second_ref, bf16[384,256]{1,0:T(8,128)(2,1)S(1)} %collective-permute-done.5.near_ref, ...), custom_call_target="tpu_custom_call" | custom-call | flops 1000000 | bytes 1048576 | tf_op jit(solution)/shard_map/weights_kernel/pallas_call | solution.py:390
  27.8 1.1 %collective-permute-done.1.refs_1_ = bf16[272,128]{1,0:T(8,128)(2,1)S(1)} collective-permute-done((bf16[272,128]{1,0:T(8,128)(2,1)}, bf16[272,128]{1,0:T(8,128)(2,1)S(1)}, u32[]{:S(2)}, u32[]{:S(2)}) %collective-permute-start.1) | collective-permute-done | bytes 69664 | tf_op jit(solution)/shard_map/ppermute | solution.py:403
  28.9 1.1 %values_kernel.1 = (bf16[128,256]{1,0:T(8,128)(2,1)S(1)}, bf16[128,256]{1,0:T(8,128)(2,1)S(1)}, bf16[512,256]{1,0:T(8,128)(2,1)S(1)}) custom-call(bf16[272,128]{1,0:T(8,128)(2,1)S(1)} %collective-permute-done.refs_0_, bf16[272,128]{1,0:T(8,128)(2,1)S(1)} %collective-permute-done.1.refs_1_, bf16[272,128]{1,0:T(8,128)(2,1)S(1)} %collective-permute-done.2.refs_2_, ...), custom_call_target="tpu_custom_call" | custom-call | flops 1000000 | bytes 1048576 | tf_op jit(solution)/shard_map/values_kernel/pallas_call | solution.py:390
  29.9 0.9 %collective-permute-start.6 = (bf16[128,256]{1,0:T(8,128)(2,1)S(1)}, bf16[128,256]{1,0:T(8,128)(2,1)S(1)}, u32[]{:S(2)}, u32[]{:S(2)}) collective-permute-start(bf16[128,256]{1,0:T(8,128)(2,1)S(1)} %get-tuple-element.42), channel_id=1, source_target_pairs={{0,8},{4,12},{8,0},{12,4},{1,9},{5,13},{9,1},{13,5},{2,10},{6,14},... | collective-permute-start | bytes 196616 | tf_op jit(solution)/shard_map/ppermute | solution.py:403
  30.8 1.7 %collective-permute-start.7 = (bf16[128,256]{1,0:T(8,128)(2,1)S(1)}, bf16[128,256]{1,0:T(8,128)(2,1)S(1)}, u32[]{:S(2)}, u32[]{:S(2)}) collective-permute-start(bf16[128,256]{1,0:T(8,128)(2,1)S(1)} %get-tuple-element.43), channel_id=1, source_target_pairs={{0,12},{4,8},{8,4},{12,0},{1,13},{5,9},{9,5},{13,1},{2,14},{6,10},... | collective-permute-start | bytes 196616 | tf_op jit(solution)/shard_map/ppermute | solution.py:403
  32.8 1.0 %collective-permute-start.8 = (bf16[64,256]{1,0:T(8,128)(2,1)S(1)}, bf16[64,256]{1,0:T(8,128)(2,1)S(1)}, u32[]{:S(2)}, u32[]{:S(2)}) collective-permute-start(bf16[64,256]{1,0:T(8,128)(2,1)S(1)} %get-tuple-element.45), channel_id=1, source_target_pairs={{0,4},{4,0},{8,12},{12,8},{1,5},{5,1},{9,13},{13,9},{2,6},{6,2},{1... | collective-permute-start | bytes 98312 | tf_op jit(solution)/shard_map/ppermute | solution.py:403
  33.9 1.1 %collective-permute-start.9 = (bf16[64,256]{1,0:T(8,128)(2,1)S(1)}, bf16[64,256]{1,0:T(8,128)(2,1)S(1)}, u32[]{:S(2)}, u32[]{:S(2)}) collective-permute-start(bf16[64,256]{1,0:T(8,128)(2,1)S(1)} %get-tuple-element.46), channel_id=1, source_target_pairs={{0,4},{4,0},{8,12},{12,8},{1,5},{5,1},{9,13},{13,9},{2,6},{6,2},{1... | collective-permute-start | bytes 98312 | tf_op jit(solution)/shard_map/ppermute | solution.py:403
  34.9 1.3 %collective-permute-done.6.second_ref.refs_0_ = bf16[128,256]{1,0:T(8,128)(2,1)S(1)} collective-permute-done((bf16[128,256]{1,0:T(8,128)(2,1)S(1)}, bf16[128,256]{1,0:T(8,128)(2,1)S(1)}, u32[]{:S(2)}, u32[]{:S(2)}) %collective-permute-start.6) | collective-permute-done | bytes 65568 | tf_op jit(solution)/shard_map/ppermute | solution.py:403
  36.7 0.7 %collective-permute-done.8.upper_ref.refs_2_ = bf16[64,256]{1,0:T(8,128)(2,1)S(1)} collective-permute-done((bf16[64,256]{1,0:T(8,128)(2,1)S(1)}, bf16[64,256]{1,0:T(8,128)(2,1)S(1)}, u32[]{:S(2)}, u32[]{:S(2)}) %collective-permute-start.8) | collective-permute-done | bytes 32800 | tf_op jit(solution)/shard_map/ppermute | solution.py:403
  39.5 1.6 %collective-permute-start.14 = (bf16[128,512]{1,0:T(8,128)(2,1)S(1)}, bf16[128,512]{1,0:T(8,128)(2,1)S(1)}, u32[]{:S(2)}, u32[]{:S(2)}) collective-permute-start(bf16[128,512]{1,0:T(8,128)(2,1)S(1)} %add_convert_fusion), channel_id=1, source_target_pairs={{0,2},{1,3},{2,0},{3,1},{4,6},{5,7},{6,4},{7,5},{8,10},{9,11},{10,... | collective-permute-start | bytes 393224 | tf_op jit(solution)/shard_map/ppermute | solution.py:403
  41.1 0.6 %collective-permute-start.15 = (bf16[128,512]{1,0:T(8,128)(2,1)S(1)}, bf16[128,512]{1,0:T(8,128)(2,1)S(1)}, u32[]{:S(2)}, u32[]{:S(2)}) collective-permute-start(bf16[128,512]{1,0:T(8,128)(2,1)S(1)} %add_convert_fusion.1.refs_6_), channel_id=1, source_target_pairs={{0,2},{1,3},{2,0},{3,1},{4,6},{5,7},{6,4},{7,5},{8,10},{9,11},{10,... | collective-permute-start | bytes 393224 | tf_op jit(solution)/shard_map/ppermute | solution.py:403
  41.7 0.7 %project_kernel.1 = (bf16[128,1024]{1,0:T(8,128)(2,1)S(1)}, bf16[128,1024]{1,0:T(8,128)(2,1)S(1)}) custom-call(bf16[128,256]{1,0:T(8,128)(2,1)S(1)} %collective-permute-done.6.second_ref.refs_0_, bf16[128,256]{1,0:T(8,128)(2,1)S(1)} %collective-permute-done.7.third_ref.refs_1_, bf16[64,256]{1,0:T(8,128)(2,1)S(1)} %collective-permute-done.8.upper_ref.refs_2_, ...), custom_call_target="tpu_custom_call" | custom-call | flops 1000000 | bytes 1048576 | tf_op jit(solution)/shard_map/project_kernel/pallas_call | solution.py:390
  43.1 2.9 %collective-permute-done.14.first_ref = bf16[128,512]{1,0:T(8,128)(2,1)S(1)} collective-permute-done((bf16[128,512]{1,0:T(8,128)(2,1)S(1)}, bf16[128,512]{1,0:T(8,128)(2,1)S(1)}, u32[]{:S(2)}, u32[]{:S(2)}) %collective-permute-start.14) | collective-permute-done | bytes 131104 | tf_op jit(solution)/shard_map/ppermute | solution.py:403
  45.9 2.0 %collective-permute-done.15.second_ref = bf16[128,512]{1,0:T(8,128)(2,1)S(1)} collective-permute-done((bf16[128,512]{1,0:T(8,128)(2,1)S(1)}, bf16[128,512]{1,0:T(8,128)(2,1)S(1)}, u32[]{:S(2)}, u32[]{:S(2)}) %collective-permute-start.15) | collective-permute-done | bytes 131104 | tf_op jit(solution)/shard_map/ppermute | solution.py:403
  48.0 0.8 %total_kernel.1 = bf16[128,1024]{1,0:T(8,128)(2,1)} custom-call(bf16[128,1024]{1,0:T(8,128)(2,1)S(1)} %get-tuple-element.51.kept_ref, bf16[64,1024]{1,0:T(8,128)(2,1)S(1)} %collective-permute-done.11.upper_ref, bf16[64,1024]{1,0:T(8,128)(2,1)S(1)} %collective-permute-done.12.lower_ref, bf16[128,512]{1,0:T(8,128)(2,1)S(1)} %collective-permute-done.14.first_ref, ...), custom_call_target="tpu_custom_call" | custom-call | flops 1000000 | bytes 1048576 | tf_op jit(solution)/shard_map/total_kernel/pallas_call | solution.py:390
  (32 shorter events, 3.6 us)
Async XLA Ops:
  0.0 26.8 %copy-start = (bf16[3,3,1024]{2,1,0:T(4,128)(2,1)S(1)}, bf16[3,3,1024]{2,1,0:T(4,128)(2,1)}, u32[]{:S(2)}) copy-start(bf16[3,3,1024]{2,1,0:T(4,128)(2,1)} %refs_6_.1) | copy-start | bytes 55300
  0.0 28.9 %copy-start.4 = (f32[1024]{0:T(1024)S(1)}, f32[1024]{0:T(1024)}, u32[]{:S(2)}) copy-start(f32[1024]{0:T(1024)} %param.10) | copy-start | bytes 12292
  1.1 12.2 %collective-permute-start.3 = (bf16[384,256]{1,0:T(8,128)(2,1)S(1)}, bf16[384,256]{1,0:T(8,128)(2,1)S(1)}, u32[]{:S(2)}, u32[]{:S(2)}) collective-permute-start(bf16[384,256]{1,0:T(8,128)(2,1)S(1)} %get-tuple-element.34), channel_id=1, source_target_pairs={{0,12},{4,8},{8,4},{12,0},{1,13},{5,9},{9,5},{13,1},{2,14},{6,10},... | collective-permute-start | bytes 589832 | tf_op jit(solution)/shard_map/ppermute | solution.py:403
  6.2 20.6 %collective-permute-start.4 = (bf16[384,256]{1,0:T(8,128)(2,1)S(1)}, bf16[384,256]{1,0:T(8,128)(2,1)S(1)}, u32[]{:S(2)}, u32[]{:S(2)}) collective-permute-start(bf16[384,256]{1,0:T(8,128)(2,1)S(1)} %get-tuple-element.35), channel_id=1, source_target_pairs={{0,8},{4,12},{8,0},{12,4},{1,9},{5,13},{9,1},{13,5},{2,10},{6,14},... | collective-permute-start | bytes 589832 | tf_op jit(solution)/shard_map/ppermute | solution.py:403
  8.7 18.1 %copy-start.1 = (bf16[384,256]{1,0:T(8,128)(2,1)S(1)}, bf16[384,256]{1,0:T(8,128)(2,1)}, u32[]{:S(2)}) copy-start(bf16[384,256]{1,0:T(8,128)(2,1)} %get-tuple-element.37.own_ref) | copy-start | bytes 589828
  8.8 20.1 %copy-start.2 = (bf16[272,128]{1,0:T(8,128)(2,1)S(1)}, bf16[272,128]{1,0:T(8,128)(2,1)}, u32[]{:S(2)}) copy-start(bf16[272,128]{1,0:T(8,128)(2,1)} %get-tuple-element.33.refs_3_) | copy-start | bytes 208900
  8.8 18.1 %collective-permute-start.5 = (bf16[384,256]{1,0:T(8,128)(2,1)}, bf16[384,256]{1,0:T(8,128)(2,1)S(1)}, u32[]{:S(2)}, u32[]{:S(2)}) collective-permute-start(bf16[384,256]{1,0:T(8,128)(2,1)} %get-tuple-element.36), channel_id=1, source_target_pairs={{0,4},{4,0},{8,12},{12,8},{1,5},{5,1},{9,13},{13,9},{2,6},{6,2},{1... | collective-permute-start | bytes 589832 | tf_op jit(solution)/shard_map/ppermute | solution.py:403
  9.5 18.3 %collective-permute-start = (bf16[272,128]{1,0:T(8,128)(2,1)}, bf16[272,128]{1,0:T(8,128)(2,1)S(1)}, u32[]{:S(2)}, u32[]{:S(2)}) collective-permute-start(bf16[272,128]{1,0:T(8,128)(2,1)} %get-tuple-element.30), channel_id=1, source_target_pairs={{0,12},{4,8},{8,4},{12,0},{1,13},{5,9},{9,5},{13,1},{2,14},{6,10},... | collective-permute-start | bytes 208904 | tf_op jit(solution)/shard_map/ppermute | solution.py:403
  13.2 15.6 %collective-permute-start.1 = (bf16[272,128]{1,0:T(8,128)(2,1)}, bf16[272,128]{1,0:T(8,128)(2,1)S(1)}, u32[]{:S(2)}, u32[]{:S(2)}) collective-permute-start(bf16[272,128]{1,0:T(8,128)(2,1)} %get-tuple-element.31), channel_id=1, source_target_pairs={{0,8},{4,12},{8,0},{12,4},{1,9},{5,13},{9,1},{13,5},{2,10},{6,14},... | collective-permute-start | bytes 208904 | tf_op jit(solution)/shard_map/ppermute | solution.py:403
  13.2 15.6 %collective-permute-start.2 = (bf16[272,128]{1,0:T(8,128)(2,1)}, bf16[272,128]{1,0:T(8,128)(2,1)S(1)}, u32[]{:S(2)}, u32[]{:S(2)}) collective-permute-start(bf16[272,128]{1,0:T(8,128)(2,1)} %get-tuple-element.32), channel_id=1, source_target_pairs={{0,4},{4,0},{8,12},{12,8},{1,5},{5,1},{9,13},{13,9},{2,6},{6,2},{1... | collective-permute-start | bytes 208904 | tf_op jit(solution)/shard_map/ppermute | solution.py:403
  21.0 0.7 %copy-start.3 = (bf16[64,128]{1,0:T(8,128)(2,1)S(1)}, bf16[64,128]{1,0:T(8,128)(2,1)}, u32[]{:S(2)}) copy-start(bf16[64,128]{1,0:T(8,128)(2,1)} %filter_ref.1) | copy-start | bytes 49156
  29.9 6.3 %collective-permute-start.6 = (bf16[128,256]{1,0:T(8,128)(2,1)S(1)}, bf16[128,256]{1,0:T(8,128)(2,1)S(1)}, u32[]{:S(2)}, u32[]{:S(2)}) collective-permute-start(bf16[128,256]{1,0:T(8,128)(2,1)S(1)} %get-tuple-element.42), channel_id=1, source_target_pairs={{0,8},{4,12},{8,0},{12,4},{1,9},{5,13},{9,1},{13,5},{2,10},{6,14},... | collective-permute-start | bytes 196616 | tf_op jit(solution)/shard_map/ppermute | solution.py:403
  30.8 6.9 %collective-permute-start.7 = (bf16[128,256]{1,0:T(8,128)(2,1)S(1)}, bf16[128,256]{1,0:T(8,128)(2,1)S(1)}, u32[]{:S(2)}, u32[]{:S(2)}) collective-permute-start(bf16[128,256]{1,0:T(8,128)(2,1)S(1)} %get-tuple-element.43), channel_id=1, source_target_pairs={{0,12},{4,8},{8,4},{12,0},{1,13},{5,9},{9,5},{13,1},{2,14},{6,10},... | collective-permute-start | bytes 196616 | tf_op jit(solution)/shard_map/ppermute | solution.py:403
  32.8 4.5 %collective-permute-start.8 = (bf16[64,256]{1,0:T(8,128)(2,1)S(1)}, bf16[64,256]{1,0:T(8,128)(2,1)S(1)}, u32[]{:S(2)}, u32[]{:S(2)}) collective-permute-start(bf16[64,256]{1,0:T(8,128)(2,1)S(1)} %get-tuple-element.45), channel_id=1, source_target_pairs={{0,4},{4,0},{8,12},{12,8},{1,5},{5,1},{9,13},{13,9},{2,6},{6,2},{1... | collective-permute-start | bytes 98312 | tf_op jit(solution)/shard_map/ppermute | solution.py:403
  33.9 3.9 %collective-permute-start.9 = (bf16[64,256]{1,0:T(8,128)(2,1)S(1)}, bf16[64,256]{1,0:T(8,128)(2,1)S(1)}, u32[]{:S(2)}, u32[]{:S(2)}) collective-permute-start(bf16[64,256]{1,0:T(8,128)(2,1)S(1)} %get-tuple-element.46), channel_id=1, source_target_pairs={{0,4},{4,0},{8,12},{12,8},{1,5},{5,1},{9,13},{13,9},{2,6},{6,2},{1... | collective-permute-start | bytes 98312 | tf_op jit(solution)/shard_map/ppermute | solution.py:403
  38.1 1.4 %collective-permute-start.13 = (bf16[128,512]{1,0:T(8,128)(2,1)S(1)}, bf16[128,512]{1,0:T(8,128)(2,1)S(1)}, u32[]{:S(2)}, u32[]{:S(2)}) collective-permute-start(bf16[128,512]{1,0:T(8,128)(2,1)S(1)} %get-tuple-element.54), channel_id=1, source_target_pairs={{0,1},{1,0},{2,3},{3,2},{4,5},{5,4},{6,7},{7,6},{8,9},{9,8},{10,11... | collective-permute-start | bytes 393224 | tf_op jit(solution)/shard_map/ppermute | solution.py:403
  38.5 2.6 %collective-permute-start.10 = (bf16[128,512]{1,0:T(8,128)(2,1)S(1)}, bf16[128,512]{1,0:T(8,128)(2,1)S(1)}, u32[]{:S(2)}, u32[]{:S(2)}) collective-permute-start(bf16[128,512]{1,0:T(8,128)(2,1)S(1)} %get-tuple-element.50), channel_id=1, source_target_pairs={{0,1},{1,0},{2,3},{3,2},{4,5},{5,4},{6,7},{7,6},{8,9},{9,8},{10,11... | collective-permute-start | bytes 393224 | tf_op jit(solution)/shard_map/ppermute | solution.py:403
  39.5 6.4 %collective-permute-start.14 = (bf16[128,512]{1,0:T(8,128)(2,1)S(1)}, bf16[128,512]{1,0:T(8,128)(2,1)S(1)}, u32[]{:S(2)}, u32[]{:S(2)}) collective-permute-start(bf16[128,512]{1,0:T(8,128)(2,1)S(1)} %add_convert_fusion), channel_id=1, source_target_pairs={{0,2},{1,3},{2,0},{3,1},{4,6},{5,7},{6,4},{7,5},{8,10},{9,11},{10,... | collective-permute-start | bytes 393224 | tf_op jit(solution)/shard_map/ppermute | solution.py:403
  41.1 6.8 %collective-permute-start.15 = (bf16[128,512]{1,0:T(8,128)(2,1)S(1)}, bf16[128,512]{1,0:T(8,128)(2,1)S(1)}, u32[]{:S(2)}, u32[]{:S(2)}) collective-permute-start(bf16[128,512]{1,0:T(8,128)(2,1)S(1)} %add_convert_fusion.1.refs_6_), channel_id=1, source_target_pairs={{0,2},{1,3},{2,0},{3,1},{4,6},{5,7},{6,4},{7,5},{8,10},{9,11},{10,... | collective-permute-start | bytes 393224 | tf_op jit(solution)/shard_map/ppermute | solution.py:403
  42.5 5.5 %collective-permute-start.12 = (bf16[64,1024]{1,0:T(8,128)(2,1)S(1)}, bf16[64,1024]{1,0:T(8,128)(2,1)S(1)}, u32[]{:S(2)}, u32[]{:S(2)}) collective-permute-start(bf16[64,1024]{1,0:T(8,128)(2,1)S(1)} %get-tuple-element.55), channel_id=1, source_target_pairs={{0,1},{1,0},{2,3},{3,2},{4,5},{5,4},{6,7},{7,6},{8,9},{9,8},{10,11... | collective-permute-start | bytes 393224 | tf_op jit(solution)/shard_map/ppermute | solution.py:403
  42.6 5.4 %collective-permute-start.11 = (bf16[64,1024]{1,0:T(8,128)(2,1)S(1)}, bf16[64,1024]{1,0:T(8,128)(2,1)S(1)}, u32[]{:S(2)}, u32[]{:S(2)}) collective-permute-start(bf16[64,1024]{1,0:T(8,128)(2,1)S(1)} %get-tuple-element.56), channel_id=1, source_target_pairs={{0,1},{1,0},{2,3},{3,2},{4,5},{5,4},{6,7},{7,6},{8,9},{9,8},{10,11... | collective-permute-start | bytes 393224 | tf_op jit(solution)/shard_map/ppermute | solution.py:403

commit v17 on v16

--- a/solution.py
+++ b/solution.py
@@ -301,31 +301,21 @@
         mix_rows(position ^ step, weight_ref, total_ref, value_ref, out_ref)
 
 
-def near_rows_kernel(weight_ref, total_ref, value_ref, *refs):
-    upper_ref, lower_ref, own_ref, near_s = refs
-    half = upper_ref.shape[0]
+def near_rows_kernel(weight_ref, total_ref, value_ref, near_ref, own_ref):
     position = lax.axis_index("ctx")
-    mix_rows(position ^ 1, weight_ref, total_ref, value_ref, near_s)
-    upper_ref[...] = near_s[0:half]
-    lower_ref[...] = near_s[half:]
-    mix_rows(position, weight_ref, total_ref, value_ref, own_ref)
-
-
-def project_kernel(spans, *refs):
-    given, weight_ref = refs[:5], refs[5]
-    out_refs, attended_s = refs[-1 - len(spans) : -1], refs[-1]
-    second, third, upper, lower, mine = given
-    half = upper.shape[0]
-    rows, own = mine.shape
+    for step, out_ref in ((1, near_ref), (0, own_ref)):
+        mix_rows(position ^ step, weight_ref, total_ref, value_ref, out_ref)
+
+
+def project_kernel(masks, second_ref, third_ref, near_ref, mine_ref, weight_ref, _, *refs):
+    out_refs, attended_s = refs[:-1], refs[-1]
+    own, width = mine_ref.shape[1], out_refs[0].shape[1]
     position, here = lax.axis_index("ctx"), lax.axis_index("mp")
-    attended_s[0:half, columns_of(position ^ 1, own)] = upper[...]
-    attended_s[half:, columns_of(position ^ 1, own)] = lower[...]
-    for step, piece in ((0, mine), (2, second), (3, third)):
+    for step, piece in ((0, mine_ref), (1, near_ref), (2, second_ref), (3, third_ref)):
         attended_s[:, columns_of(position ^ step, own)] = piece[...]
-    for (mask, part, parts), out_ref in zip(spans, out_refs):
-        columns = columns_of((here ^ mask) * parts + part, out_ref.shape[1])
+    for mask, out_ref in zip(masks, out_refs):
         out_ref[...] = jnp.dot(
-            attended_s[...], weight_ref[:, columns], preferred_element_type=jnp.float32
+            attended_s[...], weight_ref[:, columns_of(here ^ mask, width)], preferred_element_type=jnp.float32
         ).astype(jnp.bfloat16)
 
 
@@ -341,12 +331,10 @@
         )
 
 
-def project_far_kernel(part, third_ref, upper_ref, lower_ref, partial_ref, weight_ref, *refs):
-    given_ref, kept_ref = refs[-2:]
+def project_far_kernel(part, third_ref, near_ref, partial_ref, weight_ref, given_ref, kept_ref):
     own, size = third_ref.shape[1], given_ref.shape[1]
     width = partial_ref.shape[1] // 2
     position, here = lax.axis_index("ctx"), lax.axis_index("mp")
-    near = jnp.concatenate([upper_ref[...], lower_ref[...]], axis=0)
     for index, (mask, out_ref) in enumerate(((3, given_ref), (2, kept_ref))):
         columns = columns_of((here ^ mask) * (width // size) + part, size)
         start = index * width + part * size
@@ -354,7 +342,7 @@
             third_ref[...], weight_ref[columns_of(position ^ 3, own), columns], preferred_element_type=jnp.float32
         )
         total = total + jnp.dot(
-            near, weight_ref[columns_of(position ^ 1, own), columns], preferred_element_type=jnp.float32
+            near_ref[...], weight_ref[columns_of(position ^ 1, own), columns], preferred_element_type=jnp.float32
         )
         out_ref[...] = total.astype(jnp.bfloat16)
 
@@ -466,30 +454,8 @@
         ],
     )
     third_got, second_got = swapped(third, "ctx", 3), swapped(second, "ctx", 2)
-    upper, lower, mine = run_kernel(
-        near_rows_kernel,
-        (soft, totals, values),
-        [((rows // 2, own), half)] * 2 + [piece],
-        [pltpu.VMEM((rows, own), half)],
-    )
-    near = (swapped(upper, "ctx", 1), swapped(lower, "ctx", 1))
-    return project_and_share((second_got, third_got, *near, mine), weight)
-
-
-def projected(attended, out_weight, spans, after=(), cost=10**6):
-    rows = attended[-1].shape[0]
-    width = out_weight.shape[1] // lax.axis_size("mp")
-    return run_kernel(
-        functools.partial(project_kernel, spans),
-        (*attended, out_weight, *after),
-        [((rows, width // parts), jnp.bfloat16) for _, _, parts in spans],
-        [pltpu.VMEM((rows, out_weight.shape[0]), jnp.bfloat16)],
-        [IN_VMEM] * (len(attended) + 1) + [ANYWHERE] * len(after),
-        cost=cost,
-    )
-
-
-NEAR_COST = 10**6
+    near, mine = run_kernel(near_rows_kernel, (soft, totals, values), [piece] * 2)
+    return project_and_share((second_got, third_got, swapped(near, "ctx", 1), mine), weight)
 
 
 def added(*terms):
@@ -500,7 +466,7 @@
 
 
 def project_and_share(attended, out_weight):
-    second, third, upper, lower, mine = attended
+    second, third, near, mine = attended
     rows = mine.shape[0]
     width = out_weight.shape[1] // lax.axis_size("mp")
     (partial,) = run_kernel(partial_kernel, (second, mine, out_weight), [((rows, 2 * width), jnp.float32)])
@@ -508,12 +474,18 @@
     for part in range(2):
         given, kept = run_kernel(
             functools.partial(project_far_kernel, part),
-            (third, upper, lower, partial, out_weight),
+            (third, near, partial, out_weight),
             [((rows, width // 2), jnp.bfloat16)] * 2,
         )
         far_sum = added(kept, swapped(given, "mp", 1))
         crossed.append(swapped(far_sum, "mp", 2))
-    near_given, near_kept = projected(attended, out_weight, ((1, 0, 1), (0, 0, 1)), (far_sum,), NEAR_COST)
+    near_given, near_kept = run_kernel(
+        functools.partial(project_kernel, (1, 0)),
+        (*attended, out_weight, far_sum),
+        [((rows, width), jnp.bfloat16)] * 2,
+        [pltpu.VMEM((rows, out_weight.shape[0]), jnp.bfloat16)],
+        [IN_VMEM] * 5 + [ANYWHERE],
+    )
     half = near_given.shape[0] // 2
     near_got = [swapped(near_given[:half], "mp", 1), swapped(near_given[half:], "mp", 1)]
     (total,) = run_kernel(

time: 49 us -> 48.9 us (level)
  waiting for transfers between devices: 10.4 us -> 11.5 us
  starting transfers between devices: 25.4 us -> 24.3 us
    ppermute x16 -> x15, starting transfers between devices: 25.4 us -> 24.3 us  [swapped(): lax.ppermute(value, axis, [(source, source ^ step) for source in range(la...]
    ppermute x16 -> x15, waiting for transfers between devices: 10.4 us -> 11.5 us  [swapped(): lax.ppermute(value, axis, [(source, source ^ step) for source in range(la...]
  transfers between devices with their start and end apart: 16 -> 15, of which waited for: 8 -> 8; matrix products, arithmetic and copies ran while one was open for 0% -> 0% of each run, Pallas kernels for 18% -> 18%
where the time goes in v17:
time: 48.9 us; the launch traced here: 48.7 us
  starting transfers between devices  24.3 us (50%)
  Pallas kernels  11.9 us (24%)
  waiting for transfers between devices  11.5 us (24%)
  local copies, waits for them, and re-layouts  0.75 us (2%)
    ppermute x15, starting transfers between devices, swapped(): lax.ppermute(value, axis, [(source, source ^ step) for source in range(la...  24.3 us
    pallas_call x11, Pallas kernels, run_kernel(): pl.pallas_call(kernel, out_shape=[jax.ShapeDtypeStruct(shape, dtype) for...  11.9 us
    ppermute x15, waiting for transfers between devices, swapped(): lax.ppermute(value, axis, [(source, source ^ step) for source in range(la...  11.5 us
  transfers between devices with their start and end apart: 15, of which 8 were waited for; matrix products, arithmetic and copies ran while one was open for 0% of the time, Pallas kernels for 18%

profile of v17, /device:TPU:0, one launch (start us, length us, event | category | flops | bytes accessed | tf_op | source)
XLA Modules:
  0.0 48.7 jit_solution(1467553610074015946)
XLA Ops:
  0.0 1.1 %plain_kernel.1 = (bf16[384,256]{1,0:T(8,128)(2,1)S(1)}, bf16[384,256]{1,0:T(8,128)(2,1)S(1)}) custom-call(bf16[3,128,1024]{2,1,0:T(8,128)(2,1)} %bitcast.3, bf16[128,1024]{1,0:T(8,128)(2,1)} %queries_any.3, bf16[128,1024]{1,0:T(8,128)(2,1)} %keys_any.3), custom_call_target="tpu_custom_call" | custom-call | flops 1000000 | bytes 1048576 | tf_op jit(solution)/shard_map/plain_kernel/pallas_call | solution.py:378
  1.1 5.1 %collective-permute-start.3 = (bf16[384,256]{1,0:T(8,128)(2,1)S(1)}, bf16[384,256]{1,0:T(8,128)(2,1)S(1)}, u32[]{:S(2)}, u32[]{:S(2)}) collective-permute-start(bf16[384,256]{1,0:T(8,128)(2,1)S(1)} %get-tuple-element.33), channel_id=1, source_target_pairs={{0,12},{4,8},{8,4},{12,0},{1,13},{5,9},{9,5},{13,1},{2,14},{6,10},... | collective-permute-start | bytes 589832 | tf_op jit(solution)/shard_map/ppermute | solution.py:391
  6.2 2.5 %gate_kernel.1 = (bf16[272,128]{1,0:T(8,128)(2,1)}, bf16[272,128]{1,0:T(8,128)(2,1)}, bf16[272,128]{1,0:T(8,128)(2,1)}, bf16[272,128]{1,0:T(8,128)(2,1)}, bf16[3...) custom-call(bf16[3,128,1024]{2,1,0:T(8,128)(2,1)} %bitcast.4, bf16[3,3,1024]{2,1,0:T(4,128)(2,1)} %refs_6_.1, ...), custom_call_target="tpu_custom_call" | custom-call | flops 1000000 | bytes 1048576 | tf_op jit(solution)/shard_map/gate_kernel/pallas_call | solution.py:378
  8.8 0.7 %collective-permute-start.5 = (bf16[384,256]{1,0:T(8,128)(2,1)}, bf16[384,256]{1,0:T(8,128)(2,1)S(1)}, u32[]{:S(2)}, u32[]{:S(2)}) collective-permute-start(bf16[384,256]{1,0:T(8,128)(2,1)} %get-tuple-element.35), channel_id=1, source_target_pairs={{0,4},{4,0},{8,12},{12,8},{1,5},{5,1},{9,13},{13,9},{2,6},{6,2},{1... | collective-permute-start | bytes 589832 | tf_op jit(solution)/shard_map/ppermute | solution.py:391
  9.5 3.7 %collective-permute-start = (bf16[272,128]{1,0:T(8,128)(2,1)}, bf16[272,128]{1,0:T(8,128)(2,1)S(1)}, u32[]{:S(2)}, u32[]{:S(2)}) collective-permute-start(bf16[272,128]{1,0:T(8,128)(2,1)} %get-tuple-element.29), channel_id=1, source_target_pairs={{0,12},{4,8},{8,4},{12,0},{1,13},{5,9},{9,5},{13,1},{2,14},{6,10},... | collective-permute-start | bytes 208904 | tf_op jit(solution)/shard_map/ppermute | solution.py:391
  13.2 7.8 %collective-permute-start.2 = (bf16[272,128]{1,0:T(8,128)(2,1)}, bf16[272,128]{1,0:T(8,128)(2,1)S(1)}, u32[]{:S(2)}, u32[]{:S(2)}) collective-permute-start(bf16[272,128]{1,0:T(8,128)(2,1)} %get-tuple-element.31), channel_id=1, source_target_pairs={{0,4},{4,0},{8,12},{12,8},{1,5},{5,1},{9,13},{13,9},{2,6},{6,2},{1... | collective-permute-start | bytes 208904 | tf_op jit(solution)/shard_map/ppermute | solution.py:391
  21.0 0.7 %copy-done.3 = bf16[64,128]{1,0:T(8,128)(2,1)S(1)} copy-done((bf16[64,128]{1,0:T(8,128)(2,1)S(1)}, bf16[64,128]{1,0:T(8,128)(2,1)}, u32[]{:S(2)}) %copy-start.3) | copy-done | bytes 16408
  21.7 3.4 %ready_kernel.1 = (bf16[2048,256]{1,0:T(8,128)(2,1)S(1)}, bf16[1024,4096]{1,0:T(8,128)(2,1)S(1)}) custom-call(bf16[64,128]{1,0:T(8,128)(2,1)S(1)} %copy-done.3, bf16[1024,4096]{1,0:T(8,128)(2,1)} %weight_any.1), custom_call_target="tpu_custom_call" | custom-call | flops 1000000 | bytes 1048576 | tf_op jit(solution)/shard_map/ready_kernel/pallas_call | solution.py:378
  25.2 1.7 %collective-permute-done.4.second_ref = bf16[384,256]{1,0:T(8,128)(2,1)S(1)} collective-permute-done((bf16[384,256]{1,0:T(8,128)(2,1)S(1)}, bf16[384,256]{1,0:T(8,128)(2,1)S(1)}, u32[]{:S(2)}, u32[]{:S(2)}) %collective-permute-start.4) | collective-permute-done | bytes 196640 | tf_op jit(solution)/shard_map/ppermute | solution.py:391
  26.8 0.9 %weights_kernel.1 = (bf16[2,512,512]{2,1,0:T(8,128)(2,1)S(1)}, f32[512,128]{1,0:T(8,128)S(1)}, f32[512,256]{1,0:T(8,128)S(1)}) custom-call(bf16[384,256]{1,0:T(8,128)(2,1)S(1)} %collective-permute-done.3.third_ref, bf16[384,256]{1,0:T(8,128)(2,1)S(1)} %collective-permute-done.4.second_ref, bf16[384,256]{1,0:T(8,128)(2,1)S(1)} %collective-permute-done.5.near_ref, ...), custom_call_target="tpu_custom_call" | custom-call | flops 1000000 | bytes 1048576 | tf_op jit(solution)/shard_map/weights_kernel/pallas_call | solution.py:378
  27.8 1.1 %collective-permute-done.1.refs_1_ = bf16[272,128]{1,0:T(8,128)(2,1)S(1)} collective-permute-done((bf16[272,128]{1,0:T(8,128)(2,1)}, bf16[272,128]{1,0:T(8,128)(2,1)S(1)}, u32[]{:S(2)}, u32[]{:S(2)}) %collective-permute-start.1) | collective-permute-done | bytes 69664 | tf_op jit(solution)/shard_map/ppermute | solution.py:391
  28.9 1.1 %values_kernel.1 = (bf16[128,256]{1,0:T(8,128)(2,1)S(1)}, bf16[128,256]{1,0:T(8,128)(2,1)S(1)}, bf16[512,256]{1,0:T(8,128)(2,1)S(1)}) custom-call(bf16[272,128]{1,0:T(8,128)(2,1)S(1)} %collective-permute-done.refs_0_, bf16[272,128]{1,0:T(8,128)(2,1)S(1)} %collective-permute-done.1.refs_1_, bf16[272,128]{1,0:T(8,128)(2,1)S(1)} %collective-permute-done.2.refs_2_, ...), custom_call_target="tpu_custom_call" | custom-call | flops 1000000 | bytes 1048576 | tf_op jit(solution)/shard_map/values_kernel/pallas_call | solution.py:378
  29.9 0.9 %collective-permute-start.6 = (bf16[128,256]{1,0:T(8,128)(2,1)S(1)}, bf16[128,256]{1,0:T(8,128)(2,1)S(1)}, u32[]{:S(2)}, u32[]{:S(2)}) collective-permute-start(bf16[128,256]{1,0:T(8,128)(2,1)S(1)} %get-tuple-element.41), channel_id=1, source_target_pairs={{0,8},{4,12},{8,0},{12,4},{1,9},{5,13},{9,1},{13,5},{2,10},{6,14},... | collective-permute-start | bytes 196616 | tf_op jit(solution)/shard_map/ppermute | solution.py:391
  30.8 1.7 %collective-permute-start.7 = (bf16[128,256]{1,0:T(8,128)(2,1)S(1)}, bf16[128,256]{1,0:T(8,128)(2,1)S(1)}, u32[]{:S(2)}, u32[]{:S(2)}) collective-permute-start(bf16[128,256]{1,0:T(8,128)(2,1)S(1)} %get-tuple-element.42), channel_id=1, source_target_pairs={{0,12},{4,8},{8,4},{12,0},{1,13},{5,9},{9,5},{13,1},{2,14},{6,10},... | collective-permute-start | bytes 196616 | tf_op jit(solution)/shard_map/ppermute | solution.py:391
  32.8 1.0 %collective-permute-start.8 = (bf16[128,256]{1,0:T(8,128)(2,1)S(1)}, bf16[128,256]{1,0:T(8,128)(2,1)S(1)}, u32[]{:S(2)}, u32[]{:S(2)}) collective-permute-start(bf16[128,256]{1,0:T(8,128)(2,1)S(1)} %get-tuple-element.44), channel_id=1, source_target_pairs={{0,4},{4,0},{8,12},{12,8},{1,5},{5,1},{9,13},{13,9},{2,6},{6,2},{1... | collective-permute-start | bytes 196616 | tf_op jit(solution)/shard_map/ppermute | solution.py:391
  33.8 2.4 %collective-permute-done.6.second_ref = bf16[128,256]{1,0:T(8,128)(2,1)S(1)} collective-permute-done((bf16[128,256]{1,0:T(8,128)(2,1)S(1)}, bf16[128,256]{1,0:T(8,128)(2,1)S(1)}, u32[]{:S(2)}, u32[]{:S(2)}) %collective-permute-start.6) | collective-permute-done | bytes 65568 | tf_op jit(solution)/shard_map/ppermute | solution.py:391
  37.1 0.6 %collective-permute-done.8.near_ref = bf16[128,256]{1,0:T(8,128)(2,1)S(1)} collective-permute-done((bf16[128,256]{1,0:T(8,128)(2,1)S(1)}, bf16[128,256]{1,0:T(8,128)(2,1)S(1)}, u32[]{:S(2)}, u32[]{:S(2)}) %collective-permute-start.8) | collective-permute-done | bytes 65568 | tf_op jit(solution)/shard_map/ppermute | solution.py:391
  38.4 0.5 %collective-permute-start.9 = (bf16[128,512]{1,0:T(8,128)(2,1)S(1)}, bf16[128,512]{1,0:T(8,128)(2,1)S(1)}, u32[]{:S(2)}, u32[]{:S(2)}) collective-permute-start(bf16[128,512]{1,0:T(8,128)(2,1)S(1)} %get-tuple-element.48), channel_id=1, source_target_pairs={{0,1},{1,0},{2,3},{3,2},{4,5},{5,4},{6,7},{7,6},{8,9},{9,8},{10,11... | collective-permute-start | bytes 393224 | tf_op jit(solution)/shard_map/ppermute | solution.py:391
  39.5 1.6 %collective-permute-start.13 = (bf16[128,512]{1,0:T(8,128)(2,1)S(1)}, bf16[128,512]{1,0:T(8,128)(2,1)S(1)}, u32[]{:S(2)}, u32[]{:S(2)}) collective-permute-start(bf16[128,512]{1,0:T(8,128)(2,1)S(1)} %add_convert_fusion), channel_id=1, source_target_pairs={{0,2},{1,3},{2,0},{3,1},{4,6},{5,7},{6,4},{7,5},{8,10},{9,11},{10,... | collective-permute-start | bytes 393224 | tf_op jit(solution)/shard_map/ppermute | solution.py:391
  41.1 0.6 %collective-permute-start.14 = (bf16[128,512]{1,0:T(8,128)(2,1)S(1)}, bf16[128,512]{1,0:T(8,128)(2,1)S(1)}, u32[]{:S(2)}, u32[]{:S(2)}) collective-permute-start(bf16[128,512]{1,0:T(8,128)(2,1)S(1)} %add_convert_fusion.1._), channel_id=1, source_target_pairs={{0,2},{1,3},{2,0},{3,1},{4,6},{5,7},{6,4},{7,5},{8,10},{9,11},{10,... | collective-permute-start | bytes 393224 | tf_op jit(solution)/shard_map/ppermute | solution.py:391
  41.7 0.7 %project_kernel.1 = (bf16[128,1024]{1,0:T(8,128)(2,1)S(1)}, bf16[128,1024]{1,0:T(8,128)(2,1)S(1)}) custom-call(bf16[128,256]{1,0:T(8,128)(2,1)S(1)} %collective-permute-done.6.second_ref, bf16[128,256]{1,0:T(8,128)(2,1)S(1)} %collective-permute-done.7.third_ref, bf16[128,256]{1,0:T(8,128)(2,1)S(1)} %collective-permute-done.8.near_ref, ...), custom_call_target="tpu_custom_call" | custom-call | flops 1000000 | bytes 1048576 | tf_op jit(solution)/shard_map/project_kernel/pallas_call | solution.py:378
  43.0 2.9 %collective-permute-done.13.first_ref = bf16[128,512]{1,0:T(8,128)(2,1)S(1)} collective-permute-done((bf16[128,512]{1,0:T(8,128)(2,1)S(1)}, bf16[128,512]{1,0:T(8,128)(2,1)S(1)}, u32[]{:S(2)}, u32[]{:S(2)}) %collective-permute-start.13) | collective-permute-done | bytes 131104 | tf_op jit(solution)/shard_map/ppermute | solution.py:391
  45.9 2.0 %collective-permute-done.14.second_ref = bf16[128,512]{1,0:T(8,128)(2,1)S(1)} collective-permute-done((bf16[128,512]{1,0:T(8,128)(2,1)S(1)}, bf16[128,512]{1,0:T(8,128)(2,1)S(1)}, u32[]{:S(2)}, u32[]{:S(2)}) %collective-permute-start.14) | collective-permute-done | bytes 131104 | tf_op jit(solution)/shard_map/ppermute | solution.py:391
  47.9 0.8 %total_kernel.1 = bf16[128,1024]{1,0:T(8,128)(2,1)} custom-call(bf16[128,1024]{1,0:T(8,128)(2,1)S(1)} %get-tuple-element.49.kept_ref, bf16[64,1024]{1,0:T(8,128)(2,1)S(1)} %collective-permute-done.10.upper_ref, bf16[64,1024]{1,0:T(8,128)(2,1)S(1)} %collective-permute-done.11.lower_ref, bf16[128,512]{1,0:T(8,128)(2,1)S(1)} %collective-permute-done.13.first_ref, ...), custom_call_target="tpu_custom_call" | custom-call | flops 1000000 | bytes 1048576 | tf_op jit(solution)/shard_map/total_kernel/pallas_call | solution.py:378
  (30 shorter events, 3.0 us)
Async XLA Ops:
  0.0 26.8 %copy-start = (bf16[3,3,1024]{2,1,0:T(4,128)(2,1)S(1)}, bf16[3,3,1024]{2,1,0:T(4,128)(2,1)}, u32[]{:S(2)}) copy-start(bf16[3,3,1024]{2,1,0:T(4,128)(2,1)} %refs_6_.1) | copy-start | bytes 55300
  0.0 28.9 %copy-start.4 = (f32[1024]{0:T(1024)S(1)}, f32[1024]{0:T(1024)}, u32[]{:S(2)}) copy-start(f32[1024]{0:T(1024)} %param.10) | copy-start | bytes 12292
  1.1 12.1 %collective-permute-start.3 = (bf16[384,256]{1,0:T(8,128)(2,1)S(1)}, bf16[384,256]{1,0:T(8,128)(2,1)S(1)}, u32[]{:S(2)}, u32[]{:S(2)}) collective-permute-start(bf16[384,256]{1,0:T(8,128)(2,1)S(1)} %get-tuple-element.33), channel_id=1, source_target_pairs={{0,12},{4,8},{8,4},{12,0},{1,13},{5,9},{9,5},{13,1},{2,14},{6,10},... | collective-permute-start | bytes 589832 | tf_op jit(solution)/shard_map/ppermute | solution.py:391
  6.2 20.6 %collective-permute-start.4 = (bf16[384,256]{1,0:T(8,128)(2,1)S(1)}, bf16[384,256]{1,0:T(8,128)(2,1)S(1)}, u32[]{:S(2)}, u32[]{:S(2)}) collective-permute-start(bf16[384,256]{1,0:T(8,128)(2,1)S(1)} %get-tuple-element.34), channel_id=1, source_target_pairs={{0,8},{4,12},{8,0},{12,4},{1,9},{5,13},{9,1},{13,5},{2,10},{6,14},... | collective-permute-start | bytes 589832 | tf_op jit(solution)/shard_map/ppermute | solution.py:391
  8.7 18.1 %copy-start.1 = (bf16[384,256]{1,0:T(8,128)(2,1)S(1)}, bf16[384,256]{1,0:T(8,128)(2,1)}, u32[]{:S(2)}) copy-start(bf16[384,256]{1,0:T(8,128)(2,1)} %get-tuple-element.36.own_ref) | copy-start | bytes 589828
  8.8 20.1 %copy-start.2 = (bf16[272,128]{1,0:T(8,128)(2,1)S(1)}, bf16[272,128]{1,0:T(8,128)(2,1)}, u32[]{:S(2)}) copy-start(bf16[272,128]{1,0:T(8,128)(2,1)} %get-tuple-element.32.refs_3_) | copy-start | bytes 208900
  8.8 18.1 %collective-permute-start.5 = (bf16[384,256]{1,0:T(8,128)(2,1)}, bf16[384,256]{1,0:T(8,128)(2,1)S(1)}, u32[]{:S(2)}, u32[]{:S(2)}) collective-permute-start(bf16[384,256]{1,0:T(8,128)(2,1)} %get-tuple-element.35), channel_id=1, source_target_pairs={{0,4},{4,0},{8,12},{12,8},{1,5},{5,1},{9,13},{13,9},{2,6},{6,2},{1... | collective-permute-start | bytes 589832 | tf_op jit(solution)/shard_map/ppermute | solution.py:391
  9.5 18.3 %collective-permute-start = (bf16[272,128]{1,0:T(8,128)(2,1)}, bf16[272,128]{1,0:T(8,128)(2,1)S(1)}, u32[]{:S(2)}, u32[]{:S(2)}) collective-permute-start(bf16[272,128]{1,0:T(8,128)(2,1)} %get-tuple-element.29), channel_id=1, source_target_pairs={{0,12},{4,8},{8,4},{12,0},{1,13},{5,9},{9,5},{13,1},{2,14},{6,10},... | collective-permute-start | bytes 208904 | tf_op jit(solution)/shard_map/ppermute | solution.py:391
  13.2 15.6 %collective-permute-start.1 = (bf16[272,128]{1,0:T(8,128)(2,1)}, bf16[272,128]{1,0:T(8,128)(2,1)S(1)}, u32[]{:S(2)}, u32[]{:S(2)}) collective-permute-start(bf16[272,128]{1,0:T(8,128)(2,1)} %get-tuple-element.30), channel_id=1, source_target_pairs={{0,8},{4,12},{8,0},{12,4},{1,9},{5,13},{9,1},{13,5},{2,10},{6,14},... | collective-permute-start | bytes 208904 | tf_op jit(solution)/shard_map/ppermute | solution.py:391
  13.2 15.6 %collective-permute-start.2 = (bf16[272,128]{1,0:T(8,128)(2,1)}, bf16[272,128]{1,0:T(8,128)(2,1)S(1)}, u32[]{:S(2)}, u32[]{:S(2)}) collective-permute-start(bf16[272,128]{1,0:T(8,128)(2,1)} %get-tuple-element.31), channel_id=1, source_target_pairs={{0,4},{4,0},{8,12},{12,8},{1,5},{5,1},{9,13},{13,9},{2,6},{6,2},{1... | collective-permute-start | bytes 208904 | tf_op jit(solution)/shard_map/ppermute | solution.py:391
  21.0 0.7 %copy-start.3 = (bf16[64,128]{1,0:T(8,128)(2,1)S(1)}, bf16[64,128]{1,0:T(8,128)(2,1)}, u32[]{:S(2)}) copy-start(bf16[64,128]{1,0:T(8,128)(2,1)} %filter_ref.1) | copy-start | bytes 49156
  29.9 6.3 %collective-permute-start.6 = (bf16[128,256]{1,0:T(8,128)(2,1)S(1)}, bf16[128,256]{1,0:T(8,128)(2,1)S(1)}, u32[]{:S(2)}, u32[]{:S(2)}) collective-permute-start(bf16[128,256]{1,0:T(8,128)(2,1)S(1)} %get-tuple-element.41), channel_id=1, source_target_pairs={{0,8},{4,12},{8,0},{12,4},{1,9},{5,13},{9,1},{13,5},{2,10},{6,14},... | collective-permute-start | bytes 196616 | tf_op jit(solution)/shard_map/ppermute | solution.py:391
  30.8 6.2 %collective-permute-start.7 = (bf16[128,256]{1,0:T(8,128)(2,1)S(1)}, bf16[128,256]{1,0:T(8,128)(2,1)S(1)}, u32[]{:S(2)}, u32[]{:S(2)}) collective-permute-start(bf16[128,256]{1,0:T(8,128)(2,1)S(1)} %get-tuple-element.42), channel_id=1, source_target_pairs={{0,12},{4,8},{8,4},{12,0},{1,13},{5,9},{9,5},{13,1},{2,14},{6,10},... | collective-permute-start | bytes 196616 | tf_op jit(solution)/shard_map/ppermute | solution.py:391
  32.8 4.9 %collective-permute-start.8 = (bf16[128,256]{1,0:T(8,128)(2,1)S(1)}, bf16[128,256]{1,0:T(8,128)(2,1)S(1)}, u32[]{:S(2)}, u32[]{:S(2)}) collective-permute-start(bf16[128,256]{1,0:T(8,128)(2,1)S(1)} %get-tuple-element.44), channel_id=1, source_target_pairs={{0,4},{4,0},{8,12},{12,8},{1,5},{5,1},{9,13},{13,9},{2,6},{6,2},{1... | collective-permute-start | bytes 196616 | tf_op jit(solution)/shard_map/ppermute | solution.py:391
  38.0 1.4 %collective-permute-start.12 = (bf16[128,512]{1,0:T(8,128)(2,1)S(1)}, bf16[128,512]{1,0:T(8,128)(2,1)S(1)}, u32[]{:S(2)}, u32[]{:S(2)}) collective-permute-start(bf16[128,512]{1,0:T(8,128)(2,1)S(1)} %get-tuple-element.52), channel_id=1, source_target_pairs={{0,1},{1,0},{2,3},{3,2},{4,5},{5,4},{6,7},{7,6},{8,9},{9,8},{10,11... | collective-permute-start | bytes 393224 | tf_op jit(solution)/shard_map/ppermute | solution.py:391
  38.4 2.6 %collective-permute-start.9 = (bf16[128,512]{1,0:T(8,128)(2,1)S(1)}, bf16[128,512]{1,0:T(8,128)(2,1)S(1)}, u32[]{:S(2)}, u32[]{:S(2)}) collective-permute-start(bf16[128,512]{1,0:T(8,128)(2,1)S(1)} %get-tuple-element.48), channel_id=1, source_target_pairs={{0,1},{1,0},{2,3},{3,2},{4,5},{5,4},{6,7},{7,6},{8,9},{9,8},{10,11... | collective-permute-start | bytes 393224 | tf_op jit(solution)/shard_map/ppermute | solution.py:391
  39.5 6.4 %collective-permute-start.13 = (bf16[128,512]{1,0:T(8,128)(2,1)S(1)}, bf16[128,512]{1,0:T(8,128)(2,1)S(1)}, u32[]{:S(2)}, u32[]{:S(2)}) collective-permute-start(bf16[128,512]{1,0:T(8,128)(2,1)S(1)} %add_convert_fusion), channel_id=1, source_target_pairs={{0,2},{1,3},{2,0},{3,1},{4,6},{5,7},{6,4},{7,5},{8,10},{9,11},{10,... | collective-permute-start | bytes 393224 | tf_op jit(solution)/shard_map/ppermute | solution.py:391
  41.1 6.8 %collective-permute-start.14 = (bf16[128,512]{1,0:T(8,128)(2,1)S(1)}, bf16[128,512]{1,0:T(8,128)(2,1)S(1)}, u32[]{:S(2)}, u32[]{:S(2)}) collective-permute-start(bf16[128,512]{1,0:T(8,128)(2,1)S(1)} %add_convert_fusion.1._), channel_id=1, source_target_pairs={{0,2},{1,3},{2,0},{3,1},{4,6},{5,7},{6,4},{7,5},{8,10},{9,11},{10,... | collective-permute-start | bytes 393224 | tf_op jit(solution)/shard_map/ppermute | solution.py:391
  42.4 5.5 %collective-permute-start.11 = (bf16[64,1024]{1,0:T(8,128)(2,1)S(1)}, bf16[64,1024]{1,0:T(8,128)(2,1)S(1)}, u32[]{:S(2)}, u32[]{:S(2)}) collective-permute-start(bf16[64,1024]{1,0:T(8,128)(2,1)S(1)} %get-tuple-element.53), channel_id=1, source_target_pairs={{0,1},{1,0},{2,3},{3,2},{4,5},{5,4},{6,7},{7,6},{8,9},{9,8},{10,11... | collective-permute-start | bytes 393224 | tf_op jit(solution)/shard_map/ppermute | solution.py:391
  42.5 5.4 %collective-permute-start.10 = (bf16[64,1024]{1,0:T(8,128)(2,1)S(1)}, bf16[64,1024]{1,0:T(8,128)(2,1)S(1)}, u32[]{:S(2)}, u32[]{:S(2)}) collective-permute-start(bf16[64,1024]{1,0:T(8,128)(2,1)S(1)} %get-tuple-element.54), channel_id=1, source_target_pairs={{0,1},{1,0},{2,3},{3,2},{4,5},{5,4},{6,7},{7,6},{8,9},{9,8},{10,11... | collective-permute-start | bytes 393224 | tf_op jit(solution)/shard_map/ppermute | solution.py:391

commit v18 on v17

--- a/solution.py
+++ b/solution.py
@@ -331,39 +331,46 @@
         )
 
 
-def project_far_kernel(part, third_ref, near_ref, partial_ref, weight_ref, given_ref, kept_ref):
-    own, size = third_ref.shape[1], given_ref.shape[1]
+def partial_third_kernel(third_ref, partial_ref, weight_ref, out_ref):
+    own, width = third_ref.shape[1], out_ref.shape[1] // 2
+    position, here = lax.axis_index("ctx"), lax.axis_index("mp")
+    for index, mask in enumerate((3, 2)):
+        span = slice(index * width, (index + 1) * width)
+        out_ref[:, span] = partial_ref[:, span] + jnp.dot(
+            third_ref[...],
+            weight_ref[columns_of(position ^ 3, own), columns_of(here ^ mask, width)],
+            preferred_element_type=jnp.float32,
+        )
+
+
+def project_far_kernel(part, near_ref, partial_ref, weight_ref, given_ref, kept_ref):
+    own, size = near_ref.shape[1], given_ref.shape[1]
     width = partial_ref.shape[1] // 2
     position, here = lax.axis_index("ctx"), lax.axis_index("mp")
     for index, (mask, out_ref) in enumerate(((3, given_ref), (2, kept_ref))):
         columns = columns_of((here ^ mask) * (width // size) + part, size)
         start = index * width + part * size
         total = partial_ref[:, start : start + size] + jnp.dot(
-            third_ref[...], weight_ref[columns_of(position ^ 3, own), columns], preferred_element_type=jnp.float32
-        )
-        total = total + jnp.dot(
             near_ref[...], weight_ref[columns_of(position ^ 1, own), columns], preferred_element_type=jnp.float32
         )
         out_ref[...] = total.astype(jnp.bfloat16)
 
 
-def total_kernel(kept_ref, upper_ref, lower_ref, first_ref, second_ref, out_any, total_s, sems):
-    half, cut = upper_ref.shape[0], first_ref.shape[1]
-    copies = []
+def total_kernel(part, kept_ref, upper_ref, lower_ref, crossed_ref, *refs):
+    out_any, total_s, sem = refs[-3:]
+    half, size = upper_ref.shape[0], crossed_ref.shape[1]
+    columns = slice(part * size, (part + 1) * size)
     for index, near_ref in enumerate((upper_ref, lower_ref)):
         here = slice(index * half, (index + 1) * half)
-        for columns, crossed_ref in ((slice(0, cut), first_ref), (slice(cut, 2 * cut), second_ref)):
-            total = (
-                kept_ref[here, columns].astype(jnp.float32)
-                + near_ref[:, columns].astype(jnp.float32)
-                + crossed_ref[here].astype(jnp.float32)
-            )
-            total_s[here, columns] = total.astype(jnp.bfloat16)
-        copy = pltpu.make_async_copy(total_s.at[here], out_any.at[here], sems.at[index])
-        copy.start()
-        copies.append(copy)
-    for copy in copies:
-        copy.wait()
+        total = (
+            kept_ref[here, columns].astype(jnp.float32)
+            + near_ref[:, columns].astype(jnp.float32)
+            + crossed_ref[here].astype(jnp.float32)
+        )
+        total_s[here] = total.astype(jnp.bfloat16)
+    copy = pltpu.make_async_copy(total_s, out_any.at[:, columns], sem)
+    copy.start()
+    copy.wait()
 
 
 VMEM_LIMIT = 40 * 1024 * 1024
@@ -374,13 +381,14 @@
 ANYWHERE = pl.BlockSpec(memory_space=pl.ANY)
 
 
-def run_kernel(kernel, operands, outputs, scratch=(), spaces=None, limit=VMEM_LIMIT, cost=10**6, targets=None):
+def run_kernel(kernel, operands, outputs, scratch=(), spaces=None, limit=VMEM_LIMIT, cost=10**6, targets=None, aliases=None):
     return pl.pallas_call(
         kernel,
         out_shape=[jax.ShapeDtypeStruct(shape, dtype) for shape, dtype in outputs],
         in_specs=spaces or [IN_VMEM] * len(operands),
         out_specs=targets or [IN_VMEM] * len(outputs),
         scratch_shapes=scratch,
+        input_output_aliases=aliases or {},
         compiler_params=pltpu.CompilerParams(vmem_limit_bytes=limit),
         cost_estimate=pl.CostEstimate(flops=cost, bytes_accessed=2**20, transcendentals=0),
         name=getattr(kernel, "func", kernel).__name__,
@@ -470,11 +478,14 @@
     rows = mine.shape[0]
     width = out_weight.shape[1] // lax.axis_size("mp")
     (partial,) = run_kernel(partial_kernel, (second, mine, out_weight), [((rows, 2 * width), jnp.float32)])
+    (partial,) = run_kernel(
+        partial_third_kernel, (third, partial, out_weight), [((rows, 2 * width), jnp.float32)]
+    )
     crossed = []
     for part in range(2):
         given, kept = run_kernel(
             functools.partial(project_far_kernel, part),
-            (third, near, partial, out_weight),
+            (near, partial, out_weight),
             [((rows, width // 2), jnp.bfloat16)] * 2,
         )
         far_sum = added(kept, swapped(given, "mp", 1))
@@ -488,14 +499,18 @@
     )
     half = near_given.shape[0] // 2
     near_got = [swapped(near_given[:half], "mp", 1), swapped(near_given[half:], "mp", 1)]
-    (total,) = run_kernel(
-        total_kernel,
-        (near_kept, *near_got, *crossed),
-        [(near_kept.shape, near_kept.dtype)],
-        [pltpu.VMEM(near_kept.shape, near_kept.dtype), pltpu.SemaphoreType.DMA((2,))],
-        targets=[IN_HBM],
-    )
-    return total
+    total = []
+    for part, piece in enumerate(crossed):
+        total = run_kernel(
+            functools.partial(total_kernel, part),
+            (near_kept, *near_got, piece, *total),
+            [(near_kept.shape, near_kept.dtype)],
+            [pltpu.VMEM(piece.shape, piece.dtype), pltpu.SemaphoreType.DMA],
+            [IN_VMEM] * 4 + [IN_HBM] * len(total),
+            targets=[IN_HBM],
+            aliases={4: 0} if total else {},
+        )
+    return total[0]
 
 
 def per_device(inputs, short_filter, long_filter, skip_gain, queries, key_rows, out_weight):

time: 48.9 us -> 48.8 us (level)
  waiting for transfers between devices: 11.5 us -> 10.6 us
  Pallas kernels: 11.9 us -> 12.7 us
    ppermute x15, waiting for transfers between devices: 11.5 us -> 10.6 us  [swapped(): lax.ppermute(value, axis, [(source, source ^ step) for source in range(la...]
    pallas_call x11 -> x13, Pallas kernels: 11.9 us -> 12.7 us  [run_kernel(): pl.pallas_call(kernel, out_shape=[jax.ShapeDtypeStruct(shape, dtype) for...]
  transfers between devices with their start and end apart: 15 -> 15, of which waited for: 8 -> 8; matrix products, arithmetic and copies ran while one was open for 0% -> 0% of each run, Pallas kernels for 18% -> 20%
where the time goes in v18:
time: 48.8 us; the launch traced here: 48.5 us
  starting transfers between devices  24.3 us (50%)
  Pallas kernels  12.7 us (26%)
  waiting for transfers between devices  10.6 us (22%)
  local copies, waits for them, and re-layouts  0.75 us (2%)
    ppermute x15, starting transfers between devices, swapped(): lax.ppermute(value, axis, [(source, source ^ step) for source in range(la...  24.3 us
    pallas_call x13, Pallas kernels, run_kernel(): pl.pallas_call(kernel, out_shape=[jax.ShapeDtypeStruct(shape, dtype) for...  12.7 us
    ppermute x15, waiting for transfers between devices, swapped(): lax.ppermute(value, axis, [(source, source ^ step) for source in range(la...  10.6 us
  transfers between devices with their start and end apart: 15, of which 8 were waited for; matrix products, arithmetic and copies ran while one was open for 0% of the time, Pallas kernels for 20%

profile of v18, /device:TPU:0, one launch (start us, length us, event | category | flops | bytes accessed | tf_op | source)
XLA Modules:
  0.0 48.5 jit_solution(6147862834120275995)
XLA Ops:
  0.0 1.1 %plain_kernel.1 = (bf16[384,256]{1,0:T(8,128)(2,1)S(1)}, bf16[384,256]{1,0:T(8,128)(2,1)S(1)}) custom-call(bf16[3,128,1024]{2,1,0:T(8,128)(2,1)} %bitcast.3, bf16[128,1024]{1,0:T(8,128)(2,1)} %queries_any.3, bf16[128,1024]{1,0:T(8,128)(2,1)} %keys_any.3), custom_call_target="tpu_custom_call" | custom-call | flops 1000000 | bytes 1048576 | tf_op jit(solution)/shard_map/plain_kernel/pallas_call | solution.py:385
  1.1 5.1 %collective-permute-start.3 = (bf16[384,256]{1,0:T(8,128)(2,1)S(1)}, bf16[384,256]{1,0:T(8,128)(2,1)S(1)}, u32[]{:S(2)}, u32[]{:S(2)}) collective-permute-start(bf16[384,256]{1,0:T(8,128)(2,1)S(1)} %get-tuple-element.33), channel_id=1, source_target_pairs={{0,12},{4,8},{8,4},{12,0},{1,13},{5,9},{9,5},{13,1},{2,14},{6,10},... | collective-permute-start | bytes 589832 | tf_op jit(solution)/shard_map/ppermute | solution.py:399
  6.2 2.5 %gate_kernel.1 = (bf16[272,128]{1,0:T(8,128)(2,1)}, bf16[272,128]{1,0:T(8,128)(2,1)}, bf16[272,128]{1,0:T(8,128)(2,1)}, bf16[272,128]{1,0:T(8,128)(2,1)}, bf16[3...) custom-call(bf16[3,128,1024]{2,1,0:T(8,128)(2,1)} %bitcast.4, bf16[3,3,1024]{2,1,0:T(4,128)(2,1)} %refs_6_.1, ...), custom_call_target="tpu_custom_call" | custom-call | flops 1000000 | bytes 1048576 | tf_op jit(solution)/shard_map/gate_kernel/pallas_call | solution.py:385
  8.8 0.7 %collective-permute-start.5 = (bf16[384,256]{1,0:T(8,128)(2,1)}, bf16[384,256]{1,0:T(8,128)(2,1)S(1)}, u32[]{:S(2)}, u32[]{:S(2)}) collective-permute-start(bf16[384,256]{1,0:T(8,128)(2,1)} %get-tuple-element.35), channel_id=1, source_target_pairs={{0,4},{4,0},{8,12},{12,8},{1,5},{5,1},{9,13},{13,9},{2,6},{6,2},{1... | collective-permute-start | bytes 589832 | tf_op jit(solution)/shard_map/ppermute | solution.py:399
  9.5 3.7 %collective-permute-start = (bf16[272,128]{1,0:T(8,128)(2,1)}, bf16[272,128]{1,0:T(8,128)(2,1)S(1)}, u32[]{:S(2)}, u32[]{:S(2)}) collective-permute-start(bf16[272,128]{1,0:T(8,128)(2,1)} %get-tuple-element.29), channel_id=1, source_target_pairs={{0,12},{4,8},{8,4},{12,0},{1,13},{5,9},{9,5},{13,1},{2,14},{6,10},... | collective-permute-start | bytes 208904 | tf_op jit(solution)/shard_map/ppermute | solution.py:399
  13.2 7.8 %collective-permute-start.2 = (bf16[272,128]{1,0:T(8,128)(2,1)}, bf16[272,128]{1,0:T(8,128)(2,1)S(1)}, u32[]{:S(2)}, u32[]{:S(2)}) collective-permute-start(bf16[272,128]{1,0:T(8,128)(2,1)} %get-tuple-element.31), channel_id=1, source_target_pairs={{0,4},{4,0},{8,12},{12,8},{1,5},{5,1},{9,13},{13,9},{2,6},{6,2},{1... | collective-permute-start | bytes 208904 | tf_op jit(solution)/shard_map/ppermute | solution.py:399
  21.0 0.7 %copy-done.3 = bf16[64,128]{1,0:T(8,128)(2,1)S(1)} copy-done((bf16[64,128]{1,0:T(8,128)(2,1)S(1)}, bf16[64,128]{1,0:T(8,128)(2,1)}, u32[]{:S(2)}) %copy-start.3) | copy-done | bytes 16408
  21.7 3.4 %ready_kernel.1 = (bf16[2048,256]{1,0:T(8,128)(2,1)S(1)}, bf16[1024,4096]{1,0:T(8,128)(2,1)S(1)}) custom-call(bf16[64,128]{1,0:T(8,128)(2,1)S(1)} %copy-done.3, bf16[1024,4096]{1,0:T(8,128)(2,1)} %weight_any.1), custom_call_target="tpu_custom_call" | custom-call | flops 1000000 | bytes 1048576 | tf_op jit(solution)/shard_map/ready_kernel/pallas_call | solution.py:385
  25.2 1.7 %collective-permute-done.4.second_ref = bf16[384,256]{1,0:T(8,128)(2,1)S(1)} collective-permute-done((bf16[384,256]{1,0:T(8,128)(2,1)S(1)}, bf16[384,256]{1,0:T(8,128)(2,1)S(1)}, u32[]{:S(2)}, u32[]{:S(2)}) %collective-permute-start.4) | collective-permute-done | bytes 196640 | tf_op jit(solution)/shard_map/ppermute | solution.py:399
  26.8 0.9 %weights_kernel.1 = (bf16[2,512,512]{2,1,0:T(8,128)(2,1)S(1)}, f32[512,128]{1,0:T(8,128)S(1)}, f32[512,256]{1,0:T(8,128)S(1)}) custom-call(bf16[384,256]{1,0:T(8,128)(2,1)S(1)} %collective-permute-done.3.third_ref, bf16[384,256]{1,0:T(8,128)(2,1)S(1)} %collective-permute-done.4.second_ref, bf16[384,256]{1,0:T(8,128)(2,1)S(1)} %collective-permute-done.5.near_ref, ...), custom_call_target="tpu_custom_call" | custom-call | flops 1000000 | bytes 1048576 | tf_op jit(solution)/shard_map/weights_kernel/pallas_call | solution.py:385
  27.8 1.1 %collective-permute-done.1.refs_1_ = bf16[272,128]{1,0:T(8,128)(2,1)S(1)} collective-permute-done((bf16[272,128]{1,0:T(8,128)(2,1)}, bf16[272,128]{1,0:T(8,128)(2,1)S(1)}, u32[]{:S(2)}, u32[]{:S(2)}) %collective-permute-start.1) | collective-permute-done | bytes 69664 | tf_op jit(solution)/shard_map/ppermute | solution.py:399
  28.9 1.1 %values_kernel.1 = (bf16[128,256]{1,0:T(8,128)(2,1)S(1)}, bf16[128,256]{1,0:T(8,128)(2,1)S(1)}, bf16[512,256]{1,0:T(8,128)(2,1)S(1)}) custom-call(bf16[272,128]{1,0:T(8,128)(2,1)S(1)} %collective-permute-done.refs_0_, bf16[272,128]{1,0:T(8,128)(2,1)S(1)} %collective-permute-done.1.refs_1_, bf16[272,128]{1,0:T(8,128)(2,1)S(1)} %collective-permute-done.2.refs_2_, ...), custom_call_target="tpu_custom_call" | custom-call | flops 1000000 | bytes 1048576 | tf_op jit(solution)/shard_map/values_kernel/pallas_call | solution.py:385
  29.9 0.9 %collective-permute-start.6 = (bf16[128,256]{1,0:T(8,128)(2,1)S(1)}, bf16[128,256]{1,0:T(8,128)(2,1)S(1)}, u32[]{:S(2)}, u32[]{:S(2)}) collective-permute-start(bf16[128,256]{1,0:T(8,128)(2,1)S(1)} %get-tuple-element.41), channel_id=1, source_target_pairs={{0,8},{4,12},{8,0},{12,4},{1,9},{5,13},{9,1},{13,5},{2,10},{6,14},... | collective-permute-start | bytes 196616 | tf_op jit(solution)/shard_map/ppermute | solution.py:399
  30.8 1.7 %collective-permute-start.7 = (bf16[128,256]{1,0:T(8,128)(2,1)S(1)}, bf16[128,256]{1,0:T(8,128)(2,1)S(1)}, u32[]{:S(2)}, u32[]{:S(2)}) collective-permute-start(bf16[128,256]{1,0:T(8,128)(2,1)S(1)} %get-tuple-element.42), channel_id=1, source_target_pairs={{0,12},{4,8},{8,4},{12,0},{1,13},{5,9},{9,5},{13,1},{2,14},{6,10},... | collective-permute-start | bytes 196616 | tf_op jit(solution)/shard_map/ppermute | solution.py:399
  32.8 1.0 %collective-permute-start.8 = (bf16[128,256]{1,0:T(8,128)(2,1)S(1)}, bf16[128,256]{1,0:T(8,128)(2,1)S(1)}, u32[]{:S(2)}, u32[]{:S(2)}) collective-permute-start(bf16[128,256]{1,0:T(8,128)(2,1)S(1)} %get-tuple-element.44), channel_id=1, source_target_pairs={{0,4},{4,0},{8,12},{12,8},{1,5},{5,1},{9,13},{13,9},{2,6},{6,2},{1... | collective-permute-start | bytes 196616 | tf_op jit(solution)/shard_map/ppermute | solution.py:399
  33.8 2.4 %collective-permute-done.6.second_ref = bf16[128,256]{1,0:T(8,128)(2,1)S(1)} collective-permute-done((bf16[128,256]{1,0:T(8,128)(2,1)S(1)}, bf16[128,256]{1,0:T(8,128)(2,1)S(1)}, u32[]{:S(2)}, u32[]{:S(2)}) %collective-permute-start.6) | collective-permute-done | bytes 65568 | tf_op jit(solution)/shard_map/ppermute | solution.py:399
  38.3 0.5 %collective-permute-start.9 = (bf16[128,512]{1,0:T(8,128)(2,1)S(1)}, bf16[128,512]{1,0:T(8,128)(2,1)S(1)}, u32[]{:S(2)}, u32[]{:S(2)}) collective-permute-start(bf16[128,512]{1,0:T(8,128)(2,1)S(1)} %get-tuple-element.48), channel_id=1, source_target_pairs={{0,1},{1,0},{2,3},{3,2},{4,5},{5,4},{6,7},{7,6},{8,9},{9,8},{10,11... | collective-permute-start | bytes 393224 | tf_op jit(solution)/shard_map/ppermute | solution.py:399
  39.4 1.6 %collective-permute-start.14 = (bf16[128,512]{1,0:T(8,128)(2,1)S(1)}, bf16[128,512]{1,0:T(8,128)(2,1)S(1)}, u32[]{:S(2)}, u32[]{:S(2)}) collective-permute-start(bf16[128,512]{1,0:T(8,128)(2,1)S(1)} %add_convert_fusion), channel_id=1, source_target_pairs={{0,2},{1,3},{2,0},{3,1},{4,6},{5,7},{6,4},{7,5},{8,10},{9,11},{10,... | collective-permute-start | bytes 393224 | tf_op jit(solution)/shard_map/ppermute | solution.py:399
  41.0 0.7 %project_kernel.1 = (bf16[128,1024]{1,0:T(8,128)(2,1)S(1)}, bf16[128,1024]{1,0:T(8,128)(2,1)S(1)}) custom-call(bf16[128,256]{1,0:T(8,128)(2,1)S(1)} %collective-permute-done.6.second_ref, bf16[128,256]{1,0:T(8,128)(2,1)S(1)} %collective-permute-done.7.third_ref, bf16[128,256]{1,0:T(8,128)(2,1)S(1)} %collective-permute-done.8.near_ref, ...), custom_call_target="tpu_custom_call" | custom-call | flops 1000000 | bytes 1048576 | tf_op jit(solution)/shard_map/project_kernel/pallas_call | solution.py:385
  42.3 0.5 %collective-permute-start.12 = (bf16[128,512]{1,0:T(8,128)(2,1)S(1)}, bf16[128,512]{1,0:T(8,128)(2,1)S(1)}, u32[]{:S(2)}, u32[]{:S(2)}) collective-permute-start(bf16[128,512]{1,0:T(8,128)(2,1)S(1)} %add_convert_fusion.1._), channel_id=1, source_target_pairs={{0,2},{1,3},{2,0},{3,1},{4,6},{5,7},{6,4},{7,5},{8,10},{9,11},{10,... | collective-permute-start | bytes 393224 | tf_op jit(solution)/shard_map/ppermute | solution.py:399
  42.9 2.1 %collective-permute-done.14.crossed_ref = bf16[128,512]{1,0:T(8,128)(2,1)S(1)} collective-permute-done((bf16[128,512]{1,0:T(8,128)(2,1)S(1)}, bf16[128,512]{1,0:T(8,128)(2,1)S(1)}, u32[]{:S(2)}, u32[]{:S(2)}) %collective-permute-start.14) | collective-permute-done | bytes 131104 | tf_op jit(solution)/shard_map/ppermute | solution.py:399
  45.0 0.7 %total_kernel.2.refs_0_ = bf16[128,1024]{1,0:T(8,128)(2,1)} custom-call(bf16[128,1024]{1,0:T(8,128)(2,1)S(1)} %get-tuple-element.49.kept_ref, bf16[64,1024]{1,0:T(8,128)(2,1)S(1)} %collective-permute-done.10.upper_ref, bf16[64,1024]{1,0:T(8,128)(2,1)S(1)} %collective-permute-done.11.lower_ref, bf16[128,512]{1,0:T(8,128)(2,1)S(1)} %collective-permute-done.14.crossed_ref), custom_call_target="tpu_custom_call" | custom-call | flops 1000000 | bytes 1048576 | tf_op jit(solution)/shard_map/total_kernel/pallas_call | solution.py:385
  45.7 2.1 %collective-permute-done.12.crossed_ref = bf16[128,512]{1,0:T(8,128)(2,1)S(1)} collective-permute-done((bf16[128,512]{1,0:T(8,128)(2,1)S(1)}, bf16[128,512]{1,0:T(8,128)(2,1)S(1)}, u32[]{:S(2)}, u32[]{:S(2)}) %collective-permute-start.12) | collective-permute-done | bytes 131104 | tf_op jit(solution)/shard_map/ppermute | solution.py:399
  47.8 0.7 %total_kernel.3 = bf16[128,1024]{1,0:T(8,128)(2,1)} custom-call(bf16[128,1024]{1,0:T(8,128)(2,1)S(1)} %get-tuple-element.49.kept_ref, bf16[64,1024]{1,0:T(8,128)(2,1)S(1)} %collective-permute-done.10.upper_ref, bf16[64,1024]{1,0:T(8,128)(2,1)S(1)} %collective-permute-done.11.lower_ref, ...), custom_call_target="tpu_custom_call", output_to_operand_aliasing={{}: (4, {})} | custom-call | flops 1000000 | bytes 1048576 | tf_op jit(solution)/shard_map/total_kernel/pallas_call | solution.py:385
  (32 shorter events, 3.6 us)
Async XLA Ops:
  0.0 26.8 %copy-start = (bf16[3,3,1024]{2,1,0:T(4,128)(2,1)S(1)}, bf16[3,3,1024]{2,1,0:T(4,128)(2,1)}, u32[]{:S(2)}) copy-start(bf16[3,3,1024]{2,1,0:T(4,128)(2,1)} %refs_6_.1) | copy-start | bytes 55300
  0.0 28.9 %copy-start.4 = (f32[1024]{0:T(1024)S(1)}, f32[1024]{0:T(1024)}, u32[]{:S(2)}) copy-start(f32[1024]{0:T(1024)} %param.10) | copy-start | bytes 12292
  1.1 12.1 %collective-permute-start.3 = (bf16[384,256]{1,0:T(8,128)(2,1)S(1)}, bf16[384,256]{1,0:T(8,128)(2,1)S(1)}, u32[]{:S(2)}, u32[]{:S(2)}) collective-permute-start(bf16[384,256]{1,0:T(8,128)(2,1)S(1)} %get-tuple-element.33), channel_id=1, source_target_pairs={{0,12},{4,8},{8,4},{12,0},{1,13},{5,9},{9,5},{13,1},{2,14},{6,10},... | collective-permute-start | bytes 589832 | tf_op jit(solution)/shard_map/ppermute | solution.py:399
  6.2 20.6 %collective-permute-start.4 = (bf16[384,256]{1,0:T(8,128)(2,1)S(1)}, bf16[384,256]{1,0:T(8,128)(2,1)S(1)}, u32[]{:S(2)}, u32[]{:S(2)}) collective-permute-start(bf16[384,256]{1,0:T(8,128)(2,1)S(1)} %get-tuple-element.34), channel_id=1, source_target_pairs={{0,8},{4,12},{8,0},{12,4},{1,9},{5,13},{9,1},{13,5},{2,10},{6,14},... | collective-permute-start | bytes 589832 | tf_op jit(solution)/shard_map/ppermute | solution.py:399
  8.7 18.1 %copy-start.1 = (bf16[384,256]{1,0:T(8,128)(2,1)S(1)}, bf16[384,256]{1,0:T(8,128)(2,1)}, u32[]{:S(2)}) copy-start(bf16[384,256]{1,0:T(8,128)(2,1)} %get-tuple-element.36.own_ref) | copy-start | bytes 589828
  8.8 20.1 %copy-start.2 = (bf16[272,128]{1,0:T(8,128)(2,1)S(1)}, bf16[272,128]{1,0:T(8,128)(2,1)}, u32[]{:S(2)}) copy-start(bf16[272,128]{1,0:T(8,128)(2,1)} %get-tuple-element.32.refs_3_) | copy-start | bytes 208900
  8.8 18.1 %collective-permute-start.5 = (bf16[384,256]{1,0:T(8,128)(2,1)}, bf16[384,256]{1,0:T(8,128)(2,1)S(1)}, u32[]{:S(2)}, u32[]{:S(2)}) collective-permute-start(bf16[384,256]{1,0:T(8,128)(2,1)} %get-tuple-element.35), channel_id=1, source_target_pairs={{0,4},{4,0},{8,12},{12,8},{1,5},{5,1},{9,13},{13,9},{2,6},{6,2},{1... | collective-permute-start | bytes 589832 | tf_op jit(solution)/shard_map/ppermute | solution.py:399
  9.5 18.3 %collective-permute-start = (bf16[272,128]{1,0:T(8,128)(2,1)}, bf16[272,128]{1,0:T(8,128)(2,1)S(1)}, u32[]{:S(2)}, u32[]{:S(2)}) collective-permute-start(bf16[272,128]{1,0:T(8,128)(2,1)} %get-tuple-element.29), channel_id=1, source_target_pairs={{0,12},{4,8},{8,4},{12,0},{1,13},{5,9},{9,5},{13,1},{2,14},{6,10},... | collective-permute-start | bytes 208904 | tf_op jit(solution)/shard_map/ppermute | solution.py:399
  13.2 15.6 %collective-permute-start.1 = (bf16[272,128]{1,0:T(8,128)(2,1)}, bf16[272,128]{1,0:T(8,128)(2,1)S(1)}, u32[]{:S(2)}, u32[]{:S(2)}) collective-permute-start(bf16[272,128]{1,0:T(8,128)(2,1)} %get-tuple-element.30), channel_id=1, source_target_pairs={{0,8},{4,12},{8,0},{12,4},{1,9},{5,13},{9,1},{13,5},{2,10},{6,14},... | collective-permute-start | bytes 208904 | tf_op jit(solution)/shard_map/ppermute | solution.py:399
  13.2 15.6 %collective-permute-start.2 = (bf16[272,128]{1,0:T(8,128)(2,1)}, bf16[272,128]{1,0:T(8,128)(2,1)S(1)}, u32[]{:S(2)}, u32[]{:S(2)}) collective-permute-start(bf16[272,128]{1,0:T(8,128)(2,1)} %get-tuple-element.31), channel_id=1, source_target_pairs={{0,4},{4,0},{8,12},{12,8},{1,5},{5,1},{9,13},{13,9},{2,6},{6,2},{1... | collective-permute-start | bytes 208904 | tf_op jit(solution)/shard_map/ppermute | solution.py:399
  21.0 0.7 %copy-start.3 = (bf16[64,128]{1,0:T(8,128)(2,1)S(1)}, bf16[64,128]{1,0:T(8,128)(2,1)}, u32[]{:S(2)}) copy-start(bf16[64,128]{1,0:T(8,128)(2,1)} %filter_ref.1) | copy-start | bytes 49156
  29.9 6.3 %collective-permute-start.6 = (bf16[128,256]{1,0:T(8,128)(2,1)S(1)}, bf16[128,256]{1,0:T(8,128)(2,1)S(1)}, u32[]{:S(2)}, u32[]{:S(2)}) collective-permute-start(bf16[128,256]{1,0:T(8,128)(2,1)S(1)} %get-tuple-element.41), channel_id=1, source_target_pairs={{0,8},{4,12},{8,0},{12,4},{1,9},{5,13},{9,1},{13,5},{2,10},{6,14},... | collective-permute-start | bytes 196616 | tf_op jit(solution)/shard_map/ppermute | solution.py:399
  30.8 6.2 %collective-permute-start.7 = (bf16[128,256]{1,0:T(8,128)(2,1)S(1)}, bf16[128,256]{1,0:T(8,128)(2,1)S(1)}, u32[]{:S(2)}, u32[]{:S(2)}) collective-permute-start(bf16[128,256]{1,0:T(8,128)(2,1)S(1)} %get-tuple-element.42), channel_id=1, source_target_pairs={{0,12},{4,8},{8,4},{12,0},{1,13},{5,9},{9,5},{13,1},{2,14},{6,10},... | collective-permute-start | bytes 196616 | tf_op jit(solution)/shard_map/ppermute | solution.py:399
  32.8 4.9 %collective-permute-start.8 = (bf16[128,256]{1,0:T(8,128)(2,1)S(1)}, bf16[128,256]{1,0:T(8,128)(2,1)S(1)}, u32[]{:S(2)}, u32[]{:S(2)}) collective-permute-start(bf16[128,256]{1,0:T(8,128)(2,1)S(1)} %get-tuple-element.44), channel_id=1, source_target_pairs={{0,4},{4,0},{8,12},{12,8},{1,5},{5,1},{9,13},{13,9},{2,6},{6,2},{1... | collective-permute-start | bytes 196616 | tf_op jit(solution)/shard_map/ppermute | solution.py:399
  37.9 1.4 %collective-permute-start.13 = (bf16[128,512]{1,0:T(8,128)(2,1)S(1)}, bf16[128,512]{1,0:T(8,128)(2,1)S(1)}, u32[]{:S(2)}, u32[]{:S(2)}) collective-permute-start(bf16[128,512]{1,0:T(8,128)(2,1)S(1)} %get-tuple-element.52), channel_id=1, source_target_pairs={{0,1},{1,0},{2,3},{3,2},{4,5},{5,4},{6,7},{7,6},{8,9},{9,8},{10,11... | collective-permute-start | bytes 393224 | tf_op jit(solution)/shard_map/ppermute | solution.py:399
  38.3 2.7 %collective-permute-start.9 = (bf16[128,512]{1,0:T(8,128)(2,1)S(1)}, bf16[128,512]{1,0:T(8,128)(2,1)S(1)}, u32[]{:S(2)}, u32[]{:S(2)}) collective-permute-start(bf16[128,512]{1,0:T(8,128)(2,1)S(1)} %get-tuple-element.48), channel_id=1, source_target_pairs={{0,1},{1,0},{2,3},{3,2},{4,5},{5,4},{6,7},{7,6},{8,9},{9,8},{10,11... | collective-permute-start | bytes 393224 | tf_op jit(solution)/shard_map/ppermute | solution.py:399
  39.4 5.6 %collective-permute-start.14 = (bf16[128,512]{1,0:T(8,128)(2,1)S(1)}, bf16[128,512]{1,0:T(8,128)(2,1)S(1)}, u32[]{:S(2)}, u32[]{:S(2)}) collective-permute-start(bf16[128,512]{1,0:T(8,128)(2,1)S(1)} %add_convert_fusion), channel_id=1, source_target_pairs={{0,2},{1,3},{2,0},{3,1},{4,6},{5,7},{6,4},{7,5},{8,10},{9,11},{10,... | collective-permute-start | bytes 393224 | tf_op jit(solution)/shard_map/ppermute | solution.py:399
  41.8 3.2 %collective-permute-start.11 = (bf16[64,1024]{1,0:T(8,128)(2,1)S(1)}, bf16[64,1024]{1,0:T(8,128)(2,1)S(1)}, u32[]{:S(2)}, u32[]{:S(2)}) collective-permute-start(bf16[64,1024]{1,0:T(8,128)(2,1)S(1)} %get-tuple-element.53), channel_id=1, source_target_pairs={{0,1},{1,0},{2,3},{3,2},{4,5},{5,4},{6,7},{7,6},{8,9},{9,8},{10,11... | collective-permute-start | bytes 393224 | tf_op jit(solution)/shard_map/ppermute | solution.py:399
  41.8 3.2 %collective-permute-start.10 = (bf16[64,1024]{1,0:T(8,128)(2,1)S(1)}, bf16[64,1024]{1,0:T(8,128)(2,1)S(1)}, u32[]{:S(2)}, u32[]{:S(2)}) collective-permute-start(bf16[64,1024]{1,0:T(8,128)(2,1)S(1)} %get-tuple-element.54), channel_id=1, source_target_pairs={{0,1},{1,0},{2,3},{3,2},{4,5},{5,4},{6,7},{7,6},{8,9},{9,8},{10,11... | collective-permute-start | bytes 393224 | tf_op jit(solution)/shard_map/ppermute | solution.py:399
  42.3 5.5 %collective-permute-start.12 = (bf16[128,512]{1,0:T(8,128)(2,1)S(1)}, bf16[128,512]{1,0:T(8,128)(2,1)S(1)}, u32[]{:S(2)}, u32[]{:S(2)}) collective-permute-start(bf16[128,512]{1,0:T(8,128)(2,1)S(1)} %add_convert_fusion.1._), channel_id=1, source_target_pairs={{0,2},{1,3},{2,0},{3,1},{4,6},{5,7},{6,4},{7,5},{8,10},{9,11},{10,... | collective-permute-start | bytes 393224 | tf_op jit(solution)/shard_map/ppermute | solution.py:399

commit v19 on v18

--- a/solution.py
+++ b/solution.py
@@ -244,8 +244,8 @@
     count = COUNT
     gates, feature_ref = refs[:count], refs[count]
     band_ref, short_ref, gain_ref, weight_ref, total_ref = refs[count + 1 : count + 6]
-    third_ref, second_ref, value_ref = refs[count + 6 : count + 9]
-    edge_s, gate_s, filtered_s = refs[count + 9 :]
+    second_ref, value_ref = refs[count + 6 : count + 8]
+    edge_s, gate_s, filtered_s = refs[count + 8 :]
     rows, own = second_ref.shape
     per_group = own * rows // band_ref.shape[0]
     position = lax.axis_index("ctx")
@@ -297,13 +297,12 @@
     value_ref[...] = (
         feature_ref[...] * (filtered_s[...] + gain * gate_s[rows:].astype(jnp.float32))
     ).astype(jnp.bfloat16)
-    for step, out_ref in ((3, third_ref), (2, second_ref)):
-        mix_rows(position ^ step, weight_ref, total_ref, value_ref, out_ref)
-
-
-def near_rows_kernel(weight_ref, total_ref, value_ref, near_ref, own_ref):
+    mix_rows(position ^ 2, weight_ref, total_ref, value_ref, second_ref)
+
+
+def rows_kernel(weight_ref, total_ref, value_ref, *out_refs):
     position = lax.axis_index("ctx")
-    for step, out_ref in ((1, near_ref), (0, own_ref)):
+    for step, out_ref in zip((3, 1, 0), out_refs):
         mix_rows(position ^ step, weight_ref, total_ref, value_ref, out_ref)
 
 
@@ -451,19 +450,19 @@
             pltpu.VMEM((window, own), half),
         ],
     )
-    third, second, values = run_kernel(
+    second, values = run_kernel(
         values_kernel,
         (*gates, feature, band, short_filter, skip_gain.reshape(1, channels), soft, totals),
-        [piece, piece, ((window, own), half)],
+        [piece, ((window, own), half)],
         [
             pltpu.VMEM((COUNT, EDGE, own), jnp.float32),
             pltpu.VMEM((window + rows, own), half),
             pltpu.VMEM((window, own), jnp.float32),
         ],
     )
-    third_got, second_got = swapped(third, "ctx", 3), swapped(second, "ctx", 2)
-    near, mine = run_kernel(near_rows_kernel, (soft, totals, values), [piece] * 2)
-    return project_and_share((second_got, third_got, swapped(near, "ctx", 1), mine), weight)
+    third, near, mine = run_kernel(rows_kernel, (soft, totals, values), [piece] * 3)
+    swaps = [swapped(rows_out, "ctx", step) for step, rows_out in ((2, second), (3, third), (1, near))]
+    return project_and_share((*swaps, mine), weight)
 
 
 def added(*terms):

time: 48.8 us -> 48.9 us (level)
  no operation moved by 1% of the time
where the time goes in v19:
time: 48.9 us; the launch traced here: 48.7 us
  starting transfers between devices  24.3 us (50%)
  Pallas kernels  12.7 us (26%)
  waiting for transfers between devices  10.7 us (22%)
  local copies, waits for them, and re-layouts  0.75 us (2%)
    ppermute x15, starting transfers between devices, swapped(): lax.ppermute(value, axis, [(source, source ^ step) for source in range(la...  24.3 us
    pallas_call x13, Pallas kernels, run_kernel(): pl.pallas_call(kernel, out_shape=[jax.ShapeDtypeStruct(shape, dtype) for...  12.7 us
    ppermute x15, waiting for transfers between devices, swapped(): lax.ppermute(value, axis, [(source, source ^ step) for source in range(la...  10.7 us
  transfers between devices with their start and end apart: 15, of which 8 were waited for; matrix products, arithmetic and copies ran while one was open for 0% of the time, Pallas kernels for 20%

profile of v19, /device:TPU:0, one launch (start us, length us, event | category | flops | bytes accessed | tf_op | source)
XLA Modules:
  0.0 48.7 jit_solution(5329261012680220524)
XLA Ops:
  0.0 1.1 %plain_kernel.1 = (bf16[384,256]{1,0:T(8,128)(2,1)S(1)}, bf16[384,256]{1,0:T(8,128)(2,1)S(1)}) custom-call(bf16[3,128,1024]{2,1,0:T(8,128)(2,1)} %bitcast.3, bf16[128,1024]{1,0:T(8,128)(2,1)} %queries_any.3, bf16[128,1024]{1,0:T(8,128)(2,1)} %keys_any.3), custom_call_target="tpu_custom_call" | custom-call | flops 1000000 | bytes 1048576 | tf_op jit(solution)/shard_map/plain_kernel/pallas_call | solution.py:384
  1.1 5.1 %collective-permute-start.3 = (bf16[384,256]{1,0:T(8,128)(2,1)S(1)}, bf16[384,256]{1,0:T(8,128)(2,1)S(1)}, u32[]{:S(2)}, u32[]{:S(2)}) collective-permute-start(bf16[384,256]{1,0:T(8,128)(2,1)S(1)} %get-tuple-element.33), channel_id=1, source_target_pairs={{0,12},{4,8},{8,4},{12,0},{1,13},{5,9},{9,5},{13,1},{2,14},{6,10},... | collective-permute-start | bytes 589832 | tf_op jit(solution)/shard_map/ppermute | solution.py:398
  6.2 2.5 %gate_kernel.1 = (bf16[272,128]{1,0:T(8,128)(2,1)}, bf16[272,128]{1,0:T(8,128)(2,1)}, bf16[272,128]{1,0:T(8,128)(2,1)}, bf16[272,128]{1,0:T(8,128)(2,1)}, bf16[3...) custom-call(bf16[3,128,1024]{2,1,0:T(8,128)(2,1)} %bitcast.4, bf16[3,3,1024]{2,1,0:T(4,128)(2,1)} %refs_6_.1, ...), custom_call_target="tpu_custom_call" | custom-call | flops 1000000 | bytes 1048576 | tf_op jit(solution)/shard_map/gate_kernel/pallas_call | solution.py:384
  8.8 0.7 %collective-permute-start.5 = (bf16[384,256]{1,0:T(8,128)(2,1)}, bf16[384,256]{1,0:T(8,128)(2,1)S(1)}, u32[]{:S(2)}, u32[]{:S(2)}) collective-permute-start(bf16[384,256]{1,0:T(8,128)(2,1)} %get-tuple-element.35), channel_id=1, source_target_pairs={{0,4},{4,0},{8,12},{12,8},{1,5},{5,1},{9,13},{13,9},{2,6},{6,2},{1... | collective-permute-start | bytes 589832 | tf_op jit(solution)/shard_map/ppermute | solution.py:398
  9.5 3.7 %collective-permute-start = (bf16[272,128]{1,0:T(8,128)(2,1)}, bf16[272,128]{1,0:T(8,128)(2,1)S(1)}, u32[]{:S(2)}, u32[]{:S(2)}) collective-permute-start(bf16[272,128]{1,0:T(8,128)(2,1)} %get-tuple-element.29), channel_id=1, source_target_pairs={{0,12},{4,8},{8,4},{12,0},{1,13},{5,9},{9,5},{13,1},{2,14},{6,10},... | collective-permute-start | bytes 208904 | tf_op jit(solution)/shard_map/ppermute | solution.py:398
  13.2 7.8 %collective-permute-start.2 = (bf16[272,128]{1,0:T(8,128)(2,1)}, bf16[272,128]{1,0:T(8,128)(2,1)S(1)}, u32[]{:S(2)}, u32[]{:S(2)}) collective-permute-start(bf16[272,128]{1,0:T(8,128)(2,1)} %get-tuple-element.31), channel_id=1, source_target_pairs={{0,4},{4,0},{8,12},{12,8},{1,5},{5,1},{9,13},{13,9},{2,6},{6,2},{1... | collective-permute-start | bytes 208904 | tf_op jit(solution)/shard_map/ppermute | solution.py:398
  21.0 0.7 %copy-done.3 = bf16[64,128]{1,0:T(8,128)(2,1)S(1)} copy-done((bf16[64,128]{1,0:T(8,128)(2,1)S(1)}, bf16[64,128]{1,0:T(8,128)(2,1)}, u32[]{:S(2)}) %copy-start.3) | copy-done | bytes 16408
  21.7 3.4 %ready_kernel.1 = (bf16[2048,256]{1,0:T(8,128)(2,1)S(1)}, bf16[1024,4096]{1,0:T(8,128)(2,1)S(1)}) custom-call(bf16[64,128]{1,0:T(8,128)(2,1)S(1)} %copy-done.3, bf16[1024,4096]{1,0:T(8,128)(2,1)} %weight_any.1), custom_call_target="tpu_custom_call" | custom-call | flops 1000000 | bytes 1048576 | tf_op jit(solution)/shard_map/ready_kernel/pallas_call | solution.py:384
  25.2 1.7 %collective-permute-done.4.second_ref = bf16[384,256]{1,0:T(8,128)(2,1)S(1)} collective-permute-done((bf16[384,256]{1,0:T(8,128)(2,1)S(1)}, bf16[384,256]{1,0:T(8,128)(2,1)S(1)}, u32[]{:S(2)}, u32[]{:S(2)}) %collective-permute-start.4) | collective-permute-done | bytes 196640 | tf_op jit(solution)/shard_map/ppermute | solution.py:398
  26.8 0.9 %weights_kernel.1 = (bf16[2,512,512]{2,1,0:T(8,128)(2,1)S(1)}, f32[512,128]{1,0:T(8,128)S(1)}, f32[512,256]{1,0:T(8,128)S(1)}) custom-call(bf16[384,256]{1,0:T(8,128)(2,1)S(1)} %collective-permute-done.3.third_ref, bf16[384,256]{1,0:T(8,128)(2,1)S(1)} %collective-permute-done.4.second_ref, bf16[384,256]{1,0:T(8,128)(2,1)S(1)} %collective-permute-done.5.near_ref, ...), custom_call_target="tpu_custom_call" | custom-call | flops 1000000 | bytes 1048576 | tf_op jit(solution)/shard_map/weights_kernel/pallas_call | solution.py:384
  27.8 1.1 %collective-permute-done.1.refs_1_ = bf16[272,128]{1,0:T(8,128)(2,1)S(1)} collective-permute-done((bf16[272,128]{1,0:T(8,128)(2,1)}, bf16[272,128]{1,0:T(8,128)(2,1)S(1)}, u32[]{:S(2)}, u32[]{:S(2)}) %collective-permute-start.1) | collective-permute-done | bytes 69664 | tf_op jit(solution)/shard_map/ppermute | solution.py:398
  28.9 1.0 %values_kernel.1 = (bf16[128,256]{1,0:T(8,128)(2,1)S(1)}, bf16[512,256]{1,0:T(8,128)(2,1)S(1)}) custom-call(bf16[272,128]{1,0:T(8,128)(2,1)S(1)} %collective-permute-done.refs_0_, bf16[272,128]{1,0:T(8,128)(2,1)S(1)} %collective-permute-done.1.refs_1_, bf16[272,128]{1,0:T(8,128)(2,1)S(1)} %collective-permute-done.2.refs_2_, bf16[272,128]{1,0:T(8,128)(2,1)S(1)} %copy-done.2, ...), custom_call_target="tpu_custom_call" | custom-call | flops 1000000 | bytes 1048576 | tf_op jit(solution)/shard_map/values_kernel/pallas_call | solution.py:384
  29.8 0.9 %collective-permute-start.6 = (bf16[128,256]{1,0:T(8,128)(2,1)S(1)}, bf16[128,256]{1,0:T(8,128)(2,1)S(1)}, u32[]{:S(2)}, u32[]{:S(2)}) collective-permute-start(bf16[128,256]{1,0:T(8,128)(2,1)S(1)} %get-tuple-element.41), channel_id=1, source_target_pairs={{0,8},{4,12},{8,0},{12,4},{1,9},{5,13},{9,1},{13,5},{2,10},{6,14},... | collective-permute-start | bytes 196616 | tf_op jit(solution)/shard_map/ppermute | solution.py:398
  31.1 1.7 %collective-permute-start.7 = (bf16[128,256]{1,0:T(8,128)(2,1)S(1)}, bf16[128,256]{1,0:T(8,128)(2,1)S(1)}, u32[]{:S(2)}, u32[]{:S(2)}) collective-permute-start(bf16[128,256]{1,0:T(8,128)(2,1)S(1)} %get-tuple-element.43), channel_id=1, source_target_pairs={{0,12},{4,8},{8,4},{12,0},{1,13},{5,9},{9,5},{13,1},{2,14},{6,10},... | collective-permute-start | bytes 196616 | tf_op jit(solution)/shard_map/ppermute | solution.py:398
  32.8 1.0 %collective-permute-start.8 = (bf16[128,256]{1,0:T(8,128)(2,1)S(1)}, bf16[128,256]{1,0:T(8,128)(2,1)S(1)}, u32[]{:S(2)}, u32[]{:S(2)}) collective-permute-start(bf16[128,256]{1,0:T(8,128)(2,1)S(1)} %get-tuple-element.44), channel_id=1, source_target_pairs={{0,4},{4,0},{8,12},{12,8},{1,5},{5,1},{9,13},{13,9},{2,6},{6,2},{1... | collective-permute-start | bytes 196616 | tf_op jit(solution)/shard_map/ppermute | solution.py:398
  33.8 2.6 %collective-permute-done.6.second_ref = bf16[128,256]{1,0:T(8,128)(2,1)S(1)} collective-permute-done((bf16[128,256]{1,0:T(8,128)(2,1)S(1)}, bf16[128,256]{1,0:T(8,128)(2,1)S(1)}, u32[]{:S(2)}, u32[]{:S(2)}) %collective-permute-start.6) | collective-permute-done | bytes 65568 | tf_op jit(solution)/shard_map/ppermute | solution.py:398
  36.9 0.5 %collective-permute-done.7.third_ref = bf16[128,256]{1,0:T(8,128)(2,1)S(1)} collective-permute-done((bf16[128,256]{1,0:T(8,128)(2,1)S(1)}, bf16[128,256]{1,0:T(8,128)(2,1)S(1)}, u32[]{:S(2)}, u32[]{:S(2)}) %collective-permute-start.7) | collective-permute-done | bytes 65568 | tf_op jit(solution)/shard_map/ppermute | solution.py:398
  38.4 0.5 %collective-permute-start.9 = (bf16[128,512]{1,0:T(8,128)(2,1)S(1)}, bf16[128,512]{1,0:T(8,128)(2,1)S(1)}, u32[]{:S(2)}, u32[]{:S(2)}) collective-permute-start(bf16[128,512]{1,0:T(8,128)(2,1)S(1)} %get-tuple-element.48), channel_id=1, source_target_pairs={{0,1},{1,0},{2,3},{3,2},{4,5},{5,4},{6,7},{7,6},{8,9},{9,8},{10,11... | collective-permute-start | bytes 393224 | tf_op jit(solution)/shard_map/ppermute | solution.py:398
  39.5 1.6 %collective-permute-start.14 = (bf16[128,512]{1,0:T(8,128)(2,1)S(1)}, bf16[128,512]{1,0:T(8,128)(2,1)S(1)}, u32[]{:S(2)}, u32[]{:S(2)}) collective-permute-start(bf16[128,512]{1,0:T(8,128)(2,1)S(1)} %add_convert_fusion), channel_id=1, source_target_pairs={{0,2},{1,3},{2,0},{3,1},{4,6},{5,7},{6,4},{7,5},{8,10},{9,11},{10,... | collective-permute-start | bytes 393224 | tf_op jit(solution)/shard_map/ppermute | solution.py:398
  41.1 0.7 %project_kernel.1 = (bf16[128,1024]{1,0:T(8,128)(2,1)S(1)}, bf16[128,1024]{1,0:T(8,128)(2,1)S(1)}) custom-call(bf16[128,256]{1,0:T(8,128)(2,1)S(1)} %collective-permute-done.6.second_ref, bf16[128,256]{1,0:T(8,128)(2,1)S(1)} %collective-permute-done.7.third_ref, bf16[128,256]{1,0:T(8,128)(2,1)S(1)} %collective-permute-done.8.near_ref, ...), custom_call_target="tpu_custom_call" | custom-call | flops 1000000 | bytes 1048576 | tf_op jit(solution)/shard_map/project_kernel/pallas_call | solution.py:384
  43.0 2.1 %collective-permute-done.14.crossed_ref = bf16[128,512]{1,0:T(8,128)(2,1)S(1)} collective-permute-done((bf16[128,512]{1,0:T(8,128)(2,1)S(1)}, bf16[128,512]{1,0:T(8,128)(2,1)S(1)}, u32[]{:S(2)}, u32[]{:S(2)}) %collective-permute-start.14) | collective-permute-done | bytes 131104 | tf_op jit(solution)/shard_map/ppermute | solution.py:398
  45.1 0.7 %total_kernel.2.refs_0_ = bf16[128,1024]{1,0:T(8,128)(2,1)} custom-call(bf16[128,1024]{1,0:T(8,128)(2,1)S(1)} %get-tuple-element.49.kept_ref, bf16[64,1024]{1,0:T(8,128)(2,1)S(1)} %collective-permute-done.10.upper_ref, bf16[64,1024]{1,0:T(8,128)(2,1)S(1)} %collective-permute-done.11.lower_ref, bf16[128,512]{1,0:T(8,128)(2,1)S(1)} %collective-permute-done.14.crossed_ref), custom_call_target="tpu_custom_call" | custom-call | flops 1000000 | bytes 1048576 | tf_op jit(solution)/shard_map/total_kernel/pallas_call | solution.py:384
  45.9 2.1 %collective-permute-done.12.crossed_ref = bf16[128,512]{1,0:T(8,128)(2,1)S(1)} collective-permute-done((bf16[128,512]{1,0:T(8,128)(2,1)S(1)}, bf16[128,512]{1,0:T(8,128)(2,1)S(1)}, u32[]{:S(2)}, u32[]{:S(2)}) %collective-permute-start.12) | collective-permute-done | bytes 131104 | tf_op jit(solution)/shard_map/ppermute | solution.py:398
  47.9 0.7 %total_kernel.3 = bf16[128,1024]{1,0:T(8,128)(2,1)} custom-call(bf16[128,1024]{1,0:T(8,128)(2,1)S(1)} %get-tuple-element.49.kept_ref, bf16[64,1024]{1,0:T(8,128)(2,1)S(1)} %collective-permute-done.10.upper_ref, bf16[64,1024]{1,0:T(8,128)(2,1)S(1)} %collective-permute-done.11.lower_ref, ...), custom_call_target="tpu_custom_call", output_to_operand_aliasing={{}: (4, {})} | custom-call | flops 1000000 | bytes 1048576 | tf_op jit(solution)/shard_map/total_kernel/pallas_call | solution.py:384
  (32 shorter events, 3.5 us)
Async XLA Ops:
  0.0 26.8 %copy-start = (bf16[3,3,1024]{2,1,0:T(4,128)(2,1)S(1)}, bf16[3,3,1024]{2,1,0:T(4,128)(2,1)}, u32[]{:S(2)}) copy-start(bf16[3,3,1024]{2,1,0:T(4,128)(2,1)} %refs_6_.1) | copy-start | bytes 55300
  0.0 28.9 %copy-start.4 = (f32[1024]{0:T(1024)S(1)}, f32[1024]{0:T(1024)}, u32[]{:S(2)}) copy-start(f32[1024]{0:T(1024)} %param.10) | copy-start | bytes 12292
  1.1 12.1 %collective-permute-start.3 = (bf16[384,256]{1,0:T(8,128)(2,1)S(1)}, bf16[384,256]{1,0:T(8,128)(2,1)S(1)}, u32[]{:S(2)}, u32[]{:S(2)}) collective-permute-start(bf16[384,256]{1,0:T(8,128)(2,1)S(1)} %get-tuple-element.33), channel_id=1, source_target_pairs={{0,12},{4,8},{8,4},{12,0},{1,13},{5,9},{9,5},{13,1},{2,14},{6,10},... | collective-permute-start | bytes 589832 | tf_op jit(solution)/shard_map/ppermute | solution.py:398
  6.2 20.6 %collective-permute-start.4 = (bf16[384,256]{1,0:T(8,128)(2,1)S(1)}, bf16[384,256]{1,0:T(8,128)(2,1)S(1)}, u32[]{:S(2)}, u32[]{:S(2)}) collective-permute-start(bf16[384,256]{1,0:T(8,128)(2,1)S(1)} %get-tuple-element.34), channel_id=1, source_target_pairs={{0,8},{4,12},{8,0},{12,4},{1,9},{5,13},{9,1},{13,5},{2,10},{6,14},... | collective-permute-start | bytes 589832 | tf_op jit(solution)/shard_map/ppermute | solution.py:398
  8.7 18.1 %copy-start.1 = (bf16[384,256]{1,0:T(8,128)(2,1)S(1)}, bf16[384,256]{1,0:T(8,128)(2,1)}, u32[]{:S(2)}) copy-start(bf16[384,256]{1,0:T(8,128)(2,1)} %get-tuple-element.36.own_ref) | copy-start | bytes 589828
  8.8 20.1 %copy-start.2 = (bf16[272,128]{1,0:T(8,128)(2,1)S(1)}, bf16[272,128]{1,0:T(8,128)(2,1)}, u32[]{:S(2)}) copy-start(bf16[272,128]{1,0:T(8,128)(2,1)} %get-tuple-element.32.refs_3_) | copy-start | bytes 208900
  8.8 18.1 %collective-permute-start.5 = (bf16[384,256]{1,0:T(8,128)(2,1)}, bf16[384,256]{1,0:T(8,128)(2,1)S(1)}, u32[]{:S(2)}, u32[]{:S(2)}) collective-permute-start(bf16[384,256]{1,0:T(8,128)(2,1)} %get-tuple-element.35), channel_id=1, source_target_pairs={{0,4},{4,0},{8,12},{12,8},{1,5},{5,1},{9,13},{13,9},{2,6},{6,2},{1... | collective-permute-start | bytes 589832 | tf_op jit(solution)/shard_map/ppermute | solution.py:398
  9.5 18.3 %collective-permute-start = (bf16[272,128]{1,0:T(8,128)(2,1)}, bf16[272,128]{1,0:T(8,128)(2,1)S(1)}, u32[]{:S(2)}, u32[]{:S(2)}) collective-permute-start(bf16[272,128]{1,0:T(8,128)(2,1)} %get-tuple-element.29), channel_id=1, source_target_pairs={{0,12},{4,8},{8,4},{12,0},{1,13},{5,9},{9,5},{13,1},{2,14},{6,10},... | collective-permute-start | bytes 208904 | tf_op jit(solution)/shard_map/ppermute | solution.py:398
  13.2 15.6 %collective-permute-start.1 = (bf16[272,128]{1,0:T(8,128)(2,1)}, bf16[272,128]{1,0:T(8,128)(2,1)S(1)}, u32[]{:S(2)}, u32[]{:S(2)}) collective-permute-start(bf16[272,128]{1,0:T(8,128)(2,1)} %get-tuple-element.30), channel_id=1, source_target_pairs={{0,8},{4,12},{8,0},{12,4},{1,9},{5,13},{9,1},{13,5},{2,10},{6,14},... | collective-permute-start | bytes 208904 | tf_op jit(solution)/shard_map/ppermute | solution.py:398
  13.2 15.6 %collective-permute-start.2 = (bf16[272,128]{1,0:T(8,128)(2,1)}, bf16[272,128]{1,0:T(8,128)(2,1)S(1)}, u32[]{:S(2)}, u32[]{:S(2)}) collective-permute-start(bf16[272,128]{1,0:T(8,128)(2,1)} %get-tuple-element.31), channel_id=1, source_target_pairs={{0,4},{4,0},{8,12},{12,8},{1,5},{5,1},{9,13},{13,9},{2,6},{6,2},{1... | collective-permute-start | bytes 208904 | tf_op jit(solution)/shard_map/ppermute | solution.py:398
  21.0 0.7 %copy-start.3 = (bf16[64,128]{1,0:T(8,128)(2,1)S(1)}, bf16[64,128]{1,0:T(8,128)(2,1)}, u32[]{:S(2)}) copy-start(bf16[64,128]{1,0:T(8,128)(2,1)} %filter_ref.1) | copy-start | bytes 49156
  29.8 6.6 %collective-permute-start.6 = (bf16[128,256]{1,0:T(8,128)(2,1)S(1)}, bf16[128,256]{1,0:T(8,128)(2,1)S(1)}, u32[]{:S(2)}, u32[]{:S(2)}) collective-permute-start(bf16[128,256]{1,0:T(8,128)(2,1)S(1)} %get-tuple-element.41), channel_id=1, source_target_pairs={{0,8},{4,12},{8,0},{12,4},{1,9},{5,13},{9,1},{13,5},{2,10},{6,14},... | collective-permute-start | bytes 196616 | tf_op jit(solution)/shard_map/ppermute | solution.py:398
  31.1 6.3 %collective-permute-start.7 = (bf16[128,256]{1,0:T(8,128)(2,1)S(1)}, bf16[128,256]{1,0:T(8,128)(2,1)S(1)}, u32[]{:S(2)}, u32[]{:S(2)}) collective-permute-start(bf16[128,256]{1,0:T(8,128)(2,1)S(1)} %get-tuple-element.43), channel_id=1, source_target_pairs={{0,12},{4,8},{8,4},{12,0},{1,13},{5,9},{9,5},{13,1},{2,14},{6,10},... | collective-permute-start | bytes 196616 | tf_op jit(solution)/shard_map/ppermute | solution.py:398
  32.8 5.0 %collective-permute-start.8 = (bf16[128,256]{1,0:T(8,128)(2,1)S(1)}, bf16[128,256]{1,0:T(8,128)(2,1)S(1)}, u32[]{:S(2)}, u32[]{:S(2)}) collective-permute-start(bf16[128,256]{1,0:T(8,128)(2,1)S(1)} %get-tuple-element.44), channel_id=1, source_target_pairs={{0,4},{4,0},{8,12},{12,8},{1,5},{5,1},{9,13},{13,9},{2,6},{6,2},{1... | collective-permute-start | bytes 196616 | tf_op jit(solution)/shard_map/ppermute | solution.py:398
  38.1 1.4 %collective-permute-start.13 = (bf16[128,512]{1,0:T(8,128)(2,1)S(1)}, bf16[128,512]{1,0:T(8,128)(2,1)S(1)}, u32[]{:S(2)}, u32[]{:S(2)}) collective-permute-start(bf16[128,512]{1,0:T(8,128)(2,1)S(1)} %get-tuple-element.52), channel_id=1, source_target_pairs={{0,1},{1,0},{2,3},{3,2},{4,5},{5,4},{6,7},{7,6},{8,9},{9,8},{10,11... | collective-permute-start | bytes 393224 | tf_op jit(solution)/shard_map/ppermute | solution.py:398
  38.4 2.7 %collective-permute-start.9 = (bf16[128,512]{1,0:T(8,128)(2,1)S(1)}, bf16[128,512]{1,0:T(8,128)(2,1)S(1)}, u32[]{:S(2)}, u32[]{:S(2)}) collective-permute-start(bf16[128,512]{1,0:T(8,128)(2,1)S(1)} %get-tuple-element.48), channel_id=1, source_target_pairs={{0,1},{1,0},{2,3},{3,2},{4,5},{5,4},{6,7},{7,6},{8,9},{9,8},{10,11... | collective-permute-start | bytes 393224 | tf_op jit(solution)/shard_map/ppermute | solution.py:398
  39.5 5.6 %collective-permute-start.14 = (bf16[128,512]{1,0:T(8,128)(2,1)S(1)}, bf16[128,512]{1,0:T(8,128)(2,1)S(1)}, u32[]{:S(2)}, u32[]{:S(2)}) collective-permute-start(bf16[128,512]{1,0:T(8,128)(2,1)S(1)} %add_convert_fusion), channel_id=1, source_target_pairs={{0,2},{1,3},{2,0},{3,1},{4,6},{5,7},{6,4},{7,5},{8,10},{9,11},{10,... | collective-permute-start | bytes 393224 | tf_op jit(solution)/shard_map/ppermute | solution.py:398
  41.9 3.2 %collective-permute-start.11 = (bf16[64,1024]{1,0:T(8,128)(2,1)S(1)}, bf16[64,1024]{1,0:T(8,128)(2,1)S(1)}, u32[]{:S(2)}, u32[]{:S(2)}) collective-permute-start(bf16[64,1024]{1,0:T(8,128)(2,1)S(1)} %get-tuple-element.53), channel_id=1, source_target_pairs={{0,1},{1,0},{2,3},{3,2},{4,5},{5,4},{6,7},{7,6},{8,9},{9,8},{10,11... | collective-permute-start | bytes 393224 | tf_op jit(solution)/shard_map/ppermute | solution.py:398
  42.0 3.2 %collective-permute-start.10 = (bf16[64,1024]{1,0:T(8,128)(2,1)S(1)}, bf16[64,1024]{1,0:T(8,128)(2,1)S(1)}, u32[]{:S(2)}, u32[]{:S(2)}) collective-permute-start(bf16[64,1024]{1,0:T(8,128)(2,1)S(1)} %get-tuple-element.54), channel_id=1, source_target_pairs={{0,1},{1,0},{2,3},{3,2},{4,5},{5,4},{6,7},{7,6},{8,9},{9,8},{10,11... | collective-permute-start | bytes 393224 | tf_op jit(solution)/shard_map/ppermute | solution.py:398
  42.5 5.5 %collective-permute-start.12 = (bf16[128,512]{1,0:T(8,128)(2,1)S(1)}, bf16[128,512]{1,0:T(8,128)(2,1)S(1)}, u32[]{:S(2)}, u32[]{:S(2)}) collective-permute-start(bf16[128,512]{1,0:T(8,128)(2,1)S(1)} %add_convert_fusion.1._), channel_id=1, source_target_pairs={{0,2},{1,3},{2,0},{3,1},{4,6},{5,7},{6,4},{7,5},{8,10},{9,11},{10,... | collective-permute-start | bytes 393224 | tf_op jit(solution)/shard_map/ppermute | solution.py:398

commit v20 on v18

--- a/solution.py
+++ b/solution.py
@@ -375,7 +375,7 @@
 
 VMEM_LIMIT = 40 * 1024 * 1024
 PLAIN_LIMIT = 53 * 1024 * 1024 + 400 * 1024
-GATE_LIMIT = 60 * 1024 * 1024
+GATE_LIMIT = 53 * 1024 * 1024 + 200 * 1024
 IN_HBM = pl.BlockSpec(memory_space=pltpu.HBM)
 IN_VMEM = pl.BlockSpec(memory_space=pltpu.VMEM)
 ANYWHERE = pl.BlockSpec(memory_space=pl.ANY)

time: 48.8 us -> 48.9 us (level)
  Pallas kernels: 12.7 us -> 11.9 us
  local copies, waits for them, and re-layouts: 0.75 us -> 1.48 us
    pallas_call x13, Pallas kernels: 12.7 us -> 11.9 us  [run_kernel(): pl.pallas_call(kernel, out_shape=[jax.ShapeDtypeStruct(shape, dtype) for...]
    unnamed x10 -> x8, local copies, waits for them, and re-layouts: 0.73 us -> 1.46 us
  transfers between devices with their start and end apart: 15 -> 15, of which waited for: 8 -> 8; matrix products, arithmetic and copies ran while one was open for 0% -> 0% of each run, Pallas kernels for 20% -> 18%
where the time goes in v20:
time: 48.9 us; the launch traced here: 48.5 us
  starting transfers between devices  24.4 us (50%)
  Pallas kernels  11.9 us (24%)
  waiting for transfers between devices  10.6 us (22%)
  local copies, waits for them, and re-layouts  1.48 us (3%)
    ppermute x15, starting transfers between devices, swapped(): lax.ppermute(value, axis, [(source, source ^ step) for source in range(la...  24.4 us
    pallas_call x13, Pallas kernels, run_kernel(): pl.pallas_call(kernel, out_shape=[jax.ShapeDtypeStruct(shape, dtype) for...  11.9 us
    ppermute x15, waiting for transfers between devices, swapped(): lax.ppermute(value, axis, [(source, source ^ step) for source in range(la...  10.6 us
    unnamed x8, local copies, waits for them, and re-layouts  1.46 us
  transfers between devices with their start and end apart: 15, of which 8 were waited for; matrix products, arithmetic and copies ran while one was open for 0% of the time, Pallas kernels for 18%

profile of v20, /device:TPU:0, one launch (start us, length us, event | category | flops | bytes accessed | tf_op | source)
XLA Modules:
  0.0 48.5 jit_solution(7494926171868979060)
XLA Ops:
  0.0 1.1 %plain_kernel.1 = (bf16[384,256]{1,0:T(8,128)(2,1)S(1)}, bf16[384,256]{1,0:T(8,128)(2,1)S(1)}) custom-call(bf16[3,128,1024]{2,1,0:T(8,128)(2,1)} %bitcast.3, bf16[128,1024]{1,0:T(8,128)(2,1)} %queries_any.3, bf16[128,1024]{1,0:T(8,128)(2,1)} %keys_any.3), custom_call_target="tpu_custom_call" | custom-call | flops 1000000 | bytes 1048576 | tf_op jit(solution)/shard_map/plain_kernel/pallas_call | solution.py:385
  1.1 5.1 %collective-permute-start.3 = (bf16[384,256]{1,0:T(8,128)(2,1)S(1)}, bf16[384,256]{1,0:T(8,128)(2,1)S(1)}, u32[]{:S(2)}, u32[]{:S(2)}) collective-permute-start(bf16[384,256]{1,0:T(8,128)(2,1)S(1)} %get-tuple-element.33), channel_id=1, source_target_pairs={{0,12},{4,8},{8,4},{12,0},{1,13},{5,9},{9,5},{13,1},{2,14},{6,10},... | collective-permute-start | bytes 589832 | tf_op jit(solution)/shard_map/ppermute | solution.py:399
  6.2 0.7 %copy-done = bf16[3,3,1024]{2,1,0:T(4,128)(2,1)S(1)} copy-done((bf16[3,3,1024]{2,1,0:T(4,128)(2,1)S(1)}, bf16[3,3,1024]{2,1,0:T(4,128)(2,1)}, u32[]{:S(2)}) %copy-start) | copy-done | bytes 18456
  6.9 1.7 %gate_kernel.1 = (bf16[272,128]{1,0:T(8,128)(2,1)S(1)}, bf16[272,128]{1,0:T(8,128)(2,1)S(1)}, bf16[272,128]{1,0:T(8,128)(2,1)S(1)}, bf16[272,128]{1,0:T(8,128)(2...) custom-call(bf16[3,128,1024]{2,1,0:T(8,128)(2,1)} %bitcast.4, bf16[3,3,1024]{2,1,0:T(4,128)(2,1)S(1)} %copy-done, ...), custom_call_target="tpu_custom_call" | custom-call | flops 1000000 | bytes 1048576 | tf_op jit(solution)/shard_map/gate_kernel/pallas_call | solution.py:385
  8.6 0.7 %collective-permute-start.5 = (bf16[384,256]{1,0:T(8,128)(2,1)S(1)}, bf16[384,256]{1,0:T(8,128)(2,1)S(1)}, u32[]{:S(2)}, u32[]{:S(2)}) collective-permute-start(bf16[384,256]{1,0:T(8,128)(2,1)S(1)} %get-tuple-element.35), channel_id=1, source_target_pairs={{0,4},{4,0},{8,12},{12,8},{1,5},{5,1},{9,13},{13,9},{2,6},{6,2},{1... | collective-permute-start | bytes 589832 | tf_op jit(solution)/shard_map/ppermute | solution.py:399
  9.3 3.7 %collective-permute-start = (bf16[272,128]{1,0:T(8,128)(2,1)S(1)}, bf16[272,128]{1,0:T(8,128)(2,1)S(1)}, u32[]{:S(2)}, u32[]{:S(2)}) collective-permute-start(bf16[272,128]{1,0:T(8,128)(2,1)S(1)} %get-tuple-element.29), channel_id=1, source_target_pairs={{0,12},{4,8},{8,4},{12,0},{1,13},{5,9},{9,5},{13,1},{2,14},{6,10},... | collective-permute-start | bytes 208904 | tf_op jit(solution)/shard_map/ppermute | solution.py:399
  13.1 7.9 %collective-permute-start.2 = (bf16[272,128]{1,0:T(8,128)(2,1)S(1)}, bf16[272,128]{1,0:T(8,128)(2,1)S(1)}, u32[]{:S(2)}, u32[]{:S(2)}) collective-permute-start(bf16[272,128]{1,0:T(8,128)(2,1)S(1)} %get-tuple-element.31), channel_id=1, source_target_pairs={{0,4},{4,0},{8,12},{12,8},{1,5},{5,1},{9,13},{13,9},{2,6},{6,2},{1... | collective-permute-start | bytes 208904 | tf_op jit(solution)/shard_map/ppermute | solution.py:399
  21.0 0.7 %copy-done.2 = bf16[64,128]{1,0:T(8,128)(2,1)S(1)} copy-done((bf16[64,128]{1,0:T(8,128)(2,1)S(1)}, bf16[64,128]{1,0:T(8,128)(2,1)}, u32[]{:S(2)}) %copy-start.2) | copy-done | bytes 16408
  21.7 3.4 %ready_kernel.1 = (bf16[2048,256]{1,0:T(8,128)(2,1)S(1)}, bf16[1024,4096]{1,0:T(8,128)(2,1)S(1)}) custom-call(bf16[64,128]{1,0:T(8,128)(2,1)S(1)} %copy-done.2, bf16[1024,4096]{1,0:T(8,128)(2,1)} %weight_any.1), custom_call_target="tpu_custom_call" | custom-call | flops 1000000 | bytes 1048576 | tf_op jit(solution)/shard_map/ready_kernel/pallas_call | solution.py:385
  25.2 1.7 %collective-permute-done.4.second_ref = bf16[384,256]{1,0:T(8,128)(2,1)S(1)} collective-permute-done((bf16[384,256]{1,0:T(8,128)(2,1)S(1)}, bf16[384,256]{1,0:T(8,128)(2,1)S(1)}, u32[]{:S(2)}, u32[]{:S(2)}) %collective-permute-start.4) | collective-permute-done | bytes 196640 | tf_op jit(solution)/shard_map/ppermute | solution.py:399
  26.8 0.9 %weights_kernel.1 = (bf16[2,512,512]{2,1,0:T(8,128)(2,1)S(1)}, f32[512,128]{1,0:T(8,128)S(1)}, f32[512,256]{1,0:T(8,128)S(1)}) custom-call(bf16[384,256]{1,0:T(8,128)(2,1)S(1)} %collective-permute-done.3.third_ref, bf16[384,256]{1,0:T(8,128)(2,1)S(1)} %collective-permute-done.4.second_ref, bf16[384,256]{1,0:T(8,128)(2,1)S(1)} %collective-permute-done.5.near_ref, ...), custom_call_target="tpu_custom_call" | custom-call | flops 1000000 | bytes 1048576 | tf_op jit(solution)/shard_map/weights_kernel/pallas_call | solution.py:385
  27.8 1.1 %collective-permute-done.1.refs_1_ = bf16[272,128]{1,0:T(8,128)(2,1)S(1)} collective-permute-done((bf16[272,128]{1,0:T(8,128)(2,1)S(1)}, bf16[272,128]{1,0:T(8,128)(2,1)S(1)}, u32[]{:S(2)}, u32[]{:S(2)}) %collective-permute-start.1) | collective-permute-done | bytes 69664 | tf_op jit(solution)/shard_map/ppermute | solution.py:399
  28.9 1.1 %values_kernel.1 = (bf16[128,256]{1,0:T(8,128)(2,1)S(1)}, bf16[128,256]{1,0:T(8,128)(2,1)S(1)}, bf16[512,256]{1,0:T(8,128)(2,1)S(1)}) custom-call(bf16[272,128]{1,0:T(8,128)(2,1)S(1)} %collective-permute-done.refs_0_, bf16[272,128]{1,0:T(8,128)(2,1)S(1)} %collective-permute-done.1.refs_1_, bf16[272,128]{1,0:T(8,128)(2,1)S(1)} %collective-permute-done.2.refs_2_, ...), custom_call_target="tpu_custom_call" | custom-call | flops 1000000 | bytes 1048576 | tf_op jit(solution)/shard_map/values_kernel/pallas_call | solution.py:385
  29.9 0.9 %collective-permute-start.6 = (bf16[128,256]{1,0:T(8,128)(2,1)S(1)}, bf16[128,256]{1,0:T(8,128)(2,1)S(1)}, u32[]{:S(2)}, u32[]{:S(2)}) collective-permute-start(bf16[128,256]{1,0:T(8,128)(2,1)S(1)} %get-tuple-element.41), channel_id=1, source_target_pairs={{0,8},{4,12},{8,0},{12,4},{1,9},{5,13},{9,1},{13,5},{2,10},{6,14},... | collective-permute-start | bytes 196616 | tf_op jit(solution)/shard_map/ppermute | solution.py:399
  30.8 1.7 %collective-permute-start.7 = (bf16[128,256]{1,0:T(8,128)(2,1)S(1)}, bf16[128,256]{1,0:T(8,128)(2,1)S(1)}, u32[]{:S(2)}, u32[]{:S(2)}) collective-permute-start(bf16[128,256]{1,0:T(8,128)(2,1)S(1)} %get-tuple-element.42), channel_id=1, source_target_pairs={{0,12},{4,8},{8,4},{12,0},{1,13},{5,9},{9,5},{13,1},{2,14},{6,10},... | collective-permute-start | bytes 196616 | tf_op jit(solution)/shard_map/ppermute | solution.py:399
  32.8 1.0 %collective-permute-start.8 = (bf16[128,256]{1,0:T(8,128)(2,1)S(1)}, bf16[128,256]{1,0:T(8,128)(2,1)S(1)}, u32[]{:S(2)}, u32[]{:S(2)}) collective-permute-start(bf16[128,256]{1,0:T(8,128)(2,1)S(1)} %get-tuple-element.44), channel_id=1, source_target_pairs={{0,4},{4,0},{8,12},{12,8},{1,5},{5,1},{9,13},{13,9},{2,6},{6,2},{1... | collective-permute-start | bytes 196616 | tf_op jit(solution)/shard_map/ppermute | solution.py:399
  33.8 2.4 %collective-permute-done.6.second_ref = bf16[128,256]{1,0:T(8,128)(2,1)S(1)} collective-permute-done((bf16[128,256]{1,0:T(8,128)(2,1)S(1)}, bf16[128,256]{1,0:T(8,128)(2,1)S(1)}, u32[]{:S(2)}, u32[]{:S(2)}) %collective-permute-start.6) | collective-permute-done | bytes 65568 | tf_op jit(solution)/shard_map/ppermute | solution.py:399
  38.3 0.5 %collective-permute-start.9 = (bf16[128,512]{1,0:T(8,128)(2,1)S(1)}, bf16[128,512]{1,0:T(8,128)(2,1)S(1)}, u32[]{:S(2)}, u32[]{:S(2)}) collective-permute-start(bf16[128,512]{1,0:T(8,128)(2,1)S(1)} %get-tuple-element.48), channel_id=1, source_target_pairs={{0,1},{1,0},{2,3},{3,2},{4,5},{5,4},{6,7},{7,6},{8,9},{9,8},{10,11... | collective-permute-start | bytes 393224 | tf_op jit(solution)/shard_map/ppermute | solution.py:399
  39.4 1.6 %collective-permute-start.14 = (bf16[128,512]{1,0:T(8,128)(2,1)S(1)}, bf16[128,512]{1,0:T(8,128)(2,1)S(1)}, u32[]{:S(2)}, u32[]{:S(2)}) collective-permute-start(bf16[128,512]{1,0:T(8,128)(2,1)S(1)} %add_convert_fusion), channel_id=1, source_target_pairs={{0,2},{1,3},{2,0},{3,1},{4,6},{5,7},{6,4},{7,5},{8,10},{9,11},{10,... | collective-permute-start | bytes 393224 | tf_op jit(solution)/shard_map/ppermute | solution.py:399
  41.0 0.7 %project_kernel.1 = (bf16[128,1024]{1,0:T(8,128)(2,1)S(1)}, bf16[128,1024]{1,0:T(8,128)(2,1)S(1)}) custom-call(bf16[128,256]{1,0:T(8,128)(2,1)S(1)} %collective-permute-done.6.second_ref, bf16[128,256]{1,0:T(8,128)(2,1)S(1)} %collective-permute-done.7.third_ref, bf16[128,256]{1,0:T(8,128)(2,1)S(1)} %collective-permute-done.8.near_ref, ...), custom_call_target="tpu_custom_call" | custom-call | flops 1000000 | bytes 1048576 | tf_op jit(solution)/shard_map/project_kernel/pallas_call | solution.py:385
  42.9 2.1 %collective-permute-done.14.crossed_ref = bf16[128,512]{1,0:T(8,128)(2,1)S(1)} collective-permute-done((bf16[128,512]{1,0:T(8,128)(2,1)S(1)}, bf16[128,512]{1,0:T(8,128)(2,1)S(1)}, u32[]{:S(2)}, u32[]{:S(2)}) %collective-permute-start.14) | collective-permute-done | bytes 131104 | tf_op jit(solution)/shard_map/ppermute | solution.py:399
  45.0 0.7 %total_kernel.2.refs_0_ = bf16[128,1024]{1,0:T(8,128)(2,1)} custom-call(bf16[128,1024]{1,0:T(8,128)(2,1)S(1)} %get-tuple-element.49.kept_ref, bf16[64,1024]{1,0:T(8,128)(2,1)S(1)} %collective-permute-done.10.upper_ref, bf16[64,1024]{1,0:T(8,128)(2,1)S(1)} %collective-permute-done.11.lower_ref, bf16[128,512]{1,0:T(8,128)(2,1)S(1)} %collective-permute-done.14.crossed_ref), custom_call_target="tpu_custom_call" | custom-call | flops 1000000 | bytes 1048576 | tf_op jit(solution)/shard_map/total_kernel/pallas_call | solution.py:385
  45.7 2.1 %collective-permute-done.12.crossed_ref = bf16[128,512]{1,0:T(8,128)(2,1)S(1)} collective-permute-done((bf16[128,512]{1,0:T(8,128)(2,1)S(1)}, bf16[128,512]{1,0:T(8,128)(2,1)S(1)}, u32[]{:S(2)}, u32[]{:S(2)}) %collective-permute-start.12) | collective-permute-done | bytes 131104 | tf_op jit(solution)/shard_map/ppermute | solution.py:399
  47.8 0.7 %total_kernel.3 = bf16[128,1024]{1,0:T(8,128)(2,1)} custom-call(bf16[128,1024]{1,0:T(8,128)(2,1)S(1)} %get-tuple-element.49.kept_ref, bf16[64,1024]{1,0:T(8,128)(2,1)S(1)} %collective-permute-done.10.upper_ref, bf16[64,1024]{1,0:T(8,128)(2,1)S(1)} %collective-permute-done.11.lower_ref, ...), custom_call_target="tpu_custom_call", output_to_operand_aliasing={{}: (4, {})} | custom-call | flops 1000000 | bytes 1048576 | tf_op jit(solution)/shard_map/total_kernel/pallas_call | solution.py:385
  (30 shorter events, 4.1 us)
Async XLA Ops:
  0.0 26.8 %copy-start.1 = (bf16[3,3,1024]{2,1,0:T(4,128)(2,1)S(1)}, bf16[3,3,1024]{2,1,0:T(4,128)(2,1)}, u32[]{:S(2)}) copy-start(bf16[3,3,1024]{2,1,0:T(4,128)(2,1)} %refs_6_.1) | copy-start | bytes 55300
  0.0 28.9 %copy-start.3 = (f32[1024]{0:T(1024)S(1)}, f32[1024]{0:T(1024)}, u32[]{:S(2)}) copy-start(f32[1024]{0:T(1024)} %param.10) | copy-start | bytes 12292
  1.1 12.0 %collective-permute-start.3 = (bf16[384,256]{1,0:T(8,128)(2,1)S(1)}, bf16[384,256]{1,0:T(8,128)(2,1)S(1)}, u32[]{:S(2)}, u32[]{:S(2)}) collective-permute-start(bf16[384,256]{1,0:T(8,128)(2,1)S(1)} %get-tuple-element.33), channel_id=1, source_target_pairs={{0,12},{4,8},{8,4},{12,0},{1,13},{5,9},{9,5},{13,1},{2,14},{6,10},... | collective-permute-start | bytes 589832 | tf_op jit(solution)/shard_map/ppermute | solution.py:399
  6.2 20.6 %collective-permute-start.4 = (bf16[384,256]{1,0:T(8,128)(2,1)S(1)}, bf16[384,256]{1,0:T(8,128)(2,1)S(1)}, u32[]{:S(2)}, u32[]{:S(2)}) collective-permute-start(bf16[384,256]{1,0:T(8,128)(2,1)S(1)} %get-tuple-element.34), channel_id=1, source_target_pairs={{0,8},{4,12},{8,0},{12,4},{1,9},{5,13},{9,1},{13,5},{2,10},{6,14},... | collective-permute-start | bytes 589832 | tf_op jit(solution)/shard_map/ppermute | solution.py:399
  6.2 0.7 %copy-start = (bf16[3,3,1024]{2,1,0:T(4,128)(2,1)S(1)}, bf16[3,3,1024]{2,1,0:T(4,128)(2,1)}, u32[]{:S(2)}) copy-start(bf16[3,3,1024]{2,1,0:T(4,128)(2,1)} %refs_6_.1) | copy-start | bytes 55300
  8.6 18.2 %collective-permute-start.5 = (bf16[384,256]{1,0:T(8,128)(2,1)S(1)}, bf16[384,256]{1,0:T(8,128)(2,1)S(1)}, u32[]{:S(2)}, u32[]{:S(2)}) collective-permute-start(bf16[384,256]{1,0:T(8,128)(2,1)S(1)} %get-tuple-element.35), channel_id=1, source_target_pairs={{0,4},{4,0},{8,12},{12,8},{1,5},{5,1},{9,13},{13,9},{2,6},{6,2},{1... | collective-permute-start | bytes 589832 | tf_op jit(solution)/shard_map/ppermute | solution.py:399
  9.3 18.4 %collective-permute-start = (bf16[272,128]{1,0:T(8,128)(2,1)S(1)}, bf16[272,128]{1,0:T(8,128)(2,1)S(1)}, u32[]{:S(2)}, u32[]{:S(2)}) collective-permute-start(bf16[272,128]{1,0:T(8,128)(2,1)S(1)} %get-tuple-element.29), channel_id=1, source_target_pairs={{0,12},{4,8},{8,4},{12,0},{1,13},{5,9},{9,5},{13,1},{2,14},{6,10},... | collective-permute-start | bytes 208904 | tf_op jit(solution)/shard_map/ppermute | solution.py:399
  13.1 15.8 %collective-permute-start.1 = (bf16[272,128]{1,0:T(8,128)(2,1)S(1)}, bf16[272,128]{1,0:T(8,128)(2,1)S(1)}, u32[]{:S(2)}, u32[]{:S(2)}) collective-permute-start(bf16[272,128]{1,0:T(8,128)(2,1)S(1)} %get-tuple-element.30), channel_id=1, source_target_pairs={{0,8},{4,12},{8,0},{12,4},{1,9},{5,13},{9,1},{13,5},{2,10},{6,14},... | collective-permute-start | bytes 208904 | tf_op jit(solution)/shard_map/ppermute | solution.py:399
  13.1 15.8 %collective-permute-start.2 = (bf16[272,128]{1,0:T(8,128)(2,1)S(1)}, bf16[272,128]{1,0:T(8,128)(2,1)S(1)}, u32[]{:S(2)}, u32[]{:S(2)}) collective-permute-start(bf16[272,128]{1,0:T(8,128)(2,1)S(1)} %get-tuple-element.31), channel_id=1, source_target_pairs={{0,4},{4,0},{8,12},{12,8},{1,5},{5,1},{9,13},{13,9},{2,6},{6,2},{1... | collective-permute-start | bytes 208904 | tf_op jit(solution)/shard_map/ppermute | solution.py:399
  21.0 0.7 %copy-start.2 = (bf16[64,128]{1,0:T(8,128)(2,1)S(1)}, bf16[64,128]{1,0:T(8,128)(2,1)}, u32[]{:S(2)}) copy-start(bf16[64,128]{1,0:T(8,128)(2,1)} %filter_ref.1) | copy-start | bytes 49156
  29.9 6.3 %collective-permute-start.6 = (bf16[128,256]{1,0:T(8,128)(2,1)S(1)}, bf16[128,256]{1,0:T(8,128)(2,1)S(1)}, u32[]{:S(2)}, u32[]{:S(2)}) collective-permute-start(bf16[128,256]{1,0:T(8,128)(2,1)S(1)} %get-tuple-element.41), channel_id=1, source_target_pairs={{0,8},{4,12},{8,0},{12,4},{1,9},{5,13},{9,1},{13,5},{2,10},{6,14},... | collective-permute-start | bytes 196616 | tf_op jit(solution)/shard_map/ppermute | solution.py:399
  30.8 6.2 %collective-permute-start.7 = (bf16[128,256]{1,0:T(8,128)(2,1)S(1)}, bf16[128,256]{1,0:T(8,128)(2,1)S(1)}, u32[]{:S(2)}, u32[]{:S(2)}) collective-permute-start(bf16[128,256]{1,0:T(8,128)(2,1)S(1)} %get-tuple-element.42), channel_id=1, source_target_pairs={{0,12},{4,8},{8,4},{12,0},{1,13},{5,9},{9,5},{13,1},{2,14},{6,10},... | collective-permute-start | bytes 196616 | tf_op jit(solution)/shard_map/ppermute | solution.py:399
  32.8 4.9 %collective-permute-start.8 = (bf16[128,256]{1,0:T(8,128)(2,1)S(1)}, bf16[128,256]{1,0:T(8,128)(2,1)S(1)}, u32[]{:S(2)}, u32[]{:S(2)}) collective-permute-start(bf16[128,256]{1,0:T(8,128)(2,1)S(1)} %get-tuple-element.44), channel_id=1, source_target_pairs={{0,4},{4,0},{8,12},{12,8},{1,5},{5,1},{9,13},{13,9},{2,6},{6,2},{1... | collective-permute-start | bytes 196616 | tf_op jit(solution)/shard_map/ppermute | solution.py:399
  37.9 1.4 %collective-permute-start.13 = (bf16[128,512]{1,0:T(8,128)(2,1)S(1)}, bf16[128,512]{1,0:T(8,128)(2,1)S(1)}, u32[]{:S(2)}, u32[]{:S(2)}) collective-permute-start(bf16[128,512]{1,0:T(8,128)(2,1)S(1)} %get-tuple-element.52), channel_id=1, source_target_pairs={{0,1},{1,0},{2,3},{3,2},{4,5},{5,4},{6,7},{7,6},{8,9},{9,8},{10,11... | collective-permute-start | bytes 393224 | tf_op jit(solution)/shard_map/ppermute | solution.py:399
  38.3 2.7 %collective-permute-start.9 = (bf16[128,512]{1,0:T(8,128)(2,1)S(1)}, bf16[128,512]{1,0:T(8,128)(2,1)S(1)}, u32[]{:S(2)}, u32[]{:S(2)}) collective-permute-start(bf16[128,512]{1,0:T(8,128)(2,1)S(1)} %get-tuple-element.48), channel_id=1, source_target_pairs={{0,1},{1,0},{2,3},{3,2},{4,5},{5,4},{6,7},{7,6},{8,9},{9,8},{10,11... | collective-permute-start | bytes 393224 | tf_op jit(solution)/shard_map/ppermute | solution.py:399
  39.4 5.6 %collective-permute-start.14 = (bf16[128,512]{1,0:T(8,128)(2,1)S(1)}, bf16[128,512]{1,0:T(8,128)(2,1)S(1)}, u32[]{:S(2)}, u32[]{:S(2)}) collective-permute-start(bf16[128,512]{1,0:T(8,128)(2,1)S(1)} %add_convert_fusion), channel_id=1, source_target_pairs={{0,2},{1,3},{2,0},{3,1},{4,6},{5,7},{6,4},{7,5},{8,10},{9,11},{10,... | collective-permute-start | bytes 393224 | tf_op jit(solution)/shard_map/ppermute | solution.py:399
  41.7 3.3 %collective-permute-start.11 = (bf16[64,1024]{1,0:T(8,128)(2,1)S(1)}, bf16[64,1024]{1,0:T(8,128)(2,1)S(1)}, u32[]{:S(2)}, u32[]{:S(2)}) collective-permute-start(bf16[64,1024]{1,0:T(8,128)(2,1)S(1)} %get-tuple-element.53), channel_id=1, source_target_pairs={{0,1},{1,0},{2,3},{3,2},{4,5},{5,4},{6,7},{7,6},{8,9},{9,8},{10,11... | collective-permute-start | bytes 393224 | tf_op jit(solution)/shard_map/ppermute | solution.py:399
  41.8 3.2 %collective-permute-start.10 = (bf16[64,1024]{1,0:T(8,128)(2,1)S(1)}, bf16[64,1024]{1,0:T(8,128)(2,1)S(1)}, u32[]{:S(2)}, u32[]{:S(2)}) collective-permute-start(bf16[64,1024]{1,0:T(8,128)(2,1)S(1)} %get-tuple-element.54), channel_id=1, source_target_pairs={{0,1},{1,0},{2,3},{3,2},{4,5},{5,4},{6,7},{7,6},{8,9},{9,8},{10,11... | collective-permute-start | bytes 393224 | tf_op jit(solution)/shard_map/ppermute | solution.py:399
  42.3 5.5 %collective-permute-start.12 = (bf16[128,512]{1,0:T(8,128)(2,1)S(1)}, bf16[128,512]{1,0:T(8,128)(2,1)S(1)}, u32[]{:S(2)}, u32[]{:S(2)}) collective-permute-start(bf16[128,512]{1,0:T(8,128)(2,1)S(1)} %add_convert_fusion.1._), channel_id=1, source_target_pairs={{0,2},{1,3},{2,0},{3,1},{4,6},{5,7},{6,4},{7,5},{8,10},{9,11},{10,... | collective-permute-start | bytes 393224 | tf_op jit(solution)/shard_map/ppermute | solution.py:399

commit v21 on v20

--- a/solution.py
+++ b/solution.py
@@ -307,8 +307,8 @@
         mix_rows(position ^ step, weight_ref, total_ref, value_ref, out_ref)
 
 
-def project_kernel(masks, second_ref, third_ref, near_ref, mine_ref, weight_ref, _, *refs):
-    out_refs, attended_s = refs[:-1], refs[-1]
+def project_kernel(masks, second_ref, third_ref, near_ref, mine_ref, weight_ref, *refs):
+    out_refs, attended_s = refs[2:-1], refs[-1]
     own, width = mine_ref.shape[1], out_refs[0].shape[1]
     position, here = lax.axis_index("ctx"), lax.axis_index("mp")
     for step, piece in ((0, mine_ref), (1, near_ref), (2, second_ref), (3, third_ref)):
@@ -343,13 +343,13 @@
         )
 
 
-def project_far_kernel(part, near_ref, partial_ref, weight_ref, given_ref, kept_ref):
-    own, size = near_ref.shape[1], given_ref.shape[1]
+def project_far_kernel(part, masks, near_ref, partial_ref, weight_ref, *out_refs):
+    own, size = near_ref.shape[1], out_refs[0].shape[1]
     width = partial_ref.shape[1] // 2
     position, here = lax.axis_index("ctx"), lax.axis_index("mp")
-    for index, (mask, out_ref) in enumerate(((3, given_ref), (2, kept_ref))):
+    for mask, out_ref in zip(masks, out_refs):
         columns = columns_of((here ^ mask) * (width // size) + part, size)
-        start = index * width + part * size
+        start = (3 - mask) * width + part * size
         total = partial_ref[:, start : start + size] + jnp.dot(
             near_ref[...], weight_ref[columns_of(position ^ 1, own), columns], preferred_element_type=jnp.float32
         )
@@ -481,21 +481,26 @@
     (partial,) = run_kernel(
         partial_third_kernel, (third, partial, out_weight), [((rows, 2 * width), jnp.float32)]
     )
-    crossed = []
+    crossed, sums = [], []
     for part in range(2):
-        given, kept = run_kernel(
-            functools.partial(project_far_kernel, part),
-            (near, partial, out_weight),
-            [((rows, width // 2), jnp.bfloat16)] * 2,
-        )
+        given, kept = [
+            block
+            for masks in ((3,), (2,))
+            for block in run_kernel(
+                functools.partial(project_far_kernel, part, masks),
+                (near, partial, out_weight),
+                [((rows, width // 2), jnp.bfloat16)] * len(masks),
+            )
+        ]
         far_sum = added(kept, swapped(given, "mp", 1))
+        sums.append(far_sum)
         crossed.append(swapped(far_sum, "mp", 2))
     near_given, near_kept = run_kernel(
         functools.partial(project_kernel, (1, 0)),
-        (*attended, out_weight, far_sum),
+        (*attended, out_weight, *sums),
         [((rows, width), jnp.bfloat16)] * 2,
         [pltpu.VMEM((rows, out_weight.shape[0]), jnp.bfloat16)],
-        [IN_VMEM] * 5 + [ANYWHERE],
+        [IN_VMEM] * 5 + [ANYWHERE] * 2,
     )
     half = near_given.shape[0] // 2
     near_got = [swapped(near_given[:half], "mp", 1), swapped(near_given[half:], "mp", 1)]

time: 48.9 us -> 48.8 us (level)
    pallas_call x13 -> x15, Pallas kernels: 11.9 us -> 12.2 us  [run_kernel(): pl.pallas_call(kernel, out_shape=[jax.ShapeDtypeStruct(shape, dtype) for...]
  transfers between devices with their start and end apart: 15 -> 15, of which waited for: 8 -> 8; matrix products, arithmetic and copies ran while one was open for 0% -> 0% of each run, Pallas kernels for 18% -> 19%
where the time goes in v21:
time: 48.8 us; the launch traced here: 48.5 us
  starting transfers between devices  24.4 us (50%)
  Pallas kernels  12.2 us (25%)
  waiting for transfers between devices  10.2 us (21%)
  local copies, waits for them, and re-layouts  1.48 us (3%)
    ppermute x15, starting transfers between devices, swapped(): lax.ppermute(value, axis, [(source, source ^ step) for source in range(la...  24.4 us
    pallas_call x15, Pallas kernels, run_kernel(): pl.pallas_call(kernel, out_shape=[jax.ShapeDtypeStruct(shape, dtype) for...  12.2 us
    ppermute x15, waiting for transfers between devices, swapped(): lax.ppermute(value, axis, [(source, source ^ step) for source in range(la...  10.2 us
    unnamed x8, local copies, waits for them, and re-layouts  1.46 us
  transfers between devices with their start and end apart: 15, of which 8 were waited for; matrix products, arithmetic and copies ran while one was open for 0% of the time, Pallas kernels for 19%

profile of v21, /device:TPU:0, one launch (start us, length us, event | category | flops | bytes accessed | tf_op | source)
XLA Modules:
  0.0 48.5 jit_solution(12353467685451998763)
XLA Ops:
  0.0 1.1 %plain_kernel.1 = (bf16[384,256]{1,0:T(8,128)(2,1)S(1)}, bf16[384,256]{1,0:T(8,128)(2,1)S(1)}) custom-call(bf16[3,128,1024]{2,1,0:T(8,128)(2,1)} %bitcast.3, bf16[128,1024]{1,0:T(8,128)(2,1)} %queries_any.3, bf16[128,1024]{1,0:T(8,128)(2,1)} %keys_any.3), custom_call_target="tpu_custom_call" | custom-call | flops 1000000 | bytes 1048576 | tf_op jit(solution)/shard_map/plain_kernel/pallas_call | solution.py:385
  1.1 5.1 %collective-permute-start.3 = (bf16[384,256]{1,0:T(8,128)(2,1)S(1)}, bf16[384,256]{1,0:T(8,128)(2,1)S(1)}, u32[]{:S(2)}, u32[]{:S(2)}) collective-permute-start(bf16[384,256]{1,0:T(8,128)(2,1)S(1)} %get-tuple-element.29), channel_id=1, source_target_pairs={{0,12},{4,8},{8,4},{12,0},{1,13},{5,9},{9,5},{13,1},{2,14},{6,10},... | collective-permute-start | bytes 589832 | tf_op jit(solution)/shard_map/ppermute | solution.py:399
  6.2 0.7 %copy-done = bf16[3,3,1024]{2,1,0:T(4,128)(2,1)S(1)} copy-done((bf16[3,3,1024]{2,1,0:T(4,128)(2,1)S(1)}, bf16[3,3,1024]{2,1,0:T(4,128)(2,1)}, u32[]{:S(2)}) %copy-start) | copy-done | bytes 18456
  6.9 1.7 %gate_kernel.1 = (bf16[272,128]{1,0:T(8,128)(2,1)S(1)}, bf16[272,128]{1,0:T(8,128)(2,1)S(1)}, bf16[272,128]{1,0:T(8,128)(2,1)S(1)}, bf16[272,128]{1,0:T(8,128)(2...) custom-call(bf16[3,128,1024]{2,1,0:T(8,128)(2,1)} %bitcast.4, bf16[3,3,1024]{2,1,0:T(4,128)(2,1)S(1)} %copy-done, ...), custom_call_target="tpu_custom_call" | custom-call | flops 1000000 | bytes 1048576 | tf_op jit(solution)/shard_map/gate_kernel/pallas_call | solution.py:385
  8.6 0.7 %collective-permute-start.5 = (bf16[384,256]{1,0:T(8,128)(2,1)S(1)}, bf16[384,256]{1,0:T(8,128)(2,1)S(1)}, u32[]{:S(2)}, u32[]{:S(2)}) collective-permute-start(bf16[384,256]{1,0:T(8,128)(2,1)S(1)} %get-tuple-element.31), channel_id=1, source_target_pairs={{0,4},{4,0},{8,12},{12,8},{1,5},{5,1},{9,13},{13,9},{2,6},{6,2},{1... | collective-permute-start | bytes 589832 | tf_op jit(solution)/shard_map/ppermute | solution.py:399
  9.3 3.7 %collective-permute-start = (bf16[272,128]{1,0:T(8,128)(2,1)S(1)}, bf16[272,128]{1,0:T(8,128)(2,1)S(1)}, u32[]{:S(2)}, u32[]{:S(2)}) collective-permute-start(bf16[272,128]{1,0:T(8,128)(2,1)S(1)} %get-tuple-element.25), channel_id=1, source_target_pairs={{0,12},{4,8},{8,4},{12,0},{1,13},{5,9},{9,5},{13,1},{2,14},{6,10},... | collective-permute-start | bytes 208904 | tf_op jit(solution)/shard_map/ppermute | solution.py:399
  13.1 7.9 %collective-permute-start.2 = (bf16[272,128]{1,0:T(8,128)(2,1)S(1)}, bf16[272,128]{1,0:T(8,128)(2,1)S(1)}, u32[]{:S(2)}, u32[]{:S(2)}) collective-permute-start(bf16[272,128]{1,0:T(8,128)(2,1)S(1)} %get-tuple-element.27), channel_id=1, source_target_pairs={{0,4},{4,0},{8,12},{12,8},{1,5},{5,1},{9,13},{13,9},{2,6},{6,2},{1... | collective-permute-start | bytes 208904 | tf_op jit(solution)/shard_map/ppermute | solution.py:399
  21.0 0.7 %copy-done.2 = bf16[64,128]{1,0:T(8,128)(2,1)S(1)} copy-done((bf16[64,128]{1,0:T(8,128)(2,1)S(1)}, bf16[64,128]{1,0:T(8,128)(2,1)}, u32[]{:S(2)}) %copy-start.2) | copy-done | bytes 16408
  21.7 3.4 %ready_kernel.1 = (bf16[2048,256]{1,0:T(8,128)(2,1)S(1)}, bf16[1024,4096]{1,0:T(8,128)(2,1)S(1)}) custom-call(bf16[64,128]{1,0:T(8,128)(2,1)S(1)} %copy-done.2, bf16[1024,4096]{1,0:T(8,128)(2,1)} %weight_any.1), custom_call_target="tpu_custom_call" | custom-call | flops 1000000 | bytes 1048576 | tf_op jit(solution)/shard_map/ready_kernel/pallas_call | solution.py:385
  25.2 1.7 %collective-permute-done.4.second_ref = bf16[384,256]{1,0:T(8,128)(2,1)S(1)} collective-permute-done((bf16[384,256]{1,0:T(8,128)(2,1)S(1)}, bf16[384,256]{1,0:T(8,128)(2,1)S(1)}, u32[]{:S(2)}, u32[]{:S(2)}) %collective-permute-start.4) | collective-permute-done | bytes 196640 | tf_op jit(solution)/shard_map/ppermute | solution.py:399
  26.8 0.9 %weights_kernel.1 = (bf16[2,512,512]{2,1,0:T(8,128)(2,1)S(1)}, f32[512,128]{1,0:T(8,128)S(1)}, f32[512,256]{1,0:T(8,128)S(1)}) custom-call(bf16[384,256]{1,0:T(8,128)(2,1)S(1)} %collective-permute-done.3.third_ref, bf16[384,256]{1,0:T(8,128)(2,1)S(1)} %collective-permute-done.4.second_ref, bf16[384,256]{1,0:T(8,128)(2,1)S(1)} %collective-permute-done.5.near_ref, ...), custom_call_target="tpu_custom_call" | custom-call | flops 1000000 | bytes 1048576 | tf_op jit(solution)/shard_map/weights_kernel/pallas_call | solution.py:385
  27.8 1.1 %collective-permute-done.1.refs_1_ = bf16[272,128]{1,0:T(8,128)(2,1)S(1)} collective-permute-done((bf16[272,128]{1,0:T(8,128)(2,1)S(1)}, bf16[272,128]{1,0:T(8,128)(2,1)S(1)}, u32[]{:S(2)}, u32[]{:S(2)}) %collective-permute-start.1) | collective-permute-done | bytes 69664 | tf_op jit(solution)/shard_map/ppermute | solution.py:399
  28.9 1.1 %values_kernel.1 = (bf16[128,256]{1,0:T(8,128)(2,1)S(1)}, bf16[128,256]{1,0:T(8,128)(2,1)S(1)}, bf16[512,256]{1,0:T(8,128)(2,1)S(1)}) custom-call(bf16[272,128]{1,0:T(8,128)(2,1)S(1)} %collective-permute-done.refs_0_, bf16[272,128]{1,0:T(8,128)(2,1)S(1)} %collective-permute-done.1.refs_1_, bf16[272,128]{1,0:T(8,128)(2,1)S(1)} %collective-permute-done.2.refs_2_, ...), custom_call_target="tpu_custom_call" | custom-call | flops 1000000 | bytes 1048576 | tf_op jit(solution)/shard_map/values_kernel/pallas_call | solution.py:385
  29.9 0.9 %collective-permute-start.6 = (bf16[128,256]{1,0:T(8,128)(2,1)S(1)}, bf16[128,256]{1,0:T(8,128)(2,1)S(1)}, u32[]{:S(2)}, u32[]{:S(2)}) collective-permute-start(bf16[128,256]{1,0:T(8,128)(2,1)S(1)} %get-tuple-element.37), channel_id=1, source_target_pairs={{0,8},{4,12},{8,0},{12,4},{1,9},{5,13},{9,1},{13,5},{2,10},{6,14},... | collective-permute-start | bytes 196616 | tf_op jit(solution)/shard_map/ppermute | solution.py:399
  30.8 1.7 %collective-permute-start.7 = (bf16[128,256]{1,0:T(8,128)(2,1)S(1)}, bf16[128,256]{1,0:T(8,128)(2,1)S(1)}, u32[]{:S(2)}, u32[]{:S(2)}) collective-permute-start(bf16[128,256]{1,0:T(8,128)(2,1)S(1)} %get-tuple-element.38), channel_id=1, source_target_pairs={{0,12},{4,8},{8,4},{12,0},{1,13},{5,9},{9,5},{13,1},{2,14},{6,10},... | collective-permute-start | bytes 196616 | tf_op jit(solution)/shard_map/ppermute | solution.py:399
  32.8 1.0 %collective-permute-start.8 = (bf16[128,256]{1,0:T(8,128)(2,1)S(1)}, bf16[128,256]{1,0:T(8,128)(2,1)S(1)}, u32[]{:S(2)}, u32[]{:S(2)}) collective-permute-start(bf16[128,256]{1,0:T(8,128)(2,1)S(1)} %get-tuple-element.40), channel_id=1, source_target_pairs={{0,4},{4,0},{8,12},{12,8},{1,5},{5,1},{9,13},{13,9},{2,6},{6,2},{1... | collective-permute-start | bytes 196616 | tf_op jit(solution)/shard_map/ppermute | solution.py:399
  33.8 2.4 %collective-permute-done.6.second_ref = bf16[128,256]{1,0:T(8,128)(2,1)S(1)} collective-permute-done((bf16[128,256]{1,0:T(8,128)(2,1)S(1)}, bf16[128,256]{1,0:T(8,128)(2,1)S(1)}, u32[]{:S(2)}, u32[]{:S(2)}) %collective-permute-start.6) | collective-permute-done | bytes 65568 | tf_op jit(solution)/shard_map/ppermute | solution.py:399
  38.2 0.5 %collective-permute-start.10 = (bf16[128,512]{1,0:T(8,128)(2,1)S(1)}, bf16[128,512]{1,0:T(8,128)(2,1)S(1)}, u32[]{:S(2)}, u32[]{:S(2)}) collective-permute-start(bf16[128,512]{1,0:T(8,128)(2,1)S(1)} %project_far_kernel.7), channel_id=1, source_target_pairs={{0,1},{1,0},{2,3},{3,2},{4,5},{5,4},{6,7},{7,6},{8,9},{9,8},{10,11... | collective-permute-start | bytes 393224 | tf_op jit(solution)/shard_map/ppermute | solution.py:399
  39.3 1.6 %collective-permute-start.14 = (bf16[128,512]{1,0:T(8,128)(2,1)S(1)}, bf16[128,512]{1,0:T(8,128)(2,1)S(1)}, u32[]{:S(2)}, u32[]{:S(2)}) collective-permute-start(bf16[128,512]{1,0:T(8,128)(2,1)S(1)} %add_convert_fusion.1.refs_0_), channel_id=1, source_target_pairs={{0,2},{1,3},{2,0},{3,1},{4,6},{5,7},{6,4},{7,5},{8,10},{9,11},{10,... | collective-permute-start | bytes 393224 | tf_op jit(solution)/shard_map/ppermute | solution.py:399
  40.9 0.7 %project_kernel.1 = (bf16[128,1024]{1,0:T(8,128)(2,1)S(1)}, bf16[128,1024]{1,0:T(8,128)(2,1)S(1)}) custom-call(bf16[128,256]{1,0:T(8,128)(2,1)S(1)} %collective-permute-done.6.second_ref, bf16[128,256]{1,0:T(8,128)(2,1)S(1)} %collective-permute-done.7.third_ref, bf16[128,256]{1,0:T(8,128)(2,1)S(1)} %collective-permute-done.8.near_ref, ...), custom_call_target="tpu_custom_call" | custom-call | flops 1000000 | bytes 1048576 | tf_op jit(solution)/shard_map/project_kernel/pallas_call | solution.py:385
  42.8 2.1 %collective-permute-done.14.crossed_ref = bf16[128,512]{1,0:T(8,128)(2,1)S(1)} collective-permute-done((bf16[128,512]{1,0:T(8,128)(2,1)S(1)}, bf16[128,512]{1,0:T(8,128)(2,1)S(1)}, u32[]{:S(2)}, u32[]{:S(2)}) %collective-permute-start.14) | collective-permute-done | bytes 131104 | tf_op jit(solution)/shard_map/ppermute | solution.py:399
  45.0 0.7 %total_kernel.2.refs_0_ = bf16[128,1024]{1,0:T(8,128)(2,1)} custom-call(bf16[128,1024]{1,0:T(8,128)(2,1)S(1)} %get-tuple-element.43.kept_ref, bf16[64,1024]{1,0:T(8,128)(2,1)S(1)} %collective-permute-done.11.upper_ref, bf16[64,1024]{1,0:T(8,128)(2,1)S(1)} %collective-permute-done.12.lower_ref, bf16[128,512]{1,0:T(8,128)(2,1)S(1)} %collective-permute-done.14.crossed_ref), custom_call_target="tpu_custom_call" | custom-call | flops 1000000 | bytes 1048576 | tf_op jit(solution)/shard_map/total_kernel/pallas_call | solution.py:385
  45.7 2.1 %collective-permute-done.13.crossed_ref = bf16[128,512]{1,0:T(8,128)(2,1)S(1)} collective-permute-done((bf16[128,512]{1,0:T(8,128)(2,1)S(1)}, bf16[128,512]{1,0:T(8,128)(2,1)S(1)}, u32[]{:S(2)}, u32[]{:S(2)}) %collective-permute-start.13) | collective-permute-done | bytes 131104 | tf_op jit(solution)/shard_map/ppermute | solution.py:399
  47.8 0.7 %total_kernel.3 = bf16[128,1024]{1,0:T(8,128)(2,1)} custom-call(bf16[128,1024]{1,0:T(8,128)(2,1)S(1)} %get-tuple-element.43.kept_ref, bf16[64,1024]{1,0:T(8,128)(2,1)S(1)} %collective-permute-done.11.upper_ref, bf16[64,1024]{1,0:T(8,128)(2,1)S(1)} %collective-permute-done.12.lower_ref, ...), custom_call_target="tpu_custom_call", output_to_operand_aliasing={{}: (4, {})} | custom-call | flops 1000000 | bytes 1048576 | tf_op jit(solution)/shard_map/total_kernel/pallas_call | solution.py:385
  (32 shorter events, 4.0 us)
Async XLA Ops:
  0.0 26.8 %copy-start.1 = (bf16[3,3,1024]{2,1,0:T(4,128)(2,1)S(1)}, bf16[3,3,1024]{2,1,0:T(4,128)(2,1)}, u32[]{:S(2)}) copy-start(bf16[3,3,1024]{2,1,0:T(4,128)(2,1)} %refs_6_.1) | copy-start | bytes 55300
  0.0 28.9 %copy-start.3 = (f32[1024]{0:T(1024)S(1)}, f32[1024]{0:T(1024)}, u32[]{:S(2)}) copy-start(f32[1024]{0:T(1024)} %param.10) | copy-start | bytes 12292
  1.1 12.0 %collective-permute-start.3 = (bf16[384,256]{1,0:T(8,128)(2,1)S(1)}, bf16[384,256]{1,0:T(8,128)(2,1)S(1)}, u32[]{:S(2)}, u32[]{:S(2)}) collective-permute-start(bf16[384,256]{1,0:T(8,128)(2,1)S(1)} %get-tuple-element.29), channel_id=1, source_target_pairs={{0,12},{4,8},{8,4},{12,0},{1,13},{5,9},{9,5},{13,1},{2,14},{6,10},... | collective-permute-start | bytes 589832 | tf_op jit(solution)/shard_map/ppermute | solution.py:399
  6.2 20.6 %collective-permute-start.4 = (bf16[384,256]{1,0:T(8,128)(2,1)S(1)}, bf16[384,256]{1,0:T(8,128)(2,1)S(1)}, u32[]{:S(2)}, u32[]{:S(2)}) collective-permute-start(bf16[384,256]{1,0:T(8,128)(2,1)S(1)} %get-tuple-element.30), channel_id=1, source_target_pairs={{0,8},{4,12},{8,0},{12,4},{1,9},{5,13},{9,1},{13,5},{2,10},{6,14},... | collective-permute-start | bytes 589832 | tf_op jit(solution)/shard_map/ppermute | solution.py:399
  6.2 0.7 %copy-start = (bf16[3,3,1024]{2,1,0:T(4,128)(2,1)S(1)}, bf16[3,3,1024]{2,1,0:T(4,128)(2,1)}, u32[]{:S(2)}) copy-start(bf16[3,3,1024]{2,1,0:T(4,128)(2,1)} %refs_6_.1) | copy-start | bytes 55300
  8.6 18.2 %collective-permute-start.5 = (bf16[384,256]{1,0:T(8,128)(2,1)S(1)}, bf16[384,256]{1,0:T(8,128)(2,1)S(1)}, u32[]{:S(2)}, u32[]{:S(2)}) collective-permute-start(bf16[384,256]{1,0:T(8,128)(2,1)S(1)} %get-tuple-element.31), channel_id=1, source_target_pairs={{0,4},{4,0},{8,12},{12,8},{1,5},{5,1},{9,13},{13,9},{2,6},{6,2},{1... | collective-permute-start | bytes 589832 | tf_op jit(solution)/shard_map/ppermute | solution.py:399
  9.3 18.4 %collective-permute-start = (bf16[272,128]{1,0:T(8,128)(2,1)S(1)}, bf16[272,128]{1,0:T(8,128)(2,1)S(1)}, u32[]{:S(2)}, u32[]{:S(2)}) collective-permute-start(bf16[272,128]{1,0:T(8,128)(2,1)S(1)} %get-tuple-element.25), channel_id=1, source_target_pairs={{0,12},{4,8},{8,4},{12,0},{1,13},{5,9},{9,5},{13,1},{2,14},{6,10},... | collective-permute-start | bytes 208904 | tf_op jit(solution)/shard_map/ppermute | solution.py:399
  13.1 15.8 %collective-permute-start.1 = (bf16[272,128]{1,0:T(8,128)(2,1)S(1)}, bf16[272,128]{1,0:T(8,128)(2,1)S(1)}, u32[]{:S(2)}, u32[]{:S(2)}) collective-permute-start(bf16[272,128]{1,0:T(8,128)(2,1)S(1)} %get-tuple-element.26), channel_id=1, source_target_pairs={{0,8},{4,12},{8,0},{12,4},{1,9},{5,13},{9,1},{13,5},{2,10},{6,14},... | collective-permute-start | bytes 208904 | tf_op jit(solution)/shard_map/ppermute | solution.py:399
  13.1 15.8 %collective-permute-start.2 = (bf16[272,128]{1,0:T(8,128)(2,1)S(1)}, bf16[272,128]{1,0:T(8,128)(2,1)S(1)}, u32[]{:S(2)}, u32[]{:S(2)}) collective-permute-start(bf16[272,128]{1,0:T(8,128)(2,1)S(1)} %get-tuple-element.27), channel_id=1, source_target_pairs={{0,4},{4,0},{8,12},{12,8},{1,5},{5,1},{9,13},{13,9},{2,6},{6,2},{1... | collective-permute-start | bytes 208904 | tf_op jit(solution)/shard_map/ppermute | solution.py:399
  21.0 0.7 %copy-start.2 = (bf16[64,128]{1,0:T(8,128)(2,1)S(1)}, bf16[64,128]{1,0:T(8,128)(2,1)}, u32[]{:S(2)}) copy-start(bf16[64,128]{1,0:T(8,128)(2,1)} %filter_ref.1) | copy-start | bytes 49156
  29.9 6.3 %collective-permute-start.6 = (bf16[128,256]{1,0:T(8,128)(2,1)S(1)}, bf16[128,256]{1,0:T(8,128)(2,1)S(1)}, u32[]{:S(2)}, u32[]{:S(2)}) collective-permute-start(bf16[128,256]{1,0:T(8,128)(2,1)S(1)} %get-tuple-element.37), channel_id=1, source_target_pairs={{0,8},{4,12},{8,0},{12,4},{1,9},{5,13},{9,1},{13,5},{2,10},{6,14},... | collective-permute-start | bytes 196616 | tf_op jit(solution)/shard_map/ppermute | solution.py:399
  30.8 6.2 %collective-permute-start.7 = (bf16[128,256]{1,0:T(8,128)(2,1)S(1)}, bf16[128,256]{1,0:T(8,128)(2,1)S(1)}, u32[]{:S(2)}, u32[]{:S(2)}) collective-permute-start(bf16[128,256]{1,0:T(8,128)(2,1)S(1)} %get-tuple-element.38), channel_id=1, source_target_pairs={{0,12},{4,8},{8,4},{12,0},{1,13},{5,9},{9,5},{13,1},{2,14},{6,10},... | collective-permute-start | bytes 196616 | tf_op jit(solution)/shard_map/ppermute | solution.py:399
  32.8 4.9 %collective-permute-start.8 = (bf16[128,256]{1,0:T(8,128)(2,1)S(1)}, bf16[128,256]{1,0:T(8,128)(2,1)S(1)}, u32[]{:S(2)}, u32[]{:S(2)}) collective-permute-start(bf16[128,256]{1,0:T(8,128)(2,1)S(1)} %get-tuple-element.40), channel_id=1, source_target_pairs={{0,4},{4,0},{8,12},{12,8},{1,5},{5,1},{9,13},{13,9},{2,6},{6,2},{1... | collective-permute-start | bytes 196616 | tf_op jit(solution)/shard_map/ppermute | solution.py:399
  37.9 1.4 %collective-permute-start.9 = (bf16[128,512]{1,0:T(8,128)(2,1)S(1)}, bf16[128,512]{1,0:T(8,128)(2,1)S(1)}, u32[]{:S(2)}, u32[]{:S(2)}) collective-permute-start(bf16[128,512]{1,0:T(8,128)(2,1)S(1)} %project_far_kernel.5), channel_id=1, source_target_pairs={{0,1},{1,0},{2,3},{3,2},{4,5},{5,4},{6,7},{7,6},{8,9},{9,8},{10,11... | collective-permute-start | bytes 393224 | tf_op jit(solution)/shard_map/ppermute | solution.py:399
  38.2 2.7 %collective-permute-start.10 = (bf16[128,512]{1,0:T(8,128)(2,1)S(1)}, bf16[128,512]{1,0:T(8,128)(2,1)S(1)}, u32[]{:S(2)}, u32[]{:S(2)}) collective-permute-start(bf16[128,512]{1,0:T(8,128)(2,1)S(1)} %project_far_kernel.7), channel_id=1, source_target_pairs={{0,1},{1,0},{2,3},{3,2},{4,5},{5,4},{6,7},{7,6},{8,9},{9,8},{10,11... | collective-permute-start | bytes 393224 | tf_op jit(solution)/shard_map/ppermute | solution.py:399
  39.3 5.6 %collective-permute-start.14 = (bf16[128,512]{1,0:T(8,128)(2,1)S(1)}, bf16[128,512]{1,0:T(8,128)(2,1)S(1)}, u32[]{:S(2)}, u32[]{:S(2)}) collective-permute-start(bf16[128,512]{1,0:T(8,128)(2,1)S(1)} %add_convert_fusion.1.refs_0_), channel_id=1, source_target_pairs={{0,2},{1,3},{2,0},{3,1},{4,6},{5,7},{6,4},{7,5},{8,10},{9,11},{10,... | collective-permute-start | bytes 393224 | tf_op jit(solution)/shard_map/ppermute | solution.py:399
  41.7 3.3 %collective-permute-start.12 = (bf16[64,1024]{1,0:T(8,128)(2,1)S(1)}, bf16[64,1024]{1,0:T(8,128)(2,1)S(1)}, u32[]{:S(2)}, u32[]{:S(2)}) collective-permute-start(bf16[64,1024]{1,0:T(8,128)(2,1)S(1)} %get-tuple-element.45), channel_id=1, source_target_pairs={{0,1},{1,0},{2,3},{3,2},{4,5},{5,4},{6,7},{7,6},{8,9},{9,8},{10,11... | collective-permute-start | bytes 393224 | tf_op jit(solution)/shard_map/ppermute | solution.py:399
  41.8 3.2 %collective-permute-start.11 = (bf16[64,1024]{1,0:T(8,128)(2,1)S(1)}, bf16[64,1024]{1,0:T(8,128)(2,1)S(1)}, u32[]{:S(2)}, u32[]{:S(2)}) collective-permute-start(bf16[64,1024]{1,0:T(8,128)(2,1)S(1)} %get-tuple-element.46), channel_id=1, source_target_pairs={{0,1},{1,0},{2,3},{3,2},{4,5},{5,4},{6,7},{7,6},{8,9},{9,8},{10,11... | collective-permute-start | bytes 393224 | tf_op jit(solution)/shard_map/ppermute | solution.py:399
  42.3 5.5 %collective-permute-start.13 = (bf16[128,512]{1,0:T(8,128)(2,1)S(1)}, bf16[128,512]{1,0:T(8,128)(2,1)S(1)}, u32[]{:S(2)}, u32[]{:S(2)}) collective-permute-start(bf16[128,512]{1,0:T(8,128)(2,1)S(1)} %add_convert_fusion.refs_1_), channel_id=1, source_target_pairs={{0,2},{1,3},{2,0},{3,1},{4,6},{5,7},{6,4},{7,5},{8,10},{9,11},{10,... | collective-permute-start | bytes 393224 | tf_op jit(solution)/shard_map/ppermute | solution.py:399

commit v22 on v21

--- a/solution.py
+++ b/solution.py
@@ -152,9 +152,20 @@
     return copies
 
 
-def plain_kernel(inputs_any, queries_any, keys_any, *refs):
-    for copy in plain_copies((queries_any, keys_any, inputs_any.at[0]), refs[:2], ORDER[:2], refs[2]):
+def plain_kernel(inputs_any, queries_any, keys_any, third_ref, second_ref, pair_s, sems):
+    rows, own = pair_s.shape[1], third_ref.shape[1]
+    position = lax.axis_index("ctx")
+    columns = columns_of((position ^ 2) // 2, 2 * own)
+    copies = [
+        pltpu.make_async_copy(source.at[:, columns], pair_s.at[index], sems.at[index])
+        for index, source in enumerate((queries_any, keys_any, inputs_any.at[0]))
+    ]
+    for copy in copies:
+        copy.start()
+    for index, copy in enumerate(copies):
         copy.wait()
+        for step, out_ref in ((3, third_ref), (2, second_ref)):
+            out_ref[index * rows : (index + 1) * rows] = pair_s[index, :, columns_of((position ^ step) % 2, own)]
 
 
 def gate_kernel(inputs_any, short_any, queries_any, keys_any, *refs):
@@ -410,7 +421,7 @@
         plain_kernel,
         (streamed, queries, key_rows),
         [((3 * rows, own), half)] * 2,
-        [pltpu.SemaphoreType.DMA((6,))],
+        [pltpu.VMEM((3, rows, 2 * own), half), pltpu.SemaphoreType.DMA((3,))],
         [IN_HBM] * 3,
         PLAIN_LIMIT,
     )

time: 48.8 us -> 48.8 us (level)
  no operation moved by 1% of the time
where the time goes in v22:
time: 48.8 us; the launch traced here: 48.5 us
  starting transfers between devices  24.4 us (50%)
  Pallas kernels  12.2 us (25%)
  waiting for transfers between devices  10.2 us (21%)
  local copies, waits for them, and re-layouts  1.48 us (3%)
    ppermute x15, starting transfers between devices, swapped(): lax.ppermute(value, axis, [(source, source ^ step) for source in range(la...  24.4 us
    pallas_call x15, Pallas kernels, run_kernel(): pl.pallas_call(kernel, out_shape=[jax.ShapeDtypeStruct(shape, dtype) for...  12.2 us
    ppermute x15, waiting for transfers between devices, swapped(): lax.ppermute(value, axis, [(source, source ^ step) for source in range(la...  10.2 us
    unnamed x8, local copies, waits for them, and re-layouts  1.46 us
  transfers between devices with their start and end apart: 15, of which 8 were waited for; matrix products, arithmetic and copies ran while one was open for 0% of the time, Pallas kernels for 19%

profile of v22, /device:TPU:0, one launch (start us, length us, event | category | flops | bytes accessed | tf_op | source)
XLA Modules:
  0.0 48.5 jit_solution(12900723083031901646)
XLA Ops:
  0.0 1.1 %plain_kernel.1 = (bf16[384,256]{1,0:T(8,128)(2,1)S(1)}, bf16[384,256]{1,0:T(8,128)(2,1)S(1)}) custom-call(bf16[3,128,1024]{2,1,0:T(8,128)(2,1)} %bitcast.3, bf16[128,1024]{1,0:T(8,128)(2,1)} %queries_any.3, bf16[128,1024]{1,0:T(8,128)(2,1)} %keys_any.3), custom_call_target="tpu_custom_call" | custom-call | flops 1000000 | bytes 1048576 | tf_op jit(solution)/shard_map/plain_kernel/pallas_call | solution.py:396
  1.1 5.1 %collective-permute-start.3 = (bf16[384,256]{1,0:T(8,128)(2,1)S(1)}, bf16[384,256]{1,0:T(8,128)(2,1)S(1)}, u32[]{:S(2)}, u32[]{:S(2)}) collective-permute-start(bf16[384,256]{1,0:T(8,128)(2,1)S(1)} %get-tuple-element.29), channel_id=1, source_target_pairs={{0,12},{4,8},{8,4},{12,0},{1,13},{5,9},{9,5},{13,1},{2,14},{6,10},... | collective-permute-start | bytes 589832 | tf_op jit(solution)/shard_map/ppermute | solution.py:410
  6.2 0.7 %copy-done = bf16[3,3,1024]{2,1,0:T(4,128)(2,1)S(1)} copy-done((bf16[3,3,1024]{2,1,0:T(4,128)(2,1)S(1)}, bf16[3,3,1024]{2,1,0:T(4,128)(2,1)}, u32[]{:S(2)}) %copy-start) | copy-done | bytes 18456
  6.9 1.7 %gate_kernel.1 = (bf16[272,128]{1,0:T(8,128)(2,1)S(1)}, bf16[272,128]{1,0:T(8,128)(2,1)S(1)}, bf16[272,128]{1,0:T(8,128)(2,1)S(1)}, bf16[272,128]{1,0:T(8,128)(2...) custom-call(bf16[3,128,1024]{2,1,0:T(8,128)(2,1)} %bitcast.4, bf16[3,3,1024]{2,1,0:T(4,128)(2,1)S(1)} %copy-done, ...), custom_call_target="tpu_custom_call" | custom-call | flops 1000000 | bytes 1048576 | tf_op jit(solution)/shard_map/gate_kernel/pallas_call | solution.py:396
  8.7 0.7 %collective-permute-start.5 = (bf16[384,256]{1,0:T(8,128)(2,1)S(1)}, bf16[384,256]{1,0:T(8,128)(2,1)S(1)}, u32[]{:S(2)}, u32[]{:S(2)}) collective-permute-start(bf16[384,256]{1,0:T(8,128)(2,1)S(1)} %get-tuple-element.31), channel_id=1, source_target_pairs={{0,4},{4,0},{8,12},{12,8},{1,5},{5,1},{9,13},{13,9},{2,6},{6,2},{1... | collective-permute-start | bytes 589832 | tf_op jit(solution)/shard_map/ppermute | solution.py:410
  9.4 3.7 %collective-permute-start = (bf16[272,128]{1,0:T(8,128)(2,1)S(1)}, bf16[272,128]{1,0:T(8,128)(2,1)S(1)}, u32[]{:S(2)}, u32[]{:S(2)}) collective-permute-start(bf16[272,128]{1,0:T(8,128)(2,1)S(1)} %get-tuple-element.25), channel_id=1, source_target_pairs={{0,12},{4,8},{8,4},{12,0},{1,13},{5,9},{9,5},{13,1},{2,14},{6,10},... | collective-permute-start | bytes 208904 | tf_op jit(solution)/shard_map/ppermute | solution.py:410
  13.1 7.9 %collective-permute-start.2 = (bf16[272,128]{1,0:T(8,128)(2,1)S(1)}, bf16[272,128]{1,0:T(8,128)(2,1)S(1)}, u32[]{:S(2)}, u32[]{:S(2)}) collective-permute-start(bf16[272,128]{1,0:T(8,128)(2,1)S(1)} %get-tuple-element.27), channel_id=1, source_target_pairs={{0,4},{4,0},{8,12},{12,8},{1,5},{5,1},{9,13},{13,9},{2,6},{6,2},{1... | collective-permute-start | bytes 208904 | tf_op jit(solution)/shard_map/ppermute | solution.py:410
  21.0 0.7 %copy-done.2 = bf16[64,128]{1,0:T(8,128)(2,1)S(1)} copy-done((bf16[64,128]{1,0:T(8,128)(2,1)S(1)}, bf16[64,128]{1,0:T(8,128)(2,1)}, u32[]{:S(2)}) %copy-start.2) | copy-done | bytes 16408
  21.8 3.4 %ready_kernel.1 = (bf16[2048,256]{1,0:T(8,128)(2,1)S(1)}, bf16[1024,4096]{1,0:T(8,128)(2,1)S(1)}) custom-call(bf16[64,128]{1,0:T(8,128)(2,1)S(1)} %copy-done.2, bf16[1024,4096]{1,0:T(8,128)(2,1)} %weight_any.1), custom_call_target="tpu_custom_call" | custom-call | flops 1000000 | bytes 1048576 | tf_op jit(solution)/shard_map/ready_kernel/pallas_call | solution.py:396
  25.2 1.7 %collective-permute-done.4.second_ref = bf16[384,256]{1,0:T(8,128)(2,1)S(1)} collective-permute-done((bf16[384,256]{1,0:T(8,128)(2,1)S(1)}, bf16[384,256]{1,0:T(8,128)(2,1)S(1)}, u32[]{:S(2)}, u32[]{:S(2)}) %collective-permute-start.4) | collective-permute-done | bytes 196640 | tf_op jit(solution)/shard_map/ppermute | solution.py:410
  26.8 0.9 %weights_kernel.1 = (bf16[2,512,512]{2,1,0:T(8,128)(2,1)S(1)}, f32[512,128]{1,0:T(8,128)S(1)}, f32[512,256]{1,0:T(8,128)S(1)}) custom-call(bf16[384,256]{1,0:T(8,128)(2,1)S(1)} %collective-permute-done.3.third_ref, bf16[384,256]{1,0:T(8,128)(2,1)S(1)} %collective-permute-done.4.second_ref, bf16[384,256]{1,0:T(8,128)(2,1)S(1)} %collective-permute-done.5.near_ref, ...), custom_call_target="tpu_custom_call" | custom-call | flops 1000000 | bytes 1048576 | tf_op jit(solution)/shard_map/weights_kernel/pallas_call | solution.py:396
  27.8 1.1 %collective-permute-done.1.refs_1_ = bf16[272,128]{1,0:T(8,128)(2,1)S(1)} collective-permute-done((bf16[272,128]{1,0:T(8,128)(2,1)S(1)}, bf16[272,128]{1,0:T(8,128)(2,1)S(1)}, u32[]{:S(2)}, u32[]{:S(2)}) %collective-permute-start.1) | collective-permute-done | bytes 69664 | tf_op jit(solution)/shard_map/ppermute | solution.py:410
  28.9 1.1 %values_kernel.1 = (bf16[128,256]{1,0:T(8,128)(2,1)S(1)}, bf16[128,256]{1,0:T(8,128)(2,1)S(1)}, bf16[512,256]{1,0:T(8,128)(2,1)S(1)}) custom-call(bf16[272,128]{1,0:T(8,128)(2,1)S(1)} %collective-permute-done.refs_0_, bf16[272,128]{1,0:T(8,128)(2,1)S(1)} %collective-permute-done.1.refs_1_, bf16[272,128]{1,0:T(8,128)(2,1)S(1)} %collective-permute-done.2.refs_2_, ...), custom_call_target="tpu_custom_call" | custom-call | flops 1000000 | bytes 1048576 | tf_op jit(solution)/shard_map/values_kernel/pallas_call | solution.py:396
  29.9 0.9 %collective-permute-start.6 = (bf16[128,256]{1,0:T(8,128)(2,1)S(1)}, bf16[128,256]{1,0:T(8,128)(2,1)S(1)}, u32[]{:S(2)}, u32[]{:S(2)}) collective-permute-start(bf16[128,256]{1,0:T(8,128)(2,1)S(1)} %get-tuple-element.37), channel_id=1, source_target_pairs={{0,8},{4,12},{8,0},{12,4},{1,9},{5,13},{9,1},{13,5},{2,10},{6,14},... | collective-permute-start | bytes 196616 | tf_op jit(solution)/shard_map/ppermute | solution.py:410
  30.8 1.7 %collective-permute-start.7 = (bf16[128,256]{1,0:T(8,128)(2,1)S(1)}, bf16[128,256]{1,0:T(8,128)(2,1)S(1)}, u32[]{:S(2)}, u32[]{:S(2)}) collective-permute-start(bf16[128,256]{1,0:T(8,128)(2,1)S(1)} %get-tuple-element.38), channel_id=1, source_target_pairs={{0,12},{4,8},{8,4},{12,0},{1,13},{5,9},{9,5},{13,1},{2,14},{6,10},... | collective-permute-start | bytes 196616 | tf_op jit(solution)/shard_map/ppermute | solution.py:410
  32.8 1.0 %collective-permute-start.8 = (bf16[128,256]{1,0:T(8,128)(2,1)S(1)}, bf16[128,256]{1,0:T(8,128)(2,1)S(1)}, u32[]{:S(2)}, u32[]{:S(2)}) collective-permute-start(bf16[128,256]{1,0:T(8,128)(2,1)S(1)} %get-tuple-element.40), channel_id=1, source_target_pairs={{0,4},{4,0},{8,12},{12,8},{1,5},{5,1},{9,13},{13,9},{2,6},{6,2},{1... | collective-permute-start | bytes 196616 | tf_op jit(solution)/shard_map/ppermute | solution.py:410
  33.8 2.4 %collective-permute-done.6.second_ref = bf16[128,256]{1,0:T(8,128)(2,1)S(1)} collective-permute-done((bf16[128,256]{1,0:T(8,128)(2,1)S(1)}, bf16[128,256]{1,0:T(8,128)(2,1)S(1)}, u32[]{:S(2)}, u32[]{:S(2)}) %collective-permute-start.6) | collective-permute-done | bytes 65568 | tf_op jit(solution)/shard_map/ppermute | solution.py:410
  38.2 0.5 %collective-permute-start.10 = (bf16[128,512]{1,0:T(8,128)(2,1)S(1)}, bf16[128,512]{1,0:T(8,128)(2,1)S(1)}, u32[]{:S(2)}, u32[]{:S(2)}) collective-permute-start(bf16[128,512]{1,0:T(8,128)(2,1)S(1)} %project_far_kernel.7), channel_id=1, source_target_pairs={{0,1},{1,0},{2,3},{3,2},{4,5},{5,4},{6,7},{7,6},{8,9},{9,8},{10,11... | collective-permute-start | bytes 393224 | tf_op jit(solution)/shard_map/ppermute | solution.py:410
  39.4 1.6 %collective-permute-start.14 = (bf16[128,512]{1,0:T(8,128)(2,1)S(1)}, bf16[128,512]{1,0:T(8,128)(2,1)S(1)}, u32[]{:S(2)}, u32[]{:S(2)}) collective-permute-start(bf16[128,512]{1,0:T(8,128)(2,1)S(1)} %add_convert_fusion.1.refs_0_), channel_id=1, source_target_pairs={{0,2},{1,3},{2,0},{3,1},{4,6},{5,7},{6,4},{7,5},{8,10},{9,11},{10,... | collective-permute-start | bytes 393224 | tf_op jit(solution)/shard_map/ppermute | solution.py:410
  40.9 0.7 %project_kernel.1 = (bf16[128,1024]{1,0:T(8,128)(2,1)S(1)}, bf16[128,1024]{1,0:T(8,128)(2,1)S(1)}) custom-call(bf16[128,256]{1,0:T(8,128)(2,1)S(1)} %collective-permute-done.6.second_ref, bf16[128,256]{1,0:T(8,128)(2,1)S(1)} %collective-permute-done.7.third_ref, bf16[128,256]{1,0:T(8,128)(2,1)S(1)} %collective-permute-done.8.near_ref, ...), custom_call_target="tpu_custom_call" | custom-call | flops 1000000 | bytes 1048576 | tf_op jit(solution)/shard_map/project_kernel/pallas_call | solution.py:396
  42.8 2.1 %collective-permute-done.14.crossed_ref = bf16[128,512]{1,0:T(8,128)(2,1)S(1)} collective-permute-done((bf16[128,512]{1,0:T(8,128)(2,1)S(1)}, bf16[128,512]{1,0:T(8,128)(2,1)S(1)}, u32[]{:S(2)}, u32[]{:S(2)}) %collective-permute-start.14) | collective-permute-done | bytes 131104 | tf_op jit(solution)/shard_map/ppermute | solution.py:410
  45.0 0.7 %total_kernel.2.refs_0_ = bf16[128,1024]{1,0:T(8,128)(2,1)} custom-call(bf16[128,1024]{1,0:T(8,128)(2,1)S(1)} %get-tuple-element.43.kept_ref, bf16[64,1024]{1,0:T(8,128)(2,1)S(1)} %collective-permute-done.11.upper_ref, bf16[64,1024]{1,0:T(8,128)(2,1)S(1)} %collective-permute-done.12.lower_ref, bf16[128,512]{1,0:T(8,128)(2,1)S(1)} %collective-permute-done.14.crossed_ref), custom_call_target="tpu_custom_call" | custom-call | flops 1000000 | bytes 1048576 | tf_op jit(solution)/shard_map/total_kernel/pallas_call | solution.py:396
  45.7 2.1 %collective-permute-done.13.crossed_ref = bf16[128,512]{1,0:T(8,128)(2,1)S(1)} collective-permute-done((bf16[128,512]{1,0:T(8,128)(2,1)S(1)}, bf16[128,512]{1,0:T(8,128)(2,1)S(1)}, u32[]{:S(2)}, u32[]{:S(2)}) %collective-permute-start.13) | collective-permute-done | bytes 131104 | tf_op jit(solution)/shard_map/ppermute | solution.py:410
  47.8 0.7 %total_kernel.3 = bf16[128,1024]{1,0:T(8,128)(2,1)} custom-call(bf16[128,1024]{1,0:T(8,128)(2,1)S(1)} %get-tuple-element.43.kept_ref, bf16[64,1024]{1,0:T(8,128)(2,1)S(1)} %collective-permute-done.11.upper_ref, bf16[64,1024]{1,0:T(8,128)(2,1)S(1)} %collective-permute-done.12.lower_ref, ...), custom_call_target="tpu_custom_call", output_to_operand_aliasing={{}: (4, {})} | custom-call | flops 1000000 | bytes 1048576 | tf_op jit(solution)/shard_map/total_kernel/pallas_call | solution.py:396
  (32 shorter events, 4.0 us)
Async XLA Ops:
  0.0 26.8 %copy-start.1 = (bf16[3,3,1024]{2,1,0:T(4,128)(2,1)S(1)}, bf16[3,3,1024]{2,1,0:T(4,128)(2,1)}, u32[]{:S(2)}) copy-start(bf16[3,3,1024]{2,1,0:T(4,128)(2,1)} %refs_6_.1) | copy-start | bytes 55300
  0.0 28.9 %copy-start.3 = (f32[1024]{0:T(1024)S(1)}, f32[1024]{0:T(1024)}, u32[]{:S(2)}) copy-start(f32[1024]{0:T(1024)} %param.10) | copy-start | bytes 12292
  1.1 12.0 %collective-permute-start.3 = (bf16[384,256]{1,0:T(8,128)(2,1)S(1)}, bf16[384,256]{1,0:T(8,128)(2,1)S(1)}, u32[]{:S(2)}, u32[]{:S(2)}) collective-permute-start(bf16[384,256]{1,0:T(8,128)(2,1)S(1)} %get-tuple-element.29), channel_id=1, source_target_pairs={{0,12},{4,8},{8,4},{12,0},{1,13},{5,9},{9,5},{13,1},{2,14},{6,10},... | collective-permute-start | bytes 589832 | tf_op jit(solution)/shard_map/ppermute | solution.py:410
  6.2 20.6 %collective-permute-start.4 = (bf16[384,256]{1,0:T(8,128)(2,1)S(1)}, bf16[384,256]{1,0:T(8,128)(2,1)S(1)}, u32[]{:S(2)}, u32[]{:S(2)}) collective-permute-start(bf16[384,256]{1,0:T(8,128)(2,1)S(1)} %get-tuple-element.30), channel_id=1, source_target_pairs={{0,8},{4,12},{8,0},{12,4},{1,9},{5,13},{9,1},{13,5},{2,10},{6,14},... | collective-permute-start | bytes 589832 | tf_op jit(solution)/shard_map/ppermute | solution.py:410
  6.2 0.7 %copy-start = (bf16[3,3,1024]{2,1,0:T(4,128)(2,1)S(1)}, bf16[3,3,1024]{2,1,0:T(4,128)(2,1)}, u32[]{:S(2)}) copy-start(bf16[3,3,1024]{2,1,0:T(4,128)(2,1)} %refs_6_.1) | copy-start | bytes 55300
  8.7 18.2 %collective-permute-start.5 = (bf16[384,256]{1,0:T(8,128)(2,1)S(1)}, bf16[384,256]{1,0:T(8,128)(2,1)S(1)}, u32[]{:S(2)}, u32[]{:S(2)}) collective-permute-start(bf16[384,256]{1,0:T(8,128)(2,1)S(1)} %get-tuple-element.31), channel_id=1, source_target_pairs={{0,4},{4,0},{8,12},{12,8},{1,5},{5,1},{9,13},{13,9},{2,6},{6,2},{1... | collective-permute-start | bytes 589832 | tf_op jit(solution)/shard_map/ppermute | solution.py:410
  9.4 18.4 %collective-permute-start = (bf16[272,128]{1,0:T(8,128)(2,1)S(1)}, bf16[272,128]{1,0:T(8,128)(2,1)S(1)}, u32[]{:S(2)}, u32[]{:S(2)}) collective-permute-start(bf16[272,128]{1,0:T(8,128)(2,1)S(1)} %get-tuple-element.25), channel_id=1, source_target_pairs={{0,12},{4,8},{8,4},{12,0},{1,13},{5,9},{9,5},{13,1},{2,14},{6,10},... | collective-permute-start | bytes 208904 | tf_op jit(solution)/shard_map/ppermute | solution.py:410
  13.1 15.8 %collective-permute-start.1 = (bf16[272,128]{1,0:T(8,128)(2,1)S(1)}, bf16[272,128]{1,0:T(8,128)(2,1)S(1)}, u32[]{:S(2)}, u32[]{:S(2)}) collective-permute-start(bf16[272,128]{1,0:T(8,128)(2,1)S(1)} %get-tuple-element.26), channel_id=1, source_target_pairs={{0,8},{4,12},{8,0},{12,4},{1,9},{5,13},{9,1},{13,5},{2,10},{6,14},... | collective-permute-start | bytes 208904 | tf_op jit(solution)/shard_map/ppermute | solution.py:410
  13.1 15.8 %collective-permute-start.2 = (bf16[272,128]{1,0:T(8,128)(2,1)S(1)}, bf16[272,128]{1,0:T(8,128)(2,1)S(1)}, u32[]{:S(2)}, u32[]{:S(2)}) collective-permute-start(bf16[272,128]{1,0:T(8,128)(2,1)S(1)} %get-tuple-element.27), channel_id=1, source_target_pairs={{0,4},{4,0},{8,12},{12,8},{1,5},{5,1},{9,13},{13,9},{2,6},{6,2},{1... | collective-permute-start | bytes 208904 | tf_op jit(solution)/shard_map/ppermute | solution.py:410
  21.0 0.7 %copy-start.2 = (bf16[64,128]{1,0:T(8,128)(2,1)S(1)}, bf16[64,128]{1,0:T(8,128)(2,1)}, u32[]{:S(2)}) copy-start(bf16[64,128]{1,0:T(8,128)(2,1)} %filter_ref.1) | copy-start | bytes 49156
  29.9 6.3 %collective-permute-start.6 = (bf16[128,256]{1,0:T(8,128)(2,1)S(1)}, bf16[128,256]{1,0:T(8,128)(2,1)S(1)}, u32[]{:S(2)}, u32[]{:S(2)}) collective-permute-start(bf16[128,256]{1,0:T(8,128)(2,1)S(1)} %get-tuple-element.37), channel_id=1, source_target_pairs={{0,8},{4,12},{8,0},{12,4},{1,9},{5,13},{9,1},{13,5},{2,10},{6,14},... | collective-permute-start | bytes 196616 | tf_op jit(solution)/shard_map/ppermute | solution.py:410
  30.8 6.2 %collective-permute-start.7 = (bf16[128,256]{1,0:T(8,128)(2,1)S(1)}, bf16[128,256]{1,0:T(8,128)(2,1)S(1)}, u32[]{:S(2)}, u32[]{:S(2)}) collective-permute-start(bf16[128,256]{1,0:T(8,128)(2,1)S(1)} %get-tuple-element.38), channel_id=1, source_target_pairs={{0,12},{4,8},{8,4},{12,0},{1,13},{5,9},{9,5},{13,1},{2,14},{6,10},... | collective-permute-start | bytes 196616 | tf_op jit(solution)/shard_map/ppermute | solution.py:410
  32.8 4.9 %collective-permute-start.8 = (bf16[128,256]{1,0:T(8,128)(2,1)S(1)}, bf16[128,256]{1,0:T(8,128)(2,1)S(1)}, u32[]{:S(2)}, u32[]{:S(2)}) collective-permute-start(bf16[128,256]{1,0:T(8,128)(2,1)S(1)} %get-tuple-element.40), channel_id=1, source_target_pairs={{0,4},{4,0},{8,12},{12,8},{1,5},{5,1},{9,13},{13,9},{2,6},{6,2},{1... | collective-permute-start | bytes 196616 | tf_op jit(solution)/shard_map/ppermute | solution.py:410
  37.9 1.4 %collective-permute-start.9 = (bf16[128,512]{1,0:T(8,128)(2,1)S(1)}, bf16[128,512]{1,0:T(8,128)(2,1)S(1)}, u32[]{:S(2)}, u32[]{:S(2)}) collective-permute-start(bf16[128,512]{1,0:T(8,128)(2,1)S(1)} %project_far_kernel.5), channel_id=1, source_target_pairs={{0,1},{1,0},{2,3},{3,2},{4,5},{5,4},{6,7},{7,6},{8,9},{9,8},{10,11... | collective-permute-start | bytes 393224 | tf_op jit(solution)/shard_map/ppermute | solution.py:410
  38.2 2.7 %collective-permute-start.10 = (bf16[128,512]{1,0:T(8,128)(2,1)S(1)}, bf16[128,512]{1,0:T(8,128)(2,1)S(1)}, u32[]{:S(2)}, u32[]{:S(2)}) collective-permute-start(bf16[128,512]{1,0:T(8,128)(2,1)S(1)} %project_far_kernel.7), channel_id=1, source_target_pairs={{0,1},{1,0},{2,3},{3,2},{4,5},{5,4},{6,7},{7,6},{8,9},{9,8},{10,11... | collective-permute-start | bytes 393224 | tf_op jit(solution)/shard_map/ppermute | solution.py:410
  39.4 5.6 %collective-permute-start.14 = (bf16[128,512]{1,0:T(8,128)(2,1)S(1)}, bf16[128,512]{1,0:T(8,128)(2,1)S(1)}, u32[]{:S(2)}, u32[]{:S(2)}) collective-permute-start(bf16[128,512]{1,0:T(8,128)(2,1)S(1)} %add_convert_fusion.1.refs_0_), channel_id=1, source_target_pairs={{0,2},{1,3},{2,0},{3,1},{4,6},{5,7},{6,4},{7,5},{8,10},{9,11},{10,... | collective-permute-start | bytes 393224 | tf_op jit(solution)/shard_map/ppermute | solution.py:410
  41.7 3.2 %collective-permute-start.12 = (bf16[64,1024]{1,0:T(8,128)(2,1)S(1)}, bf16[64,1024]{1,0:T(8,128)(2,1)S(1)}, u32[]{:S(2)}, u32[]{:S(2)}) collective-permute-start(bf16[64,1024]{1,0:T(8,128)(2,1)S(1)} %get-tuple-element.45), channel_id=1, source_target_pairs={{0,1},{1,0},{2,3},{3,2},{4,5},{5,4},{6,7},{7,6},{8,9},{9,8},{10,11... | collective-permute-start | bytes 393224 | tf_op jit(solution)/shard_map/ppermute | solution.py:410
  41.8 3.2 %collective-permute-start.11 = (bf16[64,1024]{1,0:T(8,128)(2,1)S(1)}, bf16[64,1024]{1,0:T(8,128)(2,1)S(1)}, u32[]{:S(2)}, u32[]{:S(2)}) collective-permute-start(bf16[64,1024]{1,0:T(8,128)(2,1)S(1)} %get-tuple-element.46), channel_id=1, source_target_pairs={{0,1},{1,0},{2,3},{3,2},{4,5},{5,4},{6,7},{7,6},{8,9},{9,8},{10,11... | collective-permute-start | bytes 393224 | tf_op jit(solution)/shard_map/ppermute | solution.py:410
  42.3 5.5 %collective-permute-start.13 = (bf16[128,512]{1,0:T(8,128)(2,1)S(1)}, bf16[128,512]{1,0:T(8,128)(2,1)S(1)}, u32[]{:S(2)}, u32[]{:S(2)}) collective-permute-start(bf16[128,512]{1,0:T(8,128)(2,1)S(1)} %add_convert_fusion.refs_1_), channel_id=1, source_target_pairs={{0,2},{1,3},{2,0},{3,1},{4,6},{5,7},{6,4},{7,5},{8,10},{9,11},{10,... | collective-permute-start | bytes 393224 | tf_op jit(solution)/shard_map/ppermute | solution.py:410

commit v23 on v21

--- a/solution.py
+++ b/solution.py
@@ -294,9 +294,10 @@
             filtered = jnp.where(lane == group, mixed[group * rows : (group + 1) * rows], filtered)
         for block in range(count):
             filtered_s[block * rows : (block + 1) * rows, columns] = filtered[:, block * chunk : (block + 1) * chunk]
-    value_ref[...] = (
-        feature_ref[...] * (filtered_s[...] + gain * gate_s[rows:].astype(jnp.float32))
-    ).astype(jnp.bfloat16)
+    for block in range(count):
+        here = slice(block * rows, (block + 1) * rows)
+        gate = gate_s[(block + 1) * rows : (block + 2) * rows].astype(jnp.float32)
+        value_ref[here] = (feature_ref[here] * (filtered_s[here] + gain * gate)).astype(jnp.bfloat16)
     for step, out_ref in ((3, third_ref), (2, second_ref)):
         mix_rows(position ^ step, weight_ref, total_ref, value_ref, out_ref)
 

time: 48.8 us -> 48.8 us (level)
  no operation moved by 1% of the time
where the time goes in v23:
time: 48.8 us; the launch traced here: 48.5 us
  starting transfers between devices  24.4 us (50%)
  Pallas kernels  12.2 us (25%)
  waiting for transfers between devices  10.2 us (21%)
  local copies, waits for them, and re-layouts  1.48 us (3%)
    ppermute x15, starting transfers between devices, swapped(): lax.ppermute(value, axis, [(source, source ^ step) for source in range(la...  24.4 us
    pallas_call x15, Pallas kernels, run_kernel(): pl.pallas_call(kernel, out_shape=[jax.ShapeDtypeStruct(shape, dtype) for...  12.2 us
    ppermute x15, waiting for transfers between devices, swapped(): lax.ppermute(value, axis, [(source, source ^ step) for source in range(la...  10.2 us
    unnamed x8, local copies, waits for them, and re-layouts  1.46 us
  transfers between devices with their start and end apart: 15, of which 8 were waited for; matrix products, arithmetic and copies ran while one was open for 0% of the time, Pallas kernels for 19%

profile of v23, /device:TPU:0, one launch (start us, length us, event | category | flops | bytes accessed | tf_op | source)
XLA Modules:
  0.0 48.5 jit_solution(12353467685451998763)
XLA Ops:
  0.0 1.1 %plain_kernel.1 = (bf16[384,256]{1,0:T(8,128)(2,1)S(1)}, bf16[384,256]{1,0:T(8,128)(2,1)S(1)}) custom-call(bf16[3,128,1024]{2,1,0:T(8,128)(2,1)} %bitcast.3, bf16[128,1024]{1,0:T(8,128)(2,1)} %queries_any.3, bf16[128,1024]{1,0:T(8,128)(2,1)} %keys_any.3), custom_call_target="tpu_custom_call" | custom-call | flops 1000000 | bytes 1048576 | tf_op jit(solution)/shard_map/plain_kernel/pallas_call | solution.py:386
  1.1 5.1 %collective-permute-start.3 = (bf16[384,256]{1,0:T(8,128)(2,1)S(1)}, bf16[384,256]{1,0:T(8,128)(2,1)S(1)}, u32[]{:S(2)}, u32[]{:S(2)}) collective-permute-start(bf16[384,256]{1,0:T(8,128)(2,1)S(1)} %get-tuple-element.29), channel_id=1, source_target_pairs={{0,12},{4,8},{8,4},{12,0},{1,13},{5,9},{9,5},{13,1},{2,14},{6,10},... | collective-permute-start | bytes 589832 | tf_op jit(solution)/shard_map/ppermute | solution.py:400
  6.2 0.7 %copy-done = bf16[3,3,1024]{2,1,0:T(4,128)(2,1)S(1)} copy-done((bf16[3,3,1024]{2,1,0:T(4,128)(2,1)S(1)}, bf16[3,3,1024]{2,1,0:T(4,128)(2,1)}, u32[]{:S(2)}) %copy-start) | copy-done | bytes 18456
  6.9 1.7 %gate_kernel.1 = (bf16[272,128]{1,0:T(8,128)(2,1)S(1)}, bf16[272,128]{1,0:T(8,128)(2,1)S(1)}, bf16[272,128]{1,0:T(8,128)(2,1)S(1)}, bf16[272,128]{1,0:T(8,128)(2...) custom-call(bf16[3,128,1024]{2,1,0:T(8,128)(2,1)} %bitcast.4, bf16[3,3,1024]{2,1,0:T(4,128)(2,1)S(1)} %copy-done, ...), custom_call_target="tpu_custom_call" | custom-call | flops 1000000 | bytes 1048576 | tf_op jit(solution)/shard_map/gate_kernel/pallas_call | solution.py:386
  8.6 0.7 %collective-permute-start.5 = (bf16[384,256]{1,0:T(8,128)(2,1)S(1)}, bf16[384,256]{1,0:T(8,128)(2,1)S(1)}, u32[]{:S(2)}, u32[]{:S(2)}) collective-permute-start(bf16[384,256]{1,0:T(8,128)(2,1)S(1)} %get-tuple-element.31), channel_id=1, source_target_pairs={{0,4},{4,0},{8,12},{12,8},{1,5},{5,1},{9,13},{13,9},{2,6},{6,2},{1... | collective-permute-start | bytes 589832 | tf_op jit(solution)/shard_map/ppermute | solution.py:400
  9.3 3.7 %collective-permute-start = (bf16[272,128]{1,0:T(8,128)(2,1)S(1)}, bf16[272,128]{1,0:T(8,128)(2,1)S(1)}, u32[]{:S(2)}, u32[]{:S(2)}) collective-permute-start(bf16[272,128]{1,0:T(8,128)(2,1)S(1)} %get-tuple-element.25), channel_id=1, source_target_pairs={{0,12},{4,8},{8,4},{12,0},{1,13},{5,9},{9,5},{13,1},{2,14},{6,10},... | collective-permute-start | bytes 208904 | tf_op jit(solution)/shard_map/ppermute | solution.py:400
  13.1 7.9 %collective-permute-start.2 = (bf16[272,128]{1,0:T(8,128)(2,1)S(1)}, bf16[272,128]{1,0:T(8,128)(2,1)S(1)}, u32[]{:S(2)}, u32[]{:S(2)}) collective-permute-start(bf16[272,128]{1,0:T(8,128)(2,1)S(1)} %get-tuple-element.27), channel_id=1, source_target_pairs={{0,4},{4,0},{8,12},{12,8},{1,5},{5,1},{9,13},{13,9},{2,6},{6,2},{1... | collective-permute-start | bytes 208904 | tf_op jit(solution)/shard_map/ppermute | solution.py:400
  21.0 0.7 %copy-done.2 = bf16[64,128]{1,0:T(8,128)(2,1)S(1)} copy-done((bf16[64,128]{1,0:T(8,128)(2,1)S(1)}, bf16[64,128]{1,0:T(8,128)(2,1)}, u32[]{:S(2)}) %copy-start.2) | copy-done | bytes 16408
  21.7 3.4 %ready_kernel.1 = (bf16[2048,256]{1,0:T(8,128)(2,1)S(1)}, bf16[1024,4096]{1,0:T(8,128)(2,1)S(1)}) custom-call(bf16[64,128]{1,0:T(8,128)(2,1)S(1)} %copy-done.2, bf16[1024,4096]{1,0:T(8,128)(2,1)} %weight_any.1), custom_call_target="tpu_custom_call" | custom-call | flops 1000000 | bytes 1048576 | tf_op jit(solution)/shard_map/ready_kernel/pallas_call | solution.py:386
  25.2 1.7 %collective-permute-done.4.second_ref = bf16[384,256]{1,0:T(8,128)(2,1)S(1)} collective-permute-done((bf16[384,256]{1,0:T(8,128)(2,1)S(1)}, bf16[384,256]{1,0:T(8,128)(2,1)S(1)}, u32[]{:S(2)}, u32[]{:S(2)}) %collective-permute-start.4) | collective-permute-done | bytes 196640 | tf_op jit(solution)/shard_map/ppermute | solution.py:400
  26.8 0.9 %weights_kernel.1 = (bf16[2,512,512]{2,1,0:T(8,128)(2,1)S(1)}, f32[512,128]{1,0:T(8,128)S(1)}, f32[512,256]{1,0:T(8,128)S(1)}) custom-call(bf16[384,256]{1,0:T(8,128)(2,1)S(1)} %collective-permute-done.3.third_ref, bf16[384,256]{1,0:T(8,128)(2,1)S(1)} %collective-permute-done.4.second_ref, bf16[384,256]{1,0:T(8,128)(2,1)S(1)} %collective-permute-done.5.near_ref, ...), custom_call_target="tpu_custom_call" | custom-call | flops 1000000 | bytes 1048576 | tf_op jit(solution)/shard_map/weights_kernel/pallas_call | solution.py:386
  27.8 1.1 %collective-permute-done.1.refs_1_ = bf16[272,128]{1,0:T(8,128)(2,1)S(1)} collective-permute-done((bf16[272,128]{1,0:T(8,128)(2,1)S(1)}, bf16[272,128]{1,0:T(8,128)(2,1)S(1)}, u32[]{:S(2)}, u32[]{:S(2)}) %collective-permute-start.1) | collective-permute-done | bytes 69664 | tf_op jit(solution)/shard_map/ppermute | solution.py:400
  28.9 1.1 %values_kernel.1 = (bf16[128,256]{1,0:T(8,128)(2,1)S(1)}, bf16[128,256]{1,0:T(8,128)(2,1)S(1)}, bf16[512,256]{1,0:T(8,128)(2,1)S(1)}) custom-call(bf16[272,128]{1,0:T(8,128)(2,1)S(1)} %collective-permute-done.refs_0_, bf16[272,128]{1,0:T(8,128)(2,1)S(1)} %collective-permute-done.1.refs_1_, bf16[272,128]{1,0:T(8,128)(2,1)S(1)} %collective-permute-done.2.refs_2_, ...), custom_call_target="tpu_custom_call" | custom-call | flops 1000000 | bytes 1048576 | tf_op jit(solution)/shard_map/values_kernel/pallas_call | solution.py:386
  29.9 0.9 %collective-permute-start.6 = (bf16[128,256]{1,0:T(8,128)(2,1)S(1)}, bf16[128,256]{1,0:T(8,128)(2,1)S(1)}, u32[]{:S(2)}, u32[]{:S(2)}) collective-permute-start(bf16[128,256]{1,0:T(8,128)(2,1)S(1)} %get-tuple-element.37), channel_id=1, source_target_pairs={{0,8},{4,12},{8,0},{12,4},{1,9},{5,13},{9,1},{13,5},{2,10},{6,14},... | collective-permute-start | bytes 196616 | tf_op jit(solution)/shard_map/ppermute | solution.py:400
  30.8 1.7 %collective-permute-start.7 = (bf16[128,256]{1,0:T(8,128)(2,1)S(1)}, bf16[128,256]{1,0:T(8,128)(2,1)S(1)}, u32[]{:S(2)}, u32[]{:S(2)}) collective-permute-start(bf16[128,256]{1,0:T(8,128)(2,1)S(1)} %get-tuple-element.38), channel_id=1, source_target_pairs={{0,12},{4,8},{8,4},{12,0},{1,13},{5,9},{9,5},{13,1},{2,14},{6,10},... | collective-permute-start | bytes 196616 | tf_op jit(solution)/shard_map/ppermute | solution.py:400
  32.8 1.0 %collective-permute-start.8 = (bf16[128,256]{1,0:T(8,128)(2,1)S(1)}, bf16[128,256]{1,0:T(8,128)(2,1)S(1)}, u32[]{:S(2)}, u32[]{:S(2)}) collective-permute-start(bf16[128,256]{1,0:T(8,128)(2,1)S(1)} %get-tuple-element.40), channel_id=1, source_target_pairs={{0,4},{4,0},{8,12},{12,8},{1,5},{5,1},{9,13},{13,9},{2,6},{6,2},{1... | collective-permute-start | bytes 196616 | tf_op jit(solution)/shard_map/ppermute | solution.py:400
  33.8 2.4 %collective-permute-done.6.second_ref = bf16[128,256]{1,0:T(8,128)(2,1)S(1)} collective-permute-done((bf16[128,256]{1,0:T(8,128)(2,1)S(1)}, bf16[128,256]{1,0:T(8,128)(2,1)S(1)}, u32[]{:S(2)}, u32[]{:S(2)}) %collective-permute-start.6) | collective-permute-done | bytes 65568 | tf_op jit(solution)/shard_map/ppermute | solution.py:400
  38.2 0.5 %collective-permute-start.10 = (bf16[128,512]{1,0:T(8,128)(2,1)S(1)}, bf16[128,512]{1,0:T(8,128)(2,1)S(1)}, u32[]{:S(2)}, u32[]{:S(2)}) collective-permute-start(bf16[128,512]{1,0:T(8,128)(2,1)S(1)} %project_far_kernel.7), channel_id=1, source_target_pairs={{0,1},{1,0},{2,3},{3,2},{4,5},{5,4},{6,7},{7,6},{8,9},{9,8},{10,11... | collective-permute-start | bytes 393224 | tf_op jit(solution)/shard_map/ppermute | solution.py:400
  39.3 1.6 %collective-permute-start.14 = (bf16[128,512]{1,0:T(8,128)(2,1)S(1)}, bf16[128,512]{1,0:T(8,128)(2,1)S(1)}, u32[]{:S(2)}, u32[]{:S(2)}) collective-permute-start(bf16[128,512]{1,0:T(8,128)(2,1)S(1)} %add_convert_fusion.1.refs_0_), channel_id=1, source_target_pairs={{0,2},{1,3},{2,0},{3,1},{4,6},{5,7},{6,4},{7,5},{8,10},{9,11},{10,... | collective-permute-start | bytes 393224 | tf_op jit(solution)/shard_map/ppermute | solution.py:400
  40.9 0.7 %project_kernel.1 = (bf16[128,1024]{1,0:T(8,128)(2,1)S(1)}, bf16[128,1024]{1,0:T(8,128)(2,1)S(1)}) custom-call(bf16[128,256]{1,0:T(8,128)(2,1)S(1)} %collective-permute-done.6.second_ref, bf16[128,256]{1,0:T(8,128)(2,1)S(1)} %collective-permute-done.7.third_ref, bf16[128,256]{1,0:T(8,128)(2,1)S(1)} %collective-permute-done.8.near_ref, ...), custom_call_target="tpu_custom_call" | custom-call | flops 1000000 | bytes 1048576 | tf_op jit(solution)/shard_map/project_kernel/pallas_call | solution.py:386
  42.8 2.1 %collective-permute-done.14.crossed_ref = bf16[128,512]{1,0:T(8,128)(2,1)S(1)} collective-permute-done((bf16[128,512]{1,0:T(8,128)(2,1)S(1)}, bf16[128,512]{1,0:T(8,128)(2,1)S(1)}, u32[]{:S(2)}, u32[]{:S(2)}) %collective-permute-start.14) | collective-permute-done | bytes 131104 | tf_op jit(solution)/shard_map/ppermute | solution.py:400
  45.0 0.7 %total_kernel.2.refs_0_ = bf16[128,1024]{1,0:T(8,128)(2,1)} custom-call(bf16[128,1024]{1,0:T(8,128)(2,1)S(1)} %get-tuple-element.43.kept_ref, bf16[64,1024]{1,0:T(8,128)(2,1)S(1)} %collective-permute-done.11.upper_ref, bf16[64,1024]{1,0:T(8,128)(2,1)S(1)} %collective-permute-done.12.lower_ref, bf16[128,512]{1,0:T(8,128)(2,1)S(1)} %collective-permute-done.14.crossed_ref), custom_call_target="tpu_custom_call" | custom-call | flops 1000000 | bytes 1048576 | tf_op jit(solution)/shard_map/total_kernel/pallas_call | solution.py:386
  45.7 2.1 %collective-permute-done.13.crossed_ref = bf16[128,512]{1,0:T(8,128)(2,1)S(1)} collective-permute-done((bf16[128,512]{1,0:T(8,128)(2,1)S(1)}, bf16[128,512]{1,0:T(8,128)(2,1)S(1)}, u32[]{:S(2)}, u32[]{:S(2)}) %collective-permute-start.13) | collective-permute-done | bytes 131104 | tf_op jit(solution)/shard_map/ppermute | solution.py:400
  47.8 0.7 %total_kernel.3 = bf16[128,1024]{1,0:T(8,128)(2,1)} custom-call(bf16[128,1024]{1,0:T(8,128)(2,1)S(1)} %get-tuple-element.43.kept_ref, bf16[64,1024]{1,0:T(8,128)(2,1)S(1)} %collective-permute-done.11.upper_ref, bf16[64,1024]{1,0:T(8,128)(2,1)S(1)} %collective-permute-done.12.lower_ref, ...), custom_call_target="tpu_custom_call", output_to_operand_aliasing={{}: (4, {})} | custom-call | flops 1000000 | bytes 1048576 | tf_op jit(solution)/shard_map/total_kernel/pallas_call | solution.py:386
  (32 shorter events, 4.0 us)
Async XLA Ops:
  0.0 26.8 %copy-start.1 = (bf16[3,3,1024]{2,1,0:T(4,128)(2,1)S(1)}, bf16[3,3,1024]{2,1,0:T(4,128)(2,1)}, u32[]{:S(2)}) copy-start(bf16[3,3,1024]{2,1,0:T(4,128)(2,1)} %refs_6_.1) | copy-start | bytes 55300
  0.0 28.9 %copy-start.3 = (f32[1024]{0:T(1024)S(1)}, f32[1024]{0:T(1024)}, u32[]{:S(2)}) copy-start(f32[1024]{0:T(1024)} %param.10) | copy-start | bytes 12292
  1.1 12.0 %collective-permute-start.3 = (bf16[384,256]{1,0:T(8,128)(2,1)S(1)}, bf16[384,256]{1,0:T(8,128)(2,1)S(1)}, u32[]{:S(2)}, u32[]{:S(2)}) collective-permute-start(bf16[384,256]{1,0:T(8,128)(2,1)S(1)} %get-tuple-element.29), channel_id=1, source_target_pairs={{0,12},{4,8},{8,4},{12,0},{1,13},{5,9},{9,5},{13,1},{2,14},{6,10},... | collective-permute-start | bytes 589832 | tf_op jit(solution)/shard_map/ppermute | solution.py:400
  6.2 20.6 %collective-permute-start.4 = (bf16[384,256]{1,0:T(8,128)(2,1)S(1)}, bf16[384,256]{1,0:T(8,128)(2,1)S(1)}, u32[]{:S(2)}, u32[]{:S(2)}) collective-permute-start(bf16[384,256]{1,0:T(8,128)(2,1)S(1)} %get-tuple-element.30), channel_id=1, source_target_pairs={{0,8},{4,12},{8,0},{12,4},{1,9},{5,13},{9,1},{13,5},{2,10},{6,14},... | collective-permute-start | bytes 589832 | tf_op jit(solution)/shard_map/ppermute | solution.py:400
  6.2 0.7 %copy-start = (bf16[3,3,1024]{2,1,0:T(4,128)(2,1)S(1)}, bf16[3,3,1024]{2,1,0:T(4,128)(2,1)}, u32[]{:S(2)}) copy-start(bf16[3,3,1024]{2,1,0:T(4,128)(2,1)} %refs_6_.1) | copy-start | bytes 55300
  8.6 18.2 %collective-permute-start.5 = (bf16[384,256]{1,0:T(8,128)(2,1)S(1)}, bf16[384,256]{1,0:T(8,128)(2,1)S(1)}, u32[]{:S(2)}, u32[]{:S(2)}) collective-permute-start(bf16[384,256]{1,0:T(8,128)(2,1)S(1)} %get-tuple-element.31), channel_id=1, source_target_pairs={{0,4},{4,0},{8,12},{12,8},{1,5},{5,1},{9,13},{13,9},{2,6},{6,2},{1... | collective-permute-start | bytes 589832 | tf_op jit(solution)/shard_map/ppermute | solution.py:400
  9.3 18.4 %collective-permute-start = (bf16[272,128]{1,0:T(8,128)(2,1)S(1)}, bf16[272,128]{1,0:T(8,128)(2,1)S(1)}, u32[]{:S(2)}, u32[]{:S(2)}) collective-permute-start(bf16[272,128]{1,0:T(8,128)(2,1)S(1)} %get-tuple-element.25), channel_id=1, source_target_pairs={{0,12},{4,8},{8,4},{12,0},{1,13},{5,9},{9,5},{13,1},{2,14},{6,10},... | collective-permute-start | bytes 208904 | tf_op jit(solution)/shard_map/ppermute | solution.py:400
  13.1 15.8 %collective-permute-start.1 = (bf16[272,128]{1,0:T(8,128)(2,1)S(1)}, bf16[272,128]{1,0:T(8,128)(2,1)S(1)}, u32[]{:S(2)}, u32[]{:S(2)}) collective-permute-start(bf16[272,128]{1,0:T(8,128)(2,1)S(1)} %get-tuple-element.26), channel_id=1, source_target_pairs={{0,8},{4,12},{8,0},{12,4},{1,9},{5,13},{9,1},{13,5},{2,10},{6,14},... | collective-permute-start | bytes 208904 | tf_op jit(solution)/shard_map/ppermute | solution.py:400
  13.1 15.8 %collective-permute-start.2 = (bf16[272,128]{1,0:T(8,128)(2,1)S(1)}, bf16[272,128]{1,0:T(8,128)(2,1)S(1)}, u32[]{:S(2)}, u32[]{:S(2)}) collective-permute-start(bf16[272,128]{1,0:T(8,128)(2,1)S(1)} %get-tuple-element.27), channel_id=1, source_target_pairs={{0,4},{4,0},{8,12},{12,8},{1,5},{5,1},{9,13},{13,9},{2,6},{6,2},{1... | collective-permute-start | bytes 208904 | tf_op jit(solution)/shard_map/ppermute | solution.py:400
  21.0 0.7 %copy-start.2 = (bf16[64,128]{1,0:T(8,128)(2,1)S(1)}, bf16[64,128]{1,0:T(8,128)(2,1)}, u32[]{:S(2)}) copy-start(bf16[64,128]{1,0:T(8,128)(2,1)} %filter_ref.1) | copy-start | bytes 49156
  29.9 6.3 %collective-permute-start.6 = (bf16[128,256]{1,0:T(8,128)(2,1)S(1)}, bf16[128,256]{1,0:T(8,128)(2,1)S(1)}, u32[]{:S(2)}, u32[]{:S(2)}) collective-permute-start(bf16[128,256]{1,0:T(8,128)(2,1)S(1)} %get-tuple-element.37), channel_id=1, source_target_pairs={{0,8},{4,12},{8,0},{12,4},{1,9},{5,13},{9,1},{13,5},{2,10},{6,14},... | collective-permute-start | bytes 196616 | tf_op jit(solution)/shard_map/ppermute | solution.py:400
  30.8 6.2 %collective-permute-start.7 = (bf16[128,256]{1,0:T(8,128)(2,1)S(1)}, bf16[128,256]{1,0:T(8,128)(2,1)S(1)}, u32[]{:S(2)}, u32[]{:S(2)}) collective-permute-start(bf16[128,256]{1,0:T(8,128)(2,1)S(1)} %get-tuple-element.38), channel_id=1, source_target_pairs={{0,12},{4,8},{8,4},{12,0},{1,13},{5,9},{9,5},{13,1},{2,14},{6,10},... | collective-permute-start | bytes 196616 | tf_op jit(solution)/shard_map/ppermute | solution.py:400
  32.8 4.9 %collective-permute-start.8 = (bf16[128,256]{1,0:T(8,128)(2,1)S(1)}, bf16[128,256]{1,0:T(8,128)(2,1)S(1)}, u32[]{:S(2)}, u32[]{:S(2)}) collective-permute-start(bf16[128,256]{1,0:T(8,128)(2,1)S(1)} %get-tuple-element.40), channel_id=1, source_target_pairs={{0,4},{4,0},{8,12},{12,8},{1,5},{5,1},{9,13},{13,9},{2,6},{6,2},{1... | collective-permute-start | bytes 196616 | tf_op jit(solution)/shard_map/ppermute | solution.py:400
  37.9 1.4 %collective-permute-start.9 = (bf16[128,512]{1,0:T(8,128)(2,1)S(1)}, bf16[128,512]{1,0:T(8,128)(2,1)S(1)}, u32[]{:S(2)}, u32[]{:S(2)}) collective-permute-start(bf16[128,512]{1,0:T(8,128)(2,1)S(1)} %project_far_kernel.5), channel_id=1, source_target_pairs={{0,1},{1,0},{2,3},{3,2},{4,5},{5,4},{6,7},{7,6},{8,9},{9,8},{10,11... | collective-permute-start | bytes 393224 | tf_op jit(solution)/shard_map/ppermute | solution.py:400
  38.2 2.7 %collective-permute-start.10 = (bf16[128,512]{1,0:T(8,128)(2,1)S(1)}, bf16[128,512]{1,0:T(8,128)(2,1)S(1)}, u32[]{:S(2)}, u32[]{:S(2)}) collective-permute-start(bf16[128,512]{1,0:T(8,128)(2,1)S(1)} %project_far_kernel.7), channel_id=1, source_target_pairs={{0,1},{1,0},{2,3},{3,2},{4,5},{5,4},{6,7},{7,6},{8,9},{9,8},{10,11... | collective-permute-start | bytes 393224 | tf_op jit(solution)/shard_map/ppermute | solution.py:400
  39.3 5.6 %collective-permute-start.14 = (bf16[128,512]{1,0:T(8,128)(2,1)S(1)}, bf16[128,512]{1,0:T(8,128)(2,1)S(1)}, u32[]{:S(2)}, u32[]{:S(2)}) collective-permute-start(bf16[128,512]{1,0:T(8,128)(2,1)S(1)} %add_convert_fusion.1.refs_0_), channel_id=1, source_target_pairs={{0,2},{1,3},{2,0},{3,1},{4,6},{5,7},{6,4},{7,5},{8,10},{9,11},{10,... | collective-permute-start | bytes 393224 | tf_op jit(solution)/shard_map/ppermute | solution.py:400
  41.7 3.3 %collective-permute-start.12 = (bf16[64,1024]{1,0:T(8,128)(2,1)S(1)}, bf16[64,1024]{1,0:T(8,128)(2,1)S(1)}, u32[]{:S(2)}, u32[]{:S(2)}) collective-permute-start(bf16[64,1024]{1,0:T(8,128)(2,1)S(1)} %get-tuple-element.45), channel_id=1, source_target_pairs={{0,1},{1,0},{2,3},{3,2},{4,5},{5,4},{6,7},{7,6},{8,9},{9,8},{10,11... | collective-permute-start | bytes 393224 | tf_op jit(solution)/shard_map/ppermute | solution.py:400
  41.8 3.2 %collective-permute-start.11 = (bf16[64,1024]{1,0:T(8,128)(2,1)S(1)}, bf16[64,1024]{1,0:T(8,128)(2,1)S(1)}, u32[]{:S(2)}, u32[]{:S(2)}) collective-permute-start(bf16[64,1024]{1,0:T(8,128)(2,1)S(1)} %get-tuple-element.46), channel_id=1, source_target_pairs={{0,1},{1,0},{2,3},{3,2},{4,5},{5,4},{6,7},{7,6},{8,9},{9,8},{10,11... | collective-permute-start | bytes 393224 | tf_op jit(solution)/shard_map/ppermute | solution.py:400
  42.3 5.5 %collective-permute-start.13 = (bf16[128,512]{1,0:T(8,128)(2,1)S(1)}, bf16[128,512]{1,0:T(8,128)(2,1)S(1)}, u32[]{:S(2)}, u32[]{:S(2)}) collective-permute-start(bf16[128,512]{1,0:T(8,128)(2,1)S(1)} %add_convert_fusion.refs_1_), channel_id=1, source_target_pairs={{0,2},{1,3},{2,0},{3,1},{4,6},{5,7},{6,4},{7,5},{8,10},{9,11},{10,... | collective-permute-start | bytes 393224 | tf_op jit(solution)/shard_map/ppermute | solution.py:400
